TPU v7x, 128 devices: a whole 4x4x4 slice. The times are simulated.
128 devices in a mesh: row: 8 (over y, x_hi), col: 16 (over z, x_lo, core).
Axes of the slice: x: 4 (x_hi: 2, x_lo: 2; x = x_hi * 2 + x_lo), y: 4, z: 4, core: 2. Of those that a mesh axis runs over, the one named last changes fastest.
Arguments:
- orbitals: bfloat16 [1024, 20480], P(('row', 'col')), may hold values from -1.078125 to 1.078125
- targets: bfloat16 [128, 20480], P(('row', 'col')), may hold values from -0.0390625 to 0.0390625
- kernel: float32 [20480, 16, 1280], P('row', 'col'), may hold values from -6 to 6
- tile_owner: int32 [8, 16, 8, 16], P('row', None, None, 'col'), may hold values from 0 to 1
Outputs:
- applied: float32 [20480, 128], P(('row', 'col'))
All inputs are finite; a program needn't handle non-finite values.
Results may differ from a plain program's by a relative error of at most 0.0003.
Values may be sent and summed in bfloat16 or wider, within the bound.
No kernel may reach another device: no remote copies, remote signals or barrier semaphores. Data moves between devices by JAX's collectives and lax.ppermute only.
A program may use at most 192 MiB of HBM per device.

v0:
```python
import jax
import jax.numpy as jnp
from jax import lax
from jax.sharding import PartitionSpec as P


def spread_points(orb_points, tgt_points):
    row_orb, row_tgt = (
        lax.all_gather(orb_points, "col", axis=1, tiled=True),
        lax.all_gather(tgt_points, "col", axis=1, tiled=True),
    )
    col_orb, col_tgt = (
        lax.all_gather(orb_points, "row", axis=1, tiled=True),
        lax.all_gather(tgt_points, "row", axis=1, tiled=True),
    )
    return (row_orb, row_tgt, col_orb, col_tgt)


def local(orbitals, targets, kernel, tile_owner):
    rows_grid = lax.axis_size("row")
    cols_grid = lax.axis_size("col")
    fine_width = kernel.shape[2] // rows_grid
    orb_points, tgt_points = (
        lax.all_to_all(orbitals, ("row", "col"), split_axis=1, concat_axis=0, tiled=True),
        lax.all_to_all(targets, ("row", "col"), split_axis=1, concat_axis=0, tiled=True),
    )
    row_orb, row_tgt, col_orb, col_tgt = spread_points(orb_points, tgt_points)
    gram_tile = jnp.einsum("bi,bj->ij", row_orb, col_orb, preferred_element_type=jnp.float32)
    weighted = (gram_tile * kernel.reshape(gram_tile.shape)).reshape(
        cols_grid, fine_width, rows_grid, fine_width
    )
    owned_flags = tile_owner.reshape(cols_grid, rows_grid).astype(jnp.float32)
    same_col = lax.broadcasted_iota(jnp.int32, (cols_grid, rows_grid), 0) == lax.axis_index("col")
    same_row = lax.broadcasted_iota(jnp.int32, (cols_grid, rows_grid), 1) == lax.axis_index("row")
    mirrored = owned_flags - jnp.where(same_col & same_row, 1.0, 0.0).astype(jnp.float32)
    row_terms = (weighted * owned_flags[:, None, :, None]).reshape(gram_tile.shape)
    col_terms = (weighted * mirrored[:, None, :, None]).reshape(gram_tile.shape)
    row_out = jnp.dot(row_terms, col_tgt.astype(jnp.float32).T, precision=lax.Precision.HIGHEST)
    col_out = lax.dot_general(
        col_terms,
        row_tgt.astype(jnp.float32),
        (((0,), (1,)), ((), ())),
        precision=lax.Precision.HIGHEST,
    )
    row_share = lax.psum_scatter(row_out, "col", scatter_dimension=0, tiled=True)
    col_share = lax.psum_scatter(col_out, "row", scatter_dimension=0, tiled=True)
    return row_share + col_share


def solution(mesh):
    in_specs = (
        P(("row", "col"), None),
        P(("row", "col"), None),
        P("row", "col", None),
        P("row", None, None, "col"),
    )
    out_specs = P(("row", "col"), None)
    return jax.shard_map(local, mesh=mesh, in_specs=in_specs, out_specs=out_specs, check_vma=False)
```

profile of v0, /device:TPU:0, one launch (start us, length us, event | category | flops | bytes accessed | tf_op | source)
XLA Modules:
  0.0 310.4 jit_solution(10408937306897510373)
XLA Ops:
  6.5 0.0 all-gather.7.cloned.1.call-start
  6.5 1.6 all_to_all.26
  8.1 0.3 copy.12
  8.4 24.5 %all_to_all.36 = bf16[8,128,160]{2,0,1:T(8,128)(2,1)S(1)} all-to-all(bf16[8,128,160]{2,0,1:T(8,128)(2,1)S(1)} %copy.12), channel_id=1, replica_groups=mesh['row'=8,'col'=16] {'row','col'}, dimensions={1} | all-to-all | bytes 655360 | tf_op jit(solution)/shard_map/all_to_all | solution.py:24
  32.9 0.9 copy.13
  33.8 0.0 all-gather.7.cloned.1.call-update
  33.9 0.0 all-gather.5.cloned.1.call-start
  33.9 0.7 all-gather.5.cloned.1.call-update
  34.6 1.1 reduce
  35.7 0.8 all_to_all.33
  36.5 4.5 %all-to-all-start.1 = ((bf16[1,128,160]{2,0,1:T(2,128)(2,1)}), bf16[1,128,160]{2,0,1:T(2,128)(2,1)S(1)}, u32[]{:S(2)}, u32[]{:S(2)}) async-start(bf16[1,128,160]{2,0,1:T(2,128)(2,1)} %all_to_all.33), calls=%async_computation.1 | async-start | bytes 262144 | tf_op jit(solution)/shard_map/all_to_all | solution.py:25
  41.1 0.0 reduce-scatter.5.cloned.1.call-start
  41.2 0.8 select_subtract_fusion
  41.9 0.1 copy.19
  42.0 8.4 %mul.29 = f32[16,160,8,160]{3,2,1,0:T(8,128)} broadcast(f32[16,8]{1,0:T(8,128)S(1)} %copy.19), dimensions={0,2} | broadcast | bytes 13107712 | tf_op jit(solution)/shard_map/mul | solution.py:37
  50.4 19.9 %mul.30 = f32[2560,1280]{1,0:T(8,128)} reshape(f32[16,160,8,160]{3,2,1,0:T(8,128)} %mul.29) | data formatting | bytes 26214400 | tf_op jit(solution)/shard_map/mul | solution.py:37
  70.3 0.0 all-to-all-done.1
  70.3 0.1 copy.18
  70.4 25.4 %all-gather.1 = bf16[1,128,2560]{1,2,0:T(8,128)(2,1)S(1)} all-gather(bf16[1,128,160]{1,2,0:T(8,128)(2,1)S(1)} %copy.18), channel_id=3, replica_groups=mesh['row'=8,'col'=16] {'col'}, dimensions={2}, use_global_device_ids=true | all-gather | bytes 696320 | tf_op jit(solution)/shard_map/all_gather | solution.py:10
  95.8 0.0 all-gather.7.cloned.1.call-done
  95.8 34.8 %all-gather.5.cloned.1.call-done = bf16[1024,2560]{0,1:T(8,128)(2,1)} async-done(((bf16[1024,160]{0,1:T(8,128)(2,1)}), bf16[1024,2560]{0,1:T(8,128)(2,1)}) %all-gather.5.cloned.1.call-update) | async-done | bytes 5242896 | tf_op jit(solution)/shard_map/all_gather | solution.py:9
  130.7 13.1 %convolution_multiply_fusion = f32[2560,1280]{1,0:T(8,128)S(1)} fusion(bf16[1024,2560]{0,1:T(8,128)(2,1)} %all-gather.5.cloned.1.call-done, bf16[1024,1280]{0,1:T(8,128)(2,1)} %all-gather.7.cloned.1.call-done, f32[2560,1,1280]{2,1,0:T(1,128)} %param.6), kind=kOutput, calls=%fused_computation | convolution fusion | flops 6714163200 | bytes 34078720 | tf_op jit(solution)/shard_map/bi,bj->ij/dot_general | solution.py:28
  143.8 0.0 copy-start
  143.8 4.6 %copy-done = f32[2560,1280]{1,0:T(8,128)} copy-done((f32[2560,1280]{1,0:T(8,128)}, f32[2560,1280]{1,0:T(8,128)S(1)}, u32[]{:S(2)}) %copy-start) | copy-done | bytes 13107224
  148.4 0.0 copy-start.1
  148.4 14.6 %fusion = f32[1280,128]{1,0:T(8,128)} fusion(f32[2560,1280]{1,0:T(8,128)S(1)} %convolution_multiply_fusion, f32[2560,1280]{1,0:T(8,128)} %mul.30, bf16[1,128,2560]{1,2,0:T(8,128)(2,1)S(1)} %all-gather.1), kind=kOutput, calls=%fused_computation.1 | convolution fusion | flops 5036441600 | bytes 27525120 | tf_op jit(solution)/shard_map/dot_general | solution.py:39
  163.1 0.0 reduce-scatter.5.cloned.1.call-update
  163.1 0.0 reduce-scatter.3.cloned.1.call-start
  163.1 0.0 copy-done.1
  163.2 0.1 copy.16
  163.2 8.4 %mul.26 = f32[16,160,8,160]{3,2,1,0:T(8,128)} broadcast(f32[16,8]{1,0:T(8,128)S(1)} %copy.16), dimensions={0,2} | broadcast | bytes 13107712 | tf_op jit(solution)/shard_map/mul | solution.py:36
  171.6 19.9 %mul.27 = f32[2560,1280]{1,0:T(8,128)} reshape(f32[16,160,8,160]{3,2,1,0:T(8,128)} %mul.26) | data formatting | bytes 26214400 | tf_op jit(solution)/shard_map/mul | solution.py:36
  191.5 35.8 %all-gather = bf16[1,128,1280]{1,2,0:T(8,128)(2,1)S(1)} all-gather(bf16[1,128,160]{1,2,0:T(8,128)(2,1)S(1)} %copy.18), channel_id=2, replica_groups=mesh['row'=8,'col'=16] {'row'}, dimensions={2}, use_global_device_ids=true | all-gather | bytes 368640 | tf_op jit(solution)/shard_map/all_gather | solution.py:14
  227.3 12.8 %fusion.2 = f32[2560,128]{1,0:T(8,128)} fusion(f32[2560,1280]{1,0:T(8,128)} %copy-done, f32[2560,1280]{1,0:T(8,128)} %mul.27, bf16[1,128,1280]{1,2,0:T(8,128)(2,1)S(1)} %all-gather), kind=kOutput, calls=%fused_computation.3 | convolution fusion | flops 5036441600 | bytes 27852800 | tf_op jit(solution)/shard_map/dot_general | solution.py:38
  240.1 0.0 reduce-scatter.3.cloned.1.call-update
  240.1 0.0 reduce-scatter.5.cloned.1.call-done
  240.2 62.2 %reduce-scatter.3.cloned.1.call-done = f32[160,128]{1,0:T(8,128)} async-done(((f32[2560,128]{1,0:T(8,128)}), f32[160,128]{1,0:T(8,128)}) %reduce-scatter.3.cloned.1.call-update) | async-done | bytes 81936 | tf_op jit(solution)/shard_map/reduce_scatter | solution.py:45
  302.3 1.6 add.7
  (3 shorter events, 0.0 us)
Async XLA Ops:
  6.5 89.3 %all-gather.7.cloned.1.call-start = ((), (), s32[]{:S(2)}) async-start(), calls=%async_computation.5 | async-start | bytes 2949120 | tf_op jit(solution)/shard_map/all_gather | solution.py:13
  33.9 96.8 %all-gather.5.cloned.1.call-start = ((), (), s32[]{:S(2)}) async-start(), calls=%async_computation.4 | async-start | bytes 5570560 | tf_op jit(solution)/shard_map/all_gather | solution.py:9
  36.5 33.8 %all-to-all-start.1 = ((bf16[1,128,160]{2,0,1:T(2,128)(2,1)}), bf16[1,128,160]{2,0,1:T(2,128)(2,1)S(1)}, u32[]{:S(2)}, u32[]{:S(2)}) async-start(bf16[1,128,160]{2,0,1:T(2,128)(2,1)} %all_to_all.33), calls=%async_computation.1 | async-start | bytes 262144 | tf_op jit(solution)/shard_map/all_to_all | solution.py:25
  41.1 199.1 %reduce-scatter.5.cloned.1.call-start = ((), (), s32[]{:S(2)}) async-start(), calls=%async_computation.7 | async-start | bytes 737280 | tf_op jit(solution)/shard_map/reduce_scatter | solution.py:46
  143.8 4.6 %copy-start = (f32[2560,1280]{1,0:T(8,128)}, f32[2560,1280]{1,0:T(8,128)S(1)}, u32[]{:S(2)}) copy-start(f32[2560,1280]{1,0:T(8,128)S(1)} %convolution_multiply_fusion) | copy-start | bytes 39321604
  148.4 14.7 %copy-start.1 = (s32[1,16,8,1]{1,3,2,0:T(1,128)S(1)}, s32[1,16,8,1]{1,3,2,0:T(1,128)}, u32[]{:S(2)}) copy-start(s32[1,16,8,1]{1,3,2,0:T(1,128)} %param.7) | copy-start | bytes 1540
  163.1 139.2 %reduce-scatter.3.cloned.1.call-start = ((), (), s32[]{:S(2)}) async-start(), calls=%async_computation.6 | async-start | bytes 1392640 | tf_op jit(solution)/shard_map/reduce_scatter | solution.py:45
Sparse Core Ops, SparseCore 0:
  34.0 57.4 all-gather.6
  93.2 37.4 all-gather.4
  163.2 70.7 reduce-scatter.4
  240.3 62.0 reduce-scatter.2
where the time goes:
time: 312 us; the launch traced here: 310 us
  waiting for transfers between devices  97.8 us (31%)
  blocking collectives  85.7 us (27%)
  local copies, waits for them, and re-layouts  65.1 us (21%)
  matrix products  40.5 us (13%)
  between operations  13.2 us (4%)
  starting transfers between devices  4.67 us (1%)
  other arithmetic  3.46 us (1%)
    reduce_scatter x1, waiting for transfers between devices, local(): lax.psum_scatter(row_out, 'col', scatter_dimension=0, tiled=True)  62.2 us
    all_gather x1, blocking collectives, spread_points(): lax.all_gather(tgt_points, 'row', axis=1, tiled=True)  35.8 us
    all_gather x1, waiting for transfers between devices, spread_points(): lax.all_gather(orb_points, 'col', axis=1, tiled=True)  34.8 us
    mul x2, local copies, waits for them, and re-layouts, local(): weighted * owned_flags[:, None, :, None]  28.3 us
    mul x2, local copies, waits for them, and re-layouts, local(): col_terms = (weighted * mirrored[:, None, :, None]).reshape(gram_tile.shape)  28.3 us
    all_gather x1, blocking collectives, spread_points(): lax.all_gather(tgt_points, 'col', axis=1, tiled=True)  25.4 us
    all_to_all x1, blocking collectives, local(): lax.all_to_all(orbitals, ('row', 'col'), split_axis=1, concat_axis=0, til...  24.5 us
    dot_general x1, matrix products, local(): lax.dot_general(col_terms, row_tgt.astype(jnp.float32), (((0,), (1,)), ((...  14.6 us
  transfers between devices with their start and end apart: 5, of which 2 were waited for; matrix products, arithmetic and copies ran while one was open for 23% of the time, Pallas kernels for 0%

commit v1 on v0

v1 whole, which is shorter than its diff:
```python
import jax
import jax.numpy as jnp
from jax import lax
from jax.experimental import pallas as pl
from jax.experimental.pallas import tpu as pltpu
from jax.sharding import PartitionSpec as P

N_ROW, N_COL, FB = 8, 16, 160
ROW_PTS, COL_PTS = N_COL * FB, N_ROW * FB
AXES = ("row", "col")
Z_ORDER = (2, 1, 3, 0)
Y_ORDER = (0, 3, 1, 2)
TILE, CHUNK = 640, 256
BF, F32 = jnp.bfloat16, jnp.float32


def moved(y=0, xh=0, z=0, xl=0, k=0):
    pairs = []
    for i in range(N_ROW * N_COL):
        r, c = divmod(i, N_COL)
        r2 = ((r // 2 + y) % 4) * 2 + (r % 2 + xh) % 2
        c2 = ((c // 4 + z) % 4) * 4 + ((c // 2 % 2 + xl) % 2) * 2 + (c % 2 + k) % 2
        pairs.append((i, r2 * N_COL + c2))
    return pairs


def send(x, **steps):
    return lax.ppermute(x, AXES, moved(**steps))


def spread_kernel(xh_ref, own_ref, other_ref, out_ref):
    first = xh_ref[0] == 0
    own, other = own_ref[...], other_ref[...]
    both = jnp.concatenate([jnp.where(first, own, other), jnp.where(first, other, own)], axis=0)
    for c in range(N_COL):
        out_ref[c] = jnp.concatenate(
            [both[:, (r * N_COL + c) * FB : (r * N_COL + c + 1) * FB] for r in range(N_ROW)], axis=1
        )


def spread_points(own, other, xh):
    return pl.pallas_call(
        spread_kernel,
        out_shape=jax.ShapeDtypeStruct((N_COL, 16, COL_PTS), BF),
        in_specs=[
            pl.BlockSpec(memory_space=pltpu.SMEM),
            pl.BlockSpec(memory_space=pltpu.VMEM),
            pl.BlockSpec(memory_space=pltpu.VMEM),
        ],
        out_specs=pl.BlockSpec(memory_space=pltpu.VMEM),
        compiler_params=pltpu.CompilerParams(vmem_limit_bytes=32 * 2**20),
        name="spread",
    )(xh, own, other)


def nt(a, b):
    return lax.dot_general(a, b, (((1,), (1,)), ((), ())), preferred_element_type=F32)


def tile_kernel(
    me, rows, own, a_dn, b_dn, a_up, b_up, a_far, b_far, kern, owned, mirrored, tcol, trow,
    far_out, up_out, dn_out, own_out, c0, c1, c2, c3,
    cols, rows_t, row_acc, col_acc, col_turn, sems,
):
    s, n = pl.program_id(0), pl.program_id(1)
    y = me[1]

    @pl.when((s == 0) & (n == 0))
    def _():
        parts = ((own, 0, 16), (a_dn, 16, 8), (b_dn, 24, 8), (a_up, 32, 8), (b_up, 40, 8), (a_far, 48, 8), (b_far, 56, 8))
        copies = [
            pltpu.make_async_copy(src, cols.at[pl.ds(at, size)], sems.at[i])
            for i, (src, at, size) in enumerate(parts)
        ]
        for copy in copies:
            copy.start()
        for copy in copies:
            copy.wait()
        col_acc[...] = jnp.zeros_like(col_acc)

    @pl.when(n == 0)
    def _():
        for j, step in enumerate(Y_ORDER):
            part = rows[:, lax.rem(y + step, 4)].reshape(256, TILE)
            rows_t[:, 256 * j : 256 * (j + 1)] = part.T
        row_acc[...] = jnp.zeros_like(row_acc)

    at = pl.ds(pl.multiple_of(n * CHUNK, CHUNK), CHUNK)
    gram = jnp.dot(rows_t[...], cols[:, :, at].reshape(1024, CHUNK), preferred_element_type=F32)

    def spread(ref):
        return jnp.concatenate([jnp.broadcast_to(ref[0, i : i + 1, :], (FB, CHUNK)) for i in range(4)], axis=0)

    weighted = gram * kern[...] * spread(owned)
    high = weighted.astype(BF)
    low = (weighted - high.astype(F32)).astype(BF)
    row_acc[...] += nt(high, tcol[...]) + nt(low, tcol[...])
    keep = spread(mirrored).astype(BF)
    col_acc[:, at] += jnp.dot(trow[...], high * keep, preferred_element_type=F32) + jnp.dot(
        trow[...], low * keep, preferred_element_type=F32
    )

    for i, out in enumerate((far_out, up_out, dn_out, own_out)):

        @pl.when((s == i) & (n == 4))
        def _(out=out):
            out[...] = row_acc[...]

    @pl.when((s == 3) & (n == 4))
    def _():
        turned = col_acc[...].T
        for q in range(4):
            col_turn[q] = turned[q * 320 : (q + 1) * 320]
        for d, out in enumerate((c0, c1, c2, c3)):
            out[...] = col_turn[lax.rem(y + d, 4)]


def tile_products(me, rows, col_parts, kern, owned, mirrored, tcol, trow):
    def ztile(s, me):
        step = jnp.where(s == 0, 2, jnp.where(s == 1, 1, jnp.where(s == 2, 3, 0)))
        return lax.rem(me[0] + step, 4)

    hold = lambda s, n, me: (0, 0)
    spec = pltpu.PrefetchScalarGridSpec(
        num_scalar_prefetch=1,
        grid=(4, 5),
        in_specs=[pl.BlockSpec((16, 4, 16, TILE), lambda s, n, me: (0, 0, 0, ztile(s, me)))]
        + [pl.BlockSpec(memory_space=pl.ANY)] * 7
        + [
            pl.BlockSpec((TILE, CHUNK), lambda s, n, me: (ztile(s, me), n)),
            pl.BlockSpec((1, 4, CHUNK), lambda s, n, me: (ztile(s, me), 0, n)),
            pl.BlockSpec((1, 4, CHUNK), lambda s, n, me: (ztile(s, me), 0, n)),
            pl.BlockSpec((128, CHUNK), lambda s, n, me: (0, n)),
            pl.BlockSpec((128, TILE), lambda s, n, me: (0, ztile(s, me))),
        ],
        out_specs=[pl.BlockSpec((TILE, 128), hold)] * 4 + [pl.BlockSpec((320, 128), hold)] * 4,
        scratch_shapes=[
            pltpu.VMEM((64, 16, COL_PTS), BF),
            pltpu.VMEM((TILE, 1024), BF),
            pltpu.VMEM((TILE, 128), F32),
            pltpu.VMEM((128, COL_PTS), F32),
            pltpu.VMEM((4, 320, 128), F32),
            pltpu.SemaphoreType.DMA((7,)),
        ],
    )
    return pl.pallas_call(
        tile_kernel,
        grid_spec=spec,
        out_shape=[jax.ShapeDtypeStruct((TILE, 128), F32)] * 4 + [jax.ShapeDtypeStruct((320, 128), F32)] * 4,
        compiler_params=pltpu.CompilerParams(
            vmem_limit_bytes=40 * 2**20, dimension_semantics=("arbitrary", "arbitrary")
        ),
        cost_estimate=pl.CostEstimate(flops=10_000_000_000, bytes_accessed=24_000_000, transcendentals=0),
        name="tile_products",
    )(me, rows, *col_parts, kern, owned, mirrored, tcol, trow)


def pick(blocks, index):
    return lax.dynamic_index_in_dim(blocks, index, 0, keepdims=False)


def local(orbitals, targets, kernel, tile_owner):
    r, c = lax.axis_index("row"), lax.axis_index("col")
    y, xh = r // 2, r % 2
    z, xl, k = c // 4, c // 2 % 2, c % 2

    other = send(orbitals, xh=1)
    row_part = lax.all_to_all(orbitals, "row", split_axis=1, concat_axis=0, tiled=True)
    rows = lax.all_gather(row_part, "col", axis=0, tiled=True).reshape(16, 4, 16, ROW_PTS)

    col_part = spread_points(orbitals, other, xh.reshape(1))
    own = lax.all_to_all(col_part, "col", split_axis=0, concat_axis=0, tiled=True)
    half_a, half_b = own[:8], own[8:]
    a_dn, b_up = send(half_a, y=1), send(half_b, y=3)
    b_dn, a_up = send(half_b, y=1), send(half_a, y=3)
    a_far, b_far = send(a_dn, y=1), send(b_up, y=3)

    trow = lax.all_to_all(targets, "row", split_axis=1, concat_axis=0, tiled=True)
    trow = lax.all_gather(trow, "col", axis=0, tiled=True)
    trow = trow.reshape(N_COL, N_ROW, ROW_PTS).transpose(1, 0, 2).reshape(128, ROW_PTS)
    tcol = targets.reshape(N_ROW, N_COL, FB).transpose(1, 0, 2).reshape(N_COL, COL_PTS)
    tcol = lax.all_to_all(tcol, "col", split_axis=0, concat_axis=0, tiled=True)
    tcol = lax.all_gather(tcol, "row", axis=0, tiled=True)

    flags = tile_owner.reshape(N_COL, N_ROW).astype(F32)
    here = (lax.broadcasted_iota(jnp.int32, flags.shape, 0) == c) & (
        lax.broadcasted_iota(jnp.int32, flags.shape, 1) == r
    )
    owned = jnp.repeat(flags, FB, axis=1).reshape(4, 4, COL_PTS)
    mirrored = jnp.repeat(jnp.where(here, 0.0, flags), FB, axis=1).reshape(4, 4, COL_PTS)

    far, up, dn, mine, c0, c1, c2, c3 = tile_products(
        jnp.stack([z, y]).astype(jnp.int32),
        rows, (own, a_dn, b_dn, a_up, b_up, a_far, b_far),
        kernel.reshape(ROW_PTS, COL_PTS), owned, mirrored, tcol, trow,
    )
    row_sum = mine + send(far, z=2) + send(up, z=1) + send(dn, z=3)
    col_sum = c0 + send(c2, y=2) + send(c1, y=1) + send(c3, y=3)

    by_core = row_sum.reshape(2, 2, FB, 128).transpose(1, 0, 2, 3)
    row_sum = pick(by_core, k) + send(pick(by_core, 1 - k), k=1)
    row_share = pick(row_sum, xl) + send(pick(row_sum, 1 - xl), xl=1)
    col_sum = col_sum.reshape(2, FB, 128)
    col_share = pick(col_sum, xh) + send(pick(col_sum, 1 - xh), xh=1)
    return row_share + col_share


def solution(mesh):
    in_specs = (
        P(("row", "col"), None),
        P(("row", "col"), None),
        P("row", "col", None),
        P("row", None, None, "col"),
    )
    out_specs = P(("row", "col"), None)
    return jax.shard_map(local, mesh=mesh, in_specs=in_specs, out_specs=out_specs, check_vma=False)
```

time: 312 us -> 223 us (0.71)
  waiting for transfers between devices: 97.8 us -> 36.9 us
  local copies, waits for them, and re-layouts: 65.1 us -> 24.2 us
  matrix products: 40.5 us -> 0 us
  Pallas kernels: 0 us -> 34.5 us
  starting transfers between devices: 4.67 us -> 31.4 us
  blocking collectives: 85.7 us -> 74.7 us
    reduce_scatter x2 -> x0, waiting for transfers between devices: 62.2 us -> none  [the longest x1 62.2 us: local(): lax.psum_scatter(row_out, 'col', scatter_dimension=0, tiled=True)]
    mul x4 -> x0, local copies, waits for them, and re-layouts: 56.6 us -> none  [the longest x2 28.3 us: local(): weighted * owned_flags[:, None, :, None]]
    dot_general x3 -> x0, matrix products: 40.5 us -> none  [the longest x1 14.6 us: local(): lax.dot_general(col_terms, row_tgt.astype(jnp.float32), (((0,), (1,)), ((...]
    all_gather x2 -> x1, waiting for transfers between devices: 34.8 us -> 0.01 us  [local(): lax.all_gather(row_part, 'col', axis=0, tiled=True)]
    pallas_call x0 -> x2, Pallas kernels: none -> 34.5 us  [the longest x1 33.4 us: tile_products(): pl.pallas_call(tile_kernel, grid_spec=spec, out_shape=[jax.ShapeDtypeStru...]
    ppermute x0 -> x16, waiting for transfers between devices: none -> 21.9 us  [send(): return lax.ppermute(x, AXES, moved(**steps))]
    ppermute x0 -> x16, starting transfers between devices: none -> 18.5 us  [send(): return lax.ppermute(x, AXES, moved(**steps))]
    unnamed x4 -> x29, local copies, waits for them, and re-layouts: 4.63 us -> 21.7 us
  transfers between devices with their start and end apart: 5 -> 20, of which waited for: 2 -> 7; matrix products, arithmetic and copies ran while one was open for 23% -> 9% of each run, Pallas kernels for 0% -> 1%
where the time goes in v1:
time: 223 us; the launch traced here: 221 us
  blocking collectives  74.7 us (33%)
  waiting for transfers between devices  36.9 us (17%)
  Pallas kernels  34.5 us (15%)
  starting transfers between devices  31.4 us (14%)
  local copies, waits for them, and re-layouts  24.2 us (11%)
  between operations  13.7 us (6%)
  other arithmetic  6.01 us (3%)
    all_gather x1, blocking collectives, local(): tcol = lax.all_gather(tcol, 'row', axis=0, tiled=True)  35.1 us
    pallas_call x1, Pallas kernels, tile_products(): pl.pallas_call(tile_kernel, grid_spec=spec, out_shape=[jax.ShapeDtypeStru...  33.4 us
    all_gather x1, blocking collectives, local(): trow = lax.all_gather(trow, 'col', axis=0, tiled=True)  22.9 us
    ppermute x16, waiting for transfers between devices, send(): return lax.ppermute(x, AXES, moved(**steps))  21.9 us
    unnamed x29, local copies, waits for them, and re-layouts  21.7 us
    ppermute x16, starting transfers between devices, send(): return lax.ppermute(x, AXES, moved(**steps))  18.5 us
    all_to_all x1, blocking collectives, local(): lax.all_to_all(orbitals, 'row', split_axis=1, concat_axis=0, tiled=True)  16.7 us
    all_to_all x1, waiting for transfers between devices, local(): lax.all_to_all(col_part, 'col', split_axis=0, concat_axis=0, tiled=True)  15 us
  transfers between devices with their start and end apart: 20, of which 7 were waited for; matrix products, arithmetic and copies ran while one was open for 9% of the time, Pallas kernels for 1%

profile of v1, /device:TPU:0, one launch (start us, length us, event | category | flops | bytes accessed | tf_op | source)
XLA Modules:
  0.0 221.4 jit_solution(1967513854287367767)
XLA Ops:
  6.5 16.7 %all_to_all.53 = bf16[8,8,2560]{2,0,1:T(8,128)(2,1)} all-to-all(bf16[8,8,2560]{2,0,1:T(8,128)(2,1)} %bitcast.45), channel_id=1, replica_groups=mesh['row'=8,'col'=16] {'row'}, dimensions={1} | all-to-all | bytes 655360 | tf_op jit(solution)/shard_map/all_to_all | solution.py:168
  23.3 0.8 collective-permute-start
  24.1 8.8 %collective-permute-done.other_ref = bf16[8,20480]{1,0:T(8,128)(2,1)S(1)} collective-permute-done((bf16[8,20480]{1,0:T(8,128)(2,1)}, bf16[8,20480]{1,0:T(8,128)(2,1)S(1)}, u32[]{:S(2)}, u32[]{:S(2)}) %collective-permute-start) | collective-permute-done | bytes 327712 | tf_op jit(solution)/shard_map/ppermute | solution.py:28
  32.9 1.0 copy-done
  33.9 1.1 spread.1
  35.0 5.5 %all-to-all-start.1 = ((bf16[16,16,1280]{2,1,0:T(8,128)(2,1)}), bf16[16,16,1280]{2,1,0:T(8,128)(2,1)S(1)}, u32[]{:S(2)}, u32[]{:S(2)}) async-start(bf16[16,16,1280]{2,1,0:T(8,128)(2,1)} %spread.1), calls=%async_computation.1 | async-start | bytes 1310720 | tf_op jit(solution)/shard_map/all_to_all | solution.py:172
  40.5 0.5 broadcast.11
  41.0 1.7 reduce.2
  42.8 0.6 reshape.57
  43.4 0.8 and_select_fusion
  44.2 15.0 %all-to-all-done.1.own = bf16[16,16,1280]{2,1,0:T(8,128)(2,1)S(1)} async-done(((bf16[16,16,1280]{2,1,0:T(8,128)(2,1)}), bf16[16,16,1280]{2,1,0:T(8,128)(2,1)S(1)}, u32[]{:S(2)}, u32[]{:S(2)}) %all-to-all-start.1) | async-done | bytes 655392 | tf_op jit(solution)/shard_map/all_to_all | solution.py:172
  59.2 4.0 %all-to-all-start.3 = ((bf16[8,2,1280]{2,1,0:T(2,128)(2,1)}), bf16[8,2,1280]{2,1,0:T(2,128)(2,1)S(1)}, u32[]{:S(2)}, u32[]{:S(2)}) async-start(bf16[8,2,1280]{2,1,0:T(2,128)(2,1)} %reshape.57), calls=%async_computation.3 | async-start | bytes 81920 | tf_op jit(solution)/shard_map/all_to_all | solution.py:178
  63.2 0.8 fusion.1
  64.0 2.0 collective-permute-start.1
  66.0 1.2 collective-permute-start.4
  67.2 0.7 convert_bitcast_fusion
  68.0 1.1 reduce
  69.7 0.9 reduce.1
  70.5 0.6 reshape.55
  71.5 10.3 %copy.32 = f32[2560,1,1280]{2,0,1:T(8,128)} copy(f32[2560,1,1280]{2,1,0:T(1,128)} %param.6) | data formatting | bytes 26214400
  81.8 3.5 %all-to-all-start.2 = ((bf16[16,2,640]{2,1,0:T(2,128)(2,1)}), bf16[16,2,640]{2,1,0:T(2,128)(2,1)S(1)}, u32[]{:S(2)}, u32[]{:S(2)}) async-start(bf16[16,2,640]{2,1,0:T(2,128)(2,1)} %reshape.55), calls=%async_computation.2 | async-start | bytes 81920 | tf_op jit(solution)/shard_map/all_to_all | solution.py:182
  85.3 0.9 collective-permute-start.2
  86.2 2.4 %collective-permute-start.3 = (bf16[8,16,1280]{2,1,0:T(8,128)(2,1)S(1)}, bf16[8,16,1280]{2,1,0:T(8,128)(2,1)S(1)}, u32[]{:S(2)}, u32[]{:S(2)}) collective-permute-start(bf16[8,16,1280]{2,1,0:T(8,128)(2,1)S(1)} %get-tuple-element.22), channel_id=1, source_target_pairs={{0,96},{1,97},{2,98},{3,99},{4,100},{5,101},{6,102},{7,103},{8,104... | collective-permute-start | bytes 983048 | tf_op jit(solution)/shard_map/ppermute | solution.py:28
  88.7 3.2 %collective-permute-start.6 = (bf16[8,16,1280]{2,1,0:T(8,128)(2,1)S(1)}, bf16[8,16,1280]{2,1,0:T(8,128)(2,1)}, u32[]{:S(2)}, u32[]{:S(2)}) collective-permute-start(bf16[8,16,1280]{2,1,0:T(8,128)(2,1)S(1)} %collective-permute-done.4.b_up), channel_id=1, source_target_pairs={{0,96},{1,97},{2,98},{3,99},{4,100},{5,101},{6,102},{7,103},{8,104... | collective-permute-start | bytes 983048 | tf_op jit(solution)/shard_map/ppermute | solution.py:28
  91.9 22.9 %all-gather.1 = bf16[1,128,2560]{2,1,0:T(8,128)(2,1)S(1)} all-gather(bf16[1,8,2560]{2,1,0:T(8,128)(2,1)S(1)} %copy.27), channel_id=3, replica_groups=mesh['row'=8,'col'=16] {'col'}, dimensions={1}, use_global_device_ids=true | all-gather | bytes 696320 | tf_op jit(solution)/shard_map/all_gather | solution.py:179
  114.8 0.2 copy.28
  115.1 35.1 %all-gather = bf16[128,1,1280]{2,0,1:T(8,128)(2,1)S(1)} all-gather(bf16[16,1,1280]{2,0,1:T(8,128)(2,1)S(1)} %copy.26), channel_id=2, replica_groups=mesh['row'=8,'col'=16] {'row'}, dimensions={0}, use_global_device_ids=true | all-gather | bytes 368640 | tf_op jit(solution)/shard_map/all_gather | solution.py:183
  150.1 0.7 copy-done.6
  150.9 0.7 copy-done.8
  151.6 2.5 %copy-done.1 = bf16[1024,2560]{1,0:T(8,128)(2,1)S(1)} copy-done((bf16[1024,2560]{1,0:T(8,128)(2,1)S(1)}, bf16[1024,2560]{1,0:T(8,128)(2,1)}, u32[]{:S(2)}) %copy-start.1) | copy-done | bytes 5242904
  154.1 1.0 copy-done.3
  155.1 1.0 copy-done.5
  156.1 1.0 copy-done.7
  157.0 1.0 copy-done.9
  158.0 33.4 %tile_products.1 = (f32[640,128]{1,0:T(8,128)S(1)}, f32[640,128]{1,0:T(8,128)S(1)}, f32[640,128]{1,0:T(8,128)S(1)}, f32[640,128]{1,0:T(8,128)S(1)}, f32[320,128]...) custom-call(s32[2]{0:T(128)S(1)} %pad_add_fusion.me, ...), custom_call_target="tpu_custom_call" | custom-call | flops 10000000000 | bytes 24000000 | tf_op jit(solution)/shard_map/tile_products/pallas_call | solution.py:146
  191.4 0.7 copy-done.10
  192.1 0.7 copy-done.11
  192.7 1.0 collective-permute-start.8
  193.7 2.2 %collective-permute-start.9 = (f32[640,128]{1,0:T(8,128)S(1)}, f32[640,128]{1,0:T(8,128)S(1)}, u32[]{:S(2)}, u32[]{:S(2)}) collective-permute-start(f32[640,128]{1,0:T(8,128)S(1)} %get-tuple-element.16), channel_id=1, source_target_pairs={{0,12},{1,13},{2,14},{3,15},{4,0},{5,1},{6,2},{7,3},{8,4},{9,5},{1... | collective-permute-start | bytes 983048 | tf_op jit(solution)/shard_map/ppermute | solution.py:28
  196.0 1.5 collective-permute-start.13
  197.4 4.4 %collective-permute-done.7 = f32[640,128]{1,0:T(8,128)S(1)} collective-permute-done((f32[640,128]{1,0:T(8,128)S(1)}, f32[640,128]{1,0:T(8,128)S(1)}, u32[]{:S(2)}, u32[]{:S(2)}) %collective-permute-start.7) | collective-permute-done | bytes 327712 | tf_op jit(solution)/shard_map/ppermute | solution.py:28
  201.8 0.9 collective-permute-start.14
  202.7 2.2 collective-permute-done.8
  205.1 2.0 collective-permute-done.14
  207.2 2.1 collective-permute-start.15
  209.5 3.8 %collective-permute-done.15 = f32[160,128]{1,0:T(8,128)S(1)} collective-permute-done((f32[160,128]{1,0:T(8,128)S(1)}, f32[160,128]{1,0:T(8,128)S(1)}, u32[]{:S(2)}, u32[]{:S(2)}) %collective-permute-start.15) | collective-permute-done | bytes 81952 | tf_op jit(solution)/shard_map/ppermute | solution.py:28
  213.2 0.7 collective-permute-done.11
  213.9 0.7 fusion
  (56 shorter events, 1.4 us)
Async XLA Ops:
  6.5 145.1 %all-gather.4.cloned.1.call-start = ((), (), s32[]{:S(2)}) async-start(), calls=%async_computation.4 | async-start | bytes 5570560 | tf_op jit(solution)/shard_map/all_gather | solution.py:169
  23.3 9.6 %collective-permute-start = (bf16[8,20480]{1,0:T(8,128)(2,1)}, bf16[8,20480]{1,0:T(8,128)(2,1)S(1)}, u32[]{:S(2)}, u32[]{:S(2)}) collective-permute-start(bf16[8,20480]{1,0:T(8,128)(2,1)} %own_ref.1), channel_id=1, source_target_pairs={{0,16},{1,17},{2,18},{3,19},{4,20},{5,21},{6,22},{7,23},{8,24},{9,... | collective-permute-start | bytes 983048 | tf_op jit(solution)/shard_map/ppermute | solution.py:28
  32.9 1.0 copy-start
  35.0 24.2 %all-to-all-start.1 = ((bf16[16,16,1280]{2,1,0:T(8,128)(2,1)}), bf16[16,16,1280]{2,1,0:T(8,128)(2,1)S(1)}, u32[]{:S(2)}, u32[]{:S(2)}) async-start(bf16[16,16,1280]{2,1,0:T(8,128)(2,1)} %spread.1), calls=%async_computation.1 | async-start | bytes 1310720 | tf_op jit(solution)/shard_map/all_to_all | solution.py:172
  59.2 22.5 %all-to-all-start.3 = ((bf16[8,2,1280]{2,1,0:T(2,128)(2,1)}), bf16[8,2,1280]{2,1,0:T(2,128)(2,1)S(1)}, u32[]{:S(2)}, u32[]{:S(2)}) async-start(bf16[8,2,1280]{2,1,0:T(2,128)(2,1)} %reshape.57), calls=%async_computation.3 | async-start | bytes 81920 | tf_op jit(solution)/shard_map/all_to_all | solution.py:178
  64.0 24.7 %collective-permute-start.1 = (bf16[8,16,1280]{2,1,0:T(8,128)(2,1)S(1)}, bf16[8,16,1280]{2,1,0:T(8,128)(2,1)S(1)}, u32[]{:S(2)}, u32[]{:S(2)}) collective-permute-start(bf16[8,16,1280]{2,1,0:T(8,128)(2,1)S(1)} %get-tuple-element.22), channel_id=1, source_target_pairs={{0,32},{1,33},{2,34},{3,35},{4,36},{5,37},{6,38},{7,39},{8,40},{9,... | collective-permute-start | bytes 983048 | tf_op jit(solution)/shard_map/ppermute | solution.py:28
  66.0 22.6 %collective-permute-start.4 = (bf16[8,16,1280]{2,1,0:T(8,128)(2,1)}, bf16[8,16,1280]{2,1,0:T(8,128)(2,1)S(1)}, u32[]{:S(2)}, u32[]{:S(2)}) collective-permute-start(bf16[8,16,1280]{2,1,0:T(8,128)(2,1)} %get-tuple-element.21), channel_id=1, source_target_pairs={{0,96},{1,97},{2,98},{3,99},{4,100},{5,101},{6,102},{7,103},{8,104... | collective-permute-start | bytes 983048 | tf_op jit(solution)/shard_map/ppermute | solution.py:28
  81.8 33.2 %all-to-all-start.2 = ((bf16[16,2,640]{2,1,0:T(2,128)(2,1)}), bf16[16,2,640]{2,1,0:T(2,128)(2,1)S(1)}, u32[]{:S(2)}, u32[]{:S(2)}) async-start(bf16[16,2,640]{2,1,0:T(2,128)(2,1)} %reshape.55), calls=%async_computation.2 | async-start | bytes 81920 | tf_op jit(solution)/shard_map/all_to_all | solution.py:182
  85.3 64.8 %collective-permute-start.2 = (bf16[8,16,1280]{2,1,0:T(8,128)(2,1)}, bf16[8,16,1280]{2,1,0:T(8,128)(2,1)S(1)}, u32[]{:S(2)}, u32[]{:S(2)}) collective-permute-start(bf16[8,16,1280]{2,1,0:T(8,128)(2,1)} %get-tuple-element.21), channel_id=1, source_target_pairs={{0,32},{1,33},{2,34},{3,35},{4,36},{5,37},{6,38},{7,39},{8,40},{9,... | collective-permute-start | bytes 983048 | tf_op jit(solution)/shard_map/ppermute | solution.py:28
  86.2 64.7 %collective-permute-start.3 = (bf16[8,16,1280]{2,1,0:T(8,128)(2,1)S(1)}, bf16[8,16,1280]{2,1,0:T(8,128)(2,1)S(1)}, u32[]{:S(2)}, u32[]{:S(2)}) collective-permute-start(bf16[8,16,1280]{2,1,0:T(8,128)(2,1)S(1)} %get-tuple-element.22), channel_id=1, source_target_pairs={{0,96},{1,97},{2,98},{3,99},{4,100},{5,101},{6,102},{7,103},{8,104... | collective-permute-start | bytes 983048 | tf_op jit(solution)/shard_map/ppermute | solution.py:28
  88.6 63.0 %copy-start.2 = (bf16[8,16,1280]{2,1,0:T(8,128)(2,1)}, bf16[8,16,1280]{2,1,0:T(8,128)(2,1)S(1)}, u32[]{:S(2)}) copy-start(bf16[8,16,1280]{2,1,0:T(8,128)(2,1)S(1)} %collective-permute-done.1.a_dn) | copy-start | bytes 983044
  88.6 63.0 %collective-permute-start.5 = (bf16[8,16,1280]{2,1,0:T(8,128)(2,1)S(1)}, bf16[8,16,1280]{2,1,0:T(8,128)(2,1)}, u32[]{:S(2)}, u32[]{:S(2)}) collective-permute-start(bf16[8,16,1280]{2,1,0:T(8,128)(2,1)S(1)} %collective-permute-done.1.a_dn), channel_id=1, source_target_pairs={{0,32},{1,33},{2,34},{3,35},{4,36},{5,37},{6,38},{7,39},{8,40},{9,... | collective-permute-start | bytes 983048 | tf_op jit(solution)/shard_map/ppermute | solution.py:28
  88.7 63.0 %copy-start.4 = (bf16[8,16,1280]{2,1,0:T(8,128)(2,1)}, bf16[8,16,1280]{2,1,0:T(8,128)(2,1)S(1)}, u32[]{:S(2)}) copy-start(bf16[8,16,1280]{2,1,0:T(8,128)(2,1)S(1)} %collective-permute-done.4.b_up) | copy-start | bytes 983044
  88.7 62.9 %collective-permute-start.6 = (bf16[8,16,1280]{2,1,0:T(8,128)(2,1)S(1)}, bf16[8,16,1280]{2,1,0:T(8,128)(2,1)}, u32[]{:S(2)}, u32[]{:S(2)}) collective-permute-start(bf16[8,16,1280]{2,1,0:T(8,128)(2,1)S(1)} %collective-permute-done.4.b_up), channel_id=1, source_target_pairs={{0,96},{1,97},{2,98},{3,99},{4,100},{5,101},{6,102},{7,103},{8,104... | collective-permute-start | bytes 983048 | tf_op jit(solution)/shard_map/ppermute | solution.py:28
  150.1 0.7 copy-start.6
  150.9 0.7 copy-start.8
  151.6 2.5 %copy-start.1 = (bf16[1024,2560]{1,0:T(8,128)(2,1)S(1)}, bf16[1024,2560]{1,0:T(8,128)(2,1)}, u32[]{:S(2)}) copy-start(bf16[1024,2560]{1,0:T(8,128)(2,1)} %all-gather.4.cloned.1.call-done) | copy-start | bytes 15728644
  154.1 1.0 copy-start.3
  155.1 1.0 copy-start.5
  156.1 1.0 copy-start.7
  157.0 1.0 copy-start.9
  191.4 0.7 copy-start.10
  192.1 0.7 copy-start.11
  192.7 9.1 %collective-permute-start.7 = (f32[640,128]{1,0:T(8,128)S(1)}, f32[640,128]{1,0:T(8,128)S(1)}, u32[]{:S(2)}, u32[]{:S(2)}) collective-permute-start(f32[640,128]{1,0:T(8,128)S(1)} %get-tuple-element.14), channel_id=1, source_target_pairs={{0,8},{1,9},{2,10},{3,11},{4,12},{5,13},{6,14},{7,15},{8,0},{9,1},... | collective-permute-start | bytes 983048 | tf_op jit(solution)/shard_map/ppermute | solution.py:28
  192.7 12.2 %collective-permute-start.8 = (f32[640,128]{1,0:T(8,128)S(1)}, f32[640,128]{1,0:T(8,128)S(1)}, u32[]{:S(2)}, u32[]{:S(2)}) collective-permute-start(f32[640,128]{1,0:T(8,128)S(1)} %get-tuple-element.15), channel_id=1, source_target_pairs={{0,4},{1,5},{2,6},{3,7},{4,8},{5,9},{6,10},{7,11},{8,12},{9,13},{1... | collective-permute-start | bytes 983048 | tf_op jit(solution)/shard_map/ppermute | solution.py:28
  193.7 11.2 %collective-permute-start.9 = (f32[640,128]{1,0:T(8,128)S(1)}, f32[640,128]{1,0:T(8,128)S(1)}, u32[]{:S(2)}, u32[]{:S(2)}) collective-permute-start(f32[640,128]{1,0:T(8,128)S(1)} %get-tuple-element.16), channel_id=1, source_target_pairs={{0,12},{1,13},{2,14},{3,15},{4,0},{5,1},{6,2},{7,3},{8,4},{9,5},{1... | collective-permute-start | bytes 983048 | tf_op jit(solution)/shard_map/ppermute | solution.py:28
  196.0 9.1 %collective-permute-start.12 = (f32[320,128]{1,0:T(8,128)}, f32[320,128]{1,0:T(8,128)S(1)}, u32[]{:S(2)}, u32[]{:S(2)}) collective-permute-start(f32[320,128]{1,0:T(8,128)} %copy-done.11), channel_id=1, source_target_pairs={{0,64},{1,65},{2,66},{3,67},{4,68},{5,69},{6,70},{7,71},{8,72},{9,... | collective-permute-start | bytes 491528 | tf_op jit(solution)/shard_map/ppermute | solution.py:28
  196.0 9.1 %collective-permute-start.13 = (f32[320,128]{1,0:T(8,128)}, f32[320,128]{1,0:T(8,128)S(1)}, u32[]{:S(2)}, u32[]{:S(2)}) collective-permute-start(f32[320,128]{1,0:T(8,128)} %copy-done.10), channel_id=1, source_target_pairs={{0,32},{1,33},{2,34},{3,35},{4,36},{5,37},{6,38},{7,39},{8,40},{9,... | collective-permute-start | bytes 491528 | tf_op jit(solution)/shard_map/ppermute | solution.py:28
  201.8 5.3 %collective-permute-start.14 = (f32[320,128]{1,0:T(8,128)S(1)}, f32[320,128]{1,0:T(8,128)S(1)}, u32[]{:S(2)}, u32[]{:S(2)}) collective-permute-start(f32[320,128]{1,0:T(8,128)S(1)} %get-tuple-element.20), channel_id=1, source_target_pairs={{0,96},{1,97},{2,98},{3,99},{4,100},{5,101},{6,102},{7,103},{8,104... | collective-permute-start | bytes 491528 | tf_op jit(solution)/shard_map/ppermute | solution.py:28
  205.0 4.3 %collective-permute-start.10 = (f32[2,160,128]{2,1,0:T(8,128)S(1)}, f32[2,160,128]{2,1,0:T(8,128)S(1)}, u32[]{:S(2)}, u32[]{:S(2)}) collective-permute-start(f32[2,160,128]{2,1,0:T(8,128)S(1)} %dynamic-slice_bitcast_fusion), channel_id=1, source_target_pairs={{0,1},{1,0},{2,3},{3,2},{4,5},{5,4},{6,7},{7,6},{8,9},{9,8},{10,11... | collective-permute-start | bytes 491528 | tf_op jit(solution)/shard_map/ppermute | solution.py:28
  207.2 6.0 %collective-permute-start.15 = (f32[160,128]{1,0:T(8,128)S(1)}, f32[160,128]{1,0:T(8,128)S(1)}, u32[]{:S(2)}, u32[]{:S(2)}) collective-permute-start(f32[160,128]{1,0:T(8,128)S(1)} %dynamic-slice_bitcast_fusion.1), channel_id=1, source_target_pairs={{0,16},{1,17},{2,18},{3,19},{4,20},{5,21},{6,22},{7,23},{8,24},{9,... | collective-permute-start | bytes 245768 | tf_op jit(solution)/shard_map/ppermute | solution.py:28
  209.4 4.5 %collective-permute-start.11 = (f32[160,128]{1,0:T(8,128)S(1)}, f32[160,128]{1,0:T(8,128)S(1)}, u32[]{:S(2)}, u32[]{:S(2)}) collective-permute-start(f32[160,128]{1,0:T(8,128)S(1)} %dynamic-slice_bitcast_fusion.2), channel_id=1, source_target_pairs={{0,2},{1,3},{2,0},{3,1},{4,6},{5,7},{6,4},{7,5},{8,10},{9,11},{10,... | collective-permute-start | bytes 245768 | tf_op jit(solution)/shard_map/ppermute | solution.py:28
Sparse Core Ops, SparseCore 0:
  23.4 44.2 all-gather.3

commit v2 on v0

v2 whole, which is shorter than its diff:
```python
import itertools

import jax
import jax.numpy as jnp
from jax import lax
from jax.experimental import pallas as pl
from jax.experimental.pallas import tpu as pltpu
from jax.sharding import PartitionSpec as P

N_ROW, N_COL, FB, NB, NT = 8, 16, 160, 1024, 128
DEVICES = N_ROW * N_COL
ROW_PTS, COL_PTS = N_COL * FB, N_ROW * FB
WIDE = NB + NT
AXES = ("row", "col")
PARTS = {"y": 4, "xh": 2, "z": 4, "xl": 2, "k": 2}
TILE = 4 * FB
BF, F32 = jnp.bfloat16, jnp.float32


def index_of(y, xh, z, xl, k):
    return (y * 2 + xh) * N_COL + z * 4 + xl * 2 + k


def moved(**steps):
    pairs = []
    for at in itertools.product(*map(range, PARTS.values())):
        to = [(a + steps.get(name, 0)) % size for a, (name, size) in zip(at, PARTS.items())]
        pairs.append((index_of(*at), index_of(*to)))
    return pairs


def groups(*names):
    found = {}
    for at in itertools.product(*map(range, PARTS.values())):
        rest = tuple(a for a, name in zip(at, PARTS) if name not in names)
        found.setdefault(rest, []).append(index_of(*at))
    return list(found.values())


def send(x, **steps):
    return lax.ppermute(x, AXES, moved(**steps))


def nn(a, b):
    return jnp.dot(a, b, preferred_element_type=F32)


def nt(a, b):
    return lax.dot_general(a, b, (((1,), (1,)), ((), ())), preferred_element_type=F32)


def tn(a, b):
    return lax.dot_general(a, b, (((0,), (0,)), ((), ())), preferred_element_type=F32)


def pack_kernel(orb, tgt, out):
    row = lax.broadcasted_iota(jnp.int32, (8, 96), 0)
    for pair in range(DEVICES // 2):
        blocks = []
        for q in (2 * pair, 2 * pair + 1):
            head = jnp.broadcast_to(tgt[q : q + 1, :96], (8, 96))
            tail = jnp.broadcast_to(tgt[q : q + 1, 64:], (8, 96))
            extra = jnp.where(row == 0, head, tail)
            blocks.append(jnp.concatenate([orb[:, q * FB : (q + 1) * FB].astype(F32), extra], axis=1))
        out[16 * pair : 16 * (pair + 1), :] = jnp.concatenate(blocks, axis=0).astype(BF)


def pack(orbitals, targets):
    return pl.pallas_call(
        pack_kernel,
        out_shape=jax.ShapeDtypeStruct((DEVICES * 8, 256), BF),
        compiler_params=pltpu.CompilerParams(vmem_limit_bytes=32 * 2**20),
        name="pack",
    )(orbitals, targets.astype(F32).reshape(DEVICES, FB))


def unpack_kernel(packed, out):
    out[:, :NB] = packed[:, :FB].T
    source = lax.broadcasted_iota(jnp.int32, (NB, NT), 0)
    target = lax.broadcasted_iota(jnp.int32, (NB, NT), 1)
    first = jnp.where(source == 8 * target, 1.0, 0.0).astype(BF)
    second = jnp.where(source == 8 * target + 1, 1.0, 0.0).astype(BF)
    heads = tn(packed[...], first)
    tails = tn(packed[...], second)
    out[:96, NB:] = heads[FB:].astype(BF)
    out[96:, NB:] = tails[FB + 32 :].astype(BF)


def unpack(packed):
    return pl.pallas_call(
        unpack_kernel,
        out_shape=jax.ShapeDtypeStruct((FB, WIDE), BF),
        compiler_params=pltpu.CompilerParams(vmem_limit_bytes=32 * 2**20),
        name="unpack",
    )(packed)


def tile_step(me, rows, pair, down, up, far_own, far_other, kern, owned, mirrored, cols, sems, col_acc, col_start):
    y, xh = me[1], me[2]

    @pl.when(pl.program_id(0) == 0)
    def _():
        def block(y_step, side):
            return lax.rem(y + y_step, 4) * 2 + lax.rem(xh + side, 2)

        pieces = [(ref.at[pl.ds(FB * side, FB)], block(step, side)) for ref, step in ((pair, 0), (down, 3), (up, 1)) for side in (0, 1)]
        pieces += [(far_own, block(2, 0)), (far_other, block(2, 1))]
        copies = [pltpu.make_async_copy(src, cols.at[at], sems.at[i]) for i, (src, at) in enumerate(pieces)]
        for copy in copies:
            copy.start()
        col_start()
        for copy in copies:
            copy.wait()

    row_wide = rows[...].reshape(TILE, WIDE)
    col_wide = cols[...].reshape(COL_PTS, WIDE)
    gram = nt(row_wide[:, :NB], col_wide[:, :NB])
    stored = jnp.concatenate(
        [
            jnp.concatenate([kern[b, 0, pl.ds(j, FB, stride=COL_PTS // 128), :] for j in range(COL_PTS // 128)], axis=1)
            for b in range(4)
        ],
        axis=0,
    )

    def spread(ref):
        return jnp.concatenate([jnp.broadcast_to(ref[b, 0], (FB, COL_PTS)) for b in range(4)], axis=0)

    weighted = gram * stored * spread(owned)
    high = weighted.astype(BF)
    low = (weighted - high.astype(F32)).astype(BF)
    row_sum = nn(high, col_wide[:, NB:]) + nn(low, col_wide[:, NB:])
    keep = spread(mirrored).astype(BF)
    col_sum = tn(high * keep, row_wide[:, NB:]) + tn(low * keep, row_wide[:, NB:])
    col_acc[...] += col_sum.reshape(col_acc.shape)
    return row_sum.reshape(4, FB, NT)


def first_kernel(me, *refs):
    ins, (row_out, col_out), (cols, sems) = refs[:9], refs[9:11], refs[11:]

    def start():
        col_out[...] = jnp.zeros_like(col_out)

    row_out[...] = tile_step(me, *ins, cols, sems, col_out, start)


def second_kernel(me, *refs):
    ins, col_in, outs, (cols, sems, col_acc) = refs[:9], refs[9], refs[10:15], refs[15:]

    def start():
        col_acc[...] = col_in[...]

    outs[0][...] = tile_step(me, *ins, cols, sems, col_acc, start)

    @pl.when(pl.program_id(0) == 1)
    def _():
        for step in range(4):
            outs[1 + step][...] = col_acc[lax.rem(me[1] + step, 4)]


def tile_call(me, rows, col_parts, kern, owned, mirrored, col_in=None):
    second = col_in is not None
    in_specs = [pl.BlockSpec((4, 1, FB, WIDE), lambda g, me: (g, me[0], 0, 0))]
    in_specs += [pl.BlockSpec(memory_space=pltpu.HBM)] * len(col_parts)
    in_specs += [pl.BlockSpec((4, 1, FB * COL_PTS // 128, 128), lambda g, me: (g, me[0], 0, 0))]
    in_specs += [pl.BlockSpec((4, 1, 1, COL_PTS), lambda g, me: (g, me[0], 0, 0))] * 2
    row_out = jax.ShapeDtypeStruct((8, FB, NT), F32)
    row_spec = pl.BlockSpec((4, FB, NT), lambda g, me: (g, 0, 0))
    whole = pl.BlockSpec((4, 2 * FB, NT), lambda g, me: (0, 0, 0))
    scratch = [pltpu.VMEM((N_ROW, FB, WIDE), BF), pltpu.SemaphoreType.DMA((8,))]
    args = [me, rows, *col_parts, kern, owned, mirrored]
    if second:
        in_specs += [whole]
        args += [col_in]
        out_shape = [row_out] + [jax.ShapeDtypeStruct((2 * FB, NT), F32)] * 4
        out_specs = [row_spec] + [pl.BlockSpec((2 * FB, NT), lambda g, me: (0, 0))] * 4
        scratch += [pltpu.VMEM((4, 2 * FB, NT), F32)]
    else:
        out_shape = [row_out, jax.ShapeDtypeStruct((4, 2 * FB, NT), F32)]
        out_specs = [row_spec, whole]
    return pl.pallas_call(
        second_kernel if second else first_kernel,
        grid_spec=pltpu.PrefetchScalarGridSpec(
            num_scalar_prefetch=1, grid=(2,), in_specs=in_specs, out_specs=out_specs, scratch_shapes=scratch
        ),
        out_shape=out_shape,
        compiler_params=pltpu.CompilerParams(vmem_limit_bytes=56 * 2**20, dimension_semantics=("arbitrary",)),
        cost_estimate=pl.CostEstimate(flops=5_000_000_000, bytes_accessed=13_000_000, transcendentals=0),
        name="tiles_of_own_core" if second else "tiles_of_other_core",
    )(*args)


def local(orbitals, targets, kernel, tile_owner):
    r, c = lax.axis_index("row"), lax.axis_index("col")
    y, xh, k = r // 2, r % 2, c % 2

    packed = pack(orbitals, targets).reshape(DEVICES, 8, 256)
    packed = lax.all_to_all(packed, AXES, split_axis=0, concat_axis=0, tiled=True)
    own = unpack(packed.reshape(DEVICES * 8, 256))

    rows = lax.all_gather(own, "col", axis=0, tiled=True).reshape(8, 2, FB, WIDE)
    pair = jnp.concatenate([own, send(own, xh=1)], axis=0)
    down, up = send(pair, y=1), send(pair, y=3)
    far_own, far_other = send(down[:FB], y=1), send(up[FB:], y=3)
    col_parts = (pair, down, up, far_own, far_other)

    flags = tile_owner.reshape(N_COL, N_ROW).astype(F32)
    here = (lax.broadcasted_iota(jnp.int32, flags.shape, 0) == c) & (
        lax.broadcasted_iota(jnp.int32, flags.shape, 1) == r
    )
    owned = jnp.repeat(flags, FB, axis=1).reshape(8, 2, 1, COL_PTS)
    mirrored = jnp.repeat(jnp.where(here, 0.0, flags), FB, axis=1).reshape(8, 2, 1, COL_PTS)
    kern = kernel.reshape(8, 2, FB * COL_PTS // 128, 128)

    def place(core):
        return jnp.stack([core, y, xh]).astype(jnp.int32)

    row_other, col_part = tile_call(place(1 - k), rows, col_parts, kern, owned, mirrored)
    row_own, c0, c1, c2, c3 = tile_call(place(k), rows, col_parts, kern, owned, mirrored, col_part)

    row_sum = row_own + send(row_other, k=1)
    row_share = lax.all_to_all(
        row_sum, AXES, split_axis=0, concat_axis=0, axis_index_groups=groups("z", "xl"), tiled=True
    ).sum(axis=0)
    col_sum = (c0 + send(c1, y=1) + send(c2, y=2) + send(c3, y=3)).reshape(2, FB, NT)
    mine = lax.dynamic_index_in_dim(col_sum, xh, 0, keepdims=False)
    theirs = lax.dynamic_index_in_dim(col_sum, 1 - xh, 0, keepdims=False)
    return row_share + mine + send(theirs, xh=1)


def solution(mesh):
    in_specs = (
        P(("row", "col"), None),
        P(("row", "col"), None),
        P("row", "col", None),
        P("row", None, None, "col"),
    )
    out_specs = P(("row", "col"), None)
    return jax.shard_map(local, mesh=mesh, in_specs=in_specs, out_specs=out_specs, check_vma=False)
```

time: 312 us -> 141 us (0.45)
  blocking collectives: 85.7 us -> 24.5 us
  local copies, waits for them, and re-layouts: 65.1 us -> 4.69 us
  waiting for transfers between devices: 97.8 us -> 42.5 us
  matrix products: 40.5 us -> 0 us
  Pallas kernels: 0 us -> 31 us
  starting transfers between devices: 4.67 us -> 18.2 us
    reduce_scatter x2 -> x0, waiting for transfers between devices: 62.2 us -> none  [the longest x1 62.2 us: local(): lax.psum_scatter(row_out, 'col', scatter_dimension=0, tiled=True)]
    all_gather x2 -> x0, blocking collectives: 61.2 us -> none  [the longest x1 35.8 us: spread_points(): lax.all_gather(tgt_points, 'row', axis=1, tiled=True)]
    mul x4 -> x0, local copies, waits for them, and re-layouts: 56.6 us -> none  [the longest x2 28.3 us: local(): weighted * owned_flags[:, None, :, None]]
    dot_general x3 -> x0, matrix products: 40.5 us -> none  [the longest x1 14.6 us: local(): lax.dot_general(col_terms, row_tgt.astype(jnp.float32), (((0,), (1,)), ((...]
    all_gather x2 -> x1, waiting for transfers between devices: 34.8 us -> 0.01 us  [local(): lax.all_gather(own, 'col', axis=0, tiled=True).reshape(8, 2, FB, WIDE)]
    ppermute x0 -> x10, waiting for transfers between devices: none -> 34.2 us  [send(): return lax.ppermute(x, AXES, moved(**steps))]
    pallas_call x0 -> x4, Pallas kernels: none -> 31 us  [the longest x2 27.8 us: tile_call(): pl.pallas_call(second_kernel if second else first_kernel, grid_spec=pltpu...]
    ppermute x0 -> x10, starting transfers between devices: none -> 14.7 us  [send(): return lax.ppermute(x, AXES, moved(**steps))]
  transfers between devices with their start and end apart: 5 -> 12, of which waited for: 2 -> 6; matrix products, arithmetic and copies ran while one was open for 23% -> 5% of each run, Pallas kernels for 0% -> 10%
where the time goes in v2:
time: 141 us; the launch traced here: 140 us
  waiting for transfers between devices  42.5 us (30%)
  Pallas kernels  31 us (22%)
  blocking collectives  24.5 us (17%)
  starting transfers between devices  18.2 us (13%)
  between operations  13.6 us (10%)
  other arithmetic  5.68 us (4%)
  local copies, waits for them, and re-layouts  4.69 us (3%)
    ppermute x10, waiting for transfers between devices, send(): return lax.ppermute(x, AXES, moved(**steps))  34.2 us
    pallas_call x2, Pallas kernels, tile_call(): pl.pallas_call(second_kernel if second else first_kernel, grid_spec=pltpu...  27.8 us
    all_to_all x1, blocking collectives, local(): lax.all_to_all(packed, AXES, split_axis=0, concat_axis=0, tiled=True)  24.5 us
    ppermute x10, starting transfers between devices, send(): return lax.ppermute(x, AXES, moved(**steps))  14.7 us
    all_to_all x1, waiting for transfers between devices, local(): lax.all_to_all(row_sum, AXES, split_axis=0, concat_axis=0, axis_index_gro...  8.23 us
    all_to_all x1, starting transfers between devices, local(): lax.all_to_all(row_sum, AXES, split_axis=0, concat_axis=0, axis_index_gro...  3.54 us
  transfers between devices with their start and end apart: 12, of which 6 were waited for; matrix products, arithmetic and copies ran while one was open for 5% of the time, Pallas kernels for 10%

profile of v2, /device:TPU:0, one launch (start us, length us, event | category | flops | bytes accessed | tf_op | source)
XLA Modules:
  0.0 140.2 jit_solution(2130451223351825201)
XLA Ops:
  6.5 0.0 all-gather.2.cloned.1.call-start
  6.5 1.1 convert_reduce_fusion
  7.7 0.1 reshape.30.tgt
  7.8 0.0 copy-start
  7.8 1.0 copy-done
  8.7 2.0 %pack.1 = bf16[1024,256]{1,0:T(8,128)(2,1)S(1)} custom-call(bf16[8,20480]{1,0:T(8,128)(2,1)S(1)} %copy-done, f32[128,160]{1,0:T(8,128)S(1)} %reshape.30.tgt), custom_call_target="tpu_custom_call" | custom-call | tf_op jit(solution)/shard_map/pack/pallas_call | solution.py:69
  10.8 24.5 %all_to_all.10 = bf16[128,8,256]{2,1,0:T(8,128)(2,1)S(1)} all-to-all(bf16[128,8,256]{2,1,0:T(8,128)(2,1)S(1)} %bitcast.21), channel_id=1, replica_groups=mesh['row'=8,'col'=16] {'row','col'}, dimensions={0} | all-to-all | bytes 1048576 | tf_op jit(solution)/shard_map/all_to_all | solution.py:199
  35.2 1.3 unpack.1
  36.5 0.0 all-gather.2.cloned.1.call-update
  36.5 0.0 copy-start.7
  36.5 1.3 collective-permute-start
  37.8 15.6 %collective-permute-done = bf16[160,1152]{1,0:T(8,128)(2,1)S(1)} collective-permute-done((bf16[160,1152]{1,0:T(8,128)(2,1)}, bf16[160,1152]{1,0:T(8,128)(2,1)S(1)}, u32[]{:S(2)}, u32[]{:S(2)}) %collective-permute-start) | collective-permute-done | bytes 368672 | tf_op jit(solution)/shard_map/ppermute | solution.py:41
  53.4 1.1 pad_maximum_fusion.refs_1_
  54.5 0.1 collective-permute-start.1
  54.5 3.2 %collective-permute-start.2 = (bf16[320,1152]{1,0:T(8,128)(2,1)S(1)}, bf16[320,1152]{1,0:T(8,128)(2,1)S(1)}, u32[]{:S(2)}, u32[]{:S(2)}) collective-permute-start(bf16[320,1152]{1,0:T(8,128)(2,1)S(1)} %pad_maximum_fusion.refs_1_), channel_id=1, source_target_pairs={{0,96},{1,97},{2,98},{3,99},{4,100},{5,101},{6,102},{7,103},{8,104... | collective-permute-start | bytes 2211848 | tf_op jit(solution)/shard_map/ppermute | solution.py:41
  57.8 13.3 %collective-permute-done.1.refs_2_ = bf16[320,1152]{1,0:T(8,128)(2,1)S(1)} collective-permute-done((bf16[320,1152]{1,0:T(8,128)(2,1)S(1)}, bf16[320,1152]{1,0:T(8,128)(2,1)S(1)}, u32[]{:S(2)}, u32[]{:S(2)}) %collective-permute-start.1) | collective-permute-done | bytes 737312 | tf_op jit(solution)/shard_map/ppermute | solution.py:41
  71.1 0.1 collective-permute-start.3
  71.2 0.0 collective-permute-done.2.refs_3_
  71.2 0.9 slice.9
  72.1 3.1 %collective-permute-start.4 = (bf16[160,1152]{1,0:T(8,128)(2,1)}, bf16[160,1152]{1,0:T(8,128)(2,1)S(1)}, u32[]{:S(2)}, u32[]{:S(2)}) collective-permute-start(bf16[160,1152]{1,0:T(8,128)(2,1)} %slice.9), channel_id=1, source_target_pairs={{0,96},{1,97},{2,98},{3,99},{4,100},{5,101},{6,102},{7,103},{8,104... | collective-permute-start | bytes 1105928 | tf_op jit(solution)/shard_map/ppermute | solution.py:41
  75.3 0.1 and_select_fusion
  75.3 0.1 copy.10
  75.4 0.1 broadcast_in_dim.12
  75.5 0.8 reshape_reshape.7.refs_8_
  76.3 0.1 copy.9
  76.4 0.1 broadcast_in_dim.10
  76.5 0.8 reshape_reshape.6.refs_7_
  77.3 0.7 add_add_fusion.1
  77.9 2.0 %collective-permute-done.3.refs_4_ = bf16[160,1152]{1,0:T(8,128)(2,1)S(1)} collective-permute-done((bf16[160,1152]{1,0:T(8,128)(2,1)S(1)}, bf16[160,1152]{1,0:T(8,128)(2,1)S(1)}, u32[]{:S(2)}, u32[]{:S(2)}) %collective-permute-start.3) | collective-permute-done | bytes 368672 | tf_op jit(solution)/shard_map/ppermute | solution.py:41
  79.9 0.7 collective-permute-done.4.refs_5_
  80.6 0.0 copy-done.4
  80.7 0.7 copy-done.5
  81.4 13.7 %tiles_of_other_core.1 = (f32[8,160,128]{2,1,0:T(8,128)}, f32[4,320,128]{2,1,0:T(8,128)}) custom-call(s32[3]{0:T(128)} %get-tuple-element.20.me, bf16[8,2,160,1152]{3,2,1,0:T(8,128)(2,1)} %bitcast.24, bf16[320,1152]{1,0:T(8,128)(2,1)} %copy-done.1, bf16[320,1152]{1,0:T(8,128)(2,1)} %copy-done.2, bf16[320,1152]{1,0:T(8,128)(2,1)} %copy-done.3, ...), custom_call_target="tpu_custom_call" | custom-call | flops 5000000000 | bytes 13000000 | tf_op jit(solution)/shard_map/tiles_of_other_core/pallas_call | solution.py:182
  95.1 0.1 collective-permute-start.5
  95.2 14.1 %tiles_of_own_core.1 = (f32[8,160,128]{2,1,0:T(8,128)}, f32[320,128]{1,0:T(8,128)}, f32[320,128]{1,0:T(8,128)}, f32[320,128]{1,0:T(8,128)}, f32[320,128]{1,0:T(8,128)}) custom-call(s32[3]{0:T(128)} %get-tuple-element.19.me, bf16[8,2,160,1152]{3,2,1,0:T(8,128)(2,1)} %bitcast.25, bf16[320,1152]{1,0:T(8,128)(2,1)} %copy-done.1, bf16[320,1152]{1,0:T(8,128)(2,1)} %copy-done.2, ...), custom_call_target="tpu_custom_call" | custom-call | flops 5000000000 | bytes 13000000 | tf_op jit(solution)/shard_map/tiles_of_own_core/pallas_call | solution.py:182
  109.2 0.1 collective-permute-start.6
  109.3 5.0 %collective-permute-start.7 = (f32[320,128]{1,0:T(8,128)}, f32[320,128]{1,0:T(8,128)S(1)}, u32[]{:S(2)}, u32[]{:S(2)}) collective-permute-start(f32[320,128]{1,0:T(8,128)} %get-tuple-element.17), channel_id=1, source_target_pairs={{0,64},{1,65},{2,66},{3,67},{4,68},{5,69},{6,70},{7,71},{8,72},{9,... | collective-permute-start | bytes 491528 | tf_op jit(solution)/shard_map/ppermute | solution.py:41
  114.3 0.0 collective-permute-start.8
  114.4 0.0 collective-permute-done.5
  114.4 2.0 %add.36 = f32[8,160,128]{2,1,0:T(8,128)} add(f32[8,160,128]{2,1,0:T(8,128)} %get-tuple-element.13, f32[8,160,128]{2,1,0:T(8,128)S(1)} %collective-permute-done.5) | non-fusion elementwise | flops 163840 | bytes 1966080 | tf_op jit(solution)/shard_map/add | solution.py:222
  116.4 3.5 %all-to-all-start.1 = ((f32[8,160,128]{2,1,0:T(8,128)}), f32[8,160,128]{2,1,0:T(8,128)S(1)}, u32[]{:S(2)}, u32[]{:S(2)}) async-start(f32[8,160,128]{2,1,0:T(8,128)} %add.36), calls=%async_computation.1 | async-start | bytes 1310720 | tf_op jit(solution)/shard_map/all_to_all | solution.py:223
  120.0 0.0 collective-permute-done.6
  120.0 2.7 %collective-permute-done.7 = f32[320,128]{1,0:T(8,128)S(1)} collective-permute-done((f32[320,128]{1,0:T(8,128)}, f32[320,128]{1,0:T(8,128)S(1)}, u32[]{:S(2)}, u32[]{:S(2)}) %collective-permute-start.7) | collective-permute-done | bytes 163872 | tf_op jit(solution)/shard_map/ppermute | solution.py:41
  122.6 0.0 collective-permute-done.8
  122.7 1.7 %collective-permute-start.9 = (f32[160,128]{1,0:T(8,128)S(1)}, f32[160,128]{1,0:T(8,128)S(1)}, u32[]{:S(2)}, u32[]{:S(2)}) collective-permute-start(f32[160,128]{1,0:T(8,128)S(1)} %dynamic-slice_bitcast_fusion), channel_id=1, source_target_pairs={{0,16},{1,17},{2,18},{3,19},{4,20},{5,21},{6,22},{7,23},{8,24},{9,... | collective-permute-start | bytes 245768 | tf_op jit(solution)/shard_map/ppermute | solution.py:41
  124.4 8.2 %all-to-all-done.1 = f32[8,160,128]{2,1,0:T(8,128)S(1)} async-done(((f32[8,160,128]{2,1,0:T(8,128)}), f32[8,160,128]{2,1,0:T(8,128)S(1)}, u32[]{:S(2)}, u32[]{:S(2)}) %all-to-all-start.1) | async-done | bytes 655392 | tf_op jit(solution)/shard_map/all_to_all | solution.py:223
  132.7 0.0 collective-permute-done.9
  132.7 0.7 fusion
  (19 shorter events, 0.1 us)
Async XLA Ops:
  6.5 74.1 %all-gather.2.cloned.1.call-start = ((), (), s32[]{:S(2)}) async-start(), calls=%async_computation.2 | async-start | bytes 6266880 | tf_op jit(solution)/shard_map/all_gather | solution.py:202
  7.8 1.0 copy-start
  36.5 38.7 %copy-start.7 = (s32[1,16,8,1]{1,3,2,0:T(1,128)S(1)}, s32[1,16,8,1]{1,3,2,0:T(1,128)}, u32[]{:S(2)}) copy-start(s32[1,16,8,1]{1,3,2,0:T(1,128)} %param.7) | copy-start | bytes 1540
  36.5 16.9 %collective-permute-start = (bf16[160,1152]{1,0:T(8,128)(2,1)}, bf16[160,1152]{1,0:T(8,128)(2,1)S(1)}, u32[]{:S(2)}, u32[]{:S(2)}) collective-permute-start(bf16[160,1152]{1,0:T(8,128)(2,1)} %unpack.1), channel_id=1, source_target_pairs={{0,16},{1,17},{2,18},{3,19},{4,20},{5,21},{6,22},{7,23},{8,24},{9,... | collective-permute-start | bytes 1105928 | tf_op jit(solution)/shard_map/ppermute | solution.py:41
  54.5 26.2 %copy-start.1 = (bf16[320,1152]{1,0:T(8,128)(2,1)}, bf16[320,1152]{1,0:T(8,128)(2,1)S(1)}, u32[]{:S(2)}) copy-start(bf16[320,1152]{1,0:T(8,128)(2,1)S(1)} %pad_maximum_fusion.refs_1_) | copy-start | bytes 2211844
  54.5 16.6 %collective-permute-start.1 = (bf16[320,1152]{1,0:T(8,128)(2,1)S(1)}, bf16[320,1152]{1,0:T(8,128)(2,1)S(1)}, u32[]{:S(2)}, u32[]{:S(2)}) collective-permute-start(bf16[320,1152]{1,0:T(8,128)(2,1)S(1)} %pad_maximum_fusion.refs_1_), channel_id=1, source_target_pairs={{0,32},{1,33},{2,34},{3,35},{4,36},{5,37},{6,38},{7,39},{8,40},{9,... | collective-permute-start | bytes 2211848 | tf_op jit(solution)/shard_map/ppermute | solution.py:41
  54.5 16.7 %collective-permute-start.2 = (bf16[320,1152]{1,0:T(8,128)(2,1)S(1)}, bf16[320,1152]{1,0:T(8,128)(2,1)S(1)}, u32[]{:S(2)}, u32[]{:S(2)}) collective-permute-start(bf16[320,1152]{1,0:T(8,128)(2,1)S(1)} %pad_maximum_fusion.refs_1_), channel_id=1, source_target_pairs={{0,96},{1,97},{2,98},{3,99},{4,100},{5,101},{6,102},{7,103},{8,104... | collective-permute-start | bytes 2211848 | tf_op jit(solution)/shard_map/ppermute | solution.py:41
  71.1 9.5 %copy-start.2 = (bf16[320,1152]{1,0:T(8,128)(2,1)}, bf16[320,1152]{1,0:T(8,128)(2,1)S(1)}, u32[]{:S(2)}) copy-start(bf16[320,1152]{1,0:T(8,128)(2,1)S(1)} %collective-permute-done.1.refs_2_) | copy-start | bytes 2211844
  71.1 8.8 %collective-permute-start.3 = (bf16[160,1152]{1,0:T(8,128)(2,1)S(1)}, bf16[160,1152]{1,0:T(8,128)(2,1)S(1)}, u32[]{:S(2)}, u32[]{:S(2)}) collective-permute-start(bf16[160,1152]{1,0:T(8,128)(2,1)S(1)} %slice.8), channel_id=1, source_target_pairs={{0,32},{1,33},{2,34},{3,35},{4,36},{5,37},{6,38},{7,39},{8,40},{9,... | collective-permute-start | bytes 1105928 | tf_op jit(solution)/shard_map/ppermute | solution.py:41
  71.2 9.4 %copy-start.3 = (bf16[320,1152]{1,0:T(8,128)(2,1)}, bf16[320,1152]{1,0:T(8,128)(2,1)S(1)}, u32[]{:S(2)}) copy-start(bf16[320,1152]{1,0:T(8,128)(2,1)S(1)} %collective-permute-done.2.refs_3_) | copy-start | bytes 2211844
  72.1 8.5 %collective-permute-start.4 = (bf16[160,1152]{1,0:T(8,128)(2,1)}, bf16[160,1152]{1,0:T(8,128)(2,1)S(1)}, u32[]{:S(2)}, u32[]{:S(2)}) collective-permute-start(bf16[160,1152]{1,0:T(8,128)(2,1)} %slice.9), channel_id=1, source_target_pairs={{0,96},{1,97},{2,98},{3,99},{4,100},{5,101},{6,102},{7,103},{8,104... | collective-permute-start | bytes 1105928 | tf_op jit(solution)/shard_map/ppermute | solution.py:41
  79.9 0.8 copy-start.4
  80.6 0.7 copy-start.5
  95.1 19.3 %collective-permute-start.5 = (f32[8,160,128]{2,1,0:T(8,128)}, f32[8,160,128]{2,1,0:T(8,128)S(1)}, u32[]{:S(2)}, u32[]{:S(2)}) collective-permute-start(f32[8,160,128]{2,1,0:T(8,128)} %get-tuple-element.14), channel_id=1, source_target_pairs={{0,1},{1,0},{2,3},{3,2},{4,5},{5,4},{6,7},{7,6},{8,9},{9,8},{10,11... | collective-permute-start | bytes 1966088 | tf_op jit(solution)/shard_map/ppermute | solution.py:41
  109.2 10.7 %collective-permute-start.6 = (f32[320,128]{1,0:T(8,128)}, f32[320,128]{1,0:T(8,128)S(1)}, u32[]{:S(2)}, u32[]{:S(2)}) collective-permute-start(f32[320,128]{1,0:T(8,128)} %get-tuple-element.16), channel_id=1, source_target_pairs={{0,32},{1,33},{2,34},{3,35},{4,36},{5,37},{6,38},{7,39},{8,40},{9,... | collective-permute-start | bytes 491528 | tf_op jit(solution)/shard_map/ppermute | solution.py:41
  109.3 13.3 %collective-permute-start.7 = (f32[320,128]{1,0:T(8,128)}, f32[320,128]{1,0:T(8,128)S(1)}, u32[]{:S(2)}, u32[]{:S(2)}) collective-permute-start(f32[320,128]{1,0:T(8,128)} %get-tuple-element.17), channel_id=1, source_target_pairs={{0,64},{1,65},{2,66},{3,67},{4,68},{5,69},{6,70},{7,71},{8,72},{9,... | collective-permute-start | bytes 491528 | tf_op jit(solution)/shard_map/ppermute | solution.py:41
  114.3 8.3 %collective-permute-start.8 = (f32[320,128]{1,0:T(8,128)}, f32[320,128]{1,0:T(8,128)S(1)}, u32[]{:S(2)}, u32[]{:S(2)}) collective-permute-start(f32[320,128]{1,0:T(8,128)} %get-tuple-element.18), channel_id=1, source_target_pairs={{0,96},{1,97},{2,98},{3,99},{4,100},{5,101},{6,102},{7,103},{8,104... | collective-permute-start | bytes 491528 | tf_op jit(solution)/shard_map/ppermute | solution.py:41
  114.4 8.3 %copy-start.6 = (f32[320,128]{1,0:T(8,128)S(1)}, f32[320,128]{1,0:T(8,128)}, u32[]{:S(2)}) copy-start(f32[320,128]{1,0:T(8,128)} %get-tuple-element.15) | copy-start | bytes 491524
  116.4 16.2 %all-to-all-start.1 = ((f32[8,160,128]{2,1,0:T(8,128)}), f32[8,160,128]{2,1,0:T(8,128)S(1)}, u32[]{:S(2)}, u32[]{:S(2)}) async-start(f32[8,160,128]{2,1,0:T(8,128)} %add.36), calls=%async_computation.1 | async-start | bytes 1310720 | tf_op jit(solution)/shard_map/all_to_all | solution.py:223
  122.7 10.0 %collective-permute-start.9 = (f32[160,128]{1,0:T(8,128)S(1)}, f32[160,128]{1,0:T(8,128)S(1)}, u32[]{:S(2)}, u32[]{:S(2)}) collective-permute-start(f32[160,128]{1,0:T(8,128)S(1)} %dynamic-slice_bitcast_fusion), channel_id=1, source_target_pairs={{0,16},{1,17},{2,18},{3,19},{4,20},{5,21},{6,22},{7,23},{8,24},{9,... | collective-permute-start | bytes 245768 | tf_op jit(solution)/shard_map/ppermute | solution.py:41
Sparse Core Ops, SparseCore 0:
  36.6 39.4 all-gather.1

commit v3 on v0

v3 whole, which is shorter than its diff:
```python
import functools
import itertools

import jax
import jax.numpy as jnp
from jax import lax
from jax.experimental import pallas as pl
from jax.experimental.pallas import tpu as pltpu
from jax.sharding import PartitionSpec as P

N_ROW, N_COL, FB, NB, NT = 8, 16, 160, 1024, 128
DEVICES = N_ROW * N_COL
ROW_PTS, COL_PTS = N_COL * FB, N_ROW * FB
WIDE = NB + NT
AXES = ("row", "col")
PARTS = {"y": 4, "xh": 2, "z": 4, "xl": 2, "k": 2}
TILE = 4 * FB
BF, F32 = jnp.bfloat16, jnp.float32


def index_of(y, xh, z, xl, k):
    return (y * 2 + xh) * N_COL + z * 4 + xl * 2 + k


def moved(**steps):
    pairs = []
    for at in itertools.product(*map(range, PARTS.values())):
        to = [(a + steps.get(name, 0)) % size for a, (name, size) in zip(at, PARTS.items())]
        pairs.append((index_of(*at), index_of(*to)))
    return pairs


def send(x, **steps):
    return lax.ppermute(x, AXES, moved(**steps))


def nn(a, b):
    return jnp.dot(a, b, preferred_element_type=F32)


def nt(a, b):
    return lax.dot_general(a, b, (((1,), (1,)), ((), ())), preferred_element_type=F32)


def tn(a, b):
    return lax.dot_general(a, b, (((0,), (0,)), ((), ())), preferred_element_type=F32)


def pack_kernel(orb, tgt, out):
    row = lax.broadcasted_iota(jnp.int32, (8, FB), 0)
    for pair in range(DEVICES // 2):
        blocks = []
        for q in (2 * pair, 2 * pair + 1):
            sources = (q, q ^ 16, q ^ 2)
            extra = jnp.where(
                row == 0,
                tgt[sources[0] : sources[0] + 1, :],
                jnp.where(row == 1, tgt[sources[1] : sources[1] + 1, :], tgt[sources[2] : sources[2] + 1, :]),
            )
            pieces = [orb[:, s * FB : (s + 1) * FB].astype(F32) for s in sources]
            blocks.append(jnp.concatenate([*pieces, extra], axis=1))
        out[16 * pair : 16 * (pair + 1), :] = jnp.concatenate(blocks, axis=0).astype(BF)


def pack(orbitals, targets):
    return pl.pallas_call(
        pack_kernel,
        out_shape=jax.ShapeDtypeStruct((DEVICES * 8, 4 * FB), BF),
        compiler_params=pltpu.CompilerParams(vmem_limit_bytes=32 * 2**20),
        name="pack",
    )(orbitals, targets.astype(F32).reshape(DEVICES, FB))


def unpack_kernel(packed, cols, rows):
    turned = packed[:, : 3 * FB].T
    cols[: FB, :NB] = turned[:FB]
    cols[FB:, :NB] = turned[FB : 2 * FB]
    rows[:FB, :NB] = turned[:FB]
    rows[FB:, :NB] = turned[2 * FB :]
    source = lax.broadcasted_iota(jnp.int32, (NB, NT), 0)
    target = lax.broadcasted_iota(jnp.int32, (NB, NT), 1)
    mine, col_side, row_side = (
        tn(packed[...], jnp.where(source == 8 * target + i, 1.0, 0.0).astype(BF))[3 * FB :].astype(BF) for i in range(3)
    )
    cols[:FB, NB:] = mine
    cols[FB:, NB:] = col_side
    rows[:FB, NB:] = mine
    rows[FB:, NB:] = row_side


def unpack(packed):
    return pl.pallas_call(
        unpack_kernel,
        out_shape=[jax.ShapeDtypeStruct((2 * FB, WIDE), BF)] * 2,
        compiler_params=pltpu.CompilerParams(vmem_limit_bytes=32 * 2**20),
        name="unpack",
    )(packed)


def tile_kernel(z_steps, me, *refs):
    tiles = len(z_steps)
    far = tiles == 1
    n_rows = 4 if far else 2 * tiles
    row_refs, refs = refs[:n_rows], refs[n_rows:]
    (pair, down, up, far_own, far_other, kern, owned, mirrored), refs = refs[:8], refs[8:]
    if far:
        col_in, refs = refs[0], refs[1:]
    row_own, row_other, col_out, cols, rows, stored, sems = refs
    y, xh, z, xl, k = (me[i] for i in range(5))

    def block(y_step, side):
        return lax.rem(y + y_step, 4) * 2 + lax.rem(xh + side, 2)

    count = [0]

    def start(src, dst):
        copy = pltpu.make_async_copy(src, dst, sems.at[count[0]])
        count[0] += 1
        copy.start()
        return copy

    def tile_copies(t):
        z_at = lax.rem(z + z_steps[t], 4)
        found = []
        if far:
            found += [start(row_refs[b], rows.at[0, b]) for b in range(4)]
        else:
            found += [start(row_refs[2 * t + b], rows.at[t, pl.ds(2 * b, 2)]) for b in range(2)]
        for b in range(4):
            found.append(start(kern.at[z_at, lax.rem(xl + b % 2, 2), lax.rem(k + b // 2, 2)], stored.at[t, b]))
        return found

    pieces = [(ref.at[side], block(step, side)) for ref, step in ((pair, 0), (down, 3), (up, 1)) for side in (0, 1)]
    pieces += [(far_own, block(2, 0)), (far_other, block(2, 1))]
    col_copies = [start(src, cols.at[at]) for src, at in pieces]
    row_copies = [tile_copies(t) for t in range(tiles)]
    if far:
        col_out[...] = col_in[...]
    else:
        col_out[...] = jnp.zeros_like(col_out)
    for copy in col_copies:
        copy.wait()
    col_wide = cols[...].reshape(COL_PTS, WIDE)

    for t in range(tiles):
        z_at = lax.rem(z + z_steps[t], 4)
        for copy in row_copies[t]:
            copy.wait()
        row_wide = rows[t].reshape(TILE, WIDE)
        gram = nt(row_wide[:, :NB], col_wide[:, :NB])
        chunks = COL_PTS // 128
        values = jnp.concatenate(
            [
                jnp.concatenate([stored[t, b, pl.ds(j, FB, stride=chunks), :] for j in range(chunks)], axis=1)
                for b in range(4)
            ],
            axis=0,
        )

        def spread(ref):
            return jnp.concatenate(
                [
                    jnp.broadcast_to(ref[z_at, lax.rem(xl + b % 2, 2), lax.rem(k + b // 2, 2)], (FB, COL_PTS))
                    for b in range(4)
                ],
                axis=0,
            )

        weighted = gram * values * spread(owned)
        high = weighted.astype(BF)
        low = (weighted - high.astype(F32)).astype(BF)
        row_sum = nn(high, col_wide[:, NB:]) + nn(low, col_wide[:, NB:])
        keep = spread(mirrored).astype(BF)
        col_sum = tn(high * keep, row_wide[:, NB:]) + tn(low * keep, row_wide[:, NB:])
        col_out[...] += col_sum.reshape(col_out.shape)
        row_own[t] = row_sum[: 2 * FB]
        row_other[t] = row_sum[2 * FB :]


def tile_call(z_steps, me, rows, col_parts, kern, owned, mirrored, col_in=None):
    tiles = len(z_steps)
    vmem = pl.BlockSpec(memory_space=pltpu.VMEM)
    hbm = pl.BlockSpec(memory_space=pltpu.HBM)
    in_specs = [pl.BlockSpec(memory_space=pltpu.SMEM)] + [hbm] * (len(rows) + len(col_parts) + 1) + [vmem] * 2
    args = [me, *rows, *col_parts, kern, owned, mirrored]
    if col_in is not None:
        in_specs.append(vmem)
        args.append(col_in)
    copies = 8 + len(rows) + 4 * tiles
    return pl.pallas_call(
        functools.partial(tile_kernel, z_steps),
        in_specs=in_specs,
        out_specs=[vmem] * 3,
        out_shape=[jax.ShapeDtypeStruct((tiles, 2 * FB, NT), F32)] * 2 + [jax.ShapeDtypeStruct((N_ROW, FB, NT), F32)],
        scratch_shapes=[
            pltpu.VMEM((N_ROW, FB, WIDE), BF),
            pltpu.VMEM((tiles, 4, FB, WIDE), BF),
            pltpu.VMEM((tiles, 4, FB * COL_PTS // 128, 128), F32),
            pltpu.SemaphoreType.DMA((copies,)),
        ],
        compiler_params=pltpu.CompilerParams(vmem_limit_bytes=(46 if tiles > 1 else 32) * 2**20),
        cost_estimate=pl.CostEstimate(
            flops=2_600_000_000 * tiles, bytes_accessed=5_000_000 * tiles, transcendentals=0
        ),
        name="near_tiles" if tiles > 1 else "far_tile",
    )(*args)


def halves(pair):
    return pair.reshape(2, FB, pair.shape[-1])


def local(orbitals, targets, kernel, tile_owner):
    r, c = lax.axis_index("row"), lax.axis_index("col")
    me = jnp.stack([r // 2, r % 2, c // 4, c // 2 % 2, c % 2]).astype(jnp.int32)

    packed = pack(orbitals, targets).reshape(DEVICES, 8, 4 * FB)
    packed = lax.all_to_all(packed, AXES, split_axis=0, concat_axis=0, tiled=True)
    pair_y, pair_z = unpack(packed.reshape(DEVICES * 8, 4 * FB))

    y_down, y_up = send(pair_y, y=1), send(pair_y, y=3)
    z_down, z_up = send(pair_z, z=1), send(pair_z, z=3)
    y_far, y_far_other = send(y_down[:FB], y=1), send(y_up[FB:], y=3)
    z_far, z_far_other = send(z_down[:FB], z=1), send(z_up[FB:], z=3)
    col_parts = (halves(pair_y), halves(y_down), halves(y_up), y_far, y_far_other)
    near_rows = [halves(part) for own in (pair_z, z_up, z_down) for part in (own, send(own, k=1))]
    far_rows = [z_far, z_far_other, send(z_far, k=1), send(z_far_other, k=1)]

    flags = tile_owner.reshape(N_COL, N_ROW).astype(F32)
    here = (lax.broadcasted_iota(jnp.int32, flags.shape, 0) == c) & (
        lax.broadcasted_iota(jnp.int32, flags.shape, 1) == r
    )
    owned = jnp.repeat(flags, FB, axis=1).reshape(4, 2, 2, 1, COL_PTS)
    mirrored = jnp.repeat(jnp.where(here, 0.0, flags), FB, axis=1).reshape(4, 2, 2, 1, COL_PTS)
    kern = kernel.reshape(4, 2, 2, FB * COL_PTS // 128, 128)

    near_own, near_other, col_part = tile_call((0, 1, 3), me, near_rows, col_parts, kern, owned, mirrored)
    far_own, far_other, col_sum = tile_call((2,), me, far_rows, col_parts, kern, owned, mirrored, col_part)

    near = near_own + send(near_other, k=1)
    far = far_own + send(far_other, k=1)
    row_sum = near[0] + send(near[1], z=1) + send(near[2], z=3) + send(far[0], z=2)
    row_share = row_sum[:FB] + send(row_sum[FB:], xl=1)
    col_share = lax.all_to_all(col_sum, "row", split_axis=0, concat_axis=0, tiled=True).sum(axis=0)
    return row_share + col_share


def solution(mesh):
    in_specs = (
        P(("row", "col"), None),
        P(("row", "col"), None),
        P("row", "col", None),
        P("row", None, None, "col"),
    )
    out_specs = P(("row", "col"), None)
    return jax.shard_map(local, mesh=mesh, in_specs=in_specs, out_specs=out_specs, check_vma=False)
```

time: 312 us -> 127 us (0.41)
  waiting for transfers between devices: 97.8 us -> 33.6 us
  local copies, waits for them, and re-layouts: 65.1 us -> 11.7 us
  blocking collectives: 85.7 us -> 32.9 us
  matrix products: 40.5 us -> 0 us
  Pallas kernels: 0 us -> 25.5 us
  starting transfers between devices: 4.67 us -> 19.9 us
  between operations: 13.2 us -> 0.28 us
    reduce_scatter x2 -> x0, waiting for transfers between devices: 62.2 us -> none  [the longest x1 62.2 us: local(): lax.psum_scatter(row_out, 'col', scatter_dimension=0, tiled=True)]
    all_gather x2 -> x0, blocking collectives: 61.2 us -> none  [the longest x1 35.8 us: spread_points(): lax.all_gather(tgt_points, 'row', axis=1, tiled=True)]
    mul x4 -> x0, local copies, waits for them, and re-layouts: 56.6 us -> none  [the longest x2 28.3 us: local(): weighted * owned_flags[:, None, :, None]]
    dot_general x3 -> x0, matrix products: 40.5 us -> none  [the longest x1 14.6 us: local(): lax.dot_general(col_terms, row_tgt.astype(jnp.float32), (((0,), (1,)), ((...]
    all_gather x2 -> x0, waiting for transfers between devices: 34.8 us -> none  [the longest x1 34.8 us: spread_points(): lax.all_gather(orb_points, 'col', axis=1, tiled=True)]
    ppermute x0 -> x19, waiting for transfers between devices: none -> 32.4 us  [send(): return lax.ppermute(x, AXES, moved(**steps))]
    pallas_call x0 -> x4, Pallas kernels: none -> 25.5 us  [the longest x2 22.9 us: tile_call(): pl.pallas_call(functools.partial(tile_kernel, z_steps), in_specs=in_specs...]
    ppermute x0 -> x19, starting transfers between devices: none -> 16.4 us  [send(): return lax.ppermute(x, AXES, moved(**steps))]
  transfers between devices with their start and end apart: 5 -> 20, of which waited for: 2 -> 8; matrix products, arithmetic and copies ran while one was open for 23% -> 6% of each run, Pallas kernels for 0% -> 18%
where the time goes in v3:
time: 127 us
  waiting for transfers between devices  33.6 us (26%)
  blocking collectives  32.9 us (26%)
  Pallas kernels  25.5 us (20%)
  starting transfers between devices  19.9 us (16%)
  local copies, waits for them, and re-layouts  11.7 us (9%)
  other arithmetic  3.04 us (2%)
    all_to_all x1, blocking collectives, local(): lax.all_to_all(packed, AXES, split_axis=0, concat_axis=0, tiled=True)  32.9 us
    ppermute x19, waiting for transfers between devices, send(): return lax.ppermute(x, AXES, moved(**steps))  32.4 us
    pallas_call x2, Pallas kernels, tile_call(): pl.pallas_call(functools.partial(tile_kernel, z_steps), in_specs=in_specs...  22.9 us
    ppermute x19, starting transfers between devices, send(): return lax.ppermute(x, AXES, moved(**steps))  16.4 us
    unnamed x14, local copies, waits for them, and re-layouts  5.71 us
    all_to_all x1, starting transfers between devices, local(): lax.all_to_all(col_sum, 'row', split_axis=0, concat_axis=0, tiled=True)  3.54 us
    slice x2, local copies, waits for them, and re-layouts, local(): z_far, z_far_other = (send(z_down[:FB], z=1), send(z_up[FB:], z=3))  3.51 us
  transfers between devices with their start and end apart: 20, of which 8 were waited for; matrix products, arithmetic and copies ran while one was open for 6% of the time, Pallas kernels for 18%

profile of v3, /device:TPU:0, one launch (start us, length us, event | category | flops | bytes accessed | tf_op | source)
XLA Modules:
  0.0 127.0 jit_solution(3477062926800490351)
XLA Ops:
  0.0 1.1 convert_reduce_fusion
  1.1 0.1 reshape.58.tgt
  1.2 1.0 copy-done.5
  2.2 0.5 pack.1
  2.7 32.9 %all_to_all.10 = bf16[128,8,640]{2,1,0:T(8,128)(2,1)S(1)} all-to-all(bf16[128,8,640]{2,1,0:T(8,128)(2,1)S(1)} %bitcast.39), channel_id=1, replica_groups=mesh['row'=8,'col'=16] {'row','col'}, dimensions={0} | all-to-all | bytes 2621440 | tf_op jit(solution)/shard_map/all_to_all | solution.py:218
  35.6 2.1 %unpack.1 = (bf16[320,1152]{1,0:T(8,128)(2,1)S(1)}, bf16[320,1152]{1,0:T(8,128)(2,1)}) custom-call(bf16[1024,640]{1,0:T(8,128)(2,1)S(1)} %bitcast.38), custom_call_target="tpu_custom_call" | custom-call | tf_op jit(solution)/shard_map/unpack/pallas_call | solution.py:92
  37.8 0.8 collective-permute-start.1
  38.6 1.2 collective-permute-start.3
  39.8 3.2 %collective-permute-start.6 = (bf16[320,1152]{1,0:T(8,128)(2,1)S(1)}, bf16[320,1152]{1,0:T(8,128)(2,1)S(1)}, u32[]{:S(2)}, u32[]{:S(2)}) collective-permute-start(bf16[320,1152]{1,0:T(8,128)(2,1)S(1)} %get-tuple-element.14), channel_id=1, source_target_pairs={{0,96},{1,97},{2,98},{3,99},{4,100},{5,101},{6,102},{7,103},{8,104... | collective-permute-start | bytes 2211848 | tf_op jit(solution)/shard_map/ppermute | solution.py:34
  43.0 13.8 %collective-permute-done.5 = bf16[320,1152]{1,0:T(8,128)(2,1)S(1)} collective-permute-done((bf16[320,1152]{1,0:T(8,128)(2,1)S(1)}, bf16[320,1152]{1,0:T(8,128)(2,1)S(1)}, u32[]{:S(2)}, u32[]{:S(2)}) %collective-permute-start.5) | collective-permute-done | bytes 737312 | tf_op jit(solution)/shard_map/ppermute | solution.py:34
  56.8 0.8 slice.36
  57.7 0.1 collective-permute-start.2
  57.8 0.5 collective-permute-start.4
  58.3 0.8 slice.37
  59.1 3.2 %collective-permute-start.8 = (bf16[160,1152]{1,0:T(8,128)(2,1)}, bf16[160,1152]{1,0:T(8,128)(2,1)S(1)}, u32[]{:S(2)}, u32[]{:S(2)}) collective-permute-start(bf16[160,1152]{1,0:T(8,128)(2,1)} %slice.37), channel_id=1, source_target_pairs={{0,96},{1,97},{2,98},{3,99},{4,100},{5,101},{6,102},{7,103},{8,104... | collective-permute-start | bytes 1105928 | tf_op jit(solution)/shard_map/ppermute | solution.py:34
  62.3 1.8 %slice.41 = bf16[160,1152]{1,0:T(8,128)(2,1)} slice(bf16[320,1152]{1,0:T(8,128)(2,1)} %collective-permute-done.3), slice={[0:160], [0:1152]} | slice | bytes 737280 | tf_op jit(solution)/shard_map/slice | solution.py:224
  64.0 1.7 %slice.42 = bf16[160,1152]{1,0:T(8,128)(2,1)} slice(bf16[320,1152]{1,0:T(8,128)(2,1)} %collective-permute-done.1), slice={[160:320], [0:1152]} | slice | bytes 737280 | tf_op jit(solution)/shard_map/slice | solution.py:224
  65.8 0.2 collective-permute-start.12
  65.9 2.3 %collective-permute-done.7.refs_9_.refs_7_ = bf16[160,1152]{1,0:T(8,128)(2,1)S(1)} collective-permute-done((bf16[160,1152]{1,0:T(8,128)(2,1)}, bf16[160,1152]{1,0:T(8,128)(2,1)S(1)}, u32[]{:S(2)}, u32[]{:S(2)}) %collective-permute-start.7) | collective-permute-done | bytes 368672 | tf_op jit(solution)/shard_map/ppermute | solution.py:34
  68.2 0.8 collective-permute-start.13
  69.0 0.1 and_select_fusion
  69.1 0.1 copy.10
  69.2 0.1 broadcast_in_dim.12
  69.3 0.2 reshape_reshape.7.refs_13_.refs_11_
  69.4 0.1 copy.9
  69.5 0.1 broadcast_in_dim.10
  69.6 0.2 reshape_reshape.6.refs_12_.refs_10_
  69.8 0.1 stack.23.me
  69.9 7.6 %collective-permute-done.12.refs_0_ = bf16[160,1152]{1,0:T(8,128)(2,1)S(1)} collective-permute-done((bf16[160,1152]{1,0:T(8,128)(2,1)}, bf16[160,1152]{1,0:T(8,128)(2,1)S(1)}, u32[]{:S(2)}, u32[]{:S(2)}) %collective-permute-start.12) | collective-permute-done | bytes 368672 | tf_op jit(solution)/shard_map/ppermute | solution.py:34
  77.5 0.5 collective-permute-start.15
  78.0 15.2 %near_tiles.1 = (f32[3,320,128]{2,1,0:T(8,128)S(1)}, f32[3,320,128]{2,1,0:T(8,128)S(1)}, f32[8,160,128]{2,1,0:T(8,128)S(1)}) custom-call(s32[5]{0:T(128)S(1)} %stack.23.me, bf16[2,160,1152]{2,1,0:T(8,128)(2,1)} %bitcast.7.refs_0_, bf16[2,160,1152]{2,1,0:T(8,128)(2,1)} %bitcast.8.refs_1_, bf16[2,160,1152]{2,1,0:T(8,128)(2,1)} %bitcast.9.refs_2_, ...), custom_call_target="tpu_custom_call" | custom-call | flops 7800000000 | bytes 15000000 | tf_op jit(solution)/shard_map/near_tiles/pallas_call | solution.py:190
  93.3 0.3 collective-permute-start.9
  93.7 4.7 %copy-done = f32[2560,1,1280]{2,1,0:T(1,128)S(1)} copy-done((f32[2560,1,1280]{2,1,0:T(1,128)S(1)}, f32[2560,1,1280]{2,1,0:T(1,128)}, u32[]{:S(2)}) %copy-start) | copy-done | bytes 13107224
  98.4 7.6 %far_tile.1 = (f32[1,320,128]{2,1,0:T(8,128)S(1)}, f32[1,320,128]{2,1,0:T(8,128)S(1)}, f32[8,160,128]{2,1,0:T(8,128)}) custom-call(s32[5]{0:T(128)S(1)} %stack.23.me, bf16[160,1152]{1,0:T(8,128)(2,1)S(1)} %collective-permute-done.12.refs_0_, bf16[160,1152]{1,0:T(8,128)(2,1)} %collective-permute-done.13.refs_1_, ...), custom_call_target="tpu_custom_call" | custom-call | flops 2600000000 | bytes 5000000 | tf_op jit(solution)/shard_map/far_tile/pallas_call | solution.py:190
  106.0 0.6 collective-permute-start.16
  106.6 3.5 %all-to-all-start.1 = ((f32[8,160,128]{2,1,0:T(8,128)}), f32[8,160,128]{2,1,0:T(8,128)S(1)}, u32[]{:S(2)}, u32[]{:S(2)}) async-start(f32[8,160,128]{2,1,0:T(8,128)} %get-tuple-element.20), calls=%async_computation.1 | async-start | bytes 1310720 | tf_op jit(solution)/shard_map/all_to_all | solution.py:244
  110.1 1.2 collective-permute-start.17
  111.3 1.1 add.37
  112.4 2.4 %collective-permute-start.10 = (f32[320,128]{1,0:T(8,128)S(1)}, f32[320,128]{1,0:T(8,128)S(1)}, u32[]{:S(2)}, u32[]{:S(2)}) collective-permute-start(f32[320,128]{1,0:T(8,128)S(1)} %get-tuple-element.21), channel_id=1, source_target_pairs={{0,4},{1,5},{2,6},{3,7},{4,8},{5,9},{6,10},{7,11},{8,12},{9,13},{1... | collective-permute-start | bytes 491528 | tf_op jit(solution)/shard_map/ppermute | solution.py:34
  114.9 0.9 collective-permute-start.11
  115.8 3.0 %collective-permute-done.17 = f32[320,128]{1,0:T(8,128)S(1)} collective-permute-done((f32[320,128]{1,0:T(8,128)S(1)}, f32[320,128]{1,0:T(8,128)S(1)}, u32[]{:S(2)}, u32[]{:S(2)}) %collective-permute-start.17) | collective-permute-done | bytes 163872 | tf_op jit(solution)/shard_map/ppermute | solution.py:34
  118.8 2.6 %collective-permute-done.10 = f32[320,128]{1,0:T(8,128)S(1)} collective-permute-done((f32[320,128]{1,0:T(8,128)S(1)}, f32[320,128]{1,0:T(8,128)S(1)}, u32[]{:S(2)}, u32[]{:S(2)}) %collective-permute-start.10) | collective-permute-done | bytes 163872 | tf_op jit(solution)/shard_map/ppermute | solution.py:34
  121.4 0.3 collective-permute-done.11
  121.7 0.1 fusion.2
  121.8 0.6 collective-permute-start.18
  122.3 1.2 all-to-all-done.1
  123.5 2.8 %collective-permute-done.18 = f32[160,128]{1,0:T(8,128)S(1)} collective-permute-done((f32[160,128]{1,0:T(8,128)S(1)}, f32[160,128]{1,0:T(8,128)S(1)}, u32[]{:S(2)}, u32[]{:S(2)}) %collective-permute-start.18) | collective-permute-done | bytes 81952 | tf_op jit(solution)/shard_map/ppermute | solution.py:34
  126.3 0.6 fusion.3
  (35 shorter events, 0.2 us)
Async XLA Ops:
  1.2 1.0 copy-start.5
  37.8 19.1 %collective-permute-start.5 = (bf16[320,1152]{1,0:T(8,128)(2,1)S(1)}, bf16[320,1152]{1,0:T(8,128)(2,1)S(1)}, u32[]{:S(2)}, u32[]{:S(2)}) collective-permute-start(bf16[320,1152]{1,0:T(8,128)(2,1)S(1)} %get-tuple-element.14), channel_id=1, source_target_pairs={{0,32},{1,33},{2,34},{3,35},{4,36},{5,37},{6,38},{7,39},{8,40},{9,... | collective-permute-start | bytes 2211848 | tf_op jit(solution)/shard_map/ppermute | solution.py:34
  37.8 19.9 %collective-permute-start.1 = (bf16[320,1152]{1,0:T(8,128)(2,1)}, bf16[320,1152]{1,0:T(8,128)(2,1)}, u32[]{:S(2)}, u32[]{:S(2)}) collective-permute-start(bf16[320,1152]{1,0:T(8,128)(2,1)} %get-tuple-element.13), channel_id=1, source_target_pairs={{0,12},{1,13},{2,14},{3,15},{4,0},{5,1},{6,2},{7,3},{8,4},{9,5},{1... | collective-permute-start | bytes 2211848 | tf_op jit(solution)/shard_map/ppermute | solution.py:34
  38.6 19.2 %collective-permute-start.3 = (bf16[320,1152]{1,0:T(8,128)(2,1)}, bf16[320,1152]{1,0:T(8,128)(2,1)}, u32[]{:S(2)}, u32[]{:S(2)}) collective-permute-start(bf16[320,1152]{1,0:T(8,128)(2,1)} %get-tuple-element.13), channel_id=1, source_target_pairs={{0,4},{1,5},{2,6},{3,7},{4,8},{5,9},{6,10},{7,11},{8,12},{9,13},{1... | collective-permute-start | bytes 2211848 | tf_op jit(solution)/shard_map/ppermute | solution.py:34
  39.8 18.5 %collective-permute-start.6 = (bf16[320,1152]{1,0:T(8,128)(2,1)S(1)}, bf16[320,1152]{1,0:T(8,128)(2,1)S(1)}, u32[]{:S(2)}, u32[]{:S(2)}) collective-permute-start(bf16[320,1152]{1,0:T(8,128)(2,1)S(1)} %get-tuple-element.14), channel_id=1, source_target_pairs={{0,96},{1,97},{2,98},{3,99},{4,100},{5,101},{6,102},{7,103},{8,104... | collective-permute-start | bytes 2211848 | tf_op jit(solution)/shard_map/ppermute | solution.py:34
  43.0 22.7 %collective-permute-start = (bf16[320,1152]{1,0:T(8,128)(2,1)}, bf16[320,1152]{1,0:T(8,128)(2,1)}, u32[]{:S(2)}, u32[]{:S(2)}) collective-permute-start(bf16[320,1152]{1,0:T(8,128)(2,1)} %get-tuple-element.13), channel_id=1, source_target_pairs={{0,1},{1,0},{2,3},{3,2},{4,5},{5,4},{6,7},{7,6},{8,9},{9,8},{10,11... | collective-permute-start | bytes 2211848 | tf_op jit(solution)/shard_map/ppermute | solution.py:34
  56.8 8.9 %copy-start.1 = (bf16[320,1152]{1,0:T(8,128)(2,1)}, bf16[320,1152]{1,0:T(8,128)(2,1)S(1)}, u32[]{:S(2)}) copy-start(bf16[320,1152]{1,0:T(8,128)(2,1)S(1)} %collective-permute-done.5) | copy-start | bytes 2211844
  57.7 11.4 %copy-start.6 = (s32[1,16,8,1]{1,3,2,0:T(1,128)S(1)}, s32[1,16,8,1]{1,3,2,0:T(1,128)}, u32[]{:S(2)}) copy-start(s32[1,16,8,1]{1,3,2,0:T(1,128)} %param.7) | copy-start | bytes 1540
  57.7 10.6 %collective-permute-start.7 = (bf16[160,1152]{1,0:T(8,128)(2,1)}, bf16[160,1152]{1,0:T(8,128)(2,1)S(1)}, u32[]{:S(2)}, u32[]{:S(2)}) collective-permute-start(bf16[160,1152]{1,0:T(8,128)(2,1)} %slice.36), channel_id=1, source_target_pairs={{0,32},{1,33},{2,34},{3,35},{4,36},{5,37},{6,38},{7,39},{8,40},{9,... | collective-permute-start | bytes 1105928 | tf_op jit(solution)/shard_map/ppermute | solution.py:34
  57.7 20.3 %collective-permute-start.2 = (bf16[320,1152]{1,0:T(8,128)(2,1)}, bf16[320,1152]{1,0:T(8,128)(2,1)}, u32[]{:S(2)}, u32[]{:S(2)}) collective-permute-start(bf16[320,1152]{1,0:T(8,128)(2,1)} %collective-permute-done.1), channel_id=1, source_target_pairs={{0,1},{1,0},{2,3},{3,2},{4,5},{5,4},{6,7},{7,6},{8,9},{9,8},{10,11... | collective-permute-start | bytes 2211848 | tf_op jit(solution)/shard_map/ppermute | solution.py:34
  57.8 20.2 %collective-permute-start.4 = (bf16[320,1152]{1,0:T(8,128)(2,1)}, bf16[320,1152]{1,0:T(8,128)(2,1)}, u32[]{:S(2)}, u32[]{:S(2)}) collective-permute-start(bf16[320,1152]{1,0:T(8,128)(2,1)} %collective-permute-done.3), channel_id=1, source_target_pairs={{0,1},{1,0},{2,3},{3,2},{4,5},{5,4},{6,7},{7,6},{8,9},{9,8},{10,11... | collective-permute-start | bytes 2211848 | tf_op jit(solution)/shard_map/ppermute | solution.py:34
  58.3 11.3 %copy-start.3 = (bf16[320,1152]{1,0:T(8,128)(2,1)}, bf16[320,1152]{1,0:T(8,128)(2,1)S(1)}, u32[]{:S(2)}) copy-start(bf16[320,1152]{1,0:T(8,128)(2,1)S(1)} %collective-permute-done.6) | copy-start | bytes 2211844
  59.1 18.9 %collective-permute-start.8 = (bf16[160,1152]{1,0:T(8,128)(2,1)}, bf16[160,1152]{1,0:T(8,128)(2,1)S(1)}, u32[]{:S(2)}, u32[]{:S(2)}) collective-permute-start(bf16[160,1152]{1,0:T(8,128)(2,1)} %slice.37), channel_id=1, source_target_pairs={{0,96},{1,97},{2,98},{3,99},{4,100},{5,101},{6,102},{7,103},{8,104... | collective-permute-start | bytes 1105928 | tf_op jit(solution)/shard_map/ppermute | solution.py:34
  65.8 11.7 %collective-permute-start.12 = (bf16[160,1152]{1,0:T(8,128)(2,1)}, bf16[160,1152]{1,0:T(8,128)(2,1)S(1)}, u32[]{:S(2)}, u32[]{:S(2)}) collective-permute-start(bf16[160,1152]{1,0:T(8,128)(2,1)} %slice.41), channel_id=1, source_target_pairs={{0,4},{1,5},{2,6},{3,7},{4,8},{5,9},{6,10},{7,11},{8,12},{9,13},{1... | collective-permute-start | bytes 1105928 | tf_op jit(solution)/shard_map/ppermute | solution.py:34
  68.2 9.3 %collective-permute-start.13 = (bf16[160,1152]{1,0:T(8,128)(2,1)}, bf16[160,1152]{1,0:T(8,128)(2,1)}, u32[]{:S(2)}, u32[]{:S(2)}) collective-permute-start(bf16[160,1152]{1,0:T(8,128)(2,1)} %slice.42), channel_id=1, source_target_pairs={{0,12},{1,13},{2,14},{3,15},{4,0},{5,1},{6,2},{7,3},{8,4},{9,5},{1... | collective-permute-start | bytes 1105928 | tf_op jit(solution)/shard_map/ppermute | solution.py:34
  77.5 16.1 %collective-permute-start.14 = (bf16[160,1152]{1,0:T(8,128)(2,1)S(1)}, bf16[160,1152]{1,0:T(8,128)(2,1)S(1)}, u32[]{:S(2)}, u32[]{:S(2)}) collective-permute-start(bf16[160,1152]{1,0:T(8,128)(2,1)S(1)} %collective-permute-done.12.refs_0_), channel_id=1, source_target_pairs={{0,1},{1,0},{2,3},{3,2},{4,5},{5,4},{6,7},{7,6},{8,9},{9,8},{10,11... | collective-permute-start | bytes 1105928 | tf_op jit(solution)/shard_map/ppermute | solution.py:34
  77.5 16.1 %collective-permute-start.15 = (bf16[160,1152]{1,0:T(8,128)(2,1)}, bf16[160,1152]{1,0:T(8,128)(2,1)S(1)}, u32[]{:S(2)}, u32[]{:S(2)}) collective-permute-start(bf16[160,1152]{1,0:T(8,128)(2,1)} %collective-permute-done.13.refs_1_), channel_id=1, source_target_pairs={{0,1},{1,0},{2,3},{3,2},{4,5},{5,4},{6,7},{7,6},{8,9},{9,8},{10,11... | collective-permute-start | bytes 1105928 | tf_op jit(solution)/shard_map/ppermute | solution.py:34
  78.0 15.6 %copy-start.2 = (bf16[320,1152]{1,0:T(8,128)(2,1)S(1)}, bf16[320,1152]{1,0:T(8,128)(2,1)}, u32[]{:S(2)}) copy-start(bf16[320,1152]{1,0:T(8,128)(2,1)} %copy-done.1) | copy-start | bytes 2211844
  78.0 15.6 %copy-start.4 = (bf16[320,1152]{1,0:T(8,128)(2,1)S(1)}, bf16[320,1152]{1,0:T(8,128)(2,1)}, u32[]{:S(2)}) copy-start(bf16[320,1152]{1,0:T(8,128)(2,1)} %copy-done.3) | copy-start | bytes 2211844
  93.3 18.0 %collective-permute-start.9 = (f32[3,320,128]{2,1,0:T(8,128)S(1)}, f32[3,320,128]{2,1,0:T(8,128)}, u32[]{:S(2)}, u32[]{:S(2)}) collective-permute-start(f32[3,320,128]{2,1,0:T(8,128)S(1)} %get-tuple-element.16), channel_id=1, source_target_pairs={{0,1},{1,0},{2,3},{3,2},{4,5},{5,4},{6,7},{7,6},{8,9},{9,8},{10,11... | collective-permute-start | bytes 1474568 | tf_op jit(solution)/shard_map/ppermute | solution.py:34
  93.6 4.7 %copy-start = (f32[2560,1,1280]{2,1,0:T(1,128)S(1)}, f32[2560,1,1280]{2,1,0:T(1,128)}, u32[]{:S(2)}) copy-start(f32[2560,1,1280]{2,1,0:T(1,128)} %param.6) | copy-start | bytes 39321604
  106.0 4.1 %collective-permute-start.16 = (f32[1,320,128]{2,1,0:T(8,128)S(1)}, f32[1,320,128]{2,1,0:T(8,128)S(1)}, u32[]{:S(2)}, u32[]{:S(2)}) collective-permute-start(f32[1,320,128]{2,1,0:T(8,128)S(1)} %get-tuple-element.19), channel_id=1, source_target_pairs={{0,1},{1,0},{2,3},{3,2},{4,5},{5,4},{6,7},{7,6},{8,9},{9,8},{10,11... | collective-permute-start | bytes 491528 | tf_op jit(solution)/shard_map/ppermute | solution.py:34
  106.6 17.0 %all-to-all-start.1 = ((f32[8,160,128]{2,1,0:T(8,128)}), f32[8,160,128]{2,1,0:T(8,128)S(1)}, u32[]{:S(2)}, u32[]{:S(2)}) async-start(f32[8,160,128]{2,1,0:T(8,128)} %get-tuple-element.20), calls=%async_computation.1 | async-start | bytes 1310720 | tf_op jit(solution)/shard_map/all_to_all | solution.py:244
  110.1 8.6 %collective-permute-start.17 = (f32[320,128]{1,0:T(8,128)S(1)}, f32[320,128]{1,0:T(8,128)S(1)}, u32[]{:S(2)}, u32[]{:S(2)}) collective-permute-start(f32[320,128]{1,0:T(8,128)S(1)} %add_bitcast_fusion), channel_id=1, source_target_pairs={{0,8},{1,9},{2,10},{3,11},{4,12},{5,13},{6,14},{7,15},{8,0},{9,1},... | collective-permute-start | bytes 491528 | tf_op jit(solution)/shard_map/ppermute | solution.py:34
  112.4 8.9 %collective-permute-start.10 = (f32[320,128]{1,0:T(8,128)S(1)}, f32[320,128]{1,0:T(8,128)S(1)}, u32[]{:S(2)}, u32[]{:S(2)}) collective-permute-start(f32[320,128]{1,0:T(8,128)S(1)} %get-tuple-element.21), channel_id=1, source_target_pairs={{0,4},{1,5},{2,6},{3,7},{4,8},{5,9},{6,10},{7,11},{8,12},{9,13},{1... | collective-permute-start | bytes 491528 | tf_op jit(solution)/shard_map/ppermute | solution.py:34
  114.9 6.9 %collective-permute-start.11 = (f32[320,128]{1,0:T(8,128)S(1)}, f32[320,128]{1,0:T(8,128)S(1)}, u32[]{:S(2)}, u32[]{:S(2)}) collective-permute-start(f32[320,128]{1,0:T(8,128)S(1)} %get-tuple-element.22), channel_id=1, source_target_pairs={{0,12},{1,13},{2,14},{3,15},{4,0},{5,1},{6,2},{7,3},{8,4},{9,5},{1... | collective-permute-start | bytes 491528 | tf_op jit(solution)/shard_map/ppermute | solution.py:34
  121.8 4.5 %collective-permute-start.18 = (f32[160,128]{1,0:T(8,128)S(1)}, f32[160,128]{1,0:T(8,128)S(1)}, u32[]{:S(2)}, u32[]{:S(2)}) collective-permute-start(f32[160,128]{1,0:T(8,128)S(1)} %slice.44), channel_id=1, source_target_pairs={{0,2},{1,3},{2,0},{3,1},{4,6},{5,7},{6,4},{7,5},{8,10},{9,11},{10,... | collective-permute-start | bytes 245768 | tf_op jit(solution)/shard_map/ppermute | solution.py:34

commit v4 on v3

v4 whole, which is shorter than its diff:
```python
import itertools

import jax
import jax.numpy as jnp
from jax import lax
from jax.experimental import pallas as pl
from jax.experimental.pallas import tpu as pltpu
from jax.sharding import PartitionSpec as P

N_ROW, N_COL, FB, NB, NT = 8, 16, 160, 1024, 128
DEVICES = N_ROW * N_COL
ROW_PTS, COL_PTS = N_COL * FB, N_ROW * FB
WIDE = NB + NT
AXES = ("row", "col")
PARTS = {"y": 4, "xh": 2, "z": 4, "xl": 2, "k": 2}
TILE = 4 * FB
POINTS = 8 * FB
SENT = 2944
BF, F32 = jnp.bfloat16, jnp.float32


def index_of(y, xh, z, xl, k):
    return (y * 2 + xh) * N_COL + z * 4 + xl * 2 + k


def moved(**steps):
    pairs = []
    for at in itertools.product(*map(range, PARTS.values())):
        to = [(a + steps.get(name, 0)) % size for a, (name, size) in zip(at, PARTS.items())]
        pairs.append((index_of(*at), index_of(*to)))
    return pairs


def send(x, **steps):
    return lax.ppermute(x, AXES, moved(**steps))


def nn(a, b):
    return jnp.dot(a, b, preferred_element_type=F32)


def nt(a, b):
    return lax.dot_general(a, b, (((1,), (1,)), ((), ())), preferred_element_type=F32)


def tn(a, b):
    return lax.dot_general(a, b, (((0,), (0,)), ((), ())), preferred_element_type=F32)


def pack_kernel(orb, tgt, out, split):
    split[0] = tgt[:, :128]
    split[1, :, : FB - 128] = tgt[:, 128:]

    def joined(blocks):
        return jnp.concatenate([orb[:, q * FB : (q + 1) * FB].astype(F32) for q in blocks], axis=1)

    def paired(first, second):
        return jnp.concatenate([first, second], axis=0).astype(BF)

    def tgt_rows(start, stride):
        at = pl.ds(start, 8, stride=stride)
        return jnp.concatenate([split[0, at, :], split[1, at, :][:, : FB - 128]], axis=1)

    fill = jnp.zeros((8, SENT - 2 * POINTS - 2 * FB), F32)
    row_part = [paired(*(joined(range(r * N_COL + 1 - k, (r + 1) * N_COL, 2)) for k in (0, 1))) for r in range(N_ROW)]
    for half in range(N_COL // 2):
        col_part = paired(*(joined(range(2 * half + k, DEVICES, N_COL)) for k in (0, 1)))
        for r in range(N_ROW):
            at = pl.ds((r * N_COL + 2 * half) * 8, 16)
            out[at, :POINTS] = col_part
            out[at, POINTS : 2 * POINTS] = row_part[r]
            out[at, 2 * POINTS :] = paired(
                *(
                    jnp.concatenate([tgt_rows(2 * half + k, N_COL), tgt_rows(r * N_COL + 1 - k, 2), fill], axis=1)
                    for k in (0, 1)
                )
            )


def pack(orbitals, targets):
    return pl.pallas_call(
        pack_kernel,
        out_shape=jax.ShapeDtypeStruct((DEVICES * 8, SENT), BF),
        scratch_shapes=[pltpu.VMEM((2, DEVICES, 128), F32)],
        compiler_params=pltpu.CompilerParams(vmem_limit_bytes=40 * 2**20),
        name="pack",
    )(orbitals, targets.astype(F32).reshape(DEVICES, FB))


def unpack_kernel(packed, rows, tcol):
    source = lax.broadcasted_iota(jnp.int32, (NB, NB), 0)
    target = lax.broadcasted_iota(jnp.int32, (NB, NB), 1)
    order = jnp.where(source == lax.rem(target, NT) * 8 + target // NT, 1.0, 0.0).astype(BF)
    tgt = tn(packed[:, 2 * POINTS :], order).astype(BF)
    turned = packed[:, POINTS : 2 * POINTS].T
    for b in range(8):
        at = slice(b * NT, (b + 1) * NT)
        tcol[b * FB : (b + 1) * FB, :] = tgt[:FB, at]
        rows[b, :, :NB] = turned[b * FB : (b + 1) * FB]
        rows[b, :, NB:] = tgt[FB : 2 * FB, at]


def unpack(packed):
    return pl.pallas_call(
        unpack_kernel,
        out_shape=[jax.ShapeDtypeStruct((8, FB, WIDE), BF), jax.ShapeDtypeStruct((POINTS, NT), BF)],
        compiler_params=pltpu.CompilerParams(vmem_limit_bytes=40 * 2**20),
        name="unpack",
    )(packed)


def tile_kernel(me, rows, packed, tcol, kern, owned, mirrored, *refs):
    col_in, refs = (refs[0], refs[1:]) if len(refs) == 7 else (None, refs)
    row_out, col_out, cols, row_buf, stored, sems = refs
    z, xl, core = me[0], me[1], me[2]

    def place(t, b):
        return lax.rem(z + 2 * t + b // 2, 4), lax.rem(xl + b % 2, 2)

    count = [0]

    def start(src, dst):
        copy = pltpu.make_async_copy(src, dst, sems.at[count[0]])
        count[0] += 1
        copy.start()
        return copy

    col_copy = start(packed.at[:, pl.ds(0, POINTS)], cols)
    row_copies, kern_copies = [], []
    for t in range(2):
        spots = [place(t, b) for b in range(4)]
        row_copies.append([start(rows.at[zz * 2 + xx], row_buf.at[t, b]) for b, (zz, xx) in enumerate(spots)])
        kern_copies.append([start(kern.at[zz, xx, core], stored.at[t, b]) for b, (zz, xx) in enumerate(spots)])
    if col_in is None:
        col_out[...] = jnp.zeros_like(col_out)
    else:
        col_out[...] = col_in[...]
    col_copy.wait()

    for t in range(2):
        for copy in row_copies[t]:
            copy.wait()
        row_wide = row_buf[t].reshape(TILE, WIDE)
        gram = nn(row_wide[:, :NB], cols[...])
        for copy in kern_copies[t]:
            copy.wait()
        chunks = COL_PTS // 128
        values = jnp.concatenate(
            [
                jnp.concatenate([stored[t, b, pl.ds(j, FB, stride=chunks), :] for j in range(chunks)], axis=1)
                for b in range(4)
            ],
            axis=0,
        )

        def spread(ref):
            return jnp.concatenate(
                [jnp.broadcast_to(ref[(*place(t, b), core)], (FB, COL_PTS)) for b in range(4)], axis=0
            )

        weighted = gram * values * spread(owned)
        high = weighted.astype(BF)
        low = (weighted - high.astype(F32)).astype(BF)
        row_sum = nn(high, tcol[...]) + nn(low, tcol[...])
        keep = spread(mirrored).astype(BF)
        col_sum = tn(high * keep, row_wide[:, NB:]) + tn(low * keep, row_wide[:, NB:])
        col_out[...] += col_sum.reshape(col_out.shape)
        row_out[2 * t : 2 * t + 2] = row_sum.reshape(2, 2 * FB, NT)


def tile_call(me, rows, packed, tcol, kern, owned, mirrored, col_in=None):
    vmem = pl.BlockSpec(memory_space=pltpu.VMEM)
    hbm = pl.BlockSpec(memory_space=pltpu.HBM)
    in_specs = [pl.BlockSpec(memory_space=pltpu.SMEM), hbm, hbm, vmem, hbm, vmem, vmem]
    args = [me, rows, packed, tcol, kern, owned, mirrored]
    if col_in is not None:
        in_specs.append(vmem)
        args.append(col_in)
    return pl.pallas_call(
        tile_kernel,
        in_specs=in_specs,
        out_specs=[vmem] * 2,
        out_shape=[jax.ShapeDtypeStruct((4, 2 * FB, NT), F32), jax.ShapeDtypeStruct((N_ROW, FB, NT), F32)],
        scratch_shapes=[
            pltpu.VMEM((NB, POINTS), BF),
            pltpu.VMEM((2, 4, FB, WIDE), BF),
            pltpu.VMEM((2, 4, FB * COL_PTS // 128, 128), F32),
            pltpu.SemaphoreType.DMA((17,)),
        ],
        compiler_params=pltpu.CompilerParams(vmem_limit_bytes=52 * 2**20),
        cost_estimate=pl.CostEstimate(flops=5_000_000_000, bytes_accessed=13_000_000, transcendentals=0),
        name="own_core_tiles" if col_in is not None else "other_core_tiles",
    )(*args)


def local(orbitals, targets, kernel, tile_owner):
    r, c = lax.axis_index("row"), lax.axis_index("col")
    z, xl, k = c // 4, c // 2 % 2, c % 2

    packed = pack(orbitals, targets).reshape(DEVICES, 8, SENT)
    packed = lax.all_to_all(packed, AXES, split_axis=0, concat_axis=0, tiled=True)
    packed = packed.reshape(DEVICES * 8, SENT)
    rows_other, tcol = unpack(packed)
    rows_own = send(rows_other, k=1)

    flags = tile_owner.reshape(N_COL, N_ROW).astype(F32)
    here = (lax.broadcasted_iota(jnp.int32, flags.shape, 0) == c) & (
        lax.broadcasted_iota(jnp.int32, flags.shape, 1) == r
    )
    owned = jnp.repeat(flags, FB, axis=1).reshape(4, 2, 2, 1, COL_PTS)
    mirrored = jnp.repeat(jnp.where(here, 0.0, flags), FB, axis=1).reshape(4, 2, 2, 1, COL_PTS)
    kern = kernel.reshape(4, 2, 2, FB * COL_PTS // 128, 128)

    def me(core):
        return jnp.stack([z, xl, core]).astype(jnp.int32)

    row_other, col_part = tile_call(me(1 - k), rows_other, packed, tcol, kern, owned, mirrored)
    row_own, col_sum = tile_call(me(k), rows_own, packed, tcol, kern, owned, mirrored, col_part)

    row_sum = row_own + send(row_other, k=1)
    row_sum = row_sum[0] + send(row_sum[1], z=1) + send(row_sum[2], z=2) + send(row_sum[3], z=3)
    row_share = row_sum[:FB] + send(row_sum[FB:], xl=1)
    col_share = lax.all_to_all(col_sum, "row", split_axis=0, concat_axis=0, tiled=True).sum(axis=0)
    return row_share + col_share


def solution(mesh):
    in_specs = (
        P(("row", "col"), None),
        P(("row", "col"), None),
        P("row", "col", None),
        P("row", None, None, "col"),
    )
    out_specs = P(("row", "col"), None)
    return jax.shard_map(local, mesh=mesh, in_specs=in_specs, out_specs=out_specs, check_vma=False)
```

time: 127 us -> 144 us (1.13); the launches traced: 127 us -> 142 us
  blocking collectives: 32.9 us -> 83.5 us
  waiting for transfers between devices: 33.6 us -> 10.1 us
  starting transfers between devices: 19.9 us -> 11.6 us
  local copies, waits for them, and re-layouts: 11.7 us -> 7.05 us
    all_to_all x1, blocking collectives: 32.9 us -> 83.5 us  [local(): lax.all_to_all(packed, AXES, split_axis=0, concat_axis=0, tiled=True)]
    ppermute x19 -> x6, waiting for transfers between devices: 32.4 us -> 10.1 us  [send(): return lax.ppermute(x, AXES, moved(**steps))]
    ppermute x19 -> x6, starting transfers between devices: 16.4 us -> 8.02 us  [send(): return lax.ppermute(x, AXES, moved(**steps))]
    slice x4 -> x0, local copies, waits for them, and re-layouts: 5.14 us -> none  [the longest x2 3.51 us: local(): z_far, z_far_other = (send(z_down[:FB], z=1), send(z_up[FB:], z=3))]
    unnamed x14 -> x10, local copies, waits for them, and re-layouts: 5.71 us -> 4.36 us
  transfers between devices with their start and end apart: 20 -> 7, of which waited for: 8 -> 4; matrix products, arithmetic and copies ran while one was open for 6% -> 3% of each run, Pallas kernels for 18% -> 18%
where the time goes in v4:
time: 144 us; the launch traced here: 142 us
  blocking collectives  83.5 us (58%)
  Pallas kernels  26.5 us (18%)
  starting transfers between devices  11.6 us (8%)
  waiting for transfers between devices  10.1 us (7%)
  local copies, waits for them, and re-layouts  7.05 us (5%)
  other arithmetic  3.22 us (2%)
    all_to_all x1, blocking collectives, local(): lax.all_to_all(packed, AXES, split_axis=0, concat_axis=0, tiled=True)  83.5 us
    pallas_call x2, Pallas kernels, tile_call(): pl.pallas_call(tile_kernel, in_specs=in_specs, out_specs=[vmem] * 2, out_...  24.9 us
    ppermute x6, waiting for transfers between devices, send(): return lax.ppermute(x, AXES, moved(**steps))  10.1 us
    ppermute x6, starting transfers between devices, send(): return lax.ppermute(x, AXES, moved(**steps))  8.02 us
    unnamed x10, local copies, waits for them, and re-layouts  4.36 us
    all_to_all x1, starting transfers between devices, local(): lax.all_to_all(col_sum, 'row', split_axis=0, concat_axis=0, tiled=True)  3.55 us
  transfers between devices with their start and end apart: 7, of which 4 were waited for; matrix products, arithmetic and copies ran while one was open for 3% of the time, Pallas kernels for 18%

profile of v4, /device:TPU:0, one launch (start us, length us, event | category | flops | bytes accessed | tf_op | source)
XLA Modules:
  0.0 142.2 jit_solution(3977583307505700658)
XLA Ops:
  0.0 1.1 convert_reduce_fusion
  1.1 0.1 reshape.22.tgt
  1.2 0.0 copy-start.3
  1.2 1.0 copy-done.3
  2.2 0.6 pack.1
  2.8 83.5 %all_to_all.10 = bf16[128,8,2944]{2,1,0:T(8,128)(2,1)S(1)} all-to-all(bf16[128,8,2944]{2,1,0:T(8,128)(2,1)S(1)} %bitcast.29), channel_id=1, replica_groups=mesh['row'=8,'col'=16] {'row','col'}, dimensions={0} | all-to-all | bytes 12058624 | tf_op jit(solution)/shard_map/all_to_all | solution.py:201
  86.2 0.0 copy-start.4
  86.2 1.0 unpack.1
  87.3 0.0 copy-start
  87.3 2.6 %copy-done = bf16[128,8,2944]{2,1,0:T(8,128)(2,1)} copy-done((bf16[128,8,2944]{2,1,0:T(8,128)(2,1)}, bf16[128,8,2944]{2,1,0:T(8,128)(2,1)S(1)}, u32[]{:S(2)}) %copy-start) | copy-done | bytes 6029336
  89.8 0.0 copy-start.1
  89.8 0.0 collective-permute-start
  89.8 0.0 copy-done.4
  89.9 0.1 copy.9
  89.9 0.1 broadcast_in_dim.10
  90.0 0.2 reshape_reshape.6.owned
  90.2 0.1 and_select_fusion
  90.3 0.1 copy.10
  90.4 1.1 broadcast_in_dim.12
  91.5 1.1 reshape_reshape.7.mirrored
  92.5 0.1 pad_add_fusion.2.me
  92.6 0.0 copy-done.1
  92.6 12.1 %other_core_tiles.1 = (f32[4,320,128]{2,1,0:T(8,128)}, f32[8,160,128]{2,1,0:T(8,128)S(1)}) custom-call(s32[3]{0:T(128)S(1)} %pad_add_fusion.2.me, bf16[8,160,1152]{2,1,0:T(8,128)(2,1)} %copy-done.1, bf16[1024,2944]{1,0:T(8,128)(2,1)} %bitcast.27, bf16[1280,128]{1,0:T(8,128)(2,1)S(1)} %get-tuple-element.12.tcol, f32[4,2,2,1600,128]{4,3,2,1,0:T(8,128)} %bitcast.30, ...), custom_call_target="tpu_custom_call" | custom-call | flops 5000000000 | bytes 13000000 | tf_op jit(solution)/shard_map/other_core_tiles/pallas_call | solution.py:179
  104.7 0.0 copy-start.2
  104.8 0.8 copy-done.2
  105.6 0.2 collective-permute-start.1
  105.8 0.1 pad_add_fusion.me
  105.8 0.0 collective-permute-done.rows
  105.8 12.8 %own_core_tiles.1 = (f32[4,320,128]{2,1,0:T(8,128)S(1)}, f32[8,160,128]{2,1,0:T(8,128)}) custom-call(s32[3]{0:T(128)S(1)} %pad_add_fusion.me, bf16[8,160,1152]{2,1,0:T(8,128)(2,1)} %collective-permute-done.rows, bf16[1024,2944]{1,0:T(8,128)(2,1)} %bitcast.28, bf16[1280,128]{1,0:T(8,128)(2,1)S(1)} %get-tuple-element.12.tcol, ...), custom_call_target="tpu_custom_call" | custom-call | flops 5000000000 | bytes 13000000 | tf_op jit(solution)/shard_map/own_core_tiles/pallas_call | solution.py:179
  118.7 3.6 %all-to-all-start.1 = ((f32[8,160,128]{2,1,0:T(8,128)}), f32[8,160,128]{2,1,0:T(8,128)S(1)}, u32[]{:S(2)}, u32[]{:S(2)}) async-start(f32[8,160,128]{2,1,0:T(8,128)} %get-tuple-element.16), calls=%async_computation.1 | async-start | bytes 1310720 | tf_op jit(solution)/shard_map/all_to_all | solution.py:223
  122.2 0.0 collective-permute-done.1
  122.2 1.2 add.29
  123.4 1.9 %collective-permute-start.4 = (f32[320,128]{1,0:T(8,128)S(1)}, f32[320,128]{1,0:T(8,128)S(1)}, u32[]{:S(2)}, u32[]{:S(2)}) collective-permute-start(f32[320,128]{1,0:T(8,128)S(1)} %get-tuple-element.18), channel_id=1, source_target_pairs={{0,12},{1,13},{2,14},{3,15},{4,0},{5,1},{6,2},{7,3},{8,4},{9,5},{1... | collective-permute-start | bytes 491528 | tf_op jit(solution)/shard_map/ppermute | solution.py:35
  125.3 2.6 %collective-permute-start.3 = (f32[320,128]{1,0:T(8,128)S(1)}, f32[320,128]{1,0:T(8,128)S(1)}, u32[]{:S(2)}, u32[]{:S(2)}) collective-permute-start(f32[320,128]{1,0:T(8,128)S(1)} %get-tuple-element.19), channel_id=1, source_target_pairs={{0,8},{1,9},{2,10},{3,11},{4,12},{5,13},{6,14},{7,15},{8,0},{9,1},... | collective-permute-start | bytes 491528 | tf_op jit(solution)/shard_map/ppermute | solution.py:35
  127.9 0.6 collective-permute-start.2
  128.5 2.4 %collective-permute-done.4 = f32[320,128]{1,0:T(8,128)S(1)} collective-permute-done((f32[320,128]{1,0:T(8,128)S(1)}, f32[320,128]{1,0:T(8,128)S(1)}, u32[]{:S(2)}, u32[]{:S(2)}) %collective-permute-start.4) | collective-permute-done | bytes 163872 | tf_op jit(solution)/shard_map/ppermute | solution.py:35
  130.9 3.1 %collective-permute-done.3 = f32[320,128]{1,0:T(8,128)S(1)} collective-permute-done((f32[320,128]{1,0:T(8,128)S(1)}, f32[320,128]{1,0:T(8,128)S(1)}, u32[]{:S(2)}, u32[]{:S(2)}) %collective-permute-start.3) | collective-permute-done | bytes 163872 | tf_op jit(solution)/shard_map/ppermute | solution.py:35
  133.9 2.3 %collective-permute-done.2 = f32[320,128]{1,0:T(8,128)S(1)} collective-permute-done((f32[320,128]{1,0:T(8,128)S(1)}, f32[320,128]{1,0:T(8,128)S(1)}, u32[]{:S(2)}, u32[]{:S(2)}) %collective-permute-start.2) | collective-permute-done | bytes 163872 | tf_op jit(solution)/shard_map/ppermute | solution.py:35
  136.3 2.8 %collective-permute-start.5 = (f32[160,128]{1,0:T(8,128)S(1)}, f32[160,128]{1,0:T(8,128)S(1)}, u32[]{:S(2)}, u32[]{:S(2)}) collective-permute-start(f32[160,128]{1,0:T(8,128)S(1)} %slice.29), channel_id=1, source_target_pairs={{0,2},{1,3},{2,0},{3,1},{4,6},{5,7},{6,4},{7,5},{8,10},{9,11},{10,... | collective-permute-start | bytes 245768 | tf_op jit(solution)/shard_map/ppermute | solution.py:35
  139.1 0.0 all-to-all-done.1
  139.1 2.4 %collective-permute-done.5 = f32[160,128]{1,0:T(8,128)S(1)} collective-permute-done((f32[160,128]{1,0:T(8,128)S(1)}, f32[160,128]{1,0:T(8,128)S(1)}, u32[]{:S(2)}, u32[]{:S(2)}) %collective-permute-start.5) | collective-permute-done | bytes 81952 | tf_op jit(solution)/shard_map/ppermute | solution.py:35
  141.5 0.6 fusion.3
  (7 shorter events, 0.1 us)
Async XLA Ops:
  1.2 1.0 copy-start.3
  86.2 3.6 %copy-start.4 = (s32[1,16,8,1]{1,3,2,0:T(1,128)S(1)}, s32[1,16,8,1]{1,3,2,0:T(1,128)}, u32[]{:S(2)}) copy-start(s32[1,16,8,1]{1,3,2,0:T(1,128)} %param.7) | copy-start | bytes 1540
  87.3 2.6 %copy-start = (bf16[128,8,2944]{2,1,0:T(8,128)(2,1)}, bf16[128,8,2944]{2,1,0:T(8,128)(2,1)S(1)}, u32[]{:S(2)}) copy-start(bf16[128,8,2944]{2,1,0:T(8,128)(2,1)S(1)} %all_to_all.10) | copy-start | bytes 18087940
  89.8 2.8 %copy-start.1 = (bf16[8,160,1152]{2,1,0:T(8,128)(2,1)}, bf16[8,160,1152]{2,1,0:T(8,128)(2,1)S(1)}, u32[]{:S(2)}) copy-start(bf16[8,160,1152]{2,1,0:T(8,128)(2,1)S(1)} %get-tuple-element.11.rows) | copy-start | bytes 8847364
  89.8 16.0 %collective-permute-start = (bf16[8,160,1152]{2,1,0:T(8,128)(2,1)S(1)}, bf16[8,160,1152]{2,1,0:T(8,128)(2,1)}, u32[]{:S(2)}, u32[]{:S(2)}) collective-permute-start(bf16[8,160,1152]{2,1,0:T(8,128)(2,1)S(1)} %get-tuple-element.11.rows), channel_id=1, source_target_pairs={{0,1},{1,0},{2,3},{3,2},{4,5},{5,4},{6,7},{7,6},{8,9},{9,8},{10,11... | collective-permute-start | bytes 8847368 | tf_op jit(solution)/shard_map/ppermute | solution.py:35
  104.7 0.8 copy-start.2
  105.6 16.6 %collective-permute-start.1 = (f32[4,320,128]{2,1,0:T(8,128)}, f32[4,320,128]{2,1,0:T(8,128)}, u32[]{:S(2)}, u32[]{:S(2)}) collective-permute-start(f32[4,320,128]{2,1,0:T(8,128)} %get-tuple-element.15), channel_id=1, source_target_pairs={{0,1},{1,0},{2,3},{3,2},{4,5},{5,4},{6,7},{7,6},{8,9},{9,8},{10,11... | collective-permute-start | bytes 1966088 | tf_op jit(solution)/shard_map/ppermute | solution.py:35
  118.7 20.4 %all-to-all-start.1 = ((f32[8,160,128]{2,1,0:T(8,128)}), f32[8,160,128]{2,1,0:T(8,128)S(1)}, u32[]{:S(2)}, u32[]{:S(2)}) async-start(f32[8,160,128]{2,1,0:T(8,128)} %get-tuple-element.16), calls=%async_computation.1 | async-start | bytes 1310720 | tf_op jit(solution)/shard_map/all_to_all | solution.py:223
  123.4 7.4 %collective-permute-start.4 = (f32[320,128]{1,0:T(8,128)S(1)}, f32[320,128]{1,0:T(8,128)S(1)}, u32[]{:S(2)}, u32[]{:S(2)}) collective-permute-start(f32[320,128]{1,0:T(8,128)S(1)} %get-tuple-element.18), channel_id=1, source_target_pairs={{0,12},{1,13},{2,14},{3,15},{4,0},{5,1},{6,2},{7,3},{8,4},{9,5},{1... | collective-permute-start | bytes 491528 | tf_op jit(solution)/shard_map/ppermute | solution.py:35
  125.3 8.6 %collective-permute-start.3 = (f32[320,128]{1,0:T(8,128)S(1)}, f32[320,128]{1,0:T(8,128)S(1)}, u32[]{:S(2)}, u32[]{:S(2)}) collective-permute-start(f32[320,128]{1,0:T(8,128)S(1)} %get-tuple-element.19), channel_id=1, source_target_pairs={{0,8},{1,9},{2,10},{3,11},{4,12},{5,13},{6,14},{7,15},{8,0},{9,1},... | collective-permute-start | bytes 491528 | tf_op jit(solution)/shard_map/ppermute | solution.py:35
  127.9 8.3 %collective-permute-start.2 = (f32[320,128]{1,0:T(8,128)S(1)}, f32[320,128]{1,0:T(8,128)S(1)}, u32[]{:S(2)}, u32[]{:S(2)}) collective-permute-start(f32[320,128]{1,0:T(8,128)S(1)} %get-tuple-element.17), channel_id=1, source_target_pairs={{0,4},{1,5},{2,6},{3,7},{4,8},{5,9},{6,10},{7,11},{8,12},{9,13},{1... | collective-permute-start | bytes 491528 | tf_op jit(solution)/shard_map/ppermute | solution.py:35
  136.3 5.2 %collective-permute-start.5 = (f32[160,128]{1,0:T(8,128)S(1)}, f32[160,128]{1,0:T(8,128)S(1)}, u32[]{:S(2)}, u32[]{:S(2)}) collective-permute-start(f32[160,128]{1,0:T(8,128)S(1)} %slice.29), channel_id=1, source_target_pairs={{0,2},{1,3},{2,0},{3,1},{4,6},{5,7},{6,4},{7,5},{8,10},{9,11},{10,... | collective-permute-start | bytes 245768 | tf_op jit(solution)/shard_map/ppermute | solution.py:35

commit v5 on v3

--- a/solution.py
+++ b/solution.py
@@ -46,6 +46,10 @@
     return lax.dot_general(a, b, (((0,), (0,)), ((), ())), preferred_element_type=F32)
 
 
+def points(ref, block):
+    return ref[:, block * FB : (block + 1) * FB].astype(F32)
+
+
 def pack_kernel(orb, tgt, out):
     row = lax.broadcasted_iota(jnp.int32, (8, FB), 0)
     for pair in range(DEVICES // 2):
@@ -54,10 +58,10 @@
             sources = (q, q ^ 16, q ^ 2)
             extra = jnp.where(
                 row == 0,
-                tgt[sources[0] : sources[0] + 1, :],
-                jnp.where(row == 1, tgt[sources[1] : sources[1] + 1, :], tgt[sources[2] : sources[2] + 1, :]),
+                points(tgt, sources[0]),
+                jnp.where(row == 1, points(tgt, sources[1]), points(tgt, sources[2])),
             )
-            pieces = [orb[:, s * FB : (s + 1) * FB].astype(F32) for s in sources]
+            pieces = [points(orb, s) for s in sources]
             blocks.append(jnp.concatenate([*pieces, extra], axis=1))
         out[16 * pair : 16 * (pair + 1), :] = jnp.concatenate(blocks, axis=0).astype(BF)
 
@@ -68,7 +72,7 @@
         out_shape=jax.ShapeDtypeStruct((DEVICES * 8, 4 * FB), BF),
         compiler_params=pltpu.CompilerParams(vmem_limit_bytes=32 * 2**20),
         name="pack",
-    )(orbitals, targets.astype(F32).reshape(DEVICES, FB))
+    )(orbitals, targets)
 
 
 def unpack_kernel(packed, cols, rows):
@@ -100,7 +104,7 @@
 def tile_kernel(z_steps, me, *refs):
     tiles = len(z_steps)
     far = tiles == 1
-    n_rows = 4 if far else 2 * tiles
+    n_rows = 2 * tiles
     row_refs, refs = refs[:n_rows], refs[n_rows:]
     (pair, down, up, far_own, far_other, kern, owned, mirrored), refs = refs[:8], refs[8:]
     if far:
@@ -122,10 +126,7 @@
     def tile_copies(t):
         z_at = lax.rem(z + z_steps[t], 4)
         found = []
-        if far:
-            found += [start(row_refs[b], rows.at[0, b]) for b in range(4)]
-        else:
-            found += [start(row_refs[2 * t + b], rows.at[t, pl.ds(2 * b, 2)]) for b in range(2)]
+        found += [start(row_refs[2 * t + b], rows.at[t, pl.ds(2 * b, 2)]) for b in range(2)]
         for b in range(4):
             found.append(start(kern.at[z_at, lax.rem(xl + b % 2, 2), lax.rem(k + b // 2, 2)], stored.at[t, b]))
         return found
@@ -198,7 +199,7 @@
             pltpu.VMEM((tiles, 4, FB * COL_PTS // 128, 128), F32),
             pltpu.SemaphoreType.DMA((copies,)),
         ],
-        compiler_params=pltpu.CompilerParams(vmem_limit_bytes=(46 if tiles > 1 else 32) * 2**20),
+        compiler_params=pltpu.CompilerParams(vmem_limit_bytes=52 * 2**20),
         cost_estimate=pl.CostEstimate(
             flops=2_600_000_000 * tiles, bytes_accessed=5_000_000 * tiles, transcendentals=0
         ),
@@ -221,10 +222,10 @@
     y_down, y_up = send(pair_y, y=1), send(pair_y, y=3)
     z_down, z_up = send(pair_z, z=1), send(pair_z, z=3)
     y_far, y_far_other = send(y_down[:FB], y=1), send(y_up[FB:], y=3)
-    z_far, z_far_other = send(z_down[:FB], z=1), send(z_up[FB:], z=3)
     col_parts = (halves(pair_y), halves(y_down), halves(y_up), y_far, y_far_other)
-    near_rows = [halves(part) for own in (pair_z, z_up, z_down) for part in (own, send(own, k=1))]
-    far_rows = [z_far, z_far_other, send(z_far, k=1), send(z_far_other, k=1)]
+    across = [send(own, k=1) for own in (pair_z, z_up, z_down)]
+    near_rows = [halves(part) for both in zip((pair_z, z_up, z_down), across) for part in both]
+    far_rows = [halves(send(z_down, z=1)), halves(send(across[1], z=3))]
 
     flags = tile_owner.reshape(N_COL, N_ROW).astype(F32)
     here = (lax.broadcasted_iota(jnp.int32, flags.shape, 0) == c) & (
@@ -238,8 +239,8 @@
     far_own, far_other, col_sum = tile_call((2,), me, far_rows, col_parts, kern, owned, mirrored, col_part)
 
     near = near_own + send(near_other, k=1)
-    far = far_own + send(far_other, k=1)
-    row_sum = near[0] + send(near[1], z=1) + send(near[2], z=3) + send(far[0], z=2)
+    far = send(far_own[0], z=2) + send(far_other[0], z=2, k=1)
+    row_sum = near[0] + send(near[1], z=1) + send(near[2], z=3) + far
     row_share = row_sum[:FB] + send(row_sum[FB:], xl=1)
     col_share = lax.all_to_all(col_sum, "row", split_axis=0, concat_axis=0, tiled=True).sum(axis=0)
     return row_share + col_share

time: 127 us -> 127 us (level)
  local copies, waits for them, and re-layouts: 11.7 us -> 6.33 us
  starting transfers between devices: 19.9 us -> 24.1 us
  Pallas kernels: 25.5 us -> 28.5 us
  other arithmetic: 3.04 us -> 0.88 us
    slice x2 -> x0, local copies, waits for them, and re-layouts: 3.51 us -> none  [local(): z_far, z_far_other = (send(z_down[:FB], z=1), send(z_up[FB:], z=3))]
    unnamed x14 -> x16, local copies, waits for them, and re-layouts: 5.71 us -> 2.96 us
    all_to_all x1, starting transfers between devices: 3.54 us -> 6.08 us  [local(): lax.all_to_all(col_sum, 'row', split_axis=0, concat_axis=0, tiled=True)]
    pallas_call x1, Pallas kernels: 0.52 us -> 2.51 us  [pack(): pl.pallas_call(pack_kernel, out_shape=jax.ShapeDtypeStruct((DEVICES * 8,...]
    pallas_call x2, Pallas kernels: 22.9 us -> 24.7 us  [tile_call(): pl.pallas_call(functools.partial(tile_kernel, z_steps), in_specs=in_specs...]
    ppermute x19 -> x17, starting transfers between devices: 16.4 us -> 18.1 us  [send(): return lax.ppermute(x, AXES, moved(**steps))]
    ppermute x19 -> x17, waiting for transfers between devices: 32.4 us -> 33.1 us  [send(): return lax.ppermute(x, AXES, moved(**steps))]
  transfers between devices with their start and end apart: 20 -> 18, of which waited for: 8 -> 8; matrix products, arithmetic and copies ran while one was open for 6% -> 3% of each run, Pallas kernels for 18% -> 13%
where the time goes in v5:
time: 127 us; the launch traced here: 126 us
  waiting for transfers between devices  33.1 us (26%)
  blocking collectives  32.9 us (26%)
  Pallas kernels  28.5 us (22%)
  starting transfers between devices  24.1 us (19%)
  local copies, waits for them, and re-layouts  6.33 us (5%)
    ppermute x17, waiting for transfers between devices, send(): return lax.ppermute(x, AXES, moved(**steps))  33.1 us
    all_to_all x1, blocking collectives, local(): lax.all_to_all(packed, AXES, split_axis=0, concat_axis=0, tiled=True)  32.9 us
    pallas_call x2, Pallas kernels, tile_call(): pl.pallas_call(functools.partial(tile_kernel, z_steps), in_specs=in_specs...  24.7 us
    ppermute x17, starting transfers between devices, send(): return lax.ppermute(x, AXES, moved(**steps))  18.1 us
    all_to_all x1, starting transfers between devices, local(): lax.all_to_all(col_sum, 'row', split_axis=0, concat_axis=0, tiled=True)  6.08 us
    unnamed x16, local copies, waits for them, and re-layouts  2.96 us
    slice x2, local copies, waits for them, and re-layouts, local(): y_far, y_far_other = (send(y_down[:FB], y=1), send(y_up[FB:], y=3))  2.62 us
  transfers between devices with their start and end apart: 18, of which 8 were waited for; matrix products, arithmetic and copies ran while one was open for 3% of the time, Pallas kernels for 13%

profile of v5, /device:TPU:0, one launch (start us, length us, event | category | flops | bytes accessed | tf_op | source)
XLA Modules:
  0.0 126.0 jit_solution(12998885696350646712)
XLA Ops:
  0.0 1.0 copy-done.1
  1.0 0.9 copy-done.2
  1.9 2.5 %pack.1 = bf16[1024,640]{1,0:T(8,128)(2,1)S(1)} custom-call(bf16[8,20480]{1,0:T(8,128)(2,1)S(1)} %copy-done.1, bf16[1,20480]{1,0:T(2,128)(2,1)S(1)} %copy-done.2), custom_call_target="tpu_custom_call" | custom-call | tf_op jit(solution)/shard_map/pack/pallas_call | solution.py:70
  4.4 32.9 %all_to_all.10 = bf16[128,8,640]{2,1,0:T(8,128)(2,1)S(1)} all-to-all(bf16[128,8,640]{2,1,0:T(8,128)(2,1)S(1)} %bitcast.39), channel_id=1, replica_groups=mesh['row'=8,'col'=16] {'row','col'}, dimensions={0} | all-to-all | bytes 2621440 | tf_op jit(solution)/shard_map/all_to_all | solution.py:219
  37.3 1.2 unpack.1
  38.5 0.3 collective-permute-start.1
  38.8 1.8 %collective-permute-start.3 = (bf16[320,1152]{1,0:T(8,128)(2,1)S(1)}, bf16[320,1152]{1,0:T(8,128)(2,1)}, u32[]{:S(2)}, u32[]{:S(2)}) collective-permute-start(bf16[320,1152]{1,0:T(8,128)(2,1)S(1)} %get-tuple-element.13), channel_id=1, source_target_pairs={{0,4},{1,5},{2,6},{3,7},{4,8},{5,9},{6,10},{7,11},{8,12},{9,13},{1... | collective-permute-start | bytes 2211848 | tf_op jit(solution)/shard_map/ppermute | solution.py:34
  40.6 0.0 collective-permute-start.5
  40.6 3.2 %collective-permute-start.6 = (bf16[320,1152]{1,0:T(8,128)(2,1)S(1)}, bf16[320,1152]{1,0:T(8,128)(2,1)}, u32[]{:S(2)}, u32[]{:S(2)}) collective-permute-start(bf16[320,1152]{1,0:T(8,128)(2,1)S(1)} %get-tuple-element.14), channel_id=1, source_target_pairs={{0,96},{1,97},{2,98},{3,99},{4,100},{5,101},{6,102},{7,103},{8,104... | collective-permute-start | bytes 2211848 | tf_op jit(solution)/shard_map/ppermute | solution.py:34
  43.9 12.7 %collective-permute-done.1 = bf16[320,1152]{1,0:T(8,128)(2,1)} collective-permute-done((bf16[320,1152]{1,0:T(8,128)(2,1)S(1)}, bf16[320,1152]{1,0:T(8,128)(2,1)}, u32[]{:S(2)}, u32[]{:S(2)}) %collective-permute-start.1) | collective-permute-done | bytes 737312 | tf_op jit(solution)/shard_map/ppermute | solution.py:34
  56.6 1.3 %collective-permute-done.3 = bf16[320,1152]{1,0:T(8,128)(2,1)} collective-permute-done((bf16[320,1152]{1,0:T(8,128)(2,1)S(1)}, bf16[320,1152]{1,0:T(8,128)(2,1)}, u32[]{:S(2)}, u32[]{:S(2)}) %collective-permute-start.3) | collective-permute-done | bytes 737312 | tf_op jit(solution)/shard_map/ppermute | solution.py:34
  57.9 1.3 collective-permute-done.5
  59.2 0.9 slice.28
  60.0 0.0 collective-permute-done.6
  60.0 1.8 %slice.29 = bf16[160,1152]{1,0:T(8,128)(2,1)} slice(bf16[320,1152]{1,0:T(8,128)(2,1)} %collective-permute-done.6), slice={[160:320], [0:1152]} | slice | bytes 737280 | tf_op jit(solution)/shard_map/slice | solution.py:224
  61.8 3.2 %collective-permute-start.8 = (bf16[160,1152]{1,0:T(8,128)(2,1)}, bf16[160,1152]{1,0:T(8,128)(2,1)S(1)}, u32[]{:S(2)}, u32[]{:S(2)}) collective-permute-start(bf16[160,1152]{1,0:T(8,128)(2,1)} %slice.29), channel_id=1, source_target_pairs={{0,96},{1,97},{2,98},{3,99},{4,100},{5,101},{6,102},{7,103},{8,104... | collective-permute-start | bytes 1105928 | tf_op jit(solution)/shard_map/ppermute | solution.py:34
  65.0 0.1 and_select_fusion
  65.1 0.1 copy.7
  65.2 0.1 broadcast_in_dim.12
  65.3 0.2 reshape_reshape.7.refs_13_.refs_9_
  65.4 0.1 copy.6
  65.5 0.1 broadcast_in_dim.10
  65.6 0.2 reshape_reshape.6.refs_12_.refs_8_
  65.8 0.1 stack.23.me
  65.9 0.0 collective-permute-done
  65.9 0.3 collective-permute-start.12
  66.2 3.0 %collective-permute-start.13 = (bf16[320,1152]{1,0:T(8,128)(2,1)}, bf16[320,1152]{1,0:T(8,128)(2,1)S(1)}, u32[]{:S(2)}, u32[]{:S(2)}) collective-permute-start(bf16[320,1152]{1,0:T(8,128)(2,1)} %collective-permute-done.2), channel_id=1, source_target_pairs={{0,12},{1,13},{2,14},{3,15},{4,0},{5,1},{6,2},{7,3},{8,4},{9,5},{1... | collective-permute-start | bytes 2211848 | tf_op jit(solution)/shard_map/ppermute | solution.py:34
  69.1 2.1 %collective-permute-done.7.refs_9_.refs_5_ = bf16[160,1152]{1,0:T(8,128)(2,1)S(1)} collective-permute-done((bf16[160,1152]{1,0:T(8,128)(2,1)}, bf16[160,1152]{1,0:T(8,128)(2,1)S(1)}, u32[]{:S(2)}, u32[]{:S(2)}) %collective-permute-start.7) | collective-permute-done | bytes 368672 | tf_op jit(solution)/shard_map/ppermute | solution.py:34
  71.2 1.1 collective-permute-done.8.refs_10_.refs_6_
  72.3 0.0 collective-permute-done.4
  72.3 16.0 %near_tiles.1 = (f32[3,320,128]{2,1,0:T(8,128)S(1)}, f32[3,320,128]{2,1,0:T(8,128)S(1)}, f32[8,160,128]{2,1,0:T(8,128)}) custom-call(s32[5]{0:T(128)S(1)} %stack.23.me, bf16[2,160,1152]{2,1,0:T(8,128)(2,1)} %bitcast.42, bf16[2,160,1152]{2,1,0:T(8,128)(2,1)} %bitcast.8.refs_1_, bf16[2,160,1152]{2,1,0:T(8,128)(2,1)} %bitcast.9.refs_2_, ...), custom_call_target="tpu_custom_call" | custom-call | flops 7800000000 | bytes 15000000 | tf_op jit(solution)/shard_map/near_tiles/pallas_call | solution.py:191
  88.3 0.3 collective-permute-start.9
  88.6 1.9 %collective-permute-done.9 = f32[3,320,128]{2,1,0:T(8,128)S(1)} collective-permute-done((f32[3,320,128]{2,1,0:T(8,128)S(1)}, f32[3,320,128]{2,1,0:T(8,128)S(1)}, u32[]{:S(2)}, u32[]{:S(2)}) %collective-permute-start.9) | collective-permute-done | bytes 491552 | tf_op jit(solution)/shard_map/ppermute | solution.py:34
  90.5 0.1 add.37
  90.5 0.0 collective-permute-done.13
  90.6 0.8 copy-done.5
  91.4 0.2 copy-done.6
  91.6 8.8 %far_tile.1 = (f32[1,320,128]{2,1,0:T(8,128)S(1)}, f32[1,320,128]{2,1,0:T(8,128)S(1)}, f32[8,160,128]{2,1,0:T(8,128)}) custom-call(s32[5]{0:T(128)S(1)} %stack.23.me, bf16[2,160,1152]{2,1,0:T(8,128)(2,1)} %bitcast.49, bf16[2,160,1152]{2,1,0:T(8,128)(2,1)} %bitcast.50, bf16[2,160,1152]{2,1,0:T(8,128)(2,1)} %bitcast.41, bf16[2,160,1152]{2,1,0:T(8,128)(2,1)} %bitcast.48, ...), custom_call_target="tpu_custom_call" | custom-call | flops 2600000000 | bytes 5000000 | tf_op jit(solution)/shard_map/far_tile/pallas_call | solution.py:191
  100.4 6.1 %all-to-all-start.1 = ((f32[8,160,128]{2,1,0:T(8,128)}), f32[8,160,128]{2,1,0:T(8,128)S(1)}, u32[]{:S(2)}, u32[]{:S(2)}) async-start(f32[8,160,128]{2,1,0:T(8,128)} %get-tuple-element.20), calls=%async_computation.1 | async-start | bytes 1310720 | tf_op jit(solution)/shard_map/all_to_all | solution.py:245
  106.5 0.1 collective-permute-start.10
  106.6 3.2 %collective-permute-start.11 = (f32[320,128]{1,0:T(8,128)S(1)}, f32[320,128]{1,0:T(8,128)S(1)}, u32[]{:S(2)}, u32[]{:S(2)}) collective-permute-start(f32[320,128]{1,0:T(8,128)S(1)} %get-tuple-element.22), channel_id=1, source_target_pairs={{0,12},{1,13},{2,14},{3,15},{4,0},{5,1},{6,2},{7,3},{8,4},{9,5},{1... | collective-permute-start | bytes 491528 | tf_op jit(solution)/shard_map/ppermute | solution.py:34
  109.8 2.2 %collective-permute-start.15 = (f32[320,128]{1,0:T(8,128)S(1)}, f32[320,128]{1,0:T(8,128)S(1)}, u32[]{:S(2)}, u32[]{:S(2)}) collective-permute-start(f32[320,128]{1,0:T(8,128)S(1)} %bitcast.43), channel_id=1, source_target_pairs={{0,9},{1,8},{2,11},{3,10},{4,13},{5,12},{6,15},{7,14},{8,1},{9,0},... | collective-permute-start | bytes 491528 | tf_op jit(solution)/shard_map/ppermute | solution.py:34
  112.0 8.8 %collective-permute-done.10 = f32[320,128]{1,0:T(8,128)S(1)} collective-permute-done((f32[320,128]{1,0:T(8,128)S(1)}, f32[320,128]{1,0:T(8,128)S(1)}, u32[]{:S(2)}, u32[]{:S(2)}) %collective-permute-start.10) | collective-permute-done | bytes 163872 | tf_op jit(solution)/shard_map/ppermute | solution.py:34
  120.8 0.0 collective-permute-done.11
  120.8 0.1 fusion.2
  120.9 0.5 collective-permute-start.16
  121.4 4.0 %collective-permute-done.16 = f32[160,128]{1,0:T(8,128)S(1)} collective-permute-done((f32[160,128]{1,0:T(8,128)S(1)}, f32[160,128]{1,0:T(8,128)S(1)}, u32[]{:S(2)}, u32[]{:S(2)}) %collective-permute-start.16) | collective-permute-done | bytes 81952 | tf_op jit(solution)/shard_map/ppermute | solution.py:34
  125.4 0.6 fusion.3
  (28 shorter events, 0.1 us)
Async XLA Ops:
  0.0 1.0 copy-start.1
  1.0 0.9 copy-start.2
  37.3 27.7 %copy-start.7 = (s32[1,16,8,1]{1,3,2,0:T(1,128)S(1)}, s32[1,16,8,1]{1,3,2,0:T(1,128)}, u32[]{:S(2)}) copy-start(s32[1,16,8,1]{1,3,2,0:T(1,128)} %param.7) | copy-start | bytes 1540
  38.5 33.8 %copy-start = (bf16[320,1152]{1,0:T(8,128)(2,1)}, bf16[320,1152]{1,0:T(8,128)(2,1)S(1)}, u32[]{:S(2)}) copy-start(bf16[320,1152]{1,0:T(8,128)(2,1)S(1)} %get-tuple-element.14) | copy-start | bytes 2211844
  38.5 33.8 %copy-start.3 = (bf16[320,1152]{1,0:T(8,128)(2,1)}, bf16[320,1152]{1,0:T(8,128)(2,1)S(1)}, u32[]{:S(2)}) copy-start(bf16[320,1152]{1,0:T(8,128)(2,1)S(1)} %get-tuple-element.13) | copy-start | bytes 2211844
  38.5 18.0 %collective-permute-start.1 = (bf16[320,1152]{1,0:T(8,128)(2,1)S(1)}, bf16[320,1152]{1,0:T(8,128)(2,1)}, u32[]{:S(2)}, u32[]{:S(2)}) collective-permute-start(bf16[320,1152]{1,0:T(8,128)(2,1)S(1)} %get-tuple-element.13), channel_id=1, source_target_pairs={{0,12},{1,13},{2,14},{3,15},{4,0},{5,1},{6,2},{7,3},{8,4},{9,5},{1... | collective-permute-start | bytes 2211848 | tf_op jit(solution)/shard_map/ppermute | solution.py:34
  38.8 19.0 %collective-permute-start.3 = (bf16[320,1152]{1,0:T(8,128)(2,1)S(1)}, bf16[320,1152]{1,0:T(8,128)(2,1)}, u32[]{:S(2)}, u32[]{:S(2)}) collective-permute-start(bf16[320,1152]{1,0:T(8,128)(2,1)S(1)} %get-tuple-element.13), channel_id=1, source_target_pairs={{0,4},{1,5},{2,6},{3,7},{4,8},{5,9},{6,10},{7,11},{8,12},{9,13},{1... | collective-permute-start | bytes 2211848 | tf_op jit(solution)/shard_map/ppermute | solution.py:34
  40.6 18.5 %collective-permute-start.5 = (bf16[320,1152]{1,0:T(8,128)(2,1)S(1)}, bf16[320,1152]{1,0:T(8,128)(2,1)S(1)}, u32[]{:S(2)}, u32[]{:S(2)}) collective-permute-start(bf16[320,1152]{1,0:T(8,128)(2,1)S(1)} %get-tuple-element.14), channel_id=1, source_target_pairs={{0,32},{1,33},{2,34},{3,35},{4,36},{5,37},{6,38},{7,39},{8,40},{9,... | collective-permute-start | bytes 2211848 | tf_op jit(solution)/shard_map/ppermute | solution.py:34
  40.6 19.4 %collective-permute-start.6 = (bf16[320,1152]{1,0:T(8,128)(2,1)S(1)}, bf16[320,1152]{1,0:T(8,128)(2,1)}, u32[]{:S(2)}, u32[]{:S(2)}) collective-permute-start(bf16[320,1152]{1,0:T(8,128)(2,1)S(1)} %get-tuple-element.14), channel_id=1, source_target_pairs={{0,96},{1,97},{2,98},{3,99},{4,100},{5,101},{6,102},{7,103},{8,104... | collective-permute-start | bytes 2211848 | tf_op jit(solution)/shard_map/ppermute | solution.py:34
  43.9 22.0 %collective-permute-start = (bf16[320,1152]{1,0:T(8,128)(2,1)S(1)}, bf16[320,1152]{1,0:T(8,128)(2,1)}, u32[]{:S(2)}, u32[]{:S(2)}) collective-permute-start(bf16[320,1152]{1,0:T(8,128)(2,1)S(1)} %get-tuple-element.13), channel_id=1, source_target_pairs={{0,1},{1,0},{2,3},{3,2},{4,5},{5,4},{6,7},{7,6},{8,9},{9,8},{10,11... | collective-permute-start | bytes 2211848 | tf_op jit(solution)/shard_map/ppermute | solution.py:34
  56.6 9.6 %collective-permute-start.2 = (bf16[320,1152]{1,0:T(8,128)(2,1)}, bf16[320,1152]{1,0:T(8,128)(2,1)}, u32[]{:S(2)}, u32[]{:S(2)}) collective-permute-start(bf16[320,1152]{1,0:T(8,128)(2,1)} %collective-permute-done.1), channel_id=1, source_target_pairs={{0,1},{1,0},{2,3},{3,2},{4,5},{5,4},{6,7},{7,6},{8,9},{9,8},{10,11... | collective-permute-start | bytes 2211848 | tf_op jit(solution)/shard_map/ppermute | solution.py:34
  57.9 14.5 %collective-permute-start.4 = (bf16[320,1152]{1,0:T(8,128)(2,1)}, bf16[320,1152]{1,0:T(8,128)(2,1)}, u32[]{:S(2)}, u32[]{:S(2)}) collective-permute-start(bf16[320,1152]{1,0:T(8,128)(2,1)} %collective-permute-done.3), channel_id=1, source_target_pairs={{0,1},{1,0},{2,3},{3,2},{4,5},{5,4},{6,7},{7,6},{8,9},{9,8},{10,11... | collective-permute-start | bytes 2211848 | tf_op jit(solution)/shard_map/ppermute | solution.py:34
  59.2 13.2 %copy-start.4 = (bf16[320,1152]{1,0:T(8,128)(2,1)}, bf16[320,1152]{1,0:T(8,128)(2,1)S(1)}, u32[]{:S(2)}) copy-start(bf16[320,1152]{1,0:T(8,128)(2,1)S(1)} %collective-permute-done.5) | copy-start | bytes 2211844
  60.0 11.2 %collective-permute-start.7 = (bf16[160,1152]{1,0:T(8,128)(2,1)}, bf16[160,1152]{1,0:T(8,128)(2,1)S(1)}, u32[]{:S(2)}, u32[]{:S(2)}) collective-permute-start(bf16[160,1152]{1,0:T(8,128)(2,1)} %slice.28), channel_id=1, source_target_pairs={{0,32},{1,33},{2,34},{3,35},{4,36},{5,37},{6,38},{7,39},{8,40},{9,... | collective-permute-start | bytes 1105928 | tf_op jit(solution)/shard_map/ppermute | solution.py:34
  61.8 10.5 %collective-permute-start.8 = (bf16[160,1152]{1,0:T(8,128)(2,1)}, bf16[160,1152]{1,0:T(8,128)(2,1)S(1)}, u32[]{:S(2)}, u32[]{:S(2)}) collective-permute-start(bf16[160,1152]{1,0:T(8,128)(2,1)} %slice.29), channel_id=1, source_target_pairs={{0,96},{1,97},{2,98},{3,99},{4,100},{5,101},{6,102},{7,103},{8,104... | collective-permute-start | bytes 1105928 | tf_op jit(solution)/shard_map/ppermute | solution.py:34
  65.9 24.6 %collective-permute-start.12 = (bf16[320,1152]{1,0:T(8,128)(2,1)}, bf16[320,1152]{1,0:T(8,128)(2,1)S(1)}, u32[]{:S(2)}, u32[]{:S(2)}) collective-permute-start(bf16[320,1152]{1,0:T(8,128)(2,1)} %collective-permute-done.3), channel_id=1, source_target_pairs={{0,4},{1,5},{2,6},{3,7},{4,8},{5,9},{6,10},{7,11},{8,12},{9,13},{1... | collective-permute-start | bytes 2211848 | tf_op jit(solution)/shard_map/ppermute | solution.py:34
  66.2 24.4 %collective-permute-start.13 = (bf16[320,1152]{1,0:T(8,128)(2,1)}, bf16[320,1152]{1,0:T(8,128)(2,1)S(1)}, u32[]{:S(2)}, u32[]{:S(2)}) collective-permute-start(bf16[320,1152]{1,0:T(8,128)(2,1)} %collective-permute-done.2), channel_id=1, source_target_pairs={{0,12},{1,13},{2,14},{3,15},{4,0},{5,1},{6,2},{7,3},{8,4},{9,5},{1... | collective-permute-start | bytes 2211848 | tf_op jit(solution)/shard_map/ppermute | solution.py:34
  88.3 2.2 %collective-permute-start.9 = (f32[3,320,128]{2,1,0:T(8,128)S(1)}, f32[3,320,128]{2,1,0:T(8,128)S(1)}, u32[]{:S(2)}, u32[]{:S(2)}) collective-permute-start(f32[3,320,128]{2,1,0:T(8,128)S(1)} %get-tuple-element.16), channel_id=1, source_target_pairs={{0,1},{1,0},{2,3},{3,2},{4,5},{5,4},{6,7},{7,6},{8,9},{9,8},{10,11... | collective-permute-start | bytes 1474568 | tf_op jit(solution)/shard_map/ppermute | solution.py:34
  90.5 0.9 copy-start.5
  90.6 1.1 copy-start.6
  100.4 20.9 %all-to-all-start.1 = ((f32[8,160,128]{2,1,0:T(8,128)}), f32[8,160,128]{2,1,0:T(8,128)S(1)}, u32[]{:S(2)}, u32[]{:S(2)}) async-start(f32[8,160,128]{2,1,0:T(8,128)} %get-tuple-element.20), calls=%async_computation.1 | async-start | bytes 1310720 | tf_op jit(solution)/shard_map/all_to_all | solution.py:245
  106.5 14.3 %collective-permute-start.10 = (f32[320,128]{1,0:T(8,128)S(1)}, f32[320,128]{1,0:T(8,128)S(1)}, u32[]{:S(2)}, u32[]{:S(2)}) collective-permute-start(f32[320,128]{1,0:T(8,128)S(1)} %get-tuple-element.21), channel_id=1, source_target_pairs={{0,4},{1,5},{2,6},{3,7},{4,8},{5,9},{6,10},{7,11},{8,12},{9,13},{1... | collective-permute-start | bytes 491528 | tf_op jit(solution)/shard_map/ppermute | solution.py:34
  106.6 14.2 %collective-permute-start.11 = (f32[320,128]{1,0:T(8,128)S(1)}, f32[320,128]{1,0:T(8,128)S(1)}, u32[]{:S(2)}, u32[]{:S(2)}) collective-permute-start(f32[320,128]{1,0:T(8,128)S(1)} %get-tuple-element.22), channel_id=1, source_target_pairs={{0,12},{1,13},{2,14},{3,15},{4,0},{5,1},{6,2},{7,3},{8,4},{9,5},{1... | collective-permute-start | bytes 491528 | tf_op jit(solution)/shard_map/ppermute | solution.py:34
  109.8 11.0 %collective-permute-start.14 = (f32[320,128]{1,0:T(8,128)S(1)}, f32[320,128]{1,0:T(8,128)S(1)}, u32[]{:S(2)}, u32[]{:S(2)}) collective-permute-start(f32[320,128]{1,0:T(8,128)S(1)} %bitcast.44), channel_id=1, source_target_pairs={{0,8},{1,9},{2,10},{3,11},{4,12},{5,13},{6,14},{7,15},{8,0},{9,1},... | collective-permute-start | bytes 491528 | tf_op jit(solution)/shard_map/ppermute | solution.py:34
  109.8 11.0 %collective-permute-start.15 = (f32[320,128]{1,0:T(8,128)S(1)}, f32[320,128]{1,0:T(8,128)S(1)}, u32[]{:S(2)}, u32[]{:S(2)}) collective-permute-start(f32[320,128]{1,0:T(8,128)S(1)} %bitcast.43), channel_id=1, source_target_pairs={{0,9},{1,8},{2,11},{3,10},{4,13},{5,12},{6,15},{7,14},{8,1},{9,0},... | collective-permute-start | bytes 491528 | tf_op jit(solution)/shard_map/ppermute | solution.py:34
  120.9 4.5 %collective-permute-start.16 = (f32[160,128]{1,0:T(8,128)S(1)}, f32[160,128]{1,0:T(8,128)S(1)}, u32[]{:S(2)}, u32[]{:S(2)}) collective-permute-start(f32[160,128]{1,0:T(8,128)S(1)} %slice.34), channel_id=1, source_target_pairs={{0,2},{1,3},{2,0},{3,1},{4,6},{5,7},{6,4},{7,5},{8,10},{9,11},{10,... | collective-permute-start | bytes 245768 | tf_op jit(solution)/shard_map/ppermute | solution.py:34

commit v6 on v5

--- a/solution.py
+++ b/solution.py
@@ -58,8 +58,8 @@
             sources = (q, q ^ 16, q ^ 2)
             extra = jnp.where(
                 row == 0,
-                points(tgt, sources[0]),
-                jnp.where(row == 1, points(tgt, sources[1]), points(tgt, sources[2])),
+                tgt[sources[0] : sources[0] + 1, :],
+                jnp.where(row == 1, tgt[sources[1] : sources[1] + 1, :], tgt[sources[2] : sources[2] + 1, :]),
             )
             pieces = [points(orb, s) for s in sources]
             blocks.append(jnp.concatenate([*pieces, extra], axis=1))
@@ -72,13 +72,13 @@
         out_shape=jax.ShapeDtypeStruct((DEVICES * 8, 4 * FB), BF),
         compiler_params=pltpu.CompilerParams(vmem_limit_bytes=32 * 2**20),
         name="pack",
-    )(orbitals, targets)
-
-
-def unpack_kernel(packed, cols, rows):
+    )(orbitals, targets.astype(F32).reshape(DEVICES, FB))
+
+
+def unpack_kernel(packed, own, beside, rows):
     turned = packed[:, : 3 * FB].T
-    cols[: FB, :NB] = turned[:FB]
-    cols[FB:, :NB] = turned[FB : 2 * FB]
+    own[:, :NB] = turned[:FB]
+    beside[:, :NB] = turned[FB : 2 * FB]
     rows[:FB, :NB] = turned[:FB]
     rows[FB:, :NB] = turned[2 * FB :]
     source = lax.broadcasted_iota(jnp.int32, (NB, NT), 0)
@@ -86,8 +86,8 @@
     mine, col_side, row_side = (
         tn(packed[...], jnp.where(source == 8 * target + i, 1.0, 0.0).astype(BF))[3 * FB :].astype(BF) for i in range(3)
     )
-    cols[:FB, NB:] = mine
-    cols[FB:, NB:] = col_side
+    own[:, NB:] = mine
+    beside[:, NB:] = col_side
     rows[:FB, NB:] = mine
     rows[FB:, NB:] = row_side
 
@@ -95,7 +95,7 @@
 def unpack(packed):
     return pl.pallas_call(
         unpack_kernel,
-        out_shape=[jax.ShapeDtypeStruct((2 * FB, WIDE), BF)] * 2,
+        out_shape=[jax.ShapeDtypeStruct((n * FB, WIDE), BF) for n in (1, 1, 2)],
         compiler_params=pltpu.CompilerParams(vmem_limit_bytes=32 * 2**20),
         name="unpack",
     )(packed)
@@ -106,10 +106,10 @@
     far = tiles == 1
     n_rows = 2 * tiles
     row_refs, refs = refs[:n_rows], refs[n_rows:]
-    (pair, down, up, far_own, far_other, kern, owned, mirrored), refs = refs[:8], refs[8:]
+    col_refs, (kern, owned, mirrored), refs = refs[:8], refs[8:11], refs[11:]
     if far:
         col_in, refs = refs[0], refs[1:]
-    row_own, row_other, col_out, cols, rows, stored, sems = refs
+    row_own, row_other, *col_outs, cols, rows, stored, col_sum, sems = refs
     y, xh, z, xl, k = (me[i] for i in range(5))
 
     def block(y_step, side):
@@ -123,32 +123,37 @@
         copy.start()
         return copy
 
-    def tile_copies(t):
+    def row_copies(t):
+        return [start(row_refs[2 * t + b], rows.at[t, pl.ds(2 * b, 2)]) for b in range(2)]
+
+    def kern_copies(t):
         z_at = lax.rem(z + z_steps[t], 4)
-        found = []
-        found += [start(row_refs[2 * t + b], rows.at[t, pl.ds(2 * b, 2)]) for b in range(2)]
-        for b in range(4):
-            found.append(start(kern.at[z_at, lax.rem(xl + b % 2, 2), lax.rem(k + b // 2, 2)], stored.at[t, b]))
-        return found
-
-    pieces = [(ref.at[side], block(step, side)) for ref, step in ((pair, 0), (down, 3), (up, 1)) for side in (0, 1)]
-    pieces += [(far_own, block(2, 0)), (far_other, block(2, 1))]
-    col_copies = [start(src, cols.at[at]) for src, at in pieces]
-    row_copies = [tile_copies(t) for t in range(tiles)]
+        return [
+            start(kern.at[z_at, lax.rem(xl + b % 2, 2), lax.rem(k + b // 2, 2)], stored.at[t, b]) for b in range(4)
+        ]
+
+    pieces = [(ref, block(i // 2, i % 2)) for i, ref in enumerate(col_refs)]
+    first_copies = [start(src, cols.at[at]) for src, at in pieces] + row_copies(0)
+    next_rows, next_kern = [], kern_copies(0)
     if far:
-        col_out[...] = col_in[...]
+        col_sum[...] = col_in[...]
     else:
-        col_out[...] = jnp.zeros_like(col_out)
-    for copy in col_copies:
+        col_sum[...] = jnp.zeros_like(col_sum)
+    for copy in first_copies:
         copy.wait()
     col_wide = cols[...].reshape(COL_PTS, WIDE)
 
     for t in range(tiles):
         z_at = lax.rem(z + z_steps[t], 4)
-        for copy in row_copies[t]:
+        for copy in next_rows:
             copy.wait()
+        kern_here = next_kern
+        if t + 1 < tiles:
+            next_rows, next_kern = row_copies(t + 1), kern_copies(t + 1)
         row_wide = rows[t].reshape(TILE, WIDE)
         gram = nt(row_wide[:, :NB], col_wide[:, :NB])
+        for copy in kern_here:
+            copy.wait()
         chunks = COL_PTS // 128
         values = jnp.concatenate(
             [
@@ -172,10 +177,17 @@
         low = (weighted - high.astype(F32)).astype(BF)
         row_sum = nn(high, col_wide[:, NB:]) + nn(low, col_wide[:, NB:])
         keep = spread(mirrored).astype(BF)
-        col_sum = tn(high * keep, row_wide[:, NB:]) + tn(low * keep, row_wide[:, NB:])
-        col_out[...] += col_sum.reshape(col_out.shape)
+        added = tn(high * keep, row_wide[:, NB:]) + tn(low * keep, row_wide[:, NB:])
+        col_sum[...] += added.reshape(col_sum.shape)
         row_own[t] = row_sum[: 2 * FB]
         row_other[t] = row_sum[2 * FB :]
+
+    if not far:
+        col_outs[0][...] = col_sum[...]
+    else:
+        for step, col_out in enumerate(col_outs):
+            for side in (0, 1):
+                col_out[side * FB : (side + 1) * FB, :] = col_sum[block(step, side)]
 
 
 def tile_call(z_steps, me, rows, col_parts, kern, owned, mirrored, col_in=None):
@@ -188,18 +200,23 @@
         in_specs.append(vmem)
         args.append(col_in)
     copies = 8 + len(rows) + 4 * tiles
+    if col_in is None:
+        col_shapes = [jax.ShapeDtypeStruct((N_ROW, FB, NT), F32)]
+    else:
+        col_shapes = [jax.ShapeDtypeStruct((2 * FB, NT), F32)] * 4
     return pl.pallas_call(
         functools.partial(tile_kernel, z_steps),
         in_specs=in_specs,
-        out_specs=[vmem] * 3,
-        out_shape=[jax.ShapeDtypeStruct((tiles, 2 * FB, NT), F32)] * 2 + [jax.ShapeDtypeStruct((N_ROW, FB, NT), F32)],
+        out_specs=[vmem] * (2 + len(col_shapes)),
+        out_shape=[jax.ShapeDtypeStruct((tiles, 2 * FB, NT), F32)] * 2 + col_shapes,
         scratch_shapes=[
             pltpu.VMEM((N_ROW, FB, WIDE), BF),
             pltpu.VMEM((tiles, 4, FB, WIDE), BF),
             pltpu.VMEM((tiles, 4, FB * COL_PTS // 128, 128), F32),
+            pltpu.VMEM((N_ROW, FB, NT), F32),
             pltpu.SemaphoreType.DMA((copies,)),
         ],
-        compiler_params=pltpu.CompilerParams(vmem_limit_bytes=52 * 2**20),
+        compiler_params=pltpu.CompilerParams(vmem_limit_bytes=(46 if tiles > 1 else 52) * 2**20),
         cost_estimate=pl.CostEstimate(
             flops=2_600_000_000 * tiles, bytes_accessed=5_000_000 * tiles, transcendentals=0
         ),
@@ -217,12 +234,13 @@
 
     packed = pack(orbitals, targets).reshape(DEVICES, 8, 4 * FB)
     packed = lax.all_to_all(packed, AXES, split_axis=0, concat_axis=0, tiled=True)
-    pair_y, pair_z = unpack(packed.reshape(DEVICES * 8, 4 * FB))
-
-    y_down, y_up = send(pair_y, y=1), send(pair_y, y=3)
+    own, beside, pair_z = unpack(packed.reshape(DEVICES * 8, 4 * FB))
+
+    own_down, beside_up = send(own, y=1), send(beside, y=3)
     z_down, z_up = send(pair_z, z=1), send(pair_z, z=3)
-    y_far, y_far_other = send(y_down[:FB], y=1), send(y_up[FB:], y=3)
-    col_parts = (halves(pair_y), halves(y_down), halves(y_up), y_far, y_far_other)
+    beside_down, own_up = send(beside, y=1), send(own, y=3)
+    own_far, beside_far = send(own_down, y=1), send(beside_up, y=3)
+    col_parts = (own, beside, own_up, beside_up, own_far, beside_far, own_down, beside_down)
     across = [send(own, k=1) for own in (pair_z, z_up, z_down)]
     near_rows = [halves(part) for both in zip((pair_z, z_up, z_down), across) for part in both]
     far_rows = [halves(send(z_down, z=1)), halves(send(across[1], z=3))]
@@ -236,13 +254,15 @@
     kern = kernel.reshape(4, 2, 2, FB * COL_PTS // 128, 128)
 
     near_own, near_other, col_part = tile_call((0, 1, 3), me, near_rows, col_parts, kern, owned, mirrored)
-    far_own, far_other, col_sum = tile_call((2,), me, far_rows, col_parts, kern, owned, mirrored, col_part)
-
     near = near_own + send(near_other, k=1)
-    far = send(far_own[0], z=2) + send(far_other[0], z=2, k=1)
-    row_sum = near[0] + send(near[1], z=1) + send(near[2], z=3) + far
+    near, col_part = lax.optimization_barrier((near, col_part))
+    row_up, row_down = send(near[1], z=1), send(near[2], z=3)
+    far_own, far_other, c0, c1, c2, c3 = tile_call((2,), me, far_rows, col_parts, kern, owned, mirrored, col_part)
+
+    row_sum = near[0] + row_up + row_down + send(far_own[0], z=2) + send(far_other[0], z=2, k=1)
+    col_sum = c0 + send(c1, y=1) + send(c2, y=2) + send(c3, y=3)
     row_share = row_sum[:FB] + send(row_sum[FB:], xl=1)
-    col_share = lax.all_to_all(col_sum, "row", split_axis=0, concat_axis=0, tiled=True).sum(axis=0)
+    col_share = col_sum[:FB] + send(col_sum[FB:], xh=1)
     return row_share + col_share
 
 

time: 127 us -> 126 us (level)
  waiting for transfers between devices: 33.1 us -> 38.3 us
  local copies, waits for them, and re-layouts: 6.33 us -> 3.82 us
  starting transfers between devices: 24.1 us -> 22.1 us
  Pallas kernels: 28.5 us -> 26.8 us
    all_to_all x1 -> x0, starting transfers between devices: 6.08 us -> none  [local(): lax.all_to_all(col_sum, 'row', split_axis=0, concat_axis=0, tiled=True)]
    ppermute x17 -> x23, waiting for transfers between devices: 33.1 us -> 38.3 us  [send(): return lax.ppermute(x, AXES, moved(**steps))]
    ppermute x17 -> x23, starting transfers between devices: 18.1 us -> 22.1 us  [send(): return lax.ppermute(x, AXES, moved(**steps))]
    slice x2 -> x1, local copies, waits for them, and re-layouts: 2.62 us -> 0.01 us  [local(): col_share = col_sum[:FB] + send(col_sum[FB:], xh=1)]
    pallas_call x1, Pallas kernels: 2.51 us -> 0.52 us  [pack(): pl.pallas_call(pack_kernel, out_shape=jax.ShapeDtypeStruct((DEVICES * 8,...]
    unnamed x16 -> x22, local copies, waits for them, and re-layouts: 2.96 us -> 2.96 us
  transfers between devices with their start and end apart: 18 -> 23, of which waited for: 8 -> 12; matrix products, arithmetic and copies ran while one was open for 3% -> 1% of each run, Pallas kernels for 13% -> 19%
where the time goes in v6:
time: 126 us
  waiting for transfers between devices  38.3 us (30%)
  blocking collectives  32.9 us (26%)
  Pallas kernels  26.8 us (21%)
  starting transfers between devices  22.1 us (18%)
  local copies, waits for them, and re-layouts  3.82 us (3%)
  other arithmetic  2.01 us (2%)
    ppermute x23, waiting for transfers between devices, send(): return lax.ppermute(x, AXES, moved(**steps))  38.3 us
    all_to_all x1, blocking collectives, local(): lax.all_to_all(packed, AXES, split_axis=0, concat_axis=0, tiled=True)  32.9 us
    pallas_call x2, Pallas kernels, tile_call(): pl.pallas_call(functools.partial(tile_kernel, z_steps), in_specs=in_specs...  24.2 us
    ppermute x23, starting transfers between devices, send(): return lax.ppermute(x, AXES, moved(**steps))  22.1 us
    unnamed x22, local copies, waits for them, and re-layouts  2.96 us
  transfers between devices with their start and end apart: 23, of which 12 were waited for; matrix products, arithmetic and copies ran while one was open for 1% of the time, Pallas kernels for 19%

profile of v6, /device:TPU:0, one launch (start us, length us, event | category | flops | bytes accessed | tf_op | source)
XLA Modules:
  0.0 126.1 jit_solution(6785783422454224127)
XLA Ops:
  0.0 1.1 convert_reduce_fusion
  1.1 0.1 reshape.54.tgt
  1.2 1.0 copy-done.7
  2.2 0.5 pack.1
  2.7 32.9 %all_to_all.5 = bf16[128,8,640]{2,1,0:T(8,128)(2,1)S(1)} all-to-all(bf16[128,8,640]{2,1,0:T(8,128)(2,1)S(1)} %bitcast.36), channel_id=1, replica_groups=mesh['row'=8,'col'=16] {'row','col'}, dimensions={0} | all-to-all | bytes 2621440 | tf_op jit(solution)/shard_map/all_to_all | solution.py:236
  35.6 2.1 %unpack.1 = (bf16[160,1152]{1,0:T(8,128)(2,1)S(1)}, bf16[160,1152]{1,0:T(8,128)(2,1)S(1)}, bf16[320,1152]{1,0:T(8,128)(2,1)}) custom-call(bf16[1024,640]{1,0:T(8,128)(2,1)S(1)} %bitcast.35), custom_call_target="tpu_custom_call" | custom-call | tf_op jit(solution)/shard_map/unpack/pallas_call | solution.py:96
  37.7 0.2 collective-permute-start.1
  38.0 1.8 %collective-permute-start.3 = (bf16[320,1152]{1,0:T(8,128)(2,1)}, bf16[320,1152]{1,0:T(8,128)(2,1)}, u32[]{:S(2)}, u32[]{:S(2)}) collective-permute-start(bf16[320,1152]{1,0:T(8,128)(2,1)} %get-tuple-element.19), channel_id=1, source_target_pairs={{0,4},{1,5},{2,6},{3,7},{4,8},{5,9},{6,10},{7,11},{8,12},{9,13},{1... | collective-permute-start | bytes 2211848 | tf_op jit(solution)/shard_map/ppermute | solution.py:34
  39.8 3.2 %collective-permute-start.6 = (bf16[160,1152]{1,0:T(8,128)(2,1)S(1)}, bf16[160,1152]{1,0:T(8,128)(2,1)S(1)}, u32[]{:S(2)}, u32[]{:S(2)}) collective-permute-start(bf16[160,1152]{1,0:T(8,128)(2,1)S(1)} %get-tuple-element.21.refs_7_.refs_3_), channel_id=1, source_target_pairs={{0,96},{1,97},{2,98},{3,99},{4,100},{5,101},{6,102},{7,103},{8,104... | collective-permute-start | bytes 1105928 | tf_op jit(solution)/shard_map/ppermute | solution.py:34
  43.0 9.5 %collective-permute-done.7.refs_12_.refs_8_ = bf16[160,1152]{1,0:T(8,128)(2,1)S(1)} collective-permute-done((bf16[160,1152]{1,0:T(8,128)(2,1)S(1)}, bf16[160,1152]{1,0:T(8,128)(2,1)S(1)}, u32[]{:S(2)}, u32[]{:S(2)}) %collective-permute-start.7) | collective-permute-done | bytes 368672 | tf_op jit(solution)/shard_map/ppermute | solution.py:34
  52.5 3.4 %collective-permute-done.1 = bf16[320,1152]{1,0:T(8,128)(2,1)} collective-permute-done((bf16[320,1152]{1,0:T(8,128)(2,1)}, bf16[320,1152]{1,0:T(8,128)(2,1)}, u32[]{:S(2)}, u32[]{:S(2)}) %collective-permute-start.1) | collective-permute-done | bytes 737312 | tf_op jit(solution)/shard_map/ppermute | solution.py:34
  55.9 0.5 collective-permute-start
  56.4 0.7 collective-permute-done.3
  57.1 1.1 collective-permute-done.10.refs_13_.refs_9_
  58.3 1.7 %collective-permute-done.5.refs_8_.refs_4_ = bf16[160,1152]{1,0:T(8,128)(2,1)S(1)} collective-permute-done((bf16[160,1152]{1,0:T(8,128)(2,1)S(1)}, bf16[160,1152]{1,0:T(8,128)(2,1)S(1)}, u32[]{:S(2)}, u32[]{:S(2)}) %collective-permute-start.5) | collective-permute-done | bytes 368672 | tf_op jit(solution)/shard_map/ppermute | solution.py:34
  60.0 1.5 %collective-permute-start.9 = (bf16[160,1152]{1,0:T(8,128)(2,1)S(1)}, bf16[160,1152]{1,0:T(8,128)(2,1)S(1)}, u32[]{:S(2)}, u32[]{:S(2)}) collective-permute-start(bf16[160,1152]{1,0:T(8,128)(2,1)S(1)} %collective-permute-done.6.refs_9_.refs_5_), channel_id=1, source_target_pairs={{0,96},{1,97},{2,98},{3,99},{4,100},{5,101},{6,102},{7,103},{8,104... | collective-permute-start | bytes 1105928 | tf_op jit(solution)/shard_map/ppermute | solution.py:34
  61.5 0.1 and_select_fusion
  61.6 0.1 copy.10
  61.7 0.1 broadcast_in_dim.12
  61.8 0.2 reshape_reshape.7.refs_16_.refs_12_
  61.9 0.1 copy.9
  62.0 0.1 broadcast_in_dim.10
  62.1 0.2 reshape_reshape.6.refs_15_.refs_11_
  62.3 0.1 stack.23.me
  62.4 7.1 %collective-permute-done.8.refs_10_.refs_6_ = bf16[160,1152]{1,0:T(8,128)(2,1)S(1)} collective-permute-done((bf16[160,1152]{1,0:T(8,128)(2,1)S(1)}, bf16[160,1152]{1,0:T(8,128)(2,1)S(1)}, u32[]{:S(2)}, u32[]{:S(2)}) %collective-permute-start.8) | collective-permute-done | bytes 368672 | tf_op jit(solution)/shard_map/ppermute | solution.py:34
  69.4 0.5 collective-permute-start.14
  70.0 2.7 %collective-permute-start.15 = (bf16[320,1152]{1,0:T(8,128)(2,1)}, bf16[320,1152]{1,0:T(8,128)(2,1)S(1)}, u32[]{:S(2)}, u32[]{:S(2)}) collective-permute-start(bf16[320,1152]{1,0:T(8,128)(2,1)} %collective-permute-done.2), channel_id=1, source_target_pairs={{0,12},{1,13},{2,14},{3,15},{4,0},{5,1},{6,2},{7,3},{8,4},{9,5},{1... | collective-permute-start | bytes 2211848 | tf_op jit(solution)/shard_map/ppermute | solution.py:34
  72.7 16.3 %near_tiles.1 = (f32[3,320,128]{2,1,0:T(8,128)S(1)}, f32[3,320,128]{2,1,0:T(8,128)S(1)}, f32[8,160,128]{2,1,0:T(8,128)S(1)}) custom-call(s32[5]{0:T(128)S(1)} %stack.23.me, bf16[2,160,1152]{2,1,0:T(8,128)(2,1)} %bitcast.7.refs_0_, bf16[2,160,1152]{2,1,0:T(8,128)(2,1)} %bitcast.8.refs_1_, bf16[2,160,1152]{2,1,0:T(8,128)(2,1)} %bitcast.9.refs_2_, ...), custom_call_target="tpu_custom_call" | custom-call | flops 7800000000 | bytes 15000000 | tf_op jit(solution)/shard_map/near_tiles/pallas_call | solution.py:207
  89.0 0.8 copy-done
  89.9 1.9 %collective-permute-done.11 = f32[3,320,128]{2,1,0:T(8,128)S(1)} collective-permute-done((f32[3,320,128]{2,1,0:T(8,128)S(1)}, f32[3,320,128]{2,1,0:T(8,128)S(1)}, u32[]{:S(2)}, u32[]{:S(2)}) %collective-permute-start.11) | collective-permute-done | bytes 491552 | tf_op jit(solution)/shard_map/ppermute | solution.py:34
  91.8 0.1 collective-permute-start.12
  91.9 3.2 %collective-permute-start.13 = (f32[320,128]{1,0:T(8,128)S(1)}, f32[320,128]{1,0:T(8,128)S(1)}, u32[]{:S(2)}, u32[]{:S(2)}) collective-permute-start(f32[320,128]{1,0:T(8,128)S(1)} %get-tuple-element.34), channel_id=1, source_target_pairs={{0,12},{1,13},{2,14},{3,15},{4,0},{5,1},{6,2},{7,3},{8,4},{9,5},{1... | collective-permute-start | bytes 491528 | tf_op jit(solution)/shard_map/ppermute | solution.py:34
  95.1 0.9 copy-done.8
  96.0 0.3 copy-done.9
  96.3 7.9 %far_tile.1 = (f32[1,320,128]{2,1,0:T(8,128)S(1)}, f32[1,320,128]{2,1,0:T(8,128)S(1)}, f32[320,128]{1,0:T(8,128)S(1)}, f32[320,128]{1,0:T(8,128)S(1)}, f32[320,128]{1,0:T(8,128)S(1)}, /*index=5*/f32[320,128]{1,0:T(8,128)S(1)}) custom-call(s32[5]{0:T(128)S(1)} %stack.23.me, bf16[2,160,1152]{2,1,0:T(8,128)(2,1)} %bitcast.41, bf16[2,160,1152]{2,1,0:T(8,128)(2,1)} %bitcast.42, ...), custom_call_target="tpu_custom_call" | custom-call | flops 2600000000 | bytes 5000000 | tf_op jit(solution)/shard_map/far_tile/pallas_call | solution.py:207
  104.2 0.1 collective-permute-start.16
  104.3 2.4 %collective-permute-start.17 = (f32[320,128]{1,0:T(8,128)S(1)}, f32[320,128]{1,0:T(8,128)S(1)}, u32[]{:S(2)}, u32[]{:S(2)}) collective-permute-start(f32[320,128]{1,0:T(8,128)S(1)} %bitcast.37), channel_id=1, source_target_pairs={{0,9},{1,8},{2,11},{3,10},{4,13},{5,12},{6,15},{7,14},{8,1},{9,0},... | collective-permute-start | bytes 491528 | tf_op jit(solution)/shard_map/ppermute | solution.py:34
  106.7 1.4 %collective-permute-start.20 = (f32[320,128]{1,0:T(8,128)S(1)}, f32[320,128]{1,0:T(8,128)S(1)}, u32[]{:S(2)}, u32[]{:S(2)}) collective-permute-start(f32[320,128]{1,0:T(8,128)S(1)} %get-tuple-element.31), channel_id=1, source_target_pairs={{0,64},{1,65},{2,66},{3,67},{4,68},{5,69},{6,70},{7,71},{8,72},{9,... | collective-permute-start | bytes 491528 | tf_op jit(solution)/shard_map/ppermute | solution.py:34
  108.1 2.0 %collective-permute-start.21 = (f32[320,128]{1,0:T(8,128)S(1)}, f32[320,128]{1,0:T(8,128)S(1)}, u32[]{:S(2)}, u32[]{:S(2)}) collective-permute-start(f32[320,128]{1,0:T(8,128)S(1)} %get-tuple-element.32), channel_id=1, source_target_pairs={{0,96},{1,97},{2,98},{3,99},{4,100},{5,101},{6,102},{7,103},{8,104... | collective-permute-start | bytes 491528 | tf_op jit(solution)/shard_map/ppermute | solution.py:34
  110.0 2.9 %collective-permute-done.16 = f32[320,128]{1,0:T(8,128)S(1)} collective-permute-done((f32[320,128]{1,0:T(8,128)S(1)}, f32[320,128]{1,0:T(8,128)S(1)}, u32[]{:S(2)}, u32[]{:S(2)}) %collective-permute-start.16) | collective-permute-done | bytes 163872 | tf_op jit(solution)/shard_map/ppermute | solution.py:34
  112.9 0.6 collective-permute-done.17
  113.5 0.1 fusion.2
  113.6 0.5 collective-permute-start.18
  114.1 4.1 %collective-permute-done.19 = f32[320,128]{1,0:T(8,128)S(1)} collective-permute-done((f32[320,128]{1,0:T(8,128)S(1)}, f32[320,128]{1,0:T(8,128)S(1)}, u32[]{:S(2)}, u32[]{:S(2)}) %collective-permute-start.19) | collective-permute-done | bytes 163872 | tf_op jit(solution)/shard_map/ppermute | solution.py:34
  118.2 1.1 collective-permute-done.21
  119.4 1.9 %collective-permute-start.22 = (f32[160,128]{1,0:T(8,128)S(1)}, f32[160,128]{1,0:T(8,128)S(1)}, u32[]{:S(2)}, u32[]{:S(2)}) collective-permute-start(f32[160,128]{1,0:T(8,128)S(1)} %slice.31), channel_id=1, source_target_pairs={{0,16},{1,17},{2,18},{3,19},{4,20},{5,21},{6,22},{7,23},{8,24},{9,... | collective-permute-start | bytes 245768 | tf_op jit(solution)/shard_map/ppermute | solution.py:34
  121.4 4.1 %collective-permute-done.22 = f32[160,128]{1,0:T(8,128)S(1)} collective-permute-done((f32[160,128]{1,0:T(8,128)S(1)}, f32[160,128]{1,0:T(8,128)S(1)}, u32[]{:S(2)}, u32[]{:S(2)}) %collective-permute-start.22) | collective-permute-done | bytes 81952 | tf_op jit(solution)/shard_map/ppermute | solution.py:34
  125.5 0.7 fusion.3
  (45 shorter events, 0.2 us)
Async XLA Ops:
  1.2 1.0 copy-start.7
  35.6 25.9 %copy-start.10 = (s32[1,16,8,1]{1,3,2,0:T(1,128)S(1)}, s32[1,16,8,1]{1,3,2,0:T(1,128)}, u32[]{:S(2)}) copy-start(s32[1,16,8,1]{1,3,2,0:T(1,128)} %param.7) | copy-start | bytes 1540
  37.7 18.2 %collective-permute-start.1 = (bf16[320,1152]{1,0:T(8,128)(2,1)}, bf16[320,1152]{1,0:T(8,128)(2,1)}, u32[]{:S(2)}, u32[]{:S(2)}) collective-permute-start(bf16[320,1152]{1,0:T(8,128)(2,1)} %get-tuple-element.19), channel_id=1, source_target_pairs={{0,12},{1,13},{2,14},{3,15},{4,0},{5,1},{6,2},{7,3},{8,4},{9,5},{1... | collective-permute-start | bytes 2211848 | tf_op jit(solution)/shard_map/ppermute | solution.py:34
  38.0 19.2 %collective-permute-start.3 = (bf16[320,1152]{1,0:T(8,128)(2,1)}, bf16[320,1152]{1,0:T(8,128)(2,1)}, u32[]{:S(2)}, u32[]{:S(2)}) collective-permute-start(bf16[320,1152]{1,0:T(8,128)(2,1)} %get-tuple-element.19), channel_id=1, source_target_pairs={{0,4},{1,5},{2,6},{3,7},{4,8},{5,9},{6,10},{7,11},{8,12},{9,13},{1... | collective-permute-start | bytes 2211848 | tf_op jit(solution)/shard_map/ppermute | solution.py:34
  39.8 12.7 %collective-permute-start.7 = (bf16[160,1152]{1,0:T(8,128)(2,1)S(1)}, bf16[160,1152]{1,0:T(8,128)(2,1)S(1)}, u32[]{:S(2)}, u32[]{:S(2)}) collective-permute-start(bf16[160,1152]{1,0:T(8,128)(2,1)S(1)} %get-tuple-element.20.refs_6_.refs_2_), channel_id=1, source_target_pairs={{0,32},{1,33},{2,34},{3,35},{4,36},{5,37},{6,38},{7,39},{8,40},{9,... | collective-permute-start | bytes 1105928 | tf_op jit(solution)/shard_map/ppermute | solution.py:34
  39.8 16.2 %collective-permute-start.6 = (bf16[160,1152]{1,0:T(8,128)(2,1)S(1)}, bf16[160,1152]{1,0:T(8,128)(2,1)S(1)}, u32[]{:S(2)}, u32[]{:S(2)}) collective-permute-start(bf16[160,1152]{1,0:T(8,128)(2,1)S(1)} %get-tuple-element.21.refs_7_.refs_3_), channel_id=1, source_target_pairs={{0,96},{1,97},{2,98},{3,99},{4,100},{5,101},{6,102},{7,103},{8,104... | collective-permute-start | bytes 1105928 | tf_op jit(solution)/shard_map/ppermute | solution.py:34
  43.0 15.3 %collective-permute-start.10 = (bf16[160,1152]{1,0:T(8,128)(2,1)S(1)}, bf16[160,1152]{1,0:T(8,128)(2,1)S(1)}, u32[]{:S(2)}, u32[]{:S(2)}) collective-permute-start(bf16[160,1152]{1,0:T(8,128)(2,1)S(1)} %get-tuple-element.21.refs_7_.refs_3_), channel_id=1, source_target_pairs={{0,32},{1,33},{2,34},{3,35},{4,36},{5,37},{6,38},{7,39},{8,40},{9,... | collective-permute-start | bytes 1105928 | tf_op jit(solution)/shard_map/ppermute | solution.py:34
  52.5 36.5 %copy-start.1 = (bf16[160,1152]{1,0:T(8,128)(2,1)}, bf16[160,1152]{1,0:T(8,128)(2,1)S(1)}, u32[]{:S(2)}) copy-start(bf16[160,1152]{1,0:T(8,128)(2,1)S(1)} %collective-permute-done.7.refs_12_.refs_8_) | copy-start | bytes 1105924
  52.5 7.5 %collective-permute-start.5 = (bf16[160,1152]{1,0:T(8,128)(2,1)S(1)}, bf16[160,1152]{1,0:T(8,128)(2,1)S(1)}, u32[]{:S(2)}, u32[]{:S(2)}) collective-permute-start(bf16[160,1152]{1,0:T(8,128)(2,1)S(1)} %get-tuple-element.20.refs_6_.refs_2_), channel_id=1, source_target_pairs={{0,96},{1,97},{2,98},{3,99},{4,100},{5,101},{6,102},{7,103},{8,104... | collective-permute-start | bytes 1105928 | tf_op jit(solution)/shard_map/ppermute | solution.py:34
  55.9 14.1 %collective-permute-start.2 = (bf16[320,1152]{1,0:T(8,128)(2,1)}, bf16[320,1152]{1,0:T(8,128)(2,1)}, u32[]{:S(2)}, u32[]{:S(2)}) collective-permute-start(bf16[320,1152]{1,0:T(8,128)(2,1)} %collective-permute-done.1), channel_id=1, source_target_pairs={{0,1},{1,0},{2,3},{3,2},{4,5},{5,4},{6,7},{7,6},{8,9},{9,8},{10,11... | collective-permute-start | bytes 2211848 | tf_op jit(solution)/shard_map/ppermute | solution.py:34
  55.9 33.1 %copy-start.2 = (bf16[160,1152]{1,0:T(8,128)(2,1)}, bf16[160,1152]{1,0:T(8,128)(2,1)S(1)}, u32[]{:S(2)}) copy-start(bf16[160,1152]{1,0:T(8,128)(2,1)S(1)} %collective-permute-done.6.refs_9_.refs_5_) | copy-start | bytes 1105924
  55.9 16.8 %collective-permute-start = (bf16[320,1152]{1,0:T(8,128)(2,1)}, bf16[320,1152]{1,0:T(8,128)(2,1)}, u32[]{:S(2)}, u32[]{:S(2)}) collective-permute-start(bf16[320,1152]{1,0:T(8,128)(2,1)} %get-tuple-element.19), channel_id=1, source_target_pairs={{0,1},{1,0},{2,3},{3,2},{4,5},{5,4},{6,7},{7,6},{8,9},{9,8},{10,11... | collective-permute-start | bytes 2211848 | tf_op jit(solution)/shard_map/ppermute | solution.py:34
  57.1 15.6 %collective-permute-start.4 = (bf16[320,1152]{1,0:T(8,128)(2,1)}, bf16[320,1152]{1,0:T(8,128)(2,1)}, u32[]{:S(2)}, u32[]{:S(2)}) collective-permute-start(bf16[320,1152]{1,0:T(8,128)(2,1)} %collective-permute-done.3), channel_id=1, source_target_pairs={{0,1},{1,0},{2,3},{3,2},{4,5},{5,4},{6,7},{7,6},{8,9},{9,8},{10,11... | collective-permute-start | bytes 2211848 | tf_op jit(solution)/shard_map/ppermute | solution.py:34
  58.3 30.7 %copy-start.3 = (bf16[160,1152]{1,0:T(8,128)(2,1)}, bf16[160,1152]{1,0:T(8,128)(2,1)S(1)}, u32[]{:S(2)}) copy-start(bf16[160,1152]{1,0:T(8,128)(2,1)S(1)} %collective-permute-done.10.refs_13_.refs_9_) | copy-start | bytes 1105924
  58.3 11.2 %collective-permute-start.8 = (bf16[160,1152]{1,0:T(8,128)(2,1)S(1)}, bf16[160,1152]{1,0:T(8,128)(2,1)S(1)}, u32[]{:S(2)}, u32[]{:S(2)}) collective-permute-start(bf16[160,1152]{1,0:T(8,128)(2,1)S(1)} %collective-permute-done.7.refs_12_.refs_8_), channel_id=1, source_target_pairs={{0,32},{1,33},{2,34},{3,35},{4,36},{5,37},{6,38},{7,39},{8,40},{9,... | collective-permute-start | bytes 1105928 | tf_op jit(solution)/shard_map/ppermute | solution.py:34
  60.0 29.0 %copy-start.4 = (bf16[160,1152]{1,0:T(8,128)(2,1)}, bf16[160,1152]{1,0:T(8,128)(2,1)S(1)}, u32[]{:S(2)}) copy-start(bf16[160,1152]{1,0:T(8,128)(2,1)S(1)} %collective-permute-done.5.refs_8_.refs_4_) | copy-start | bytes 1105924
  60.0 12.7 %collective-permute-start.9 = (bf16[160,1152]{1,0:T(8,128)(2,1)S(1)}, bf16[160,1152]{1,0:T(8,128)(2,1)S(1)}, u32[]{:S(2)}, u32[]{:S(2)}) collective-permute-start(bf16[160,1152]{1,0:T(8,128)(2,1)S(1)} %collective-permute-done.6.refs_9_.refs_5_), channel_id=1, source_target_pairs={{0,96},{1,97},{2,98},{3,99},{4,100},{5,101},{6,102},{7,103},{8,104... | collective-permute-start | bytes 1105928 | tf_op jit(solution)/shard_map/ppermute | solution.py:34
  69.4 19.6 %copy-start.5 = (bf16[160,1152]{1,0:T(8,128)(2,1)}, bf16[160,1152]{1,0:T(8,128)(2,1)S(1)}, u32[]{:S(2)}) copy-start(bf16[160,1152]{1,0:T(8,128)(2,1)S(1)} %collective-permute-done.8.refs_10_.refs_6_) | copy-start | bytes 1105924
  69.4 25.7 %collective-permute-start.14 = (bf16[320,1152]{1,0:T(8,128)(2,1)}, bf16[320,1152]{1,0:T(8,128)(2,1)S(1)}, u32[]{:S(2)}, u32[]{:S(2)}) collective-permute-start(bf16[320,1152]{1,0:T(8,128)(2,1)} %collective-permute-done.3), channel_id=1, source_target_pairs={{0,4},{1,5},{2,6},{3,7},{4,8},{5,9},{6,10},{7,11},{8,12},{9,13},{1... | collective-permute-start | bytes 2211848 | tf_op jit(solution)/shard_map/ppermute | solution.py:34
  70.0 25.1 %collective-permute-start.15 = (bf16[320,1152]{1,0:T(8,128)(2,1)}, bf16[320,1152]{1,0:T(8,128)(2,1)S(1)}, u32[]{:S(2)}, u32[]{:S(2)}) collective-permute-start(bf16[320,1152]{1,0:T(8,128)(2,1)} %collective-permute-done.2), channel_id=1, source_target_pairs={{0,12},{1,13},{2,14},{3,15},{4,0},{5,1},{6,2},{7,3},{8,4},{9,5},{1... | collective-permute-start | bytes 2211848 | tf_op jit(solution)/shard_map/ppermute | solution.py:34
  72.7 16.3 %copy-start.6 = (bf16[160,1152]{1,0:T(8,128)(2,1)}, bf16[160,1152]{1,0:T(8,128)(2,1)S(1)}, u32[]{:S(2)}) copy-start(bf16[160,1152]{1,0:T(8,128)(2,1)S(1)} %collective-permute-done.9.refs_11_.refs_7_) | copy-start | bytes 1105924
  89.0 0.8 copy-start
  89.9 1.9 %collective-permute-start.11 = (f32[3,320,128]{2,1,0:T(8,128)S(1)}, f32[3,320,128]{2,1,0:T(8,128)S(1)}, u32[]{:S(2)}, u32[]{:S(2)}) collective-permute-start(f32[3,320,128]{2,1,0:T(8,128)S(1)} %get-tuple-element.23), channel_id=1, source_target_pairs={{0,1},{1,0},{2,3},{3,2},{4,5},{5,4},{6,7},{7,6},{8,9},{9,8},{10,11... | collective-permute-start | bytes 1474568 | tf_op jit(solution)/shard_map/ppermute | solution.py:34
  91.8 14.9 %collective-permute-start.12 = (f32[320,128]{1,0:T(8,128)S(1)}, f32[320,128]{1,0:T(8,128)S(1)}, u32[]{:S(2)}, u32[]{:S(2)}) collective-permute-start(f32[320,128]{1,0:T(8,128)S(1)} %get-tuple-element.33), channel_id=1, source_target_pairs={{0,4},{1,5},{2,6},{3,7},{4,8},{5,9},{6,10},{7,11},{8,12},{9,13},{1... | collective-permute-start | bytes 491528 | tf_op jit(solution)/shard_map/ppermute | solution.py:34
  91.9 16.2 %collective-permute-start.13 = (f32[320,128]{1,0:T(8,128)S(1)}, f32[320,128]{1,0:T(8,128)S(1)}, u32[]{:S(2)}, u32[]{:S(2)}) collective-permute-start(f32[320,128]{1,0:T(8,128)S(1)} %get-tuple-element.34), channel_id=1, source_target_pairs={{0,12},{1,13},{2,14},{3,15},{4,0},{5,1},{6,2},{7,3},{8,4},{9,5},{1... | collective-permute-start | bytes 491528 | tf_op jit(solution)/shard_map/ppermute | solution.py:34
  95.1 0.9 copy-start.8
  95.1 1.1 copy-start.9
  104.2 8.7 %collective-permute-start.16 = (f32[320,128]{1,0:T(8,128)S(1)}, f32[320,128]{1,0:T(8,128)S(1)}, u32[]{:S(2)}, u32[]{:S(2)}) collective-permute-start(f32[320,128]{1,0:T(8,128)S(1)} %bitcast.38), channel_id=1, source_target_pairs={{0,8},{1,9},{2,10},{3,11},{4,12},{5,13},{6,14},{7,15},{8,0},{9,1},... | collective-permute-start | bytes 491528 | tf_op jit(solution)/shard_map/ppermute | solution.py:34
  104.3 9.2 %collective-permute-start.17 = (f32[320,128]{1,0:T(8,128)S(1)}, f32[320,128]{1,0:T(8,128)S(1)}, u32[]{:S(2)}, u32[]{:S(2)}) collective-permute-start(f32[320,128]{1,0:T(8,128)S(1)} %bitcast.37), channel_id=1, source_target_pairs={{0,9},{1,8},{2,11},{3,10},{4,13},{5,12},{6,15},{7,14},{8,1},{9,0},... | collective-permute-start | bytes 491528 | tf_op jit(solution)/shard_map/ppermute | solution.py:34
  106.7 11.5 %collective-permute-start.19 = (f32[320,128]{1,0:T(8,128)S(1)}, f32[320,128]{1,0:T(8,128)S(1)}, u32[]{:S(2)}, u32[]{:S(2)}) collective-permute-start(f32[320,128]{1,0:T(8,128)S(1)} %get-tuple-element.30), channel_id=1, source_target_pairs={{0,32},{1,33},{2,34},{3,35},{4,36},{5,37},{6,38},{7,39},{8,40},{9,... | collective-permute-start | bytes 491528 | tf_op jit(solution)/shard_map/ppermute | solution.py:34
  106.7 11.5 %collective-permute-start.20 = (f32[320,128]{1,0:T(8,128)S(1)}, f32[320,128]{1,0:T(8,128)S(1)}, u32[]{:S(2)}, u32[]{:S(2)}) collective-permute-start(f32[320,128]{1,0:T(8,128)S(1)} %get-tuple-element.31), channel_id=1, source_target_pairs={{0,64},{1,65},{2,66},{3,67},{4,68},{5,69},{6,70},{7,71},{8,72},{9,... | collective-permute-start | bytes 491528 | tf_op jit(solution)/shard_map/ppermute | solution.py:34
  108.1 11.3 %collective-permute-start.21 = (f32[320,128]{1,0:T(8,128)S(1)}, f32[320,128]{1,0:T(8,128)S(1)}, u32[]{:S(2)}, u32[]{:S(2)}) collective-permute-start(f32[320,128]{1,0:T(8,128)S(1)} %get-tuple-element.32), channel_id=1, source_target_pairs={{0,96},{1,97},{2,98},{3,99},{4,100},{5,101},{6,102},{7,103},{8,104... | collective-permute-start | bytes 491528 | tf_op jit(solution)/shard_map/ppermute | solution.py:34
  113.6 7.8 %collective-permute-start.18 = (f32[160,128]{1,0:T(8,128)S(1)}, f32[160,128]{1,0:T(8,128)S(1)}, u32[]{:S(2)}, u32[]{:S(2)}) collective-permute-start(f32[160,128]{1,0:T(8,128)S(1)} %slice.29), channel_id=1, source_target_pairs={{0,2},{1,3},{2,0},{3,1},{4,6},{5,7},{6,4},{7,5},{8,10},{9,11},{10,... | collective-permute-start | bytes 245768 | tf_op jit(solution)/shard_map/ppermute | solution.py:34
  119.4 6.0 %collective-permute-start.22 = (f32[160,128]{1,0:T(8,128)S(1)}, f32[160,128]{1,0:T(8,128)S(1)}, u32[]{:S(2)}, u32[]{:S(2)}) collective-permute-start(f32[160,128]{1,0:T(8,128)S(1)} %slice.31), channel_id=1, source_target_pairs={{0,16},{1,17},{2,18},{3,19},{4,20},{5,21},{6,22},{7,23},{8,24},{9,... | collective-permute-start | bytes 245768 | tf_op jit(solution)/shard_map/ppermute | solution.py:34

commit v7 on v6

v7 whole, which is shorter than its diff:
```python
import itertools

import jax
import jax.numpy as jnp
from jax import lax
from jax.experimental import pallas as pl
from jax.experimental.pallas import tpu as pltpu
from jax.sharding import PartitionSpec as P

N_ROW, N_COL, FB, NB, NT = 8, 16, 160, 1024, 128
DEVICES = N_ROW * N_COL
ROW_PTS, COL_PTS = N_COL * FB, N_ROW * FB
WIDE = NB + NT
AXES = ("row", "col")
PARTS = {"y": 4, "xh": 2, "z": 4, "xl": 2, "k": 2}
TILE = 4 * FB
BF, F32 = jnp.bfloat16, jnp.float32


def index_of(y, xh, z, xl, k):
    return (y * 2 + xh) * N_COL + z * 4 + xl * 2 + k


def moved(**steps):
    pairs = []
    for at in itertools.product(*map(range, PARTS.values())):
        to = [(a + steps.get(name, 0)) % size for a, (name, size) in zip(at, PARTS.items())]
        pairs.append((index_of(*at), index_of(*to)))
    return pairs


def send(x, **steps):
    return lax.ppermute(x, AXES, moved(**steps))


def nn(a, b):
    return jnp.dot(a, b, preferred_element_type=F32)


def nt(a, b):
    return lax.dot_general(a, b, (((1,), (1,)), ((), ())), preferred_element_type=F32)


def tn(a, b):
    return lax.dot_general(a, b, (((0,), (0,)), ((), ())), preferred_element_type=F32)


def points(ref, block):
    return ref[:, block * FB : (block + 1) * FB].astype(F32)


def pack_kernel(orb, tgt, out):
    row = lax.broadcasted_iota(jnp.int32, (8, FB), 0)
    for pair in range(DEVICES // 2):
        blocks = []
        for q in (2 * pair, 2 * pair + 1):
            sources = (q, q ^ 16, q ^ 2)
            extra = jnp.where(
                row == 0,
                tgt[sources[0] : sources[0] + 1, :],
                jnp.where(row == 1, tgt[sources[1] : sources[1] + 1, :], tgt[sources[2] : sources[2] + 1, :]),
            )
            pieces = [points(orb, s) for s in sources]
            blocks.append(jnp.concatenate([*pieces, extra], axis=1))
        out[16 * pair : 16 * (pair + 1), :] = jnp.concatenate(blocks, axis=0).astype(BF)


def pack(orbitals, targets):
    return pl.pallas_call(
        pack_kernel,
        out_shape=jax.ShapeDtypeStruct((DEVICES * 8, 4 * FB), BF),
        compiler_params=pltpu.CompilerParams(vmem_limit_bytes=32 * 2**20),
        name="pack",
    )(orbitals, targets.astype(F32).reshape(DEVICES, FB))


def unpack_kernel(packed, own, col_side, row_side):
    turned = packed[:, : 3 * FB].T
    source = lax.broadcasted_iota(jnp.int32, (NB, NT), 0)
    target = lax.broadcasted_iota(jnp.int32, (NB, NT), 1)
    for i, out in enumerate((own, col_side, row_side)):
        out[:, :NB] = turned[i * FB : (i + 1) * FB]
        chosen = jnp.where(source == 8 * target + i, 1.0, 0.0).astype(BF)
        out[:, NB:] = tn(packed[:, 3 * FB :], chosen).astype(BF)


def unpack(packed):
    return pl.pallas_call(
        unpack_kernel,
        out_shape=[jax.ShapeDtypeStruct((FB, WIDE), BF)] * 3,
        compiler_params=pltpu.CompilerParams(vmem_limit_bytes=32 * 2**20),
        name="unpack",
    )(packed)


def tile_kernel(me, *refs):
    row_refs, col_refs, (kern, owned, mirrored), refs = refs[:16], refs[16:24], refs[24:27], refs[27:]
    row_own, row_other, c0, c1, c2, c3, cols, rows, stored, col_sum, sems = refs
    y, xh, z, xl, k = (me[i] for i in range(5))
    count = [0]

    def start(src, dst):
        copy = pltpu.make_async_copy(src, dst, sems.at[count[0]])
        count[0] += 1
        copy.start()
        return copy

    def block(y_step, side):
        return lax.rem(y + y_step, 4) * 2 + lax.rem(xh + side, 2)

    def place(t, b):
        return lax.rem(z + t, 4), lax.rem(xl + b % 2, 2), lax.rem(k + b // 2, 2)

    def row_copies(t):
        return [start(row_refs[4 * t + b], rows.at[t, b]) for b in range(4)]

    def kern_copies(t):
        return [start(kern.at[place(t, b)], stored.at[t % 2, b]) for b in range(4)]

    first_copies = [start(ref, cols.at[block(i // 2, i % 2)]) for i, ref in enumerate(col_refs)] + row_copies(0)
    next_rows, next_kern = [], kern_copies(0)
    col_sum[...] = jnp.zeros_like(col_sum)
    for copy in first_copies:
        copy.wait()
    col_wide = cols[...].reshape(COL_PTS, WIDE)

    for t in range(4):
        for copy in next_rows:
            copy.wait()
        kern_here = next_kern
        if t < 3:
            next_rows, next_kern = row_copies(t + 1), kern_copies(t + 1)
        row_wide = rows[t].reshape(TILE, WIDE)
        gram = nt(row_wide[:, :NB], col_wide[:, :NB])
        for copy in kern_here:
            copy.wait()
        chunks = COL_PTS // 128
        values = jnp.concatenate(
            [
                jnp.concatenate([stored[t % 2, b, pl.ds(j, FB, stride=chunks), :] for j in range(chunks)], axis=1)
                for b in range(4)
            ],
            axis=0,
        )

        def spread(ref):
            return jnp.concatenate([jnp.broadcast_to(ref[place(t, b)], (FB, COL_PTS)) for b in range(4)], axis=0)

        weighted = gram * values * spread(owned)
        high = weighted.astype(BF)
        low = (weighted - high.astype(F32)).astype(BF)
        row_sum = nn(high, col_wide[:, NB:]) + nn(low, col_wide[:, NB:])
        keep = spread(mirrored).astype(BF)
        added = tn(high * keep, row_wide[:, NB:]) + tn(low * keep, row_wide[:, NB:])
        col_sum[...] += added.reshape(col_sum.shape)
        row_own[t] = row_sum[: 2 * FB]
        row_other[t] = row_sum[2 * FB :]

    for step, col_out in enumerate((c0, c1, c2, c3)):
        for side in (0, 1):
            col_out[side * FB : (side + 1) * FB, :] = col_sum[block(step, side)]


def tile_call(me, row_parts, col_parts, kern, owned, mirrored):
    vmem = pl.BlockSpec(memory_space=pltpu.VMEM)
    hbm = pl.BlockSpec(memory_space=pltpu.HBM)
    return pl.pallas_call(
        tile_kernel,
        in_specs=[pl.BlockSpec(memory_space=pltpu.SMEM)] + [hbm] * 25 + [vmem] * 2,
        out_specs=[vmem] * 6,
        out_shape=[jax.ShapeDtypeStruct((4, 2 * FB, NT), F32)] * 2 + [jax.ShapeDtypeStruct((2 * FB, NT), F32)] * 4,
        scratch_shapes=[
            pltpu.VMEM((N_ROW, FB, WIDE), BF),
            pltpu.VMEM((4, 4, FB, WIDE), BF),
            pltpu.VMEM((2, 4, FB * COL_PTS // 128, 128), F32),
            pltpu.VMEM((N_ROW, FB, NT), F32),
            pltpu.SemaphoreType.DMA((40,)),
        ],
        compiler_params=pltpu.CompilerParams(vmem_limit_bytes=52 * 2**20),
        cost_estimate=pl.CostEstimate(flops=10_000_000_000, bytes_accessed=24_000_000, transcendentals=0),
        name="tiles",
    )(me, *row_parts, *col_parts, kern, owned, mirrored)


def ring(block, beside, axis):
    down, beside_up = send(block, **{axis: 1}), send(beside, **{axis: 3})
    beside_down, up = send(beside, **{axis: 1}), send(block, **{axis: 3})
    far, beside_far = send(down, **{axis: 1}), send(beside_up, **{axis: 3})
    return (block, beside, up, beside_up, far, beside_far, down, beside_down)


def local(orbitals, targets, kernel, tile_owner):
    r, c = lax.axis_index("row"), lax.axis_index("col")
    me = jnp.stack([r // 2, r % 2, c // 4, c // 2 % 2, c % 2]).astype(jnp.int32)

    packed = pack(orbitals, targets).reshape(DEVICES, 8, 4 * FB)
    packed = lax.all_to_all(packed, AXES, split_axis=0, concat_axis=0, tiled=True)
    own, col_side, row_side = unpack(packed.reshape(DEVICES * 8, 4 * FB))
    col_parts = ring(own, col_side, "y")
    same = ring(own, row_side, "z")
    other = [send(block, k=1) for block in same]
    row_parts = [block for t in range(0, 8, 2) for block in (*same[t : t + 2], *other[t : t + 2])]

    flags = tile_owner.reshape(N_COL, N_ROW).astype(F32)
    here = (lax.broadcasted_iota(jnp.int32, flags.shape, 0) == c) & (
        lax.broadcasted_iota(jnp.int32, flags.shape, 1) == r
    )
    owned = jnp.repeat(flags, FB, axis=1).reshape(4, 2, 2, 1, COL_PTS)
    mirrored = jnp.repeat(jnp.where(here, 0.0, flags), FB, axis=1).reshape(4, 2, 2, 1, COL_PTS)
    kern = kernel.reshape(4, 2, 2, FB * COL_PTS // 128, 128)

    row_own, row_other, c0, c1, c2, c3 = tile_call(me, row_parts, col_parts, kern, owned, mirrored)

    col_sum = c0 + send(c2, y=2) + send(c1, y=1) + send(c3, y=3)
    row_sum = row_own + send(row_other, k=1)
    row_sum = row_sum[0] + send(row_sum[2], z=2) + send(row_sum[1], z=1) + send(row_sum[3], z=3)
    row_share = row_sum[:FB] + send(row_sum[FB:], xl=1)
    col_share = col_sum[:FB] + send(col_sum[FB:], xh=1)
    return row_share + col_share


def solution(mesh):
    in_specs = (
        P(("row", "col"), None),
        P(("row", "col"), None),
        P("row", "col", None),
        P("row", None, None, "col"),
    )
    out_specs = P(("row", "col"), None)
    return jax.shard_map(local, mesh=mesh, in_specs=in_specs, out_specs=out_specs, check_vma=False)
```

time: 126 us -> 123 us (0.976)
  starting transfers between devices: 22.1 us -> 27.6 us
  waiting for transfers between devices: 38.3 us -> 33.5 us
  Pallas kernels: 26.8 us -> 23.3 us
  local copies, waits for them, and re-layouts: 3.82 us -> 1.87 us
    ppermute x23 -> x29, starting transfers between devices: 22.1 us -> 27.6 us  [send(): return lax.ppermute(x, AXES, moved(**steps))]
    ppermute x23 -> x29, waiting for transfers between devices: 38.3 us -> 33.5 us  [send(): return lax.ppermute(x, AXES, moved(**steps))]
    pallas_call x3 -> x2, Pallas kernels: 26.3 us -> 22.8 us  [the longest x1 21.4 us: tile_call(): pl.pallas_call(tile_kernel, in_specs=[pl.BlockSpec(memory_space=pltpu.SME...]
    unnamed x22 -> x18, local copies, waits for them, and re-layouts: 2.96 us -> 1 us
  transfers between devices with their start and end apart: 23 -> 29, of which waited for: 12 -> 13; matrix products, arithmetic and copies ran while one was open for 1% -> 2% of each run, Pallas kernels for 19% -> 0%
where the time goes in v7:
time: 123 us
  waiting for transfers between devices  33.5 us (27%)
  blocking collectives  32.9 us (27%)
  starting transfers between devices  27.6 us (22%)
  Pallas kernels  23.3 us (19%)
  other arithmetic  3.07 us (2%)
  local copies, waits for them, and re-layouts  1.87 us (2%)
    ppermute x29, waiting for transfers between devices, send(): return lax.ppermute(x, AXES, moved(**steps))  33.5 us
    all_to_all x1, blocking collectives, local(): lax.all_to_all(packed, AXES, split_axis=0, concat_axis=0, tiled=True)  32.9 us
    ppermute x29, starting transfers between devices, send(): return lax.ppermute(x, AXES, moved(**steps))  27.6 us
    pallas_call x1, Pallas kernels, tile_call(): pl.pallas_call(tile_kernel, in_specs=[pl.BlockSpec(memory_space=pltpu.SME...  21.4 us
  transfers between devices with their start and end apart: 29, of which 13 were waited for; matrix products, arithmetic and copies ran while one was open for 2% of the time, Pallas kernels for 0%

profile of v7, /device:TPU:0, one launch (start us, length us, event | category | flops | bytes accessed | tf_op | source)
XLA Modules:
  0.0 122.6 jit_solution(4067302005149314573)
XLA Ops:
  0.0 1.1 convert_reduce_fusion
  1.1 0.1 reshape.22.tgt
  1.2 1.0 copy-done
  2.2 0.5 pack.1
  2.7 32.9 %all_to_all.5 = bf16[128,8,640]{2,1,0:T(8,128)(2,1)S(1)} all-to-all(bf16[128,8,640]{2,1,0:T(8,128)(2,1)S(1)} %bitcast.28), channel_id=1, replica_groups=mesh['row'=8,'col'=16] {'row','col'}, dimensions={0} | all-to-all | bytes 2621440 | tf_op jit(solution)/shard_map/all_to_all | solution.py:197
  35.6 1.3 %unpack.1 = (bf16[160,1152]{1,0:T(8,128)(2,1)S(1)}, bf16[160,1152]{1,0:T(8,128)(2,1)S(1)}, bf16[160,1152]{1,0:T(8,128)(2,1)S(1)}) custom-call(bf16[1024,640]{1,0:T(8,128)(2,1)S(1)} %bitcast.27), custom_call_target="tpu_custom_call" | custom-call | tf_op jit(solution)/shard_map/unpack/pallas_call | solution.py:88
  37.0 0.1 collective-permute-start.19
  37.1 3.2 %collective-permute-start.15 = (bf16[160,1152]{1,0:T(8,128)(2,1)S(1)}, bf16[160,1152]{1,0:T(8,128)(2,1)S(1)}, u32[]{:S(2)}, u32[]{:S(2)}) collective-permute-start(bf16[160,1152]{1,0:T(8,128)(2,1)S(1)} %get-tuple-element.16.refs_17_), channel_id=1, source_target_pairs={{0,96},{1,97},{2,98},{3,99},{4,100},{5,101},{6,102},{7,103},{8,104... | collective-permute-start | bytes 1105928 | tf_op jit(solution)/shard_map/ppermute | solution.py:33
  40.3 3.2 %collective-permute-start.3 = (bf16[160,1152]{1,0:T(8,128)(2,1)S(1)}, bf16[160,1152]{1,0:T(8,128)(2,1)S(1)}, u32[]{:S(2)}, u32[]{:S(2)}) collective-permute-start(bf16[160,1152]{1,0:T(8,128)(2,1)S(1)} %get-tuple-element.15.refs_1_), channel_id=1, source_target_pairs={{0,12},{1,13},{2,14},{3,15},{4,0},{5,1},{6,2},{7,3},{8,4},{9,5},{1... | collective-permute-start | bytes 1105928 | tf_op jit(solution)/shard_map/ppermute | solution.py:33
  43.5 4.7 %collective-permute-done.19.refs_23_ = bf16[160,1152]{1,0:T(8,128)(2,1)S(1)} collective-permute-done((bf16[160,1152]{1,0:T(8,128)(2,1)S(1)}, bf16[160,1152]{1,0:T(8,128)(2,1)S(1)}, u32[]{:S(2)}, u32[]{:S(2)}) %collective-permute-start.19) | collective-permute-done | bytes 368672 | tf_op jit(solution)/shard_map/ppermute | solution.py:33
  48.2 3.2 %collective-permute-start.14 = (bf16[160,1152]{1,0:T(8,128)(2,1)S(1)}, bf16[160,1152]{1,0:T(8,128)(2,1)S(1)}, u32[]{:S(2)}, u32[]{:S(2)}) collective-permute-start(bf16[160,1152]{1,0:T(8,128)(2,1)S(1)} %get-tuple-element.14.refs_0_.refs_16_), channel_id=1, source_target_pairs={{0,96},{1,97},{2,98},{3,99},{4,100},{5,101},{6,102},{7,103},{8,104... | collective-permute-start | bytes 1105928 | tf_op jit(solution)/shard_map/ppermute | solution.py:33
  51.5 0.2 collective-permute-start.6
  51.6 3.1 %collective-permute-start.2 = (bf16[160,1152]{1,0:T(8,128)(2,1)S(1)}, bf16[160,1152]{1,0:T(8,128)(2,1)}, u32[]{:S(2)}, u32[]{:S(2)}) collective-permute-start(bf16[160,1152]{1,0:T(8,128)(2,1)S(1)} %get-tuple-element.14.refs_0_.refs_16_), channel_id=1, source_target_pairs={{0,12},{1,13},{2,14},{3,15},{4,0},{5,1},{6,2},{7,3},{8,4},{9,5},{1... | collective-permute-start | bytes 1105928 | tf_op jit(solution)/shard_map/ppermute | solution.py:33
  54.7 3.9 %collective-permute-done.16.refs_22_ = bf16[160,1152]{1,0:T(8,128)(2,1)} collective-permute-done((bf16[160,1152]{1,0:T(8,128)(2,1)S(1)}, bf16[160,1152]{1,0:T(8,128)(2,1)}, u32[]{:S(2)}, u32[]{:S(2)}) %collective-permute-start.16) | collective-permute-done | bytes 368672 | tf_op jit(solution)/shard_map/ppermute | solution.py:33
  58.6 0.2 collective-permute-done.14.refs_18_
  58.8 2.4 %collective-permute-done.6.refs_12_ = bf16[160,1152]{1,0:T(8,128)(2,1)} collective-permute-done((bf16[160,1152]{1,0:T(8,128)(2,1)S(1)}, bf16[160,1152]{1,0:T(8,128)(2,1)}, u32[]{:S(2)}, u32[]{:S(2)}) %collective-permute-start.6) | collective-permute-done | bytes 368672 | tf_op jit(solution)/shard_map/ppermute | solution.py:33
  61.3 2.1 %collective-permute-start.7 = (bf16[160,1152]{1,0:T(8,128)(2,1)}, bf16[160,1152]{1,0:T(8,128)(2,1)}, u32[]{:S(2)}, u32[]{:S(2)}) collective-permute-start(bf16[160,1152]{1,0:T(8,128)(2,1)} %collective-permute-done.6.refs_12_), channel_id=1, source_target_pairs={{0,4},{1,5},{2,6},{3,7},{4,8},{5,9},{6,10},{7,11},{8,12},{9,13},{1... | collective-permute-start | bytes 1105928 | tf_op jit(solution)/shard_map/ppermute | solution.py:33
  63.4 3.3 %collective-permute-done.18.refs_21_ = bf16[160,1152]{1,0:T(8,128)(2,1)S(1)} collective-permute-done((bf16[160,1152]{1,0:T(8,128)(2,1)S(1)}, bf16[160,1152]{1,0:T(8,128)(2,1)S(1)}, u32[]{:S(2)}, u32[]{:S(2)}) %collective-permute-start.18) | collective-permute-done | bytes 368672 | tf_op jit(solution)/shard_map/ppermute | solution.py:33
  66.7 0.1 collective-permute-start.17
  66.8 3.2 %collective-permute-done.8.refs_9_ = bf16[160,1152]{1,0:T(8,128)(2,1)} collective-permute-done((bf16[160,1152]{1,0:T(8,128)(2,1)S(1)}, bf16[160,1152]{1,0:T(8,128)(2,1)}, u32[]{:S(2)}, u32[]{:S(2)}) %collective-permute-start.8) | collective-permute-done | bytes 368672 | tf_op jit(solution)/shard_map/ppermute | solution.py:33
  69.9 0.5 collective-permute-start.10
  70.5 4.0 %collective-permute-done.7.refs_8_ = bf16[160,1152]{1,0:T(8,128)(2,1)} collective-permute-done((bf16[160,1152]{1,0:T(8,128)(2,1)}, bf16[160,1152]{1,0:T(8,128)(2,1)}, u32[]{:S(2)}, u32[]{:S(2)}) %collective-permute-start.7) | collective-permute-done | bytes 368672 | tf_op jit(solution)/shard_map/ppermute | solution.py:33
  74.5 0.1 and_select_fusion
  74.5 0.1 copy.10
  74.6 0.1 copy.9
  74.7 0.1 broadcast_in_dim.10
  74.8 0.2 reshape_reshape.6.refs_25_
  74.9 0.1 broadcast_in_dim.12
  75.0 0.2 reshape_reshape.7.refs_26_
  75.2 0.1 stack.23.me
  75.3 3.9 %collective-permute-done.17.refs_20_ = bf16[160,1152]{1,0:T(8,128)(2,1)} collective-permute-done((bf16[160,1152]{1,0:T(8,128)(2,1)}, bf16[160,1152]{1,0:T(8,128)(2,1)}, u32[]{:S(2)}, u32[]{:S(2)}) %collective-permute-start.17) | collective-permute-done | bytes 368672 | tf_op jit(solution)/shard_map/ppermute | solution.py:33
  79.3 21.4 %tiles.1 = (f32[4,320,128]{2,1,0:T(8,128)}, f32[4,320,128]{2,1,0:T(8,128)}, f32[320,128]{1,0:T(8,128)S(1)}, f32[320,128]{1,0:T(8,128)S(1)}, f32[320,128]{1,0:T(8,128)S(1)}, /*index=5*/f32[320,128]{1,0:T(8,128)S(1)}) custom-call(s32[5]{0:T(128)S(1)} %stack.23.me, bf16[160,1152]{1,0:T(8,128)(2,1)S(1)} %get-tuple-element.14.refs_0_.refs_16_, ...), custom_call_target="tpu_custom_call" | custom-call | flops 10000000000 | bytes 24000000 | tf_op jit(solution)/shard_map/tiles/pallas_call | solution.py:167
  100.7 0.1 collective-permute-start.20
  100.8 0.5 collective-permute-start.25
  101.3 1.9 %collective-permute-start.26 = (f32[320,128]{1,0:T(8,128)S(1)}, f32[320,128]{1,0:T(8,128)S(1)}, u32[]{:S(2)}, u32[]{:S(2)}) collective-permute-start(f32[320,128]{1,0:T(8,128)S(1)} %get-tuple-element.21), channel_id=1, source_target_pairs={{0,32},{1,33},{2,34},{3,35},{4,36},{5,37},{6,38},{7,39},{8,40},{9,... | collective-permute-start | bytes 491528 | tf_op jit(solution)/shard_map/ppermute | solution.py:33
  103.2 1.4 %collective-permute-start.27 = (f32[320,128]{1,0:T(8,128)S(1)}, f32[320,128]{1,0:T(8,128)S(1)}, u32[]{:S(2)}, u32[]{:S(2)}) collective-permute-start(f32[320,128]{1,0:T(8,128)S(1)} %get-tuple-element.22), channel_id=1, source_target_pairs={{0,96},{1,97},{2,98},{3,99},{4,100},{5,101},{6,102},{7,103},{8,104... | collective-permute-start | bytes 491528 | tf_op jit(solution)/shard_map/ppermute | solution.py:33
  104.6 1.2 add.46
  105.8 0.2 collective-permute-start.21
  106.0 4.2 %collective-permute-start.23 = (f32[320,128]{1,0:T(8,128)S(1)}, f32[320,128]{1,0:T(8,128)S(1)}, u32[]{:S(2)}, u32[]{:S(2)}) collective-permute-start(f32[320,128]{1,0:T(8,128)S(1)} %get-tuple-element.24), channel_id=1, source_target_pairs={{0,12},{1,13},{2,14},{3,15},{4,0},{5,1},{6,2},{7,3},{8,4},{9,5},{1... | collective-permute-start | bytes 491528 | tf_op jit(solution)/shard_map/ppermute | solution.py:33
  110.1 1.3 %collective-permute-start.22 = (f32[320,128]{1,0:T(8,128)S(1)}, f32[320,128]{1,0:T(8,128)S(1)}, u32[]{:S(2)}, u32[]{:S(2)}) collective-permute-start(f32[320,128]{1,0:T(8,128)S(1)} %get-tuple-element.25), channel_id=1, source_target_pairs={{0,4},{1,5},{2,6},{3,7},{4,8},{5,9},{6,10},{7,11},{8,12},{9,13},{1... | collective-permute-start | bytes 491528 | tf_op jit(solution)/shard_map/ppermute | solution.py:33
  111.4 0.9 collective-permute-done.26
  112.4 1.4 %collective-permute-start.28 = (f32[160,128]{1,0:T(8,128)S(1)}, f32[160,128]{1,0:T(8,128)S(1)}, u32[]{:S(2)}, u32[]{:S(2)}) collective-permute-start(f32[160,128]{1,0:T(8,128)S(1)} %slice.39), channel_id=1, source_target_pairs={{0,16},{1,17},{2,18},{3,19},{4,20},{5,21},{6,22},{7,23},{8,24},{9,... | collective-permute-start | bytes 245768 | tf_op jit(solution)/shard_map/ppermute | solution.py:33
  113.8 0.7 collective-permute-done.21
  114.5 0.6 collective-permute-done.23
  115.1 2.2 %collective-permute-done.22 = f32[320,128]{1,0:T(8,128)S(1)} collective-permute-done((f32[320,128]{1,0:T(8,128)S(1)}, f32[320,128]{1,0:T(8,128)S(1)}, u32[]{:S(2)}, u32[]{:S(2)}) %collective-permute-start.22) | collective-permute-done | bytes 163872 | tf_op jit(solution)/shard_map/ppermute | solution.py:33
  117.4 1.0 collective-permute-start.24
  118.4 3.5 %collective-permute-done.24 = f32[160,128]{1,0:T(8,128)S(1)} collective-permute-done((f32[160,128]{1,0:T(8,128)S(1)}, f32[160,128]{1,0:T(8,128)S(1)}, u32[]{:S(2)}, u32[]{:S(2)}) %collective-permute-start.24) | collective-permute-done | bytes 81952 | tf_op jit(solution)/shard_map/ppermute | solution.py:33
  121.9 0.7 fusion.3
  (52 shorter events, 0.2 us)
Async XLA Ops:
  1.2 1.0 copy-start
  35.6 38.8 %copy-start.2 = (s32[1,16,8,1]{1,3,2,0:T(1,128)S(1)}, s32[1,16,8,1]{1,3,2,0:T(1,128)}, u32[]{:S(2)}) copy-start(s32[1,16,8,1]{1,3,2,0:T(1,128)} %param.7) | copy-start | bytes 1540
  37.0 42.3 %copy-start.1 = (bf16[160,1152]{1,0:T(8,128)(2,1)}, bf16[160,1152]{1,0:T(8,128)(2,1)S(1)}, u32[]{:S(2)}) copy-start(bf16[160,1152]{1,0:T(8,128)(2,1)S(1)} %get-tuple-element.16.refs_17_) | copy-start | bytes 1105924
  37.0 11.2 %collective-permute-start.19 = (bf16[160,1152]{1,0:T(8,128)(2,1)S(1)}, bf16[160,1152]{1,0:T(8,128)(2,1)S(1)}, u32[]{:S(2)}, u32[]{:S(2)}) collective-permute-start(bf16[160,1152]{1,0:T(8,128)(2,1)S(1)} %get-tuple-element.16.refs_17_), channel_id=1, source_target_pairs={{0,32},{1,33},{2,34},{3,35},{4,36},{5,37},{6,38},{7,39},{8,40},{9,... | collective-permute-start | bytes 1105928 | tf_op jit(solution)/shard_map/ppermute | solution.py:33
  37.1 11.2 %collective-permute-start.15 = (bf16[160,1152]{1,0:T(8,128)(2,1)S(1)}, bf16[160,1152]{1,0:T(8,128)(2,1)S(1)}, u32[]{:S(2)}, u32[]{:S(2)}) collective-permute-start(bf16[160,1152]{1,0:T(8,128)(2,1)S(1)} %get-tuple-element.16.refs_17_), channel_id=1, source_target_pairs={{0,96},{1,97},{2,98},{3,99},{4,100},{5,101},{6,102},{7,103},{8,104... | collective-permute-start | bytes 1105928 | tf_op jit(solution)/shard_map/ppermute | solution.py:33
  40.3 11.2 %collective-permute-start.11 = (bf16[160,1152]{1,0:T(8,128)(2,1)S(1)}, bf16[160,1152]{1,0:T(8,128)(2,1)S(1)}, u32[]{:S(2)}, u32[]{:S(2)}) collective-permute-start(bf16[160,1152]{1,0:T(8,128)(2,1)S(1)} %get-tuple-element.15.refs_1_), channel_id=1, source_target_pairs={{0,4},{1,5},{2,6},{3,7},{4,8},{5,9},{6,10},{7,11},{8,12},{9,13},{1... | collective-permute-start | bytes 1105928 | tf_op jit(solution)/shard_map/ppermute | solution.py:33
  40.3 11.3 %collective-permute-start.3 = (bf16[160,1152]{1,0:T(8,128)(2,1)S(1)}, bf16[160,1152]{1,0:T(8,128)(2,1)S(1)}, u32[]{:S(2)}, u32[]{:S(2)}) collective-permute-start(bf16[160,1152]{1,0:T(8,128)(2,1)S(1)} %get-tuple-element.15.refs_1_), channel_id=1, source_target_pairs={{0,12},{1,13},{2,14},{3,15},{4,0},{5,1},{6,2},{7,3},{8,4},{9,5},{1... | collective-permute-start | bytes 1105928 | tf_op jit(solution)/shard_map/ppermute | solution.py:33
  43.5 11.2 %collective-permute-start.1 = (bf16[160,1152]{1,0:T(8,128)(2,1)S(1)}, bf16[160,1152]{1,0:T(8,128)(2,1)}, u32[]{:S(2)}, u32[]{:S(2)}) collective-permute-start(bf16[160,1152]{1,0:T(8,128)(2,1)S(1)} %get-tuple-element.15.refs_1_), channel_id=1, source_target_pairs={{0,1},{1,0},{2,3},{3,2},{4,5},{5,4},{6,7},{7,6},{8,9},{9,8},{10,11... | collective-permute-start | bytes 1105928 | tf_op jit(solution)/shard_map/ppermute | solution.py:33
  48.2 31.0 %copy-start.3 = (bf16[160,1152]{1,0:T(8,128)(2,1)}, bf16[160,1152]{1,0:T(8,128)(2,1)S(1)}, u32[]{:S(2)}) copy-start(bf16[160,1152]{1,0:T(8,128)(2,1)S(1)} %collective-permute-done.19.refs_23_) | copy-start | bytes 1105924
  48.2 10.3 %collective-permute-start.16 = (bf16[160,1152]{1,0:T(8,128)(2,1)S(1)}, bf16[160,1152]{1,0:T(8,128)(2,1)}, u32[]{:S(2)}, u32[]{:S(2)}) collective-permute-start(bf16[160,1152]{1,0:T(8,128)(2,1)S(1)} %get-tuple-element.14.refs_0_.refs_16_), channel_id=1, source_target_pairs={{0,32},{1,33},{2,34},{3,35},{4,36},{5,37},{6,38},{7,39},{8,40},{9,... | collective-permute-start | bytes 1105928 | tf_op jit(solution)/shard_map/ppermute | solution.py:33
  48.2 31.0 %copy-start.4 = (bf16[160,1152]{1,0:T(8,128)(2,1)}, bf16[160,1152]{1,0:T(8,128)(2,1)S(1)}, u32[]{:S(2)}) copy-start(bf16[160,1152]{1,0:T(8,128)(2,1)S(1)} %collective-permute-done.15.refs_19_) | copy-start | bytes 1105924
  48.2 10.6 %collective-permute-start.14 = (bf16[160,1152]{1,0:T(8,128)(2,1)S(1)}, bf16[160,1152]{1,0:T(8,128)(2,1)S(1)}, u32[]{:S(2)}, u32[]{:S(2)}) collective-permute-start(bf16[160,1152]{1,0:T(8,128)(2,1)S(1)} %get-tuple-element.14.refs_0_.refs_16_), channel_id=1, source_target_pairs={{0,96},{1,97},{2,98},{3,99},{4,100},{5,101},{6,102},{7,103},{8,104... | collective-permute-start | bytes 1105928 | tf_op jit(solution)/shard_map/ppermute | solution.py:33
  51.5 27.8 %copy-start.5 = (bf16[160,1152]{1,0:T(8,128)(2,1)}, bf16[160,1152]{1,0:T(8,128)(2,1)S(1)}, u32[]{:S(2)}) copy-start(bf16[160,1152]{1,0:T(8,128)(2,1)S(1)} %collective-permute-done.11.refs_13_) | copy-start | bytes 1105924
  51.5 9.8 %collective-permute-start.6 = (bf16[160,1152]{1,0:T(8,128)(2,1)S(1)}, bf16[160,1152]{1,0:T(8,128)(2,1)}, u32[]{:S(2)}, u32[]{:S(2)}) collective-permute-start(bf16[160,1152]{1,0:T(8,128)(2,1)S(1)} %get-tuple-element.14.refs_0_.refs_16_), channel_id=1, source_target_pairs={{0,4},{1,5},{2,6},{3,7},{4,8},{5,9},{6,10},{7,11},{8,12},{9,13},{1... | collective-permute-start | bytes 1105928 | tf_op jit(solution)/shard_map/ppermute | solution.py:33
  51.6 27.6 %copy-start.6 = (bf16[160,1152]{1,0:T(8,128)(2,1)}, bf16[160,1152]{1,0:T(8,128)(2,1)S(1)}, u32[]{:S(2)}) copy-start(bf16[160,1152]{1,0:T(8,128)(2,1)S(1)} %collective-permute-done.3.refs_5_) | copy-start | bytes 1105924
  51.6 9.6 %collective-permute-start.2 = (bf16[160,1152]{1,0:T(8,128)(2,1)S(1)}, bf16[160,1152]{1,0:T(8,128)(2,1)}, u32[]{:S(2)}, u32[]{:S(2)}) collective-permute-start(bf16[160,1152]{1,0:T(8,128)(2,1)S(1)} %get-tuple-element.14.refs_0_.refs_16_), channel_id=1, source_target_pairs={{0,12},{1,13},{2,14},{3,15},{4,0},{5,1},{6,2},{7,3},{8,4},{9,5},{1... | collective-permute-start | bytes 1105928 | tf_op jit(solution)/shard_map/ppermute | solution.py:33
  54.7 6.6 %collective-permute-start = (bf16[160,1152]{1,0:T(8,128)(2,1)S(1)}, bf16[160,1152]{1,0:T(8,128)(2,1)S(1)}, u32[]{:S(2)}, u32[]{:S(2)}) collective-permute-start(bf16[160,1152]{1,0:T(8,128)(2,1)S(1)} %get-tuple-element.14.refs_0_.refs_16_), channel_id=1, source_target_pairs={{0,1},{1,0},{2,3},{3,2},{4,5},{5,4},{6,7},{7,6},{8,9},{9,8},{10,11... | collective-permute-start | bytes 1105928 | tf_op jit(solution)/shard_map/ppermute | solution.py:33
  58.6 8.1 %collective-permute-start.18 = (bf16[160,1152]{1,0:T(8,128)(2,1)S(1)}, bf16[160,1152]{1,0:T(8,128)(2,1)S(1)}, u32[]{:S(2)}, u32[]{:S(2)}) collective-permute-start(bf16[160,1152]{1,0:T(8,128)(2,1)S(1)} %collective-permute-done.15.refs_19_), channel_id=1, source_target_pairs={{0,96},{1,97},{2,98},{3,99},{4,100},{5,101},{6,102},{7,103},{8,104... | collective-permute-start | bytes 1105928 | tf_op jit(solution)/shard_map/ppermute | solution.py:33
  58.8 2.5 %copy-start.7 = (bf16[160,1152]{1,0:T(8,128)(2,1)}, bf16[160,1152]{1,0:T(8,128)(2,1)S(1)}, u32[]{:S(2)}) copy-start(bf16[160,1152]{1,0:T(8,128)(2,1)S(1)} %collective-permute-done.14.refs_18_) | copy-start | bytes 1105924
  58.8 7.9 %collective-permute-start.13 = (bf16[160,1152]{1,0:T(8,128)(2,1)S(1)}, bf16[160,1152]{1,0:T(8,128)(2,1)}, u32[]{:S(2)}, u32[]{:S(2)}) collective-permute-start(bf16[160,1152]{1,0:T(8,128)(2,1)S(1)} %collective-permute-done.11.refs_13_), channel_id=1, source_target_pairs={{0,1},{1,0},{2,3},{3,2},{4,5},{5,4},{6,7},{7,6},{8,9},{9,8},{10,11... | collective-permute-start | bytes 1105928 | tf_op jit(solution)/shard_map/ppermute | solution.py:33
  61.3 8.7 %collective-permute-start.8 = (bf16[160,1152]{1,0:T(8,128)(2,1)S(1)}, bf16[160,1152]{1,0:T(8,128)(2,1)}, u32[]{:S(2)}, u32[]{:S(2)}) collective-permute-start(bf16[160,1152]{1,0:T(8,128)(2,1)S(1)} %collective-permute-done.3.refs_5_), channel_id=1, source_target_pairs={{0,12},{1,13},{2,14},{3,15},{4,0},{5,1},{6,2},{7,3},{8,4},{9,5},{1... | collective-permute-start | bytes 1105928 | tf_op jit(solution)/shard_map/ppermute | solution.py:33
  61.3 8.7 %collective-permute-start.5 = (bf16[160,1152]{1,0:T(8,128)(2,1)S(1)}, bf16[160,1152]{1,0:T(8,128)(2,1)}, u32[]{:S(2)}, u32[]{:S(2)}) collective-permute-start(bf16[160,1152]{1,0:T(8,128)(2,1)S(1)} %collective-permute-done.3.refs_5_), channel_id=1, source_target_pairs={{0,1},{1,0},{2,3},{3,2},{4,5},{5,4},{6,7},{7,6},{8,9},{9,8},{10,11... | collective-permute-start | bytes 1105928 | tf_op jit(solution)/shard_map/ppermute | solution.py:33
  61.3 13.1 %collective-permute-start.7 = (bf16[160,1152]{1,0:T(8,128)(2,1)}, bf16[160,1152]{1,0:T(8,128)(2,1)}, u32[]{:S(2)}, u32[]{:S(2)}) collective-permute-start(bf16[160,1152]{1,0:T(8,128)(2,1)} %collective-permute-done.6.refs_12_), channel_id=1, source_target_pairs={{0,4},{1,5},{2,6},{3,7},{4,8},{5,9},{6,10},{7,11},{8,12},{9,13},{1... | collective-permute-start | bytes 1105928 | tf_op jit(solution)/shard_map/ppermute | solution.py:33
  66.7 7.8 %copy-start.8 = (bf16[160,1152]{1,0:T(8,128)(2,1)}, bf16[160,1152]{1,0:T(8,128)(2,1)S(1)}, u32[]{:S(2)}) copy-start(bf16[160,1152]{1,0:T(8,128)(2,1)S(1)} %collective-permute-done.18.refs_21_) | copy-start | bytes 1105924
  66.7 12.5 %collective-permute-start.12 = (bf16[160,1152]{1,0:T(8,128)(2,1)}, bf16[160,1152]{1,0:T(8,128)(2,1)}, u32[]{:S(2)}, u32[]{:S(2)}) collective-permute-start(bf16[160,1152]{1,0:T(8,128)(2,1)} %collective-permute-done.6.refs_12_), channel_id=1, source_target_pairs={{0,1},{1,0},{2,3},{3,2},{4,5},{5,4},{6,7},{7,6},{8,9},{9,8},{10,11... | collective-permute-start | bytes 1105928 | tf_op jit(solution)/shard_map/ppermute | solution.py:33
  66.7 12.5 %collective-permute-start.17 = (bf16[160,1152]{1,0:T(8,128)(2,1)}, bf16[160,1152]{1,0:T(8,128)(2,1)}, u32[]{:S(2)}, u32[]{:S(2)}) collective-permute-start(bf16[160,1152]{1,0:T(8,128)(2,1)} %collective-permute-done.16.refs_22_), channel_id=1, source_target_pairs={{0,32},{1,33},{2,34},{3,35},{4,36},{5,37},{6,38},{7,39},{8,40},{9,... | collective-permute-start | bytes 1105928 | tf_op jit(solution)/shard_map/ppermute | solution.py:33
  69.9 9.3 %collective-permute-start.4 = (bf16[160,1152]{1,0:T(8,128)(2,1)}, bf16[160,1152]{1,0:T(8,128)(2,1)}, u32[]{:S(2)}, u32[]{:S(2)}) collective-permute-start(bf16[160,1152]{1,0:T(8,128)(2,1)} %collective-permute-done.2.refs_4_), channel_id=1, source_target_pairs={{0,1},{1,0},{2,3},{3,2},{4,5},{5,4},{6,7},{7,6},{8,9},{9,8},{10,11... | collective-permute-start | bytes 1105928 | tf_op jit(solution)/shard_map/ppermute | solution.py:33
  69.9 9.3 %collective-permute-start.10 = (bf16[160,1152]{1,0:T(8,128)(2,1)}, bf16[160,1152]{1,0:T(8,128)(2,1)}, u32[]{:S(2)}, u32[]{:S(2)}) collective-permute-start(bf16[160,1152]{1,0:T(8,128)(2,1)} %collective-permute-done.8.refs_9_), channel_id=1, source_target_pairs={{0,1},{1,0},{2,3},{3,2},{4,5},{5,4},{6,7},{7,6},{8,9},{9,8},{10,11... | collective-permute-start | bytes 1105928 | tf_op jit(solution)/shard_map/ppermute | solution.py:33
  74.4 4.8 %collective-permute-start.9 = (bf16[160,1152]{1,0:T(8,128)(2,1)}, bf16[160,1152]{1,0:T(8,128)(2,1)}, u32[]{:S(2)}, u32[]{:S(2)}) collective-permute-start(bf16[160,1152]{1,0:T(8,128)(2,1)} %collective-permute-done.7.refs_8_), channel_id=1, source_target_pairs={{0,1},{1,0},{2,3},{3,2},{4,5},{5,4},{6,7},{7,6},{8,9},{9,8},{10,11... | collective-permute-start | bytes 1105928 | tf_op jit(solution)/shard_map/ppermute | solution.py:33
  100.7 3.8 %collective-permute-start.20 = (f32[4,320,128]{2,1,0:T(8,128)}, f32[4,320,128]{2,1,0:T(8,128)S(1)}, u32[]{:S(2)}, u32[]{:S(2)}) collective-permute-start(f32[4,320,128]{2,1,0:T(8,128)} %get-tuple-element.18), channel_id=1, source_target_pairs={{0,1},{1,0},{2,3},{3,2},{4,5},{5,4},{6,7},{7,6},{8,9},{9,8},{10,11... | collective-permute-start | bytes 1966088 | tf_op jit(solution)/shard_map/ppermute | solution.py:33
  100.8 9.3 %collective-permute-start.25 = (f32[320,128]{1,0:T(8,128)S(1)}, f32[320,128]{1,0:T(8,128)S(1)}, u32[]{:S(2)}, u32[]{:S(2)}) collective-permute-start(f32[320,128]{1,0:T(8,128)S(1)} %get-tuple-element.20), channel_id=1, source_target_pairs={{0,64},{1,65},{2,66},{3,67},{4,68},{5,69},{6,70},{7,71},{8,72},{9,... | collective-permute-start | bytes 491528 | tf_op jit(solution)/shard_map/ppermute | solution.py:33
  101.3 11.0 %collective-permute-start.26 = (f32[320,128]{1,0:T(8,128)S(1)}, f32[320,128]{1,0:T(8,128)S(1)}, u32[]{:S(2)}, u32[]{:S(2)}) collective-permute-start(f32[320,128]{1,0:T(8,128)S(1)} %get-tuple-element.21), channel_id=1, source_target_pairs={{0,32},{1,33},{2,34},{3,35},{4,36},{5,37},{6,38},{7,39},{8,40},{9,... | collective-permute-start | bytes 491528 | tf_op jit(solution)/shard_map/ppermute | solution.py:33
  103.2 9.1 %collective-permute-start.27 = (f32[320,128]{1,0:T(8,128)S(1)}, f32[320,128]{1,0:T(8,128)S(1)}, u32[]{:S(2)}, u32[]{:S(2)}) collective-permute-start(f32[320,128]{1,0:T(8,128)S(1)} %get-tuple-element.22), channel_id=1, source_target_pairs={{0,96},{1,97},{2,98},{3,99},{4,100},{5,101},{6,102},{7,103},{8,104... | collective-permute-start | bytes 491528 | tf_op jit(solution)/shard_map/ppermute | solution.py:33
  105.8 8.7 %collective-permute-start.21 = (f32[320,128]{1,0:T(8,128)S(1)}, f32[320,128]{1,0:T(8,128)S(1)}, u32[]{:S(2)}, u32[]{:S(2)}) collective-permute-start(f32[320,128]{1,0:T(8,128)S(1)} %get-tuple-element.23), channel_id=1, source_target_pairs={{0,8},{1,9},{2,10},{3,11},{4,12},{5,13},{6,14},{7,15},{8,0},{9,1},... | collective-permute-start | bytes 491528 | tf_op jit(solution)/shard_map/ppermute | solution.py:33
  106.0 9.1 %collective-permute-start.23 = (f32[320,128]{1,0:T(8,128)S(1)}, f32[320,128]{1,0:T(8,128)S(1)}, u32[]{:S(2)}, u32[]{:S(2)}) collective-permute-start(f32[320,128]{1,0:T(8,128)S(1)} %get-tuple-element.24), channel_id=1, source_target_pairs={{0,12},{1,13},{2,14},{3,15},{4,0},{5,1},{6,2},{7,3},{8,4},{9,5},{1... | collective-permute-start | bytes 491528 | tf_op jit(solution)/shard_map/ppermute | solution.py:33
  110.1 7.2 %collective-permute-start.22 = (f32[320,128]{1,0:T(8,128)S(1)}, f32[320,128]{1,0:T(8,128)S(1)}, u32[]{:S(2)}, u32[]{:S(2)}) collective-permute-start(f32[320,128]{1,0:T(8,128)S(1)} %get-tuple-element.25), channel_id=1, source_target_pairs={{0,4},{1,5},{2,6},{3,7},{4,8},{5,9},{6,10},{7,11},{8,12},{9,13},{1... | collective-permute-start | bytes 491528 | tf_op jit(solution)/shard_map/ppermute | solution.py:33
  112.4 6.1 %collective-permute-start.28 = (f32[160,128]{1,0:T(8,128)S(1)}, f32[160,128]{1,0:T(8,128)S(1)}, u32[]{:S(2)}, u32[]{:S(2)}) collective-permute-start(f32[160,128]{1,0:T(8,128)S(1)} %slice.39), channel_id=1, source_target_pairs={{0,16},{1,17},{2,18},{3,19},{4,20},{5,21},{6,22},{7,23},{8,24},{9,... | collective-permute-start | bytes 245768 | tf_op jit(solution)/shard_map/ppermute | solution.py:33
  117.4 4.5 %collective-permute-start.24 = (f32[160,128]{1,0:T(8,128)S(1)}, f32[160,128]{1,0:T(8,128)S(1)}, u32[]{:S(2)}, u32[]{:S(2)}) collective-permute-start(f32[160,128]{1,0:T(8,128)S(1)} %slice.37), channel_id=1, source_target_pairs={{0,2},{1,3},{2,0},{3,1},{4,6},{5,7},{6,4},{7,5},{8,10},{9,11},{10,... | collective-permute-start | bytes 245768 | tf_op jit(solution)/shard_map/ppermute | solution.py:33

commit v8 on v7

--- a/solution.py
+++ b/solution.py
@@ -74,27 +74,43 @@
     )(orbitals, targets.astype(F32).reshape(DEVICES, FB))
 
 
-def unpack_kernel(packed, own, col_side, row_side):
+def unpack_kernel(packed, col_pair, row_pair):
     turned = packed[:, : 3 * FB].T
     source = lax.broadcasted_iota(jnp.int32, (NB, NT), 0)
     target = lax.broadcasted_iota(jnp.int32, (NB, NT), 1)
-    for i, out in enumerate((own, col_side, row_side)):
-        out[:, :NB] = turned[i * FB : (i + 1) * FB]
+    for i, spots in enumerate((((col_pair, 0), (row_pair, 0)), ((col_pair, 1),), ((row_pair, 1),))):
         chosen = jnp.where(source == 8 * target + i, 1.0, 0.0).astype(BF)
-        out[:, NB:] = tn(packed[:, 3 * FB :], chosen).astype(BF)
+        tgt = tn(packed[:, 3 * FB :], chosen).astype(BF)
+        for out, side in spots:
+            out[side, :, :NB] = turned[i * FB : (i + 1) * FB]
+            out[side, :, NB:] = tgt
 
 
 def unpack(packed):
     return pl.pallas_call(
         unpack_kernel,
-        out_shape=[jax.ShapeDtypeStruct((FB, WIDE), BF)] * 3,
+        out_shape=[jax.ShapeDtypeStruct((2, FB, WIDE), BF)] * 2,
         compiler_params=pltpu.CompilerParams(vmem_limit_bytes=32 * 2**20),
         name="unpack",
     )(packed)
 
 
+def cut_kernel(*refs):
+    for i, (pair, out) in enumerate(zip(refs[:4], refs[4:])):
+        out[...] = pair[i % 2]
+
+
+def cut(*pairs):
+    return pl.pallas_call(
+        cut_kernel,
+        out_shape=[jax.ShapeDtypeStruct((FB, WIDE), BF)] * 4,
+        compiler_params=pltpu.CompilerParams(vmem_limit_bytes=16 * 2**20),
+        name="cut",
+    )(*pairs)
+
+
 def tile_kernel(me, *refs):
-    row_refs, col_refs, (kern, owned, mirrored), refs = refs[:16], refs[16:24], refs[24:27], refs[27:]
+    row_refs, col_refs, (kern, owned, mirrored), refs = refs[:10], refs[10:15], refs[15:18], refs[18:]
     row_own, row_other, c0, c1, c2, c3, cols, rows, stored, col_sum, sems = refs
     y, xh, z, xl, k = (me[i] for i in range(5))
     count = [0]
@@ -112,12 +128,16 @@
         return lax.rem(z + t, 4), lax.rem(xl + b % 2, 2), lax.rem(k + b // 2, 2)
 
     def row_copies(t):
-        return [start(row_refs[4 * t + b], rows.at[t, b]) for b in range(4)]
+        if t == 2:
+            return [start(row_refs[4 + b], rows.at[t, b]) for b in range(4)]
+        at = (0, 2, 0, 8)[t]
+        return [start(row_refs[at + b], rows.at[t, pl.ds(2 * b, 2)]) for b in range(2)]
 
     def kern_copies(t):
         return [start(kern.at[place(t, b)], stored.at[t % 2, b]) for b in range(4)]
 
-    first_copies = [start(ref, cols.at[block(i // 2, i % 2)]) for i, ref in enumerate(col_refs)] + row_copies(0)
+    first_copies = [start(col_refs[i].at[b], cols.at[block(step, b)]) for i, step in enumerate((0, 1, 3)) for b in (0, 1)]
+    first_copies += [start(col_refs[3 + b], cols.at[block(2, b)]) for b in (0, 1)] + row_copies(0)
     next_rows, next_kern = [], kern_copies(0)
     col_sum[...] = jnp.zeros_like(col_sum)
     for copy in first_copies:
@@ -131,9 +151,13 @@
         if t < 3:
             next_rows, next_kern = row_copies(t + 1), kern_copies(t + 1)
         row_wide = rows[t].reshape(TILE, WIDE)
+        if t > 0:
+            for copy in kern_here:
+                copy.wait()
         gram = nt(row_wide[:, :NB], col_wide[:, :NB])
-        for copy in kern_here:
-            copy.wait()
+        if t == 0:
+            for copy in kern_here:
+                copy.wait()
         chunks = COL_PTS // 128
         values = jnp.concatenate(
             [
@@ -150,8 +174,10 @@
         high = weighted.astype(BF)
         low = (weighted - high.astype(F32)).astype(BF)
         row_sum = nn(high, col_wide[:, NB:]) + nn(low, col_wide[:, NB:])
-        keep = spread(mirrored).astype(BF)
-        added = tn(high * keep, row_wide[:, NB:]) + tn(low * keep, row_wide[:, NB:])
+        if t == 0:
+            keep = spread(mirrored).astype(BF)
+            high, low = high * keep, low * keep
+        added = tn(high, row_wide[:, NB:]) + tn(low, row_wide[:, NB:])
         col_sum[...] += added.reshape(col_sum.shape)
         row_own[t] = row_sum[: 2 * FB]
         row_other[t] = row_sum[2 * FB :]
@@ -166,7 +192,7 @@
     hbm = pl.BlockSpec(memory_space=pltpu.HBM)
     return pl.pallas_call(
         tile_kernel,
-        in_specs=[pl.BlockSpec(memory_space=pltpu.SMEM)] + [hbm] * 25 + [vmem] * 2,
+        in_specs=[pl.BlockSpec(memory_space=pltpu.SMEM)] + [hbm] * 16 + [vmem] * 2,
         out_specs=[vmem] * 6,
         out_shape=[jax.ShapeDtypeStruct((4, 2 * FB, NT), F32)] * 2 + [jax.ShapeDtypeStruct((2 * FB, NT), F32)] * 4,
         scratch_shapes=[
@@ -182,24 +208,22 @@
     )(me, *row_parts, *col_parts, kern, owned, mirrored)
 
 
-def ring(block, beside, axis):
-    down, beside_up = send(block, **{axis: 1}), send(beside, **{axis: 3})
-    beside_down, up = send(beside, **{axis: 1}), send(block, **{axis: 3})
-    far, beside_far = send(down, **{axis: 1}), send(beside_up, **{axis: 3})
-    return (block, beside, up, beside_up, far, beside_far, down, beside_down)
-
-
 def local(orbitals, targets, kernel, tile_owner):
     r, c = lax.axis_index("row"), lax.axis_index("col")
     me = jnp.stack([r // 2, r % 2, c // 4, c // 2 % 2, c % 2]).astype(jnp.int32)
 
     packed = pack(orbitals, targets).reshape(DEVICES, 8, 4 * FB)
     packed = lax.all_to_all(packed, AXES, split_axis=0, concat_axis=0, tiled=True)
-    own, col_side, row_side = unpack(packed.reshape(DEVICES * 8, 4 * FB))
-    col_parts = ring(own, col_side, "y")
-    same = ring(own, row_side, "z")
-    other = [send(block, k=1) for block in same]
-    row_parts = [block for t in range(0, 8, 2) for block in (*same[t : t + 2], *other[t : t + 2])]
+    col_pair, row_pair = unpack(packed.reshape(DEVICES * 8, 4 * FB))
+
+    y_down, y_up = send(col_pair, y=1), send(col_pair, y=3)
+    z_down, z_up = send(row_pair, z=1), send(row_pair, z=3)
+    parts = cut(y_down, y_up, z_down, z_up)
+    y_far, y_far_side = send(parts[0], y=1), send(parts[1], y=3)
+    z_far, z_far_side = send(parts[2], z=1), send(parts[3], z=3)
+    col_parts = (col_pair, y_up, y_down, y_far, y_far_side)
+    row_parts = (row_pair, send(row_pair, k=1), z_up, send(z_up, k=1))
+    row_parts += (z_far, z_far_side, send(z_far, k=1), send(z_far_side, k=1), z_down, send(z_down, k=1))
 
     flags = tile_owner.reshape(N_COL, N_ROW).astype(F32)
     here = (lax.broadcasted_iota(jnp.int32, flags.shape, 0) == c) & (

time: 123 us -> 120 us (0.976)
  starting transfers between devices: 27.6 us -> 22 us
  waiting for transfers between devices: 33.5 us -> 36.2 us
    ppermute x29 -> x22, starting transfers between devices: 27.6 us -> 22 us  [send(): return lax.ppermute(x, AXES, moved(**steps))]
    ppermute x29 -> x22, waiting for transfers between devices: 33.5 us -> 36.2 us  [send(): return lax.ppermute(x, AXES, moved(**steps))]
    pallas_call x1 -> x2, Pallas kernels: 1.34 us -> 2.51 us  [the longest x1 1.34 us: unpack(): pl.pallas_call(unpack_kernel, out_shape=[jax.ShapeDtypeStruct((2, FB, WID...]
  transfers between devices with their start and end apart: 29 -> 22, of which waited for: 13 -> 13; matrix products, arithmetic and copies ran while one was open for 2% -> 2% of each run, Pallas kernels for 0% -> 1%
where the time goes in v8:
time: 120 us
  waiting for transfers between devices  36.2 us (30%)
  blocking collectives  32.9 us (27%)
  Pallas kernels  23.5 us (20%)
  starting transfers between devices  22 us (18%)
  other arithmetic  3.11 us (3%)
  local copies, waits for them, and re-layouts  2.17 us (2%)
    ppermute x22, waiting for transfers between devices, send(): return lax.ppermute(x, AXES, moved(**steps))  36.2 us
    all_to_all x1, blocking collectives, local(): lax.all_to_all(packed, AXES, split_axis=0, concat_axis=0, tiled=True)  32.9 us
    ppermute x22, starting transfers between devices, send(): return lax.ppermute(x, AXES, moved(**steps))  22 us
    pallas_call x1, Pallas kernels, tile_call(): pl.pallas_call(tile_kernel, in_specs=[pl.BlockSpec(memory_space=pltpu.SME...  20.5 us
  transfers between devices with their start and end apart: 22, of which 13 were waited for; matrix products, arithmetic and copies ran while one was open for 2% of the time, Pallas kernels for 1%

profile of v8, /device:TPU:0, one launch (start us, length us, event | category | flops | bytes accessed | tf_op | source)
XLA Modules:
  0.0 120.1 jit_solution(13986986325670026753)
XLA Ops:
  0.0 1.1 convert_reduce_fusion
  1.1 0.1 reshape.22.tgt
  1.2 1.0 copy-done.4
  2.2 0.5 pack.1
  2.7 32.9 %all_to_all.5 = bf16[128,8,640]{2,1,0:T(8,128)(2,1)S(1)} all-to-all(bf16[128,8,640]{2,1,0:T(8,128)(2,1)S(1)} %bitcast.28), channel_id=1, replica_groups=mesh['row'=8,'col'=16] {'row','col'}, dimensions={0} | all-to-all | bytes 2621440 | tf_op jit(solution)/shard_map/all_to_all | solution.py:216
  35.6 1.3 %unpack.1 = (bf16[2,160,1152]{2,1,0:T(8,128)(2,1)S(1)}, bf16[2,160,1152]{2,1,0:T(8,128)(2,1)S(1)}) custom-call(bf16[1024,640]{1,0:T(8,128)(2,1)S(1)} %bitcast.27), custom_call_target="tpu_custom_call" | custom-call | tf_op jit(solution)/shard_map/unpack/pallas_call | solution.py:90
  37.0 0.9 collective-permute-start.4
  37.9 1.2 %collective-permute-start.3 = (bf16[2,160,1152]{2,1,0:T(8,128)(2,1)S(1)}, bf16[2,160,1152]{2,1,0:T(8,128)(2,1)S(1)}, u32[]{:S(2)}, u32[]{:S(2)}) collective-permute-start(bf16[2,160,1152]{2,1,0:T(8,128)(2,1)S(1)} %get-tuple-element.18.refs_10_), channel_id=1, source_target_pairs={{0,32},{1,33},{2,34},{3,35},{4,36},{5,37},{6,38},{7,39},{8,40},{9,... | collective-permute-start | bytes 2211848 | tf_op jit(solution)/shard_map/ppermute | solution.py:33
  39.1 3.2 %collective-permute-start.1 = (bf16[2,160,1152]{2,1,0:T(8,128)(2,1)S(1)}, bf16[2,160,1152]{2,1,0:T(8,128)(2,1)S(1)}, u32[]{:S(2)}, u32[]{:S(2)}) collective-permute-start(bf16[2,160,1152]{2,1,0:T(8,128)(2,1)S(1)} %get-tuple-element.17.refs_0_), channel_id=1, source_target_pairs={{0,12},{1,13},{2,14},{3,15},{4,0},{5,1},{6,2},{7,3},{8,4},{9,5},{1... | collective-permute-start | bytes 2211848 | tf_op jit(solution)/shard_map/ppermute | solution.py:33
  42.3 12.6 %collective-permute-done.4.refs_1_.refs_11_ = bf16[2,160,1152]{2,1,0:T(8,128)(2,1)S(1)} collective-permute-done((bf16[2,160,1152]{2,1,0:T(8,128)(2,1)S(1)}, bf16[2,160,1152]{2,1,0:T(8,128)(2,1)S(1)}, u32[]{:S(2)}, u32[]{:S(2)}) %collective-permute-start.4) | collective-permute-done | bytes 737312 | tf_op jit(solution)/shard_map/ppermute | solution.py:33
  54.9 2.0 %collective-permute-done.3.refs_0_.refs_12_ = bf16[2,160,1152]{2,1,0:T(8,128)(2,1)S(1)} collective-permute-done((bf16[2,160,1152]{2,1,0:T(8,128)(2,1)S(1)}, bf16[2,160,1152]{2,1,0:T(8,128)(2,1)S(1)}, u32[]{:S(2)}, u32[]{:S(2)}) %collective-permute-start.3) | collective-permute-done | bytes 737312 | tf_op jit(solution)/shard_map/ppermute | solution.py:33
  57.0 0.6 collective-permute-done.5.refs_2_.refs_8_
  57.6 1.2 cut.1
  58.8 3.2 %collective-permute-start.7 = (bf16[160,1152]{1,0:T(8,128)(2,1)}, bf16[160,1152]{1,0:T(8,128)(2,1)S(1)}, u32[]{:S(2)}, u32[]{:S(2)}) collective-permute-start(bf16[160,1152]{1,0:T(8,128)(2,1)} %get-tuple-element.20), channel_id=1, source_target_pairs={{0,12},{1,13},{2,14},{3,15},{4,0},{5,1},{6,2},{7,3},{8,4},{9,5},{1... | collective-permute-start | bytes 1105928 | tf_op jit(solution)/shard_map/ppermute | solution.py:33
  62.0 0.6 collective-permute-start.11
  62.7 0.6 collective-permute-start.2
  63.3 0.3 copy-done.8
  63.6 5.1 %collective-permute-done.6.refs_4_ = bf16[160,1152]{1,0:T(8,128)(2,1)S(1)} collective-permute-done((bf16[160,1152]{1,0:T(8,128)(2,1)}, bf16[160,1152]{1,0:T(8,128)(2,1)S(1)}, u32[]{:S(2)}, u32[]{:S(2)}) %collective-permute-start.6) | collective-permute-done | bytes 368672 | tf_op jit(solution)/shard_map/ppermute | solution.py:33
  68.7 2.6 %collective-permute-start.12 = (bf16[160,1152]{1,0:T(8,128)(2,1)S(1)}, bf16[160,1152]{1,0:T(8,128)(2,1)}, u32[]{:S(2)}, u32[]{:S(2)}) collective-permute-start(bf16[160,1152]{1,0:T(8,128)(2,1)S(1)} %get-tuple-element.22), channel_id=1, source_target_pairs={{0,96},{1,97},{2,98},{3,99},{4,100},{5,101},{6,102},{7,103},{8,104... | collective-permute-start | bytes 1105928 | tf_op jit(solution)/shard_map/ppermute | solution.py:33
  71.3 0.2 collective-permute-done.11.refs_13_
  71.5 0.3 collective-permute-start.9
  71.9 0.1 copy.10
  72.0 0.1 copy.9
  72.0 0.1 broadcast_in_dim.10
  72.1 0.2 reshape_reshape.6.refs_16_
  72.3 0.1 broadcast_in_dim.12
  72.4 0.2 reshape_reshape.7.refs_17_
  72.6 0.1 stack.23.me
  72.7 4.0 %collective-permute-done.12.refs_14_ = bf16[160,1152]{1,0:T(8,128)(2,1)} collective-permute-done((bf16[160,1152]{1,0:T(8,128)(2,1)S(1)}, bf16[160,1152]{1,0:T(8,128)(2,1)}, u32[]{:S(2)}, u32[]{:S(2)}) %collective-permute-start.12) | collective-permute-done | bytes 368672 | tf_op jit(solution)/shard_map/ppermute | solution.py:33
  76.7 20.5 %tiles.1 = (f32[4,320,128]{2,1,0:T(8,128)}, f32[4,320,128]{2,1,0:T(8,128)}, f32[320,128]{1,0:T(8,128)S(1)}, f32[320,128]{1,0:T(8,128)S(1)}, f32[320,128]{1,0:T(8,128)S(1)}, /*index=5*/f32[320,128]{1,0:T(8,128)S(1)}) custom-call(s32[5]{0:T(128)S(1)} %stack.23.me, bf16[2,160,1152]{2,1,0:T(8,128)(2,1)} %copy-done.6, bf16[2,160,1152]{2,1,0:T(8,128)(2,1)} %copy-done.8, ...), custom_call_target="tpu_custom_call" | custom-call | flops 10000000000 | bytes 24000000 | tf_op jit(solution)/shard_map/tiles/pallas_call | solution.py:193
  97.2 0.1 collective-permute-start.13
  97.2 2.4 %collective-permute-start.18 = (f32[320,128]{1,0:T(8,128)S(1)}, f32[320,128]{1,0:T(8,128)S(1)}, u32[]{:S(2)}, u32[]{:S(2)}) collective-permute-start(f32[320,128]{1,0:T(8,128)S(1)} %get-tuple-element.26), channel_id=1, source_target_pairs={{0,64},{1,65},{2,66},{3,67},{4,68},{5,69},{6,70},{7,71},{8,72},{9,... | collective-permute-start | bytes 491528 | tf_op jit(solution)/shard_map/ppermute | solution.py:33
  99.6 2.3 %collective-permute-start.19 = (f32[320,128]{1,0:T(8,128)S(1)}, f32[320,128]{1,0:T(8,128)S(1)}, u32[]{:S(2)}, u32[]{:S(2)}) collective-permute-start(f32[320,128]{1,0:T(8,128)S(1)} %get-tuple-element.27), channel_id=1, source_target_pairs={{0,32},{1,33},{2,34},{3,35},{4,36},{5,37},{6,38},{7,39},{8,40},{9,... | collective-permute-start | bytes 491528 | tf_op jit(solution)/shard_map/ppermute | solution.py:33
  102.0 0.9 collective-permute-start.20
  102.9 1.2 add.46
  104.1 0.4 collective-permute-start.14
  104.5 1.8 %collective-permute-start.16 = (f32[320,128]{1,0:T(8,128)S(1)}, f32[320,128]{1,0:T(8,128)S(1)}, u32[]{:S(2)}, u32[]{:S(2)}) collective-permute-start(f32[320,128]{1,0:T(8,128)S(1)} %get-tuple-element.30), channel_id=1, source_target_pairs={{0,12},{1,13},{2,14},{3,15},{4,0},{5,1},{6,2},{7,3},{8,4},{9,5},{1... | collective-permute-start | bytes 491528 | tf_op jit(solution)/shard_map/ppermute | solution.py:33
  106.3 0.2 collective-permute-start.15
  106.5 2.4 %collective-permute-done.19 = f32[320,128]{1,0:T(8,128)S(1)} collective-permute-done((f32[320,128]{1,0:T(8,128)S(1)}, f32[320,128]{1,0:T(8,128)S(1)}, u32[]{:S(2)}, u32[]{:S(2)}) %collective-permute-start.19) | collective-permute-done | bytes 163872 | tf_op jit(solution)/shard_map/ppermute | solution.py:33
  108.9 1.2 collective-permute-done.20
  110.1 1.1 collective-permute-start.21
  111.2 1.6 %collective-permute-done.14 = f32[320,128]{1,0:T(8,128)S(1)} collective-permute-done((f32[320,128]{1,0:T(8,128)S(1)}, f32[320,128]{1,0:T(8,128)S(1)}, u32[]{:S(2)}, u32[]{:S(2)}) %collective-permute-start.14) | collective-permute-done | bytes 163872 | tf_op jit(solution)/shard_map/ppermute | solution.py:33
  112.8 0.7 collective-permute-done.16
  113.5 1.4 %collective-permute-done.15 = f32[320,128]{1,0:T(8,128)S(1)} collective-permute-done((f32[320,128]{1,0:T(8,128)S(1)}, f32[320,128]{1,0:T(8,128)S(1)}, u32[]{:S(2)}, u32[]{:S(2)}) %collective-permute-start.15) | collective-permute-done | bytes 163872 | tf_op jit(solution)/shard_map/ppermute | solution.py:33
  114.9 0.2 collective-permute-start.17
  115.1 1.0 collective-permute-done.21
  116.1 3.3 %collective-permute-done.17 = f32[160,128]{1,0:T(8,128)S(1)} collective-permute-done((f32[160,128]{1,0:T(8,128)S(1)}, f32[160,128]{1,0:T(8,128)S(1)}, u32[]{:S(2)}, u32[]{:S(2)}) %collective-permute-start.17) | collective-permute-done | bytes 81952 | tf_op jit(solution)/shard_map/ppermute | solution.py:33
  119.5 0.7 fusion.3
  (39 shorter events, 0.3 us)
Async XLA Ops:
  1.2 1.0 copy-start.4
  37.0 26.3 %copy-start.5 = (bf16[2,160,1152]{2,1,0:T(8,128)(2,1)}, bf16[2,160,1152]{2,1,0:T(8,128)(2,1)S(1)}, u32[]{:S(2)}) copy-start(bf16[2,160,1152]{2,1,0:T(8,128)(2,1)S(1)} %get-tuple-element.18.refs_10_) | copy-start | bytes 2211844
  37.0 26.3 %copy-start.6 = (bf16[2,160,1152]{2,1,0:T(8,128)(2,1)}, bf16[2,160,1152]{2,1,0:T(8,128)(2,1)S(1)}, u32[]{:S(2)}) copy-start(bf16[2,160,1152]{2,1,0:T(8,128)(2,1)S(1)} %get-tuple-element.17.refs_0_) | copy-start | bytes 2211844
  37.0 17.9 %collective-permute-start.4 = (bf16[2,160,1152]{2,1,0:T(8,128)(2,1)S(1)}, bf16[2,160,1152]{2,1,0:T(8,128)(2,1)S(1)}, u32[]{:S(2)}, u32[]{:S(2)}) collective-permute-start(bf16[2,160,1152]{2,1,0:T(8,128)(2,1)S(1)} %get-tuple-element.18.refs_10_), channel_id=1, source_target_pairs={{0,96},{1,97},{2,98},{3,99},{4,100},{5,101},{6,102},{7,103},{8,104... | collective-permute-start | bytes 2211848 | tf_op jit(solution)/shard_map/ppermute | solution.py:33
  37.9 19.1 %collective-permute-start.3 = (bf16[2,160,1152]{2,1,0:T(8,128)(2,1)S(1)}, bf16[2,160,1152]{2,1,0:T(8,128)(2,1)S(1)}, u32[]{:S(2)}, u32[]{:S(2)}) collective-permute-start(bf16[2,160,1152]{2,1,0:T(8,128)(2,1)S(1)} %get-tuple-element.18.refs_10_), channel_id=1, source_target_pairs={{0,32},{1,33},{2,34},{3,35},{4,36},{5,37},{6,38},{7,39},{8,40},{9,... | collective-permute-start | bytes 2211848 | tf_op jit(solution)/shard_map/ppermute | solution.py:33
  39.1 32.7 %copy-start.7 = (s32[1,16,8,1]{1,3,2,0:T(1,128)S(1)}, s32[1,16,8,1]{1,3,2,0:T(1,128)}, u32[]{:S(2)}) copy-start(s32[1,16,8,1]{1,3,2,0:T(1,128)} %param.7) | copy-start | bytes 1540
  39.1 18.5 %collective-permute-start.5 = (bf16[2,160,1152]{2,1,0:T(8,128)(2,1)S(1)}, bf16[2,160,1152]{2,1,0:T(8,128)(2,1)S(1)}, u32[]{:S(2)}, u32[]{:S(2)}) collective-permute-start(bf16[2,160,1152]{2,1,0:T(8,128)(2,1)S(1)} %get-tuple-element.17.refs_0_), channel_id=1, source_target_pairs={{0,4},{1,5},{2,6},{3,7},{4,8},{5,9},{6,10},{7,11},{8,12},{9,13},{1... | collective-permute-start | bytes 2211848 | tf_op jit(solution)/shard_map/ppermute | solution.py:33
  39.1 18.5 %collective-permute-start.1 = (bf16[2,160,1152]{2,1,0:T(8,128)(2,1)S(1)}, bf16[2,160,1152]{2,1,0:T(8,128)(2,1)S(1)}, u32[]{:S(2)}, u32[]{:S(2)}) collective-permute-start(bf16[2,160,1152]{2,1,0:T(8,128)(2,1)S(1)} %get-tuple-element.17.refs_0_), channel_id=1, source_target_pairs={{0,12},{1,13},{2,14},{3,15},{4,0},{5,1},{6,2},{7,3},{8,4},{9,5},{1... | collective-permute-start | bytes 2211848 | tf_op jit(solution)/shard_map/ppermute | solution.py:33
  42.3 20.3 %collective-permute-start = (bf16[2,160,1152]{2,1,0:T(8,128)(2,1)S(1)}, bf16[2,160,1152]{2,1,0:T(8,128)(2,1)S(1)}, u32[]{:S(2)}, u32[]{:S(2)}) collective-permute-start(bf16[2,160,1152]{2,1,0:T(8,128)(2,1)S(1)} %get-tuple-element.17.refs_0_), channel_id=1, source_target_pairs={{0,1},{1,0},{2,3},{3,2},{4,5},{5,4},{6,7},{7,6},{8,9},{9,8},{10,11... | collective-permute-start | bytes 2211848 | tf_op jit(solution)/shard_map/ppermute | solution.py:33
  54.9 3.9 %copy-start = (bf16[2,160,1152]{2,1,0:T(8,128)(2,1)}, bf16[2,160,1152]{2,1,0:T(8,128)(2,1)S(1)}, u32[]{:S(2)}) copy-start(bf16[2,160,1152]{2,1,0:T(8,128)(2,1)S(1)} %collective-permute-done.4.refs_1_.refs_11_) | copy-start | bytes 2211844
  57.0 1.8 %copy-start.1 = (bf16[2,160,1152]{2,1,0:T(8,128)(2,1)}, bf16[2,160,1152]{2,1,0:T(8,128)(2,1)S(1)}, u32[]{:S(2)}) copy-start(bf16[2,160,1152]{2,1,0:T(8,128)(2,1)S(1)} %collective-permute-done.3.refs_0_.refs_12_) | copy-start | bytes 2211844
  57.6 5.1 %copy-start.2 = (bf16[2,160,1152]{2,1,0:T(8,128)(2,1)}, bf16[2,160,1152]{2,1,0:T(8,128)(2,1)S(1)}, u32[]{:S(2)}) copy-start(bf16[2,160,1152]{2,1,0:T(8,128)(2,1)S(1)} %collective-permute-done.5.refs_2_.refs_8_) | copy-start | bytes 2211844
  57.6 5.1 %copy-start.3 = (bf16[2,160,1152]{2,1,0:T(8,128)(2,1)}, bf16[2,160,1152]{2,1,0:T(8,128)(2,1)S(1)}, u32[]{:S(2)}) copy-start(bf16[2,160,1152]{2,1,0:T(8,128)(2,1)S(1)} %collective-permute-done.1.refs_3_.refs_2_) | copy-start | bytes 2211844
  58.8 9.9 %collective-permute-start.6 = (bf16[160,1152]{1,0:T(8,128)(2,1)}, bf16[160,1152]{1,0:T(8,128)(2,1)S(1)}, u32[]{:S(2)}, u32[]{:S(2)}) collective-permute-start(bf16[160,1152]{1,0:T(8,128)(2,1)} %get-tuple-element.19), channel_id=1, source_target_pairs={{0,4},{1,5},{2,6},{3,7},{4,8},{5,9},{6,10},{7,11},{8,12},{9,13},{1... | collective-permute-start | bytes 1105928 | tf_op jit(solution)/shard_map/ppermute | solution.py:33
  58.8 12.5 %collective-permute-start.7 = (bf16[160,1152]{1,0:T(8,128)(2,1)}, bf16[160,1152]{1,0:T(8,128)(2,1)S(1)}, u32[]{:S(2)}, u32[]{:S(2)}) collective-permute-start(bf16[160,1152]{1,0:T(8,128)(2,1)} %get-tuple-element.20), channel_id=1, source_target_pairs={{0,12},{1,13},{2,14},{3,15},{4,0},{5,1},{6,2},{7,3},{8,4},{9,5},{1... | collective-permute-start | bytes 1105928 | tf_op jit(solution)/shard_map/ppermute | solution.py:33
  62.0 9.5 %collective-permute-start.11 = (bf16[160,1152]{1,0:T(8,128)(2,1)}, bf16[160,1152]{1,0:T(8,128)(2,1)}, u32[]{:S(2)}, u32[]{:S(2)}) collective-permute-start(bf16[160,1152]{1,0:T(8,128)(2,1)} %get-tuple-element.21), channel_id=1, source_target_pairs={{0,32},{1,33},{2,34},{3,35},{4,36},{5,37},{6,38},{7,39},{8,40},{9,... | collective-permute-start | bytes 1105928 | tf_op jit(solution)/shard_map/ppermute | solution.py:33
  62.7 14.0 %collective-permute-start.10 = (bf16[2,160,1152]{2,1,0:T(8,128)(2,1)S(1)}, bf16[2,160,1152]{2,1,0:T(8,128)(2,1)}, u32[]{:S(2)}, u32[]{:S(2)}) collective-permute-start(bf16[2,160,1152]{2,1,0:T(8,128)(2,1)S(1)} %collective-permute-done.5.refs_2_.refs_8_), channel_id=1, source_target_pairs={{0,1},{1,0},{2,3},{3,2},{4,5},{5,4},{6,7},{7,6},{8,9},{9,8},{10,11... | collective-permute-start | bytes 2211848 | tf_op jit(solution)/shard_map/ppermute | solution.py:33
  62.7 0.9 copy-start.8
  62.7 14.0 %collective-permute-start.2 = (bf16[2,160,1152]{2,1,0:T(8,128)(2,1)S(1)}, bf16[2,160,1152]{2,1,0:T(8,128)(2,1)}, u32[]{:S(2)}, u32[]{:S(2)}) collective-permute-start(bf16[2,160,1152]{2,1,0:T(8,128)(2,1)S(1)} %collective-permute-done.1.refs_3_.refs_2_), channel_id=1, source_target_pairs={{0,1},{1,0},{2,3},{3,2},{4,5},{5,4},{6,7},{7,6},{8,9},{9,8},{10,11... | collective-permute-start | bytes 2211848 | tf_op jit(solution)/shard_map/ppermute | solution.py:33
  68.7 7.9 %collective-permute-start.12 = (bf16[160,1152]{1,0:T(8,128)(2,1)S(1)}, bf16[160,1152]{1,0:T(8,128)(2,1)}, u32[]{:S(2)}, u32[]{:S(2)}) collective-permute-start(bf16[160,1152]{1,0:T(8,128)(2,1)S(1)} %get-tuple-element.22), channel_id=1, source_target_pairs={{0,96},{1,97},{2,98},{3,99},{4,100},{5,101},{6,102},{7,103},{8,104... | collective-permute-start | bytes 1105928 | tf_op jit(solution)/shard_map/ppermute | solution.py:33
  71.3 5.4 %collective-permute-start.8 = (bf16[160,1152]{1,0:T(8,128)(2,1)S(1)}, bf16[160,1152]{1,0:T(8,128)(2,1)S(1)}, u32[]{:S(2)}, u32[]{:S(2)}) collective-permute-start(bf16[160,1152]{1,0:T(8,128)(2,1)S(1)} %collective-permute-done.6.refs_4_), channel_id=1, source_target_pairs={{0,1},{1,0},{2,3},{3,2},{4,5},{5,4},{6,7},{7,6},{8,9},{9,8},{10,11... | collective-permute-start | bytes 1105928 | tf_op jit(solution)/shard_map/ppermute | solution.py:33
  71.5 5.2 %collective-permute-start.9 = (bf16[160,1152]{1,0:T(8,128)(2,1)S(1)}, bf16[160,1152]{1,0:T(8,128)(2,1)}, u32[]{:S(2)}, u32[]{:S(2)}) collective-permute-start(bf16[160,1152]{1,0:T(8,128)(2,1)S(1)} %collective-permute-done.7.refs_5_), channel_id=1, source_target_pairs={{0,1},{1,0},{2,3},{3,2},{4,5},{5,4},{6,7},{7,6},{8,9},{9,8},{10,11... | collective-permute-start | bytes 1105928 | tf_op jit(solution)/shard_map/ppermute | solution.py:33
  97.2 5.7 %collective-permute-start.13 = (f32[4,320,128]{2,1,0:T(8,128)}, f32[4,320,128]{2,1,0:T(8,128)S(1)}, u32[]{:S(2)}, u32[]{:S(2)}) collective-permute-start(f32[4,320,128]{2,1,0:T(8,128)} %get-tuple-element.24), channel_id=1, source_target_pairs={{0,1},{1,0},{2,3},{3,2},{4,5},{5,4},{6,7},{7,6},{8,9},{9,8},{10,11... | collective-permute-start | bytes 1966088 | tf_op jit(solution)/shard_map/ppermute | solution.py:33
  97.2 9.0 %collective-permute-start.18 = (f32[320,128]{1,0:T(8,128)S(1)}, f32[320,128]{1,0:T(8,128)S(1)}, u32[]{:S(2)}, u32[]{:S(2)}) collective-permute-start(f32[320,128]{1,0:T(8,128)S(1)} %get-tuple-element.26), channel_id=1, source_target_pairs={{0,64},{1,65},{2,66},{3,67},{4,68},{5,69},{6,70},{7,71},{8,72},{9,... | collective-permute-start | bytes 491528 | tf_op jit(solution)/shard_map/ppermute | solution.py:33
  99.6 9.2 %collective-permute-start.19 = (f32[320,128]{1,0:T(8,128)S(1)}, f32[320,128]{1,0:T(8,128)S(1)}, u32[]{:S(2)}, u32[]{:S(2)}) collective-permute-start(f32[320,128]{1,0:T(8,128)S(1)} %get-tuple-element.27), channel_id=1, source_target_pairs={{0,32},{1,33},{2,34},{3,35},{4,36},{5,37},{6,38},{7,39},{8,40},{9,... | collective-permute-start | bytes 491528 | tf_op jit(solution)/shard_map/ppermute | solution.py:33
  102.0 8.1 %collective-permute-start.20 = (f32[320,128]{1,0:T(8,128)S(1)}, f32[320,128]{1,0:T(8,128)S(1)}, u32[]{:S(2)}, u32[]{:S(2)}) collective-permute-start(f32[320,128]{1,0:T(8,128)S(1)} %get-tuple-element.28), channel_id=1, source_target_pairs={{0,96},{1,97},{2,98},{3,99},{4,100},{5,101},{6,102},{7,103},{8,104... | collective-permute-start | bytes 491528 | tf_op jit(solution)/shard_map/ppermute | solution.py:33
  104.1 8.7 %collective-permute-start.14 = (f32[320,128]{1,0:T(8,128)S(1)}, f32[320,128]{1,0:T(8,128)S(1)}, u32[]{:S(2)}, u32[]{:S(2)}) collective-permute-start(f32[320,128]{1,0:T(8,128)S(1)} %get-tuple-element.29), channel_id=1, source_target_pairs={{0,8},{1,9},{2,10},{3,11},{4,12},{5,13},{6,14},{7,15},{8,0},{9,1},... | collective-permute-start | bytes 491528 | tf_op jit(solution)/shard_map/ppermute | solution.py:33
  104.5 9.0 %collective-permute-start.16 = (f32[320,128]{1,0:T(8,128)S(1)}, f32[320,128]{1,0:T(8,128)S(1)}, u32[]{:S(2)}, u32[]{:S(2)}) collective-permute-start(f32[320,128]{1,0:T(8,128)S(1)} %get-tuple-element.30), channel_id=1, source_target_pairs={{0,12},{1,13},{2,14},{3,15},{4,0},{5,1},{6,2},{7,3},{8,4},{9,5},{1... | collective-permute-start | bytes 491528 | tf_op jit(solution)/shard_map/ppermute | solution.py:33
  106.3 8.6 %collective-permute-start.15 = (f32[320,128]{1,0:T(8,128)S(1)}, f32[320,128]{1,0:T(8,128)S(1)}, u32[]{:S(2)}, u32[]{:S(2)}) collective-permute-start(f32[320,128]{1,0:T(8,128)S(1)} %get-tuple-element.31), channel_id=1, source_target_pairs={{0,4},{1,5},{2,6},{3,7},{4,8},{5,9},{6,10},{7,11},{8,12},{9,13},{1... | collective-permute-start | bytes 491528 | tf_op jit(solution)/shard_map/ppermute | solution.py:33
  110.1 6.0 %collective-permute-start.21 = (f32[160,128]{1,0:T(8,128)S(1)}, f32[160,128]{1,0:T(8,128)S(1)}, u32[]{:S(2)}, u32[]{:S(2)}) collective-permute-start(f32[160,128]{1,0:T(8,128)S(1)} %slice.39), channel_id=1, source_target_pairs={{0,16},{1,17},{2,18},{3,19},{4,20},{5,21},{6,22},{7,23},{8,24},{9,... | collective-permute-start | bytes 245768 | tf_op jit(solution)/shard_map/ppermute | solution.py:33
  114.9 4.5 %collective-permute-start.17 = (f32[160,128]{1,0:T(8,128)S(1)}, f32[160,128]{1,0:T(8,128)S(1)}, u32[]{:S(2)}, u32[]{:S(2)}) collective-permute-start(f32[160,128]{1,0:T(8,128)S(1)} %slice.37), channel_id=1, source_target_pairs={{0,2},{1,3},{2,0},{3,1},{4,6},{5,7},{6,4},{7,5},{8,10},{9,11},{10,... | collective-permute-start | bytes 245768 | tf_op jit(solution)/shard_map/ppermute | solution.py:33

commit v9 on v8

--- a/solution.py
+++ b/solution.py
@@ -1,3 +1,4 @@
+import functools
 import itertools
 
 import jax
@@ -96,22 +97,26 @@
 
 
 def cut_kernel(*refs):
-    for i, (pair, out) in enumerate(zip(refs[:4], refs[4:])):
+    for i, (pair, out) in enumerate(zip(refs[:2], refs[2:])):
         out[...] = pair[i % 2]
 
 
 def cut(*pairs):
     return pl.pallas_call(
         cut_kernel,
-        out_shape=[jax.ShapeDtypeStruct((FB, WIDE), BF)] * 4,
+        out_shape=[jax.ShapeDtypeStruct((FB, WIDE), BF)] * 2,
         compiler_params=pltpu.CompilerParams(vmem_limit_bytes=16 * 2**20),
         name="cut",
     )(*pairs)
 
 
-def tile_kernel(me, *refs):
-    row_refs, col_refs, (kern, owned, mirrored), refs = refs[:10], refs[10:15], refs[15:18], refs[18:]
-    row_own, row_other, c0, c1, c2, c3, cols, rows, stored, col_sum, sems = refs
+def tile_kernel(z_steps, me, *refs):
+    tiles, last = len(z_steps), len(z_steps) == 1
+    row_refs, refs = refs[: 2 * tiles], refs[2 * tiles :]
+    col_refs, (kern, owned, mirrored), refs = refs[:5], refs[5:8], refs[8:]
+    if last:
+        (near_own, near_other, col_in), refs = refs[:3], refs[3:]
+    row_own, row_other, *col_outs, cols, rows, stored, col_sum, sems = refs
     y, xh, z, xl, k = (me[i] for i in range(5))
     count = [0]
 
@@ -125,13 +130,10 @@
         return lax.rem(y + y_step, 4) * 2 + lax.rem(xh + side, 2)
 
     def place(t, b):
-        return lax.rem(z + t, 4), lax.rem(xl + b % 2, 2), lax.rem(k + b // 2, 2)
+        return lax.rem(z + z_steps[t], 4), lax.rem(xl + b % 2, 2), lax.rem(k + b // 2, 2)
 
     def row_copies(t):
-        if t == 2:
-            return [start(row_refs[4 + b], rows.at[t, b]) for b in range(4)]
-        at = (0, 2, 0, 8)[t]
-        return [start(row_refs[at + b], rows.at[t, pl.ds(2 * b, 2)]) for b in range(2)]
+        return [start(row_refs[2 * t + b], rows.at[t, pl.ds(2 * b, 2)]) for b in range(2)]
 
     def kern_copies(t):
         return [start(kern.at[place(t, b)], stored.at[t % 2, b]) for b in range(4)]
@@ -139,16 +141,22 @@
     first_copies = [start(col_refs[i].at[b], cols.at[block(step, b)]) for i, step in enumerate((0, 1, 3)) for b in (0, 1)]
     first_copies += [start(col_refs[3 + b], cols.at[block(2, b)]) for b in (0, 1)] + row_copies(0)
     next_rows, next_kern = [], kern_copies(0)
-    col_sum[...] = jnp.zeros_like(col_sum)
+    if last:
+        col_sum[...] = col_in[...]
+        for i, at in enumerate((0, 1, 3)):
+            row_own[at] = near_own[i]
+            row_other[at] = near_other[i]
+    else:
+        col_sum[...] = jnp.zeros_like(col_sum)
     for copy in first_copies:
         copy.wait()
     col_wide = cols[...].reshape(COL_PTS, WIDE)
 
-    for t in range(4):
+    for t in range(tiles):
         for copy in next_rows:
             copy.wait()
         kern_here = next_kern
-        if t < 3:
+        if t + 1 < tiles:
             next_rows, next_kern = row_copies(t + 1), kern_copies(t + 1)
         row_wide = rows[t].reshape(TILE, WIDE)
         if t > 0:
@@ -174,38 +182,53 @@
         high = weighted.astype(BF)
         low = (weighted - high.astype(F32)).astype(BF)
         row_sum = nn(high, col_wide[:, NB:]) + nn(low, col_wide[:, NB:])
-        if t == 0:
+        if z_steps[t] == 0:
             keep = spread(mirrored).astype(BF)
             high, low = high * keep, low * keep
         added = tn(high, row_wide[:, NB:]) + tn(low, row_wide[:, NB:])
         col_sum[...] += added.reshape(col_sum.shape)
-        row_own[t] = row_sum[: 2 * FB]
-        row_other[t] = row_sum[2 * FB :]
-
-    for step, col_out in enumerate((c0, c1, c2, c3)):
-        for side in (0, 1):
-            col_out[side * FB : (side + 1) * FB, :] = col_sum[block(step, side)]
-
-
-def tile_call(me, row_parts, col_parts, kern, owned, mirrored):
+        at = 2 if last else t
+        row_own[at] = row_sum[: 2 * FB]
+        row_other[at] = row_sum[2 * FB :]
+
+    if last:
+        for step, col_out in enumerate(col_outs):
+            for side in (0, 1):
+                col_out[side * FB : (side + 1) * FB, :] = col_sum[block(step, side)]
+    else:
+        col_outs[0][...] = col_sum[...]
+
+
+def tile_call(z_steps, me, row_parts, col_parts, kern, owned, mirrored, *before):
+    tiles = len(z_steps)
     vmem = pl.BlockSpec(memory_space=pltpu.VMEM)
     hbm = pl.BlockSpec(memory_space=pltpu.HBM)
-    return pl.pallas_call(
-        tile_kernel,
-        in_specs=[pl.BlockSpec(memory_space=pltpu.SMEM)] + [hbm] * 16 + [vmem] * 2,
-        out_specs=[vmem] * 6,
-        out_shape=[jax.ShapeDtypeStruct((4, 2 * FB, NT), F32)] * 2 + [jax.ShapeDtypeStruct((2 * FB, NT), F32)] * 4,
+    places = 4 if before else tiles
+    out_shape = [jax.ShapeDtypeStruct((places, 2 * FB, NT), F32)] * 2
+    if before:
+        out_shape += [jax.ShapeDtypeStruct((2 * FB, NT), F32)] * 4
+    else:
+        out_shape += [jax.ShapeDtypeStruct((N_ROW, FB, NT), F32)]
+    return pl.pallas_call(
+        functools.partial(tile_kernel, z_steps),
+        in_specs=[pl.BlockSpec(memory_space=pltpu.SMEM)]
+        + [hbm] * (len(row_parts) + len(col_parts) + 1)
+        + [vmem] * (2 + len(before)),
+        out_specs=[vmem] * len(out_shape),
+        out_shape=out_shape,
         scratch_shapes=[
             pltpu.VMEM((N_ROW, FB, WIDE), BF),
-            pltpu.VMEM((4, 4, FB, WIDE), BF),
-            pltpu.VMEM((2, 4, FB * COL_PTS // 128, 128), F32),
+            pltpu.VMEM((tiles, 4, FB, WIDE), BF),
+            pltpu.VMEM((min(tiles, 2), 4, FB * COL_PTS // 128, 128), F32),
             pltpu.VMEM((N_ROW, FB, NT), F32),
-            pltpu.SemaphoreType.DMA((40,)),
+            pltpu.SemaphoreType.DMA((8 + 6 * tiles,)),
         ],
-        compiler_params=pltpu.CompilerParams(vmem_limit_bytes=52 * 2**20),
-        cost_estimate=pl.CostEstimate(flops=10_000_000_000, bytes_accessed=24_000_000, transcendentals=0),
-        name="tiles",
-    )(me, *row_parts, *col_parts, kern, owned, mirrored)
+        compiler_params=pltpu.CompilerParams(vmem_limit_bytes=48 * 2**20),
+        cost_estimate=pl.CostEstimate(
+            flops=2_600_000_000 * tiles, bytes_accessed=5_000_000 * tiles, transcendentals=0
+        ),
+        name="far_tile" if before else "near_tiles",
+    )(me, *row_parts, *col_parts, kern, owned, mirrored, *before)
 
 
 def local(orbitals, targets, kernel, tile_owner):
@@ -218,12 +241,12 @@
 
     y_down, y_up = send(col_pair, y=1), send(col_pair, y=3)
     z_down, z_up = send(row_pair, z=1), send(row_pair, z=3)
-    parts = cut(y_down, y_up, z_down, z_up)
-    y_far, y_far_side = send(parts[0], y=1), send(parts[1], y=3)
-    z_far, z_far_side = send(parts[2], z=1), send(parts[3], z=3)
+    y_far, y_far_side = cut(y_down, y_up)
+    y_far, y_far_side = send(y_far, y=1), send(y_far_side, y=3)
     col_parts = (col_pair, y_up, y_down, y_far, y_far_side)
-    row_parts = (row_pair, send(row_pair, k=1), z_up, send(z_up, k=1))
-    row_parts += (z_far, z_far_side, send(z_far, k=1), send(z_far_side, k=1), z_down, send(z_down, k=1))
+    up_other = send(z_up, k=1)
+    near_rows = (row_pair, send(row_pair, k=1), z_up, up_other, z_down, send(z_down, k=1))
+    far_rows = (send(z_down, z=1), send(up_other, z=3))
 
     flags = tile_owner.reshape(N_COL, N_ROW).astype(F32)
     here = (lax.broadcasted_iota(jnp.int32, flags.shape, 0) == c) & (
@@ -233,7 +256,9 @@
     mirrored = jnp.repeat(jnp.where(here, 0.0, flags), FB, axis=1).reshape(4, 2, 2, 1, COL_PTS)
     kern = kernel.reshape(4, 2, 2, FB * COL_PTS // 128, 128)
 
-    row_own, row_other, c0, c1, c2, c3 = tile_call(me, row_parts, col_parts, kern, owned, mirrored)
+    masks = (owned, mirrored)
+    near = tile_call((0, 1, 3), me, near_rows, col_parts, kern, *masks)
+    row_own, row_other, c0, c1, c2, c3 = tile_call((2,), me, far_rows, col_parts, kern, *masks, *near)
 
     col_sum = c0 + send(c2, y=2) + send(c1, y=1) + send(c3, y=3)
     row_sum = row_own + send(row_other, k=1)

time: 120 us -> 114 us (0.950)
  waiting for transfers between devices: 36.2 us -> 27.9 us
  local copies, waits for them, and re-layouts: 2.17 us -> 5.38 us
  Pallas kernels: 23.5 us -> 24.9 us
    ppermute x22 -> x20, waiting for transfers between devices: 36.2 us -> 27.9 us  [send(): return lax.ppermute(x, AXES, moved(**steps))]
    unnamed x18 -> x14, local copies, waits for them, and re-layouts: 1.31 us -> 2.96 us
    pallas_call x1 -> x2, Pallas kernels: 20.5 us -> 21.9 us  [tile_call(): pl.pallas_call(functools.partial(tile_kernel, z_steps), in_specs=[pl.Bloc...]
    ppermute x22 -> x20, starting transfers between devices: 22 us -> 20.8 us  [send(): return lax.ppermute(x, AXES, moved(**steps))]
  transfers between devices with their start and end apart: 22 -> 20, of which waited for: 13 -> 10; matrix products, arithmetic and copies ran while one was open for 2% -> 2% of each run, Pallas kernels for 1% -> 14%
where the time goes in v9:
time: 114 us
  blocking collectives  32.9 us (29%)
  waiting for transfers between devices  27.9 us (24%)
  Pallas kernels  24.9 us (22%)
  starting transfers between devices  20.8 us (18%)
  local copies, waits for them, and re-layouts  5.38 us (5%)
  other arithmetic  2 us (2%)
    all_to_all x1, blocking collectives, local(): lax.all_to_all(packed, AXES, split_axis=0, concat_axis=0, tiled=True)  32.9 us
    ppermute x20, waiting for transfers between devices, send(): return lax.ppermute(x, AXES, moved(**steps))  27.9 us
    pallas_call x2, Pallas kernels, tile_call(): pl.pallas_call(functools.partial(tile_kernel, z_steps), in_specs=[pl.Bloc...  21.9 us
    ppermute x20, starting transfers between devices, send(): return lax.ppermute(x, AXES, moved(**steps))  20.8 us
    unnamed x14, local copies, waits for them, and re-layouts  2.96 us
  transfers between devices with their start and end apart: 20, of which 10 were waited for; matrix products, arithmetic and copies ran while one was open for 2% of the time, Pallas kernels for 14%

profile of v9, /device:TPU:0, one launch (start us, length us, event | category | flops | bytes accessed | tf_op | source)
XLA Modules:
  0.0 114.1 jit_solution(7327246649863103481)
XLA Ops:
  0.0 1.1 convert_reduce_fusion
  1.1 0.1 reshape.22.tgt
  1.2 1.0 copy-done.3
  2.2 0.5 pack.1
  2.7 32.9 %all_to_all.5 = bf16[128,8,640]{2,1,0:T(8,128)(2,1)S(1)} all-to-all(bf16[128,8,640]{2,1,0:T(8,128)(2,1)S(1)} %bitcast.28), channel_id=1, replica_groups=mesh['row'=8,'col'=16] {'row','col'}, dimensions={0} | all-to-all | bytes 2621440 | tf_op jit(solution)/shard_map/all_to_all | solution.py:239
  35.6 1.3 %unpack.1 = (bf16[2,160,1152]{2,1,0:T(8,128)(2,1)S(1)}, bf16[2,160,1152]{2,1,0:T(8,128)(2,1)S(1)}) custom-call(bf16[1024,640]{1,0:T(8,128)(2,1)S(1)} %bitcast.27), custom_call_target="tpu_custom_call" | custom-call | tf_op jit(solution)/shard_map/unpack/pallas_call | solution.py:91
  37.0 0.3 collective-permute-start.2
  37.3 1.8 %collective-permute-start = (bf16[2,160,1152]{2,1,0:T(8,128)(2,1)S(1)}, bf16[2,160,1152]{2,1,0:T(8,128)(2,1)}, u32[]{:S(2)}, u32[]{:S(2)}) collective-permute-start(bf16[2,160,1152]{2,1,0:T(8,128)(2,1)S(1)} %get-tuple-element.18.refs_0_), channel_id=1, source_target_pairs={{0,4},{1,5},{2,6},{3,7},{4,8},{5,9},{6,10},{7,11},{8,12},{9,13},{1... | collective-permute-start | bytes 2211848 | tf_op jit(solution)/shard_map/ppermute | solution.py:34
  39.1 0.8 collective-permute-start.5
  39.9 1.2 %collective-permute-start.6 = (bf16[2,160,1152]{2,1,0:T(8,128)(2,1)S(1)}, bf16[2,160,1152]{2,1,0:T(8,128)(2,1)S(1)}, u32[]{:S(2)}, u32[]{:S(2)}) collective-permute-start(bf16[2,160,1152]{2,1,0:T(8,128)(2,1)S(1)} %get-tuple-element.19.refs_6_.refs_2_), channel_id=1, source_target_pairs={{0,32},{1,33},{2,34},{3,35},{4,36},{5,37},{6,38},{7,39},{8,40},{9,... | collective-permute-start | bytes 2211848 | tf_op jit(solution)/shard_map/ppermute | solution.py:34
  41.1 0.9 copy-done.4
  42.0 13.0 %collective-permute-done.2.refs_2_ = bf16[2,160,1152]{2,1,0:T(8,128)(2,1)} collective-permute-done((bf16[2,160,1152]{2,1,0:T(8,128)(2,1)S(1)}, bf16[2,160,1152]{2,1,0:T(8,128)(2,1)}, u32[]{:S(2)}, u32[]{:S(2)}) %collective-permute-start.2) | collective-permute-done | bytes 737312 | tf_op jit(solution)/shard_map/ppermute | solution.py:34
  55.0 1.3 %collective-permute-done.refs_4_ = bf16[2,160,1152]{2,1,0:T(8,128)(2,1)} collective-permute-done((bf16[2,160,1152]{2,1,0:T(8,128)(2,1)S(1)}, bf16[2,160,1152]{2,1,0:T(8,128)(2,1)}, u32[]{:S(2)}, u32[]{:S(2)}) %collective-permute-start) | collective-permute-done | bytes 737312 | tf_op jit(solution)/shard_map/ppermute | solution.py:34
  56.4 2.0 %collective-permute-done.6.refs_0_.refs_8_.refs_4_ = bf16[2,160,1152]{2,1,0:T(8,128)(2,1)S(1)} collective-permute-done((bf16[2,160,1152]{2,1,0:T(8,128)(2,1)S(1)}, bf16[2,160,1152]{2,1,0:T(8,128)(2,1)S(1)}, u32[]{:S(2)}, u32[]{:S(2)}) %collective-permute-start.6) | collective-permute-done | bytes 737312 | tf_op jit(solution)/shard_map/ppermute | solution.py:34
  58.4 1.1 cut.1
  59.5 3.2 %collective-permute-start.8 = (bf16[160,1152]{1,0:T(8,128)(2,1)}, bf16[160,1152]{1,0:T(8,128)(2,1)}, u32[]{:S(2)}, u32[]{:S(2)}) collective-permute-start(bf16[160,1152]{1,0:T(8,128)(2,1)} %get-tuple-element.21), channel_id=1, source_target_pairs={{0,96},{1,97},{2,98},{3,99},{4,100},{5,101},{6,102},{7,103},{8,104... | collective-permute-start | bytes 1105928 | tf_op jit(solution)/shard_map/ppermute | solution.py:34
  62.8 0.1 and_select_fusion
  62.9 0.3 collective-permute-start.1
  63.2 3.0 %collective-permute-start.4 = (bf16[2,160,1152]{2,1,0:T(8,128)(2,1)}, bf16[2,160,1152]{2,1,0:T(8,128)(2,1)}, u32[]{:S(2)}, u32[]{:S(2)}) collective-permute-start(bf16[2,160,1152]{2,1,0:T(8,128)(2,1)} %collective-permute-done.3.refs_3_), channel_id=1, source_target_pairs={{0,12},{1,13},{2,14},{3,15},{4,0},{5,1},{6,2},{7,3},{8,4},{9,5},{1... | collective-permute-start | bytes 2211848 | tf_op jit(solution)/shard_map/ppermute | solution.py:34
  66.1 0.1 copy.10
  66.2 0.1 broadcast_in_dim.12
  66.3 0.2 reshape_reshape.7.refs_13_.refs_9_
  66.4 0.1 copy.9
  66.5 0.7 broadcast_in_dim.10
  67.3 1.1 reshape_reshape.6.refs_12_.refs_8_
  68.4 0.1 stack.23.me
  68.4 1.4 %collective-permute-done.7.refs_9_.refs_5_ = bf16[160,1152]{1,0:T(8,128)(2,1)S(1)} collective-permute-done((bf16[160,1152]{1,0:T(8,128)(2,1)}, bf16[160,1152]{1,0:T(8,128)(2,1)S(1)}, u32[]{:S(2)}, u32[]{:S(2)}) %collective-permute-start.7) | collective-permute-done | bytes 368672 | tf_op jit(solution)/shard_map/ppermute | solution.py:34
  69.9 1.1 copy-done.5
  71.0 14.9 %near_tiles.1 = (f32[3,320,128]{2,1,0:T(8,128)S(1)}, f32[3,320,128]{2,1,0:T(8,128)S(1)}, f32[8,160,128]{2,1,0:T(8,128)S(1)}) custom-call(s32[5]{0:T(128)S(1)} %stack.23.me, bf16[2,160,1152]{2,1,0:T(8,128)(2,1)S(1)} %copy-done.5, bf16[2,160,1152]{2,1,0:T(8,128)(2,1)} %collective-permute-done.9.refs_1_, bf16[2,160,1152]{2,1,0:T(8,128)(2,1)} %collective-permute-done.2.refs_2_, ...), custom_call_target="tpu_custom_call" | custom-call | flops 7800000000 | bytes 15000000 | tf_op jit(solution)/shard_map/near_tiles/pallas_call | solution.py:212
  85.9 7.0 %far_tile.1 = (f32[4,320,128]{2,1,0:T(8,128)S(1)}, f32[4,320,128]{2,1,0:T(8,128)S(1)}, f32[320,128]{1,0:T(8,128)S(1)}, f32[320,128]{1,0:T(8,128)S(1)}, f32[320,128]{1,0:T(8,128)S(1)}, /*index=5*/f32[320,128]{1,0:T(8,128)S(1)}) custom-call(s32[5]{0:T(128)S(1)} %stack.23.me, bf16[2,160,1152]{2,1,0:T(8,128)(2,1)S(1)} %collective-permute-done.1.refs_0_, ...), custom_call_target="tpu_custom_call" | custom-call | flops 2600000000 | bytes 5000000 | tf_op jit(solution)/shard_map/far_tile/pallas_call | solution.py:212
  93.0 0.1 collective-permute-start.11
  93.0 1.6 %collective-permute-start.16 = (f32[320,128]{1,0:T(8,128)S(1)}, f32[320,128]{1,0:T(8,128)S(1)}, u32[]{:S(2)}, u32[]{:S(2)}) collective-permute-start(f32[320,128]{1,0:T(8,128)S(1)} %get-tuple-element.28), channel_id=1, source_target_pairs={{0,64},{1,65},{2,66},{3,67},{4,68},{5,69},{6,70},{7,71},{8,72},{9,... | collective-permute-start | bytes 491528 | tf_op jit(solution)/shard_map/ppermute | solution.py:34
  94.7 2.3 %collective-permute-start.17 = (f32[320,128]{1,0:T(8,128)S(1)}, f32[320,128]{1,0:T(8,128)S(1)}, u32[]{:S(2)}, u32[]{:S(2)}) collective-permute-start(f32[320,128]{1,0:T(8,128)S(1)} %get-tuple-element.29), channel_id=1, source_target_pairs={{0,32},{1,33},{2,34},{3,35},{4,36},{5,37},{6,38},{7,39},{8,40},{9,... | collective-permute-start | bytes 491528 | tf_op jit(solution)/shard_map/ppermute | solution.py:34
  97.0 0.9 collective-permute-start.18
  97.9 0.1 add.46
  98.0 0.9 collective-permute-start.12
  98.9 1.1 collective-permute-start.13
  99.9 1.7 %collective-permute-done.16 = f32[320,128]{1,0:T(8,128)S(1)} collective-permute-done((f32[320,128]{1,0:T(8,128)S(1)}, f32[320,128]{1,0:T(8,128)S(1)}, u32[]{:S(2)}, u32[]{:S(2)}) %collective-permute-start.16) | collective-permute-done | bytes 163872 | tf_op jit(solution)/shard_map/ppermute | solution.py:34
  101.7 0.9 collective-permute-start.14
  102.6 2.1 %collective-permute-done.17 = f32[320,128]{1,0:T(8,128)S(1)} collective-permute-done((f32[320,128]{1,0:T(8,128)S(1)}, f32[320,128]{1,0:T(8,128)S(1)}, u32[]{:S(2)}, u32[]{:S(2)}) %collective-permute-start.17) | collective-permute-done | bytes 163872 | tf_op jit(solution)/shard_map/ppermute | solution.py:34
  104.7 0.4 collective-permute-done.18
  105.1 0.1 add_add_fusion
  105.1 1.9 %collective-permute-start.19 = (f32[160,128]{1,0:T(8,128)S(1)}, f32[160,128]{1,0:T(8,128)S(1)}, u32[]{:S(2)}, u32[]{:S(2)}) collective-permute-start(f32[160,128]{1,0:T(8,128)S(1)} %slice.39), channel_id=1, source_target_pairs={{0,16},{1,17},{2,18},{3,19},{4,20},{5,21},{6,22},{7,23},{8,24},{9,... | collective-permute-start | bytes 245768 | tf_op jit(solution)/shard_map/ppermute | solution.py:34
  107.0 1.8 %collective-permute-done.13 = f32[320,128]{1,0:T(8,128)S(1)} collective-permute-done((f32[320,128]{1,0:T(8,128)S(1)}, f32[320,128]{1,0:T(8,128)S(1)}, u32[]{:S(2)}, u32[]{:S(2)}) %collective-permute-start.13) | collective-permute-done | bytes 163872 | tf_op jit(solution)/shard_map/ppermute | solution.py:34
  108.9 0.5 collective-permute-start.15
  109.4 1.7 %collective-permute-done.19 = f32[160,128]{1,0:T(8,128)S(1)} collective-permute-done((f32[160,128]{1,0:T(8,128)S(1)}, f32[160,128]{1,0:T(8,128)S(1)}, u32[]{:S(2)}, u32[]{:S(2)}) %collective-permute-start.19) | collective-permute-done | bytes 81952 | tf_op jit(solution)/shard_map/ppermute | solution.py:34
  111.2 2.2 %collective-permute-done.15 = f32[160,128]{1,0:T(8,128)S(1)} collective-permute-done((f32[160,128]{1,0:T(8,128)S(1)}, f32[160,128]{1,0:T(8,128)S(1)}, u32[]{:S(2)}, u32[]{:S(2)}) %collective-permute-start.15) | collective-permute-done | bytes 81952 | tf_op jit(solution)/shard_map/ppermute | solution.py:34
  113.4 0.7 fusion.3
  (32 shorter events, 0.2 us)
Async XLA Ops:
  1.2 1.0 copy-start.3
  35.6 27.1 %copy-start.6 = (s32[1,16,8,1]{1,3,2,0:T(1,128)S(1)}, s32[1,16,8,1]{1,3,2,0:T(1,128)}, u32[]{:S(2)}) copy-start(s32[1,16,8,1]{1,3,2,0:T(1,128)} %param.7) | copy-start | bytes 1540
  37.0 32.9 %copy-start.2 = (bf16[2,160,1152]{2,1,0:T(8,128)(2,1)}, bf16[2,160,1152]{2,1,0:T(8,128)(2,1)S(1)}, u32[]{:S(2)}) copy-start(bf16[2,160,1152]{2,1,0:T(8,128)(2,1)S(1)} %get-tuple-element.19.refs_6_.refs_2_) | copy-start | bytes 2211844
  37.0 18.0 %collective-permute-start.2 = (bf16[2,160,1152]{2,1,0:T(8,128)(2,1)S(1)}, bf16[2,160,1152]{2,1,0:T(8,128)(2,1)}, u32[]{:S(2)}, u32[]{:S(2)}) collective-permute-start(bf16[2,160,1152]{2,1,0:T(8,128)(2,1)S(1)} %get-tuple-element.18.refs_0_), channel_id=1, source_target_pairs={{0,12},{1,13},{2,14},{3,15},{4,0},{5,1},{6,2},{7,3},{8,4},{9,5},{1... | collective-permute-start | bytes 2211848 | tf_op jit(solution)/shard_map/ppermute | solution.py:34
  37.3 19.0 %collective-permute-start = (bf16[2,160,1152]{2,1,0:T(8,128)(2,1)S(1)}, bf16[2,160,1152]{2,1,0:T(8,128)(2,1)}, u32[]{:S(2)}, u32[]{:S(2)}) collective-permute-start(bf16[2,160,1152]{2,1,0:T(8,128)(2,1)S(1)} %get-tuple-element.18.refs_0_), channel_id=1, source_target_pairs={{0,4},{1,5},{2,6},{3,7},{4,8},{5,9},{6,10},{7,11},{8,12},{9,13},{1... | collective-permute-start | bytes 2211848 | tf_op jit(solution)/shard_map/ppermute | solution.py:34
  39.1 17.3 %collective-permute-start.5 = (bf16[2,160,1152]{2,1,0:T(8,128)(2,1)S(1)}, bf16[2,160,1152]{2,1,0:T(8,128)(2,1)S(1)}, u32[]{:S(2)}, u32[]{:S(2)}) collective-permute-start(bf16[2,160,1152]{2,1,0:T(8,128)(2,1)S(1)} %get-tuple-element.19.refs_6_.refs_2_), channel_id=1, source_target_pairs={{0,96},{1,97},{2,98},{3,99},{4,100},{5,101},{6,102},{7,103},{8,104... | collective-permute-start | bytes 2211848 | tf_op jit(solution)/shard_map/ppermute | solution.py:34
  39.9 18.5 %collective-permute-start.6 = (bf16[2,160,1152]{2,1,0:T(8,128)(2,1)S(1)}, bf16[2,160,1152]{2,1,0:T(8,128)(2,1)S(1)}, u32[]{:S(2)}, u32[]{:S(2)}) collective-permute-start(bf16[2,160,1152]{2,1,0:T(8,128)(2,1)S(1)} %get-tuple-element.19.refs_6_.refs_2_), channel_id=1, source_target_pairs={{0,32},{1,33},{2,34},{3,35},{4,36},{5,37},{6,38},{7,39},{8,40},{9,... | collective-permute-start | bytes 2211848 | tf_op jit(solution)/shard_map/ppermute | solution.py:34
  41.1 21.7 %collective-permute-start.9 = (bf16[2,160,1152]{2,1,0:T(8,128)(2,1)S(1)}, bf16[2,160,1152]{2,1,0:T(8,128)(2,1)}, u32[]{:S(2)}, u32[]{:S(2)}) collective-permute-start(bf16[2,160,1152]{2,1,0:T(8,128)(2,1)S(1)} %get-tuple-element.18.refs_0_), channel_id=1, source_target_pairs={{0,1},{1,0},{2,3},{3,2},{4,5},{5,4},{6,7},{7,6},{8,9},{9,8},{10,11... | collective-permute-start | bytes 2211848 | tf_op jit(solution)/shard_map/ppermute | solution.py:34
  41.1 0.9 copy-start.4
  55.0 8.1 %collective-permute-start.3 = (bf16[2,160,1152]{2,1,0:T(8,128)(2,1)}, bf16[2,160,1152]{2,1,0:T(8,128)(2,1)}, u32[]{:S(2)}, u32[]{:S(2)}) collective-permute-start(bf16[2,160,1152]{2,1,0:T(8,128)(2,1)} %collective-permute-done.2.refs_2_), channel_id=1, source_target_pairs={{0,1},{1,0},{2,3},{3,2},{4,5},{5,4},{6,7},{7,6},{8,9},{9,8},{10,11... | collective-permute-start | bytes 2211848 | tf_op jit(solution)/shard_map/ppermute | solution.py:34
  56.3 13.6 %collective-permute-start.10 = (bf16[2,160,1152]{2,1,0:T(8,128)(2,1)}, bf16[2,160,1152]{2,1,0:T(8,128)(2,1)}, u32[]{:S(2)}, u32[]{:S(2)}) collective-permute-start(bf16[2,160,1152]{2,1,0:T(8,128)(2,1)} %collective-permute-done.refs_4_), channel_id=1, source_target_pairs={{0,1},{1,0},{2,3},{3,2},{4,5},{5,4},{6,7},{7,6},{8,9},{9,8},{10,11... | collective-permute-start | bytes 2211848 | tf_op jit(solution)/shard_map/ppermute | solution.py:34
  56.4 13.5 %copy-start = (bf16[2,160,1152]{2,1,0:T(8,128)(2,1)}, bf16[2,160,1152]{2,1,0:T(8,128)(2,1)S(1)}, u32[]{:S(2)}) copy-start(bf16[2,160,1152]{2,1,0:T(8,128)(2,1)S(1)} %collective-permute-done.5.refs_1_.refs_7_.refs_3_) | copy-start | bytes 2211844
  58.4 11.5 %copy-start.1 = (bf16[2,160,1152]{2,1,0:T(8,128)(2,1)}, bf16[2,160,1152]{2,1,0:T(8,128)(2,1)S(1)}, u32[]{:S(2)}) copy-start(bf16[2,160,1152]{2,1,0:T(8,128)(2,1)S(1)} %collective-permute-done.6.refs_0_.refs_8_.refs_4_) | copy-start | bytes 2211844
  59.5 10.3 %collective-permute-start.7 = (bf16[160,1152]{1,0:T(8,128)(2,1)}, bf16[160,1152]{1,0:T(8,128)(2,1)S(1)}, u32[]{:S(2)}, u32[]{:S(2)}) collective-permute-start(bf16[160,1152]{1,0:T(8,128)(2,1)} %get-tuple-element.20), channel_id=1, source_target_pairs={{0,32},{1,33},{2,34},{3,35},{4,36},{5,37},{6,38},{7,39},{8,40},{9,... | collective-permute-start | bytes 1105928 | tf_op jit(solution)/shard_map/ppermute | solution.py:34
  59.5 10.3 %collective-permute-start.8 = (bf16[160,1152]{1,0:T(8,128)(2,1)}, bf16[160,1152]{1,0:T(8,128)(2,1)}, u32[]{:S(2)}, u32[]{:S(2)}) collective-permute-start(bf16[160,1152]{1,0:T(8,128)(2,1)} %get-tuple-element.21), channel_id=1, source_target_pairs={{0,96},{1,97},{2,98},{3,99},{4,100},{5,101},{6,102},{7,103},{8,104... | collective-permute-start | bytes 1105928 | tf_op jit(solution)/shard_map/ppermute | solution.py:34
  62.9 23.1 %collective-permute-start.1 = (bf16[2,160,1152]{2,1,0:T(8,128)(2,1)}, bf16[2,160,1152]{2,1,0:T(8,128)(2,1)S(1)}, u32[]{:S(2)}, u32[]{:S(2)}) collective-permute-start(bf16[2,160,1152]{2,1,0:T(8,128)(2,1)} %collective-permute-done.refs_4_), channel_id=1, source_target_pairs={{0,4},{1,5},{2,6},{3,7},{4,8},{5,9},{6,10},{7,11},{8,12},{9,13},{1... | collective-permute-start | bytes 2211848 | tf_op jit(solution)/shard_map/ppermute | solution.py:34
  63.2 22.8 %collective-permute-start.4 = (bf16[2,160,1152]{2,1,0:T(8,128)(2,1)}, bf16[2,160,1152]{2,1,0:T(8,128)(2,1)}, u32[]{:S(2)}, u32[]{:S(2)}) collective-permute-start(bf16[2,160,1152]{2,1,0:T(8,128)(2,1)} %collective-permute-done.3.refs_3_), channel_id=1, source_target_pairs={{0,12},{1,13},{2,14},{3,15},{4,0},{5,1},{6,2},{7,3},{8,4},{9,5},{1... | collective-permute-start | bytes 2211848 | tf_op jit(solution)/shard_map/ppermute | solution.py:34
  69.9 1.1 copy-start.5
  93.0 5.0 %collective-permute-start.11 = (f32[4,320,128]{2,1,0:T(8,128)S(1)}, f32[4,320,128]{2,1,0:T(8,128)S(1)}, u32[]{:S(2)}, u32[]{:S(2)}) collective-permute-start(f32[4,320,128]{2,1,0:T(8,128)S(1)} %get-tuple-element.26), channel_id=1, source_target_pairs={{0,1},{1,0},{2,3},{3,2},{4,5},{5,4},{6,7},{7,6},{8,9},{9,8},{10,11... | collective-permute-start | bytes 1966088 | tf_op jit(solution)/shard_map/ppermute | solution.py:34
  93.0 8.6 %collective-permute-start.16 = (f32[320,128]{1,0:T(8,128)S(1)}, f32[320,128]{1,0:T(8,128)S(1)}, u32[]{:S(2)}, u32[]{:S(2)}) collective-permute-start(f32[320,128]{1,0:T(8,128)S(1)} %get-tuple-element.28), channel_id=1, source_target_pairs={{0,64},{1,65},{2,66},{3,67},{4,68},{5,69},{6,70},{7,71},{8,72},{9,... | collective-permute-start | bytes 491528 | tf_op jit(solution)/shard_map/ppermute | solution.py:34
  94.7 10.0 %collective-permute-start.17 = (f32[320,128]{1,0:T(8,128)S(1)}, f32[320,128]{1,0:T(8,128)S(1)}, u32[]{:S(2)}, u32[]{:S(2)}) collective-permute-start(f32[320,128]{1,0:T(8,128)S(1)} %get-tuple-element.29), channel_id=1, source_target_pairs={{0,32},{1,33},{2,34},{3,35},{4,36},{5,37},{6,38},{7,39},{8,40},{9,... | collective-permute-start | bytes 491528 | tf_op jit(solution)/shard_map/ppermute | solution.py:34
  97.0 8.1 %collective-permute-start.18 = (f32[320,128]{1,0:T(8,128)S(1)}, f32[320,128]{1,0:T(8,128)S(1)}, u32[]{:S(2)}, u32[]{:S(2)}) collective-permute-start(f32[320,128]{1,0:T(8,128)S(1)} %get-tuple-element.30), channel_id=1, source_target_pairs={{0,96},{1,97},{2,98},{3,99},{4,100},{5,101},{6,102},{7,103},{8,104... | collective-permute-start | bytes 491528 | tf_op jit(solution)/shard_map/ppermute | solution.py:34
  98.0 9.0 %collective-permute-start.12 = (f32[320,128]{1,0:T(8,128)S(1)}, f32[320,128]{1,0:T(8,128)S(1)}, u32[]{:S(2)}, u32[]{:S(2)}) collective-permute-start(f32[320,128]{1,0:T(8,128)S(1)} %get-tuple-element.31), channel_id=1, source_target_pairs={{0,8},{1,9},{2,10},{3,11},{4,12},{5,13},{6,14},{7,15},{8,0},{9,1},... | collective-permute-start | bytes 491528 | tf_op jit(solution)/shard_map/ppermute | solution.py:34
  98.9 9.9 %collective-permute-start.13 = (f32[320,128]{1,0:T(8,128)S(1)}, f32[320,128]{1,0:T(8,128)S(1)}, u32[]{:S(2)}, u32[]{:S(2)}) collective-permute-start(f32[320,128]{1,0:T(8,128)S(1)} %get-tuple-element.33), channel_id=1, source_target_pairs={{0,4},{1,5},{2,6},{3,7},{4,8},{5,9},{6,10},{7,11},{8,12},{9,13},{1... | collective-permute-start | bytes 491528 | tf_op jit(solution)/shard_map/ppermute | solution.py:34
  101.7 7.1 %collective-permute-start.14 = (f32[320,128]{1,0:T(8,128)S(1)}, f32[320,128]{1,0:T(8,128)S(1)}, u32[]{:S(2)}, u32[]{:S(2)}) collective-permute-start(f32[320,128]{1,0:T(8,128)S(1)} %get-tuple-element.32), channel_id=1, source_target_pairs={{0,12},{1,13},{2,14},{3,15},{4,0},{5,1},{6,2},{7,3},{8,4},{9,5},{1... | collective-permute-start | bytes 491528 | tf_op jit(solution)/shard_map/ppermute | solution.py:34
  105.1 6.0 %collective-permute-start.19 = (f32[160,128]{1,0:T(8,128)S(1)}, f32[160,128]{1,0:T(8,128)S(1)}, u32[]{:S(2)}, u32[]{:S(2)}) collective-permute-start(f32[160,128]{1,0:T(8,128)S(1)} %slice.39), channel_id=1, source_target_pairs={{0,16},{1,17},{2,18},{3,19},{4,20},{5,21},{6,22},{7,23},{8,24},{9,... | collective-permute-start | bytes 245768 | tf_op jit(solution)/shard_map/ppermute | solution.py:34
  108.9 4.5 %collective-permute-start.15 = (f32[160,128]{1,0:T(8,128)S(1)}, f32[160,128]{1,0:T(8,128)S(1)}, u32[]{:S(2)}, u32[]{:S(2)}) collective-permute-start(f32[160,128]{1,0:T(8,128)S(1)} %slice.37), channel_id=1, source_target_pairs={{0,2},{1,3},{2,0},{3,1},{4,6},{5,7},{6,4},{7,5},{8,10},{9,11},{10,... | collective-permute-start | bytes 245768 | tf_op jit(solution)/shard_map/ppermute | solution.py:34

commit v10 on v9

--- a/solution.py
+++ b/solution.py
@@ -75,25 +75,32 @@
     )(orbitals, targets.astype(F32).reshape(DEVICES, FB))
 
 
-def unpack_kernel(packed, col_pair, row_pair):
-    turned = packed[:, : 3 * FB].T
+def targets_of(packed, i):
     source = lax.broadcasted_iota(jnp.int32, (NB, NT), 0)
     target = lax.broadcasted_iota(jnp.int32, (NB, NT), 1)
-    for i, spots in enumerate((((col_pair, 0), (row_pair, 0)), ((col_pair, 1),), ((row_pair, 1),))):
-        chosen = jnp.where(source == 8 * target + i, 1.0, 0.0).astype(BF)
-        tgt = tn(packed[:, 3 * FB :], chosen).astype(BF)
-        for out, side in spots:
-            out[side, :, :NB] = turned[i * FB : (i + 1) * FB]
-            out[side, :, NB:] = tgt
-
-
-def unpack(packed):
-    return pl.pallas_call(
-        unpack_kernel,
-        out_shape=[jax.ShapeDtypeStruct((2, FB, WIDE), BF)] * 2,
+    return tn(packed[:, 3 * FB :], jnp.where(source == 8 * target + i, 1.0, 0.0).astype(BF)).astype(BF)
+
+
+def unpack_cols_kernel(packed, pair):
+    turned = packed[:, : 2 * FB].T
+    for side in (0, 1):
+        pair[side, :, :NB] = turned[side * FB : (side + 1) * FB]
+        pair[side, :, NB:] = targets_of(packed, side)
+
+
+def unpack_rows_kernel(packed, col_pair, pair):
+    pair[0] = col_pair[0]
+    pair[1, :, :NB] = packed[:, 256:512].T[2 * FB - 256 : 3 * FB - 256]
+    pair[1, :, NB:] = targets_of(packed, 2)
+
+
+def unpack(kernel, name, *args):
+    return pl.pallas_call(
+        kernel,
+        out_shape=jax.ShapeDtypeStruct((2, FB, WIDE), BF),
         compiler_params=pltpu.CompilerParams(vmem_limit_bytes=32 * 2**20),
-        name="unpack",
-    )(packed)
+        name=name,
+    )(*args)
 
 
 def cut_kernel(*refs):
@@ -225,7 +232,7 @@
         ],
         compiler_params=pltpu.CompilerParams(vmem_limit_bytes=48 * 2**20),
         cost_estimate=pl.CostEstimate(
-            flops=2_600_000_000 * tiles, bytes_accessed=5_000_000 * tiles, transcendentals=0
+            flops=20_000_000_000 * tiles, bytes_accessed=40_000_000 * tiles, transcendentals=0
         ),
         name="far_tile" if before else "near_tiles",
     )(me, *row_parts, *col_parts, kern, owned, mirrored, *before)
@@ -237,9 +244,11 @@
 
     packed = pack(orbitals, targets).reshape(DEVICES, 8, 4 * FB)
     packed = lax.all_to_all(packed, AXES, split_axis=0, concat_axis=0, tiled=True)
-    col_pair, row_pair = unpack(packed.reshape(DEVICES * 8, 4 * FB))
-
+    packed = packed.reshape(DEVICES * 8, 4 * FB)
+
+    col_pair = unpack(unpack_cols_kernel, "unpack_cols", packed)
     y_down, y_up = send(col_pair, y=1), send(col_pair, y=3)
+    row_pair = unpack(unpack_rows_kernel, "unpack_rows", packed, col_pair)
     z_down, z_up = send(row_pair, z=1), send(row_pair, z=3)
     y_far, y_far_side = cut(y_down, y_up)
     y_far, y_far_side = send(y_far, y=1), send(y_far_side, y=3)

time: 114 us -> 113 us (level)
  local copies, waits for them, and re-layouts: 5.38 us -> 1.85 us
  waiting for transfers between devices: 27.9 us -> 30.5 us
    ppermute x20, waiting for transfers between devices: 27.9 us -> 30.5 us  [send(): return lax.ppermute(x, AXES, moved(**steps))]
    unnamed x14 -> x10, local copies, waits for them, and re-layouts: 2.96 us -> 0.99 us
  transfers between devices with their start and end apart: 20 -> 20, of which waited for: 10 -> 10; matrix products, arithmetic and copies ran while one was open for 2% -> 1% of each run, Pallas kernels for 14% -> 14%
where the time goes in v10:
time: 113 us
  blocking collectives  32.9 us (29%)
  waiting for transfers between devices  30.5 us (27%)
  Pallas kernels  24.4 us (22%)
  starting transfers between devices  20.6 us (18%)
  other arithmetic  2.02 us (2%)
  local copies, waits for them, and re-layouts  1.85 us (2%)
    all_to_all x1, blocking collectives, local(): lax.all_to_all(packed, AXES, split_axis=0, concat_axis=0, tiled=True)  32.9 us
    ppermute x20, waiting for transfers between devices, send(): return lax.ppermute(x, AXES, moved(**steps))  30.5 us
    pallas_call x2, Pallas kernels, tile_call(): pl.pallas_call(functools.partial(tile_kernel, z_steps), in_specs=[pl.Bloc...  21.3 us
    ppermute x20, starting transfers between devices, send(): return lax.ppermute(x, AXES, moved(**steps))  20.6 us
  transfers between devices with their start and end apart: 20, of which 10 were waited for; matrix products, arithmetic and copies ran while one was open for 1% of the time, Pallas kernels for 14%

profile of v10, /device:TPU:0, one launch (start us, length us, event | category | flops | bytes accessed | tf_op | source)
XLA Modules:
  0.0 112.5 jit_solution(16458107768793862242)
XLA Ops:
  0.0 1.1 convert_reduce_fusion
  1.1 0.1 reshape.22.tgt
  1.2 0.0 copy-start.3
  1.2 1.0 copy-done.3
  2.2 0.5 pack.1
  2.7 32.9 %all_to_all.5 = bf16[128,8,640]{2,1,0:T(8,128)(2,1)S(1)} all-to-all(bf16[128,8,640]{2,1,0:T(8,128)(2,1)S(1)} %bitcast.29), channel_id=1, replica_groups=mesh['row'=8,'col'=16] {'row','col'}, dimensions={0} | all-to-all | bytes 2621440 | tf_op jit(solution)/shard_map/all_to_all | solution.py:246
  35.6 1.0 unpack_cols.1.col_pair.refs_6_.refs_2_
  36.6 0.6 unpack_rows.1.refs_0_
  37.3 0.3 collective-permute-start.2
  37.6 1.8 %collective-permute-start = (bf16[2,160,1152]{2,1,0:T(8,128)(2,1)S(1)}, bf16[2,160,1152]{2,1,0:T(8,128)(2,1)}, u32[]{:S(2)}, u32[]{:S(2)}) collective-permute-start(bf16[2,160,1152]{2,1,0:T(8,128)(2,1)S(1)} %unpack_rows.1.refs_0_), channel_id=1, source_target_pairs={{0,4},{1,5},{2,6},{3,7},{4,8},{5,9},{6,10},{7,11},{8,12},{9,13},{1... | collective-permute-start | bytes 2211848 | tf_op jit(solution)/shard_map/ppermute | solution.py:34
  39.4 0.8 collective-permute-start.5
  40.2 1.2 %collective-permute-start.6 = (bf16[2,160,1152]{2,1,0:T(8,128)(2,1)S(1)}, bf16[2,160,1152]{2,1,0:T(8,128)(2,1)S(1)}, u32[]{:S(2)}, u32[]{:S(2)}) collective-permute-start(bf16[2,160,1152]{2,1,0:T(8,128)(2,1)S(1)} %unpack_cols.1.col_pair.refs_6_.refs_2_), channel_id=1, source_target_pairs={{0,32},{1,33},{2,34},{3,35},{4,36},{5,37},{6,38},{7,39},{8,40},{9,... | collective-permute-start | bytes 2211848 | tf_op jit(solution)/shard_map/ppermute | solution.py:34
  41.4 13.9 %collective-permute-done.2.refs_2_ = bf16[2,160,1152]{2,1,0:T(8,128)(2,1)} collective-permute-done((bf16[2,160,1152]{2,1,0:T(8,128)(2,1)S(1)}, bf16[2,160,1152]{2,1,0:T(8,128)(2,1)}, u32[]{:S(2)}, u32[]{:S(2)}) %collective-permute-start.2) | collective-permute-done | bytes 737312 | tf_op jit(solution)/shard_map/ppermute | solution.py:34
  55.3 1.3 %collective-permute-done.refs_4_ = bf16[2,160,1152]{2,1,0:T(8,128)(2,1)} collective-permute-done((bf16[2,160,1152]{2,1,0:T(8,128)(2,1)S(1)}, bf16[2,160,1152]{2,1,0:T(8,128)(2,1)}, u32[]{:S(2)}, u32[]{:S(2)}) %collective-permute-start) | collective-permute-done | bytes 737312 | tf_op jit(solution)/shard_map/ppermute | solution.py:34
  56.6 0.0 collective-permute-done.5.refs_1_.refs_7_.refs_3_
  56.7 2.0 %collective-permute-done.6.refs_0_.refs_8_.refs_4_ = bf16[2,160,1152]{2,1,0:T(8,128)(2,1)S(1)} collective-permute-done((bf16[2,160,1152]{2,1,0:T(8,128)(2,1)S(1)}, bf16[2,160,1152]{2,1,0:T(8,128)(2,1)S(1)}, u32[]{:S(2)}, u32[]{:S(2)}) %collective-permute-start.6) | collective-permute-done | bytes 737312 | tf_op jit(solution)/shard_map/ppermute | solution.py:34
  58.7 1.0 cut.1
  59.7 3.2 %collective-permute-start.8 = (bf16[160,1152]{1,0:T(8,128)(2,1)}, bf16[160,1152]{1,0:T(8,128)(2,1)S(1)}, u32[]{:S(2)}, u32[]{:S(2)}) collective-permute-start(bf16[160,1152]{1,0:T(8,128)(2,1)} %get-tuple-element.17), channel_id=1, source_target_pairs={{0,96},{1,97},{2,98},{3,99},{4,100},{5,101},{6,102},{7,103},{8,104... | collective-permute-start | bytes 1105928 | tf_op jit(solution)/shard_map/ppermute | solution.py:34
  62.9 0.1 and_select_fusion
  63.0 0.1 copy.10
  63.1 0.1 broadcast_in_dim.12
  63.2 0.2 reshape_reshape.7.refs_13_.refs_9_
  63.4 0.1 copy.9
  63.4 0.1 broadcast_in_dim.10
  63.5 0.2 reshape_reshape.6.refs_12_.refs_8_
  63.7 0.1 stack.23.me
  63.8 0.3 collective-permute-start.1
  64.1 3.0 %collective-permute-start.4 = (bf16[2,160,1152]{2,1,0:T(8,128)(2,1)}, bf16[2,160,1152]{2,1,0:T(8,128)(2,1)S(1)}, u32[]{:S(2)}, u32[]{:S(2)}) collective-permute-start(bf16[2,160,1152]{2,1,0:T(8,128)(2,1)} %collective-permute-done.3.refs_3_), channel_id=1, source_target_pairs={{0,12},{1,13},{2,14},{3,15},{4,0},{5,1},{6,2},{7,3},{8,4},{9,5},{1... | collective-permute-start | bytes 2211848 | tf_op jit(solution)/shard_map/ppermute | solution.py:34
  67.1 3.0 %collective-permute-done.7.refs_9_.refs_5_ = bf16[160,1152]{1,0:T(8,128)(2,1)S(1)} collective-permute-done((bf16[160,1152]{1,0:T(8,128)(2,1)}, bf16[160,1152]{1,0:T(8,128)(2,1)S(1)}, u32[]{:S(2)}, u32[]{:S(2)}) %collective-permute-start.7) | collective-permute-done | bytes 368672 | tf_op jit(solution)/shard_map/ppermute | solution.py:34
  70.1 14.8 %near_tiles.1 = (f32[3,320,128]{2,1,0:T(8,128)S(1)}, f32[3,320,128]{2,1,0:T(8,128)S(1)}, f32[8,160,128]{2,1,0:T(8,128)S(1)}) custom-call(s32[5]{0:T(128)S(1)} %stack.23.me, bf16[2,160,1152]{2,1,0:T(8,128)(2,1)S(1)} %unpack_rows.1.refs_0_, bf16[2,160,1152]{2,1,0:T(8,128)(2,1)} %collective-permute-done.9.refs_1_, ...), custom_call_target="tpu_custom_call" | custom-call | flops 60000002048 | bytes 120000000 | tf_op jit(solution)/shard_map/near_tiles/pallas_call | solution.py:219
  85.0 6.5 %far_tile.1 = (f32[4,320,128]{2,1,0:T(8,128)S(1)}, f32[4,320,128]{2,1,0:T(8,128)S(1)}, f32[320,128]{1,0:T(8,128)S(1)}, f32[320,128]{1,0:T(8,128)S(1)}, f32[320,128]{1,0:T(8,128)S(1)}, /*index=5*/f32[320,128]{1,0:T(8,128)S(1)}) custom-call(s32[5]{0:T(128)S(1)} %stack.23.me, bf16[2,160,1152]{2,1,0:T(8,128)(2,1)S(1)} %collective-permute-done.1.refs_0_, ...), custom_call_target="tpu_custom_call" | custom-call | flops 20000000000 | bytes 40000000 | tf_op jit(solution)/shard_map/far_tile/pallas_call | solution.py:219
  91.5 0.1 collective-permute-start.11
  91.6 1.5 %collective-permute-start.16 = (f32[320,128]{1,0:T(8,128)S(1)}, f32[320,128]{1,0:T(8,128)S(1)}, u32[]{:S(2)}, u32[]{:S(2)}) collective-permute-start(f32[320,128]{1,0:T(8,128)S(1)} %get-tuple-element.24), channel_id=1, source_target_pairs={{0,64},{1,65},{2,66},{3,67},{4,68},{5,69},{6,70},{7,71},{8,72},{9,... | collective-permute-start | bytes 491528 | tf_op jit(solution)/shard_map/ppermute | solution.py:34
  93.1 2.4 %collective-permute-start.17 = (f32[320,128]{1,0:T(8,128)S(1)}, f32[320,128]{1,0:T(8,128)S(1)}, u32[]{:S(2)}, u32[]{:S(2)}) collective-permute-start(f32[320,128]{1,0:T(8,128)S(1)} %get-tuple-element.25), channel_id=1, source_target_pairs={{0,32},{1,33},{2,34},{3,35},{4,36},{5,37},{6,38},{7,39},{8,40},{9,... | collective-permute-start | bytes 491528 | tf_op jit(solution)/shard_map/ppermute | solution.py:34
  95.5 0.9 collective-permute-start.18
  96.3 0.1 add.46
  96.5 0.9 collective-permute-start.12
  97.4 1.0 collective-permute-start.13
  98.3 1.9 %collective-permute-done.16 = f32[320,128]{1,0:T(8,128)S(1)} collective-permute-done((f32[320,128]{1,0:T(8,128)S(1)}, f32[320,128]{1,0:T(8,128)S(1)}, u32[]{:S(2)}, u32[]{:S(2)}) %collective-permute-start.16) | collective-permute-done | bytes 163872 | tf_op jit(solution)/shard_map/ppermute | solution.py:34
  100.2 0.9 collective-permute-start.14
  101.1 2.1 %collective-permute-done.17 = f32[320,128]{1,0:T(8,128)S(1)} collective-permute-done((f32[320,128]{1,0:T(8,128)S(1)}, f32[320,128]{1,0:T(8,128)S(1)}, u32[]{:S(2)}, u32[]{:S(2)}) %collective-permute-start.17) | collective-permute-done | bytes 163872 | tf_op jit(solution)/shard_map/ppermute | solution.py:34
  103.2 0.3 collective-permute-done.18
  103.6 1.8 %collective-permute-start.19 = (f32[160,128]{1,0:T(8,128)S(1)}, f32[160,128]{1,0:T(8,128)S(1)}, u32[]{:S(2)}, u32[]{:S(2)}) collective-permute-start(f32[160,128]{1,0:T(8,128)S(1)} %slice.39), channel_id=1, source_target_pairs={{0,16},{1,17},{2,18},{3,19},{4,20},{5,21},{6,22},{7,23},{8,24},{9,... | collective-permute-start | bytes 245768 | tf_op jit(solution)/shard_map/ppermute | solution.py:34
  105.4 1.9 %collective-permute-done.13 = f32[320,128]{1,0:T(8,128)S(1)} collective-permute-done((f32[320,128]{1,0:T(8,128)S(1)}, f32[320,128]{1,0:T(8,128)S(1)}, u32[]{:S(2)}, u32[]{:S(2)}) %collective-permute-start.13) | collective-permute-done | bytes 163872 | tf_op jit(solution)/shard_map/ppermute | solution.py:34
  107.3 0.5 collective-permute-start.15
  107.9 1.7 %collective-permute-done.19 = f32[160,128]{1,0:T(8,128)S(1)} collective-permute-done((f32[160,128]{1,0:T(8,128)S(1)}, f32[160,128]{1,0:T(8,128)S(1)}, u32[]{:S(2)}, u32[]{:S(2)}) %collective-permute-start.19) | collective-permute-done | bytes 81952 | tf_op jit(solution)/shard_map/ppermute | solution.py:34
  109.6 2.3 %collective-permute-done.15 = f32[160,128]{1,0:T(8,128)S(1)} collective-permute-done((f32[160,128]{1,0:T(8,128)S(1)}, f32[160,128]{1,0:T(8,128)S(1)}, u32[]{:S(2)}, u32[]{:S(2)}) %collective-permute-start.15) | collective-permute-done | bytes 81952 | tf_op jit(solution)/shard_map/ppermute | solution.py:34
  111.9 0.7 fusion.3
  (29 shorter events, 0.2 us)
Async XLA Ops:
  1.2 1.0 copy-start.3
  36.6 3.6 %copy-start = (bf16[2,160,1152]{2,1,0:T(8,128)(2,1)}, bf16[2,160,1152]{2,1,0:T(8,128)(2,1)S(1)}, u32[]{:S(2)}) copy-start(bf16[2,160,1152]{2,1,0:T(8,128)(2,1)S(1)} %unpack_cols.1.col_pair.refs_6_.refs_2_) | copy-start | bytes 2211844
  37.3 25.7 %copy-start.4 = (s32[1,16,8,1]{1,3,2,0:T(1,128)S(1)}, s32[1,16,8,1]{1,3,2,0:T(1,128)}, u32[]{:S(2)}) copy-start(s32[1,16,8,1]{1,3,2,0:T(1,128)} %param.7) | copy-start | bytes 1540
  37.3 18.0 %collective-permute-start.2 = (bf16[2,160,1152]{2,1,0:T(8,128)(2,1)S(1)}, bf16[2,160,1152]{2,1,0:T(8,128)(2,1)}, u32[]{:S(2)}, u32[]{:S(2)}) collective-permute-start(bf16[2,160,1152]{2,1,0:T(8,128)(2,1)S(1)} %unpack_rows.1.refs_0_), channel_id=1, source_target_pairs={{0,12},{1,13},{2,14},{3,15},{4,0},{5,1},{6,2},{7,3},{8,4},{9,5},{1... | collective-permute-start | bytes 2211848 | tf_op jit(solution)/shard_map/ppermute | solution.py:34
  37.6 19.0 %collective-permute-start = (bf16[2,160,1152]{2,1,0:T(8,128)(2,1)S(1)}, bf16[2,160,1152]{2,1,0:T(8,128)(2,1)}, u32[]{:S(2)}, u32[]{:S(2)}) collective-permute-start(bf16[2,160,1152]{2,1,0:T(8,128)(2,1)S(1)} %unpack_rows.1.refs_0_), channel_id=1, source_target_pairs={{0,4},{1,5},{2,6},{3,7},{4,8},{5,9},{6,10},{7,11},{8,12},{9,13},{1... | collective-permute-start | bytes 2211848 | tf_op jit(solution)/shard_map/ppermute | solution.py:34
  39.4 17.3 %collective-permute-start.5 = (bf16[2,160,1152]{2,1,0:T(8,128)(2,1)S(1)}, bf16[2,160,1152]{2,1,0:T(8,128)(2,1)S(1)}, u32[]{:S(2)}, u32[]{:S(2)}) collective-permute-start(bf16[2,160,1152]{2,1,0:T(8,128)(2,1)S(1)} %unpack_cols.1.col_pair.refs_6_.refs_2_), channel_id=1, source_target_pairs={{0,96},{1,97},{2,98},{3,99},{4,100},{5,101},{6,102},{7,103},{8,104... | collective-permute-start | bytes 2211848 | tf_op jit(solution)/shard_map/ppermute | solution.py:34
  40.2 18.5 %collective-permute-start.6 = (bf16[2,160,1152]{2,1,0:T(8,128)(2,1)S(1)}, bf16[2,160,1152]{2,1,0:T(8,128)(2,1)S(1)}, u32[]{:S(2)}, u32[]{:S(2)}) collective-permute-start(bf16[2,160,1152]{2,1,0:T(8,128)(2,1)S(1)} %unpack_cols.1.col_pair.refs_6_.refs_2_), channel_id=1, source_target_pairs={{0,32},{1,33},{2,34},{3,35},{4,36},{5,37},{6,38},{7,39},{8,40},{9,... | collective-permute-start | bytes 2211848 | tf_op jit(solution)/shard_map/ppermute | solution.py:34
  41.4 22.4 %collective-permute-start.9 = (bf16[2,160,1152]{2,1,0:T(8,128)(2,1)S(1)}, bf16[2,160,1152]{2,1,0:T(8,128)(2,1)}, u32[]{:S(2)}, u32[]{:S(2)}) collective-permute-start(bf16[2,160,1152]{2,1,0:T(8,128)(2,1)S(1)} %unpack_rows.1.refs_0_), channel_id=1, source_target_pairs={{0,1},{1,0},{2,3},{3,2},{4,5},{5,4},{6,7},{7,6},{8,9},{9,8},{10,11... | collective-permute-start | bytes 2211848 | tf_op jit(solution)/shard_map/ppermute | solution.py:34
  55.3 8.8 %collective-permute-start.3 = (bf16[2,160,1152]{2,1,0:T(8,128)(2,1)}, bf16[2,160,1152]{2,1,0:T(8,128)(2,1)}, u32[]{:S(2)}, u32[]{:S(2)}) collective-permute-start(bf16[2,160,1152]{2,1,0:T(8,128)(2,1)} %collective-permute-done.2.refs_2_), channel_id=1, source_target_pairs={{0,1},{1,0},{2,3},{3,2},{4,5},{5,4},{6,7},{7,6},{8,9},{9,8},{10,11... | collective-permute-start | bytes 2211848 | tf_op jit(solution)/shard_map/ppermute | solution.py:34
  56.6 13.5 %collective-permute-start.10 = (bf16[2,160,1152]{2,1,0:T(8,128)(2,1)}, bf16[2,160,1152]{2,1,0:T(8,128)(2,1)}, u32[]{:S(2)}, u32[]{:S(2)}) collective-permute-start(bf16[2,160,1152]{2,1,0:T(8,128)(2,1)} %collective-permute-done.refs_4_), channel_id=1, source_target_pairs={{0,1},{1,0},{2,3},{3,2},{4,5},{5,4},{6,7},{7,6},{8,9},{9,8},{10,11... | collective-permute-start | bytes 2211848 | tf_op jit(solution)/shard_map/ppermute | solution.py:34
  56.7 13.4 %copy-start.1 = (bf16[2,160,1152]{2,1,0:T(8,128)(2,1)}, bf16[2,160,1152]{2,1,0:T(8,128)(2,1)S(1)}, u32[]{:S(2)}) copy-start(bf16[2,160,1152]{2,1,0:T(8,128)(2,1)S(1)} %collective-permute-done.5.refs_1_.refs_7_.refs_3_) | copy-start | bytes 2211844
  58.7 11.4 %copy-start.2 = (bf16[2,160,1152]{2,1,0:T(8,128)(2,1)}, bf16[2,160,1152]{2,1,0:T(8,128)(2,1)S(1)}, u32[]{:S(2)}) copy-start(bf16[2,160,1152]{2,1,0:T(8,128)(2,1)S(1)} %collective-permute-done.6.refs_0_.refs_8_.refs_4_) | copy-start | bytes 2211844
  59.7 10.4 %collective-permute-start.7 = (bf16[160,1152]{1,0:T(8,128)(2,1)}, bf16[160,1152]{1,0:T(8,128)(2,1)S(1)}, u32[]{:S(2)}, u32[]{:S(2)}) collective-permute-start(bf16[160,1152]{1,0:T(8,128)(2,1)} %get-tuple-element.16), channel_id=1, source_target_pairs={{0,32},{1,33},{2,34},{3,35},{4,36},{5,37},{6,38},{7,39},{8,40},{9,... | collective-permute-start | bytes 1105928 | tf_op jit(solution)/shard_map/ppermute | solution.py:34
  59.7 10.4 %collective-permute-start.8 = (bf16[160,1152]{1,0:T(8,128)(2,1)}, bf16[160,1152]{1,0:T(8,128)(2,1)S(1)}, u32[]{:S(2)}, u32[]{:S(2)}) collective-permute-start(bf16[160,1152]{1,0:T(8,128)(2,1)} %get-tuple-element.17), channel_id=1, source_target_pairs={{0,96},{1,97},{2,98},{3,99},{4,100},{5,101},{6,102},{7,103},{8,104... | collective-permute-start | bytes 1105928 | tf_op jit(solution)/shard_map/ppermute | solution.py:34
  63.8 21.2 %collective-permute-start.1 = (bf16[2,160,1152]{2,1,0:T(8,128)(2,1)}, bf16[2,160,1152]{2,1,0:T(8,128)(2,1)S(1)}, u32[]{:S(2)}, u32[]{:S(2)}) collective-permute-start(bf16[2,160,1152]{2,1,0:T(8,128)(2,1)} %collective-permute-done.refs_4_), channel_id=1, source_target_pairs={{0,4},{1,5},{2,6},{3,7},{4,8},{5,9},{6,10},{7,11},{8,12},{9,13},{1... | collective-permute-start | bytes 2211848 | tf_op jit(solution)/shard_map/ppermute | solution.py:34
  64.1 20.9 %collective-permute-start.4 = (bf16[2,160,1152]{2,1,0:T(8,128)(2,1)}, bf16[2,160,1152]{2,1,0:T(8,128)(2,1)S(1)}, u32[]{:S(2)}, u32[]{:S(2)}) collective-permute-start(bf16[2,160,1152]{2,1,0:T(8,128)(2,1)} %collective-permute-done.3.refs_3_), channel_id=1, source_target_pairs={{0,12},{1,13},{2,14},{3,15},{4,0},{5,1},{6,2},{7,3},{8,4},{9,5},{1... | collective-permute-start | bytes 2211848 | tf_op jit(solution)/shard_map/ppermute | solution.py:34
  91.5 4.9 %collective-permute-start.11 = (f32[4,320,128]{2,1,0:T(8,128)S(1)}, f32[4,320,128]{2,1,0:T(8,128)S(1)}, u32[]{:S(2)}, u32[]{:S(2)}) collective-permute-start(f32[4,320,128]{2,1,0:T(8,128)S(1)} %get-tuple-element.22), channel_id=1, source_target_pairs={{0,1},{1,0},{2,3},{3,2},{4,5},{5,4},{6,7},{7,6},{8,9},{9,8},{10,11... | collective-permute-start | bytes 1966088 | tf_op jit(solution)/shard_map/ppermute | solution.py:34
  91.6 8.6 %collective-permute-start.16 = (f32[320,128]{1,0:T(8,128)S(1)}, f32[320,128]{1,0:T(8,128)S(1)}, u32[]{:S(2)}, u32[]{:S(2)}) collective-permute-start(f32[320,128]{1,0:T(8,128)S(1)} %get-tuple-element.24), channel_id=1, source_target_pairs={{0,64},{1,65},{2,66},{3,67},{4,68},{5,69},{6,70},{7,71},{8,72},{9,... | collective-permute-start | bytes 491528 | tf_op jit(solution)/shard_map/ppermute | solution.py:34
  93.1 10.1 %collective-permute-start.17 = (f32[320,128]{1,0:T(8,128)S(1)}, f32[320,128]{1,0:T(8,128)S(1)}, u32[]{:S(2)}, u32[]{:S(2)}) collective-permute-start(f32[320,128]{1,0:T(8,128)S(1)} %get-tuple-element.25), channel_id=1, source_target_pairs={{0,32},{1,33},{2,34},{3,35},{4,36},{5,37},{6,38},{7,39},{8,40},{9,... | collective-permute-start | bytes 491528 | tf_op jit(solution)/shard_map/ppermute | solution.py:34
  95.5 8.1 %collective-permute-start.18 = (f32[320,128]{1,0:T(8,128)S(1)}, f32[320,128]{1,0:T(8,128)S(1)}, u32[]{:S(2)}, u32[]{:S(2)}) collective-permute-start(f32[320,128]{1,0:T(8,128)S(1)} %get-tuple-element.26), channel_id=1, source_target_pairs={{0,96},{1,97},{2,98},{3,99},{4,100},{5,101},{6,102},{7,103},{8,104... | collective-permute-start | bytes 491528 | tf_op jit(solution)/shard_map/ppermute | solution.py:34
  96.5 8.9 %collective-permute-start.12 = (f32[320,128]{1,0:T(8,128)S(1)}, f32[320,128]{1,0:T(8,128)S(1)}, u32[]{:S(2)}, u32[]{:S(2)}) collective-permute-start(f32[320,128]{1,0:T(8,128)S(1)} %get-tuple-element.27), channel_id=1, source_target_pairs={{0,8},{1,9},{2,10},{3,11},{4,12},{5,13},{6,14},{7,15},{8,0},{9,1},... | collective-permute-start | bytes 491528 | tf_op jit(solution)/shard_map/ppermute | solution.py:34
  97.4 9.9 %collective-permute-start.13 = (f32[320,128]{1,0:T(8,128)S(1)}, f32[320,128]{1,0:T(8,128)S(1)}, u32[]{:S(2)}, u32[]{:S(2)}) collective-permute-start(f32[320,128]{1,0:T(8,128)S(1)} %get-tuple-element.29), channel_id=1, source_target_pairs={{0,4},{1,5},{2,6},{3,7},{4,8},{5,9},{6,10},{7,11},{8,12},{9,13},{1... | collective-permute-start | bytes 491528 | tf_op jit(solution)/shard_map/ppermute | solution.py:34
  100.2 7.1 %collective-permute-start.14 = (f32[320,128]{1,0:T(8,128)S(1)}, f32[320,128]{1,0:T(8,128)S(1)}, u32[]{:S(2)}, u32[]{:S(2)}) collective-permute-start(f32[320,128]{1,0:T(8,128)S(1)} %get-tuple-element.28), channel_id=1, source_target_pairs={{0,12},{1,13},{2,14},{3,15},{4,0},{5,1},{6,2},{7,3},{8,4},{9,5},{1... | collective-permute-start | bytes 491528 | tf_op jit(solution)/shard_map/ppermute | solution.py:34
  103.6 6.0 %collective-permute-start.19 = (f32[160,128]{1,0:T(8,128)S(1)}, f32[160,128]{1,0:T(8,128)S(1)}, u32[]{:S(2)}, u32[]{:S(2)}) collective-permute-start(f32[160,128]{1,0:T(8,128)S(1)} %slice.39), channel_id=1, source_target_pairs={{0,16},{1,17},{2,18},{3,19},{4,20},{5,21},{6,22},{7,23},{8,24},{9,... | collective-permute-start | bytes 245768 | tf_op jit(solution)/shard_map/ppermute | solution.py:34
  107.3 4.5 %collective-permute-start.15 = (f32[160,128]{1,0:T(8,128)S(1)}, f32[160,128]{1,0:T(8,128)S(1)}, u32[]{:S(2)}, u32[]{:S(2)}) collective-permute-start(f32[160,128]{1,0:T(8,128)S(1)} %slice.37), channel_id=1, source_target_pairs={{0,2},{1,3},{2,0},{3,1},{4,6},{5,7},{6,4},{7,5},{8,10},{9,11},{10,... | collective-permute-start | bytes 245768 | tf_op jit(solution)/shard_map/ppermute | solution.py:34

commit v11 on v10

--- a/solution.py
+++ b/solution.py
@@ -103,18 +103,16 @@
     )(*args)
 
 
-def cut_kernel(*refs):
-    for i, (pair, out) in enumerate(zip(refs[:2], refs[2:])):
-        out[...] = pair[i % 2]
-
-
-def cut(*pairs):
+def cut(pair, side):
+    def cut_kernel(pair, out):
+        out[...] = pair[side]
+
     return pl.pallas_call(
         cut_kernel,
-        out_shape=[jax.ShapeDtypeStruct((FB, WIDE), BF)] * 2,
+        out_shape=jax.ShapeDtypeStruct((FB, WIDE), BF),
         compiler_params=pltpu.CompilerParams(vmem_limit_bytes=16 * 2**20),
         name="cut",
-    )(*pairs)
+    )(pair)
 
 
 def tile_kernel(z_steps, me, *refs):
@@ -250,8 +248,7 @@
     y_down, y_up = send(col_pair, y=1), send(col_pair, y=3)
     row_pair = unpack(unpack_rows_kernel, "unpack_rows", packed, col_pair)
     z_down, z_up = send(row_pair, z=1), send(row_pair, z=3)
-    y_far, y_far_side = cut(y_down, y_up)
-    y_far, y_far_side = send(y_far, y=1), send(y_far_side, y=3)
+    y_far, y_far_side = send(cut(y_down, 0), y=1), send(cut(y_up, 1), y=3)
     col_parts = (col_pair, y_up, y_down, y_far, y_far_side)
     up_other = send(z_up, k=1)
     near_rows = (row_pair, send(row_pair, k=1), z_up, up_other, z_down, send(z_down, k=1))

time: 113 us -> 112 us (level)
  transfers between devices with their start and end apart: 20 -> 20, of which waited for: 10 -> 10; matrix products, arithmetic and copies ran while one was open for 1% -> 1% of each run, Pallas kernels for 14% -> 13%
where the time goes in v11:
time: 112 us
  blocking collectives  32.9 us (29%)
  waiting for transfers between devices  29.9 us (27%)
  Pallas kernels  23.9 us (21%)
  starting transfers between devices  21.1 us (19%)
  other arithmetic  1.98 us (2%)
  local copies, waits for them, and re-layouts  1.85 us (2%)
    all_to_all x1, blocking collectives, local(): lax.all_to_all(packed, AXES, split_axis=0, concat_axis=0, tiled=True)  32.9 us
    ppermute x20, waiting for transfers between devices, send(): return lax.ppermute(x, AXES, moved(**steps))  29.9 us
    pallas_call x2, Pallas kernels, tile_call(): pl.pallas_call(functools.partial(tile_kernel, z_steps), in_specs=[pl.Bloc...  21.7 us
    ppermute x20, starting transfers between devices, send(): return lax.ppermute(x, AXES, moved(**steps))  21.1 us
  transfers between devices with their start and end apart: 20, of which 10 were waited for; matrix products, arithmetic and copies ran while one was open for 1% of the time, Pallas kernels for 13%

profile of v11, /device:TPU:0, one launch (start us, length us, event | category | flops | bytes accessed | tf_op | source)
XLA Modules:
  0.0 111.9 jit_solution(16772548316915860392)
XLA Ops:
  0.0 1.1 convert_reduce_fusion
  1.1 0.1 reshape.22.tgt
  1.2 0.0 copy-start.3
  1.2 1.0 copy-done.3
  2.2 0.5 pack.1
  2.7 32.9 %all_to_all.5 = bf16[128,8,640]{2,1,0:T(8,128)(2,1)S(1)} all-to-all(bf16[128,8,640]{2,1,0:T(8,128)(2,1)S(1)} %bitcast.29), channel_id=1, replica_groups=mesh['row'=8,'col'=16] {'row','col'}, dimensions={0} | all-to-all | bytes 2621440 | tf_op jit(solution)/shard_map/all_to_all | solution.py:244
  35.6 1.0 unpack_cols.1.col_pair.refs_6_.refs_2_
  36.6 0.6 unpack_rows.1.refs_0_
  37.3 0.0 copy-start.4
  37.3 0.3 collective-permute-start.2
  37.6 1.8 %collective-permute-start = (bf16[2,160,1152]{2,1,0:T(8,128)(2,1)S(1)}, bf16[2,160,1152]{2,1,0:T(8,128)(2,1)}, u32[]{:S(2)}, u32[]{:S(2)}) collective-permute-start(bf16[2,160,1152]{2,1,0:T(8,128)(2,1)S(1)} %unpack_rows.1.refs_0_), channel_id=1, source_target_pairs={{0,4},{1,5},{2,6},{3,7},{4,8},{5,9},{6,10},{7,11},{8,12},{9,13},{1... | collective-permute-start | bytes 2211848 | tf_op jit(solution)/shard_map/ppermute | solution.py:34
  39.4 0.0 collective-permute-start.6
  39.4 3.2 %collective-permute-start.5 = (bf16[2,160,1152]{2,1,0:T(8,128)(2,1)S(1)}, bf16[2,160,1152]{2,1,0:T(8,128)(2,1)S(1)}, u32[]{:S(2)}, u32[]{:S(2)}) collective-permute-start(bf16[2,160,1152]{2,1,0:T(8,128)(2,1)S(1)} %unpack_cols.1.col_pair.refs_6_.refs_2_), channel_id=1, source_target_pairs={{0,96},{1,97},{2,98},{3,99},{4,100},{5,101},{6,102},{7,103},{8,104... | collective-permute-start | bytes 2211848 | tf_op jit(solution)/shard_map/ppermute | solution.py:34
  42.6 12.7 %collective-permute-done.2.refs_2_ = bf16[2,160,1152]{2,1,0:T(8,128)(2,1)} collective-permute-done((bf16[2,160,1152]{2,1,0:T(8,128)(2,1)S(1)}, bf16[2,160,1152]{2,1,0:T(8,128)(2,1)}, u32[]{:S(2)}, u32[]{:S(2)}) %collective-permute-start.2) | collective-permute-done | bytes 737312 | tf_op jit(solution)/shard_map/ppermute | solution.py:34
  55.3 1.3 %collective-permute-done.refs_4_ = bf16[2,160,1152]{2,1,0:T(8,128)(2,1)} collective-permute-done((bf16[2,160,1152]{2,1,0:T(8,128)(2,1)S(1)}, bf16[2,160,1152]{2,1,0:T(8,128)(2,1)}, u32[]{:S(2)}, u32[]{:S(2)}) %collective-permute-start) | collective-permute-done | bytes 737312 | tf_op jit(solution)/shard_map/ppermute | solution.py:34
  56.6 1.3 %collective-permute-done.6.pair.refs_8_.refs_4_ = bf16[2,160,1152]{2,1,0:T(8,128)(2,1)S(1)} collective-permute-done((bf16[2,160,1152]{2,1,0:T(8,128)(2,1)S(1)}, bf16[2,160,1152]{2,1,0:T(8,128)(2,1)S(1)}, u32[]{:S(2)}, u32[]{:S(2)}) %collective-permute-start.6) | collective-permute-done | bytes 737312 | tf_op jit(solution)/shard_map/ppermute | solution.py:34
  57.9 0.1 collective-permute-start.7
  58.1 3.3 %collective-permute-start.8 = (bf16[160,1152]{1,0:T(8,128)(2,1)S(1)}, bf16[160,1152]{1,0:T(8,128)(2,1)}, u32[]{:S(2)}, u32[]{:S(2)}) collective-permute-start(bf16[160,1152]{1,0:T(8,128)(2,1)S(1)} %cut.3), channel_id=1, source_target_pairs={{0,96},{1,97},{2,98},{3,99},{4,100},{5,101},{6,102},{7,103},{8,104... | collective-permute-start | bytes 1105928 | tf_op jit(solution)/shard_map/ppermute | solution.py:34
  61.3 0.1 and_select_fusion
  61.4 0.1 copy.10
  61.5 0.1 broadcast_in_dim.12
  61.6 0.2 reshape_reshape.7.refs_13_.refs_9_
  61.8 0.1 copy.9
  61.8 0.1 broadcast_in_dim.10
  61.9 0.2 reshape_reshape.6.refs_12_.refs_8_
  62.1 0.1 stack.23.me
  62.2 0.3 collective-permute-start.1
  62.5 3.0 %collective-permute-start.4 = (bf16[2,160,1152]{2,1,0:T(8,128)(2,1)}, bf16[2,160,1152]{2,1,0:T(8,128)(2,1)S(1)}, u32[]{:S(2)}, u32[]{:S(2)}) collective-permute-start(bf16[2,160,1152]{2,1,0:T(8,128)(2,1)} %collective-permute-done.3.refs_3_), channel_id=1, source_target_pairs={{0,12},{1,13},{2,14},{3,15},{4,0},{5,1},{6,2},{7,3},{8,4},{9,5},{1... | collective-permute-start | bytes 2211848 | tf_op jit(solution)/shard_map/ppermute | solution.py:34
  65.5 3.6 %collective-permute-done.7.refs_9_.refs_5_ = bf16[160,1152]{1,0:T(8,128)(2,1)} collective-permute-done((bf16[160,1152]{1,0:T(8,128)(2,1)S(1)}, bf16[160,1152]{1,0:T(8,128)(2,1)}, u32[]{:S(2)}, u32[]{:S(2)}) %collective-permute-start.7) | collective-permute-done | bytes 368672 | tf_op jit(solution)/shard_map/ppermute | solution.py:34
  69.1 15.0 %near_tiles.1 = (f32[3,320,128]{2,1,0:T(8,128)S(1)}, f32[3,320,128]{2,1,0:T(8,128)S(1)}, f32[8,160,128]{2,1,0:T(8,128)S(1)}) custom-call(s32[5]{0:T(128)S(1)} %stack.23.me, bf16[2,160,1152]{2,1,0:T(8,128)(2,1)S(1)} %unpack_rows.1.refs_0_, bf16[2,160,1152]{2,1,0:T(8,128)(2,1)} %collective-permute-done.9.refs_1_, ...), custom_call_target="tpu_custom_call" | custom-call | flops 60000002048 | bytes 120000000 | tf_op jit(solution)/shard_map/near_tiles/pallas_call | solution.py:217
  84.1 6.7 %far_tile.1 = (f32[4,320,128]{2,1,0:T(8,128)S(1)}, f32[4,320,128]{2,1,0:T(8,128)S(1)}, f32[320,128]{1,0:T(8,128)S(1)}, f32[320,128]{1,0:T(8,128)S(1)}, f32[320,128]{1,0:T(8,128)S(1)}, /*index=5*/f32[320,128]{1,0:T(8,128)S(1)}) custom-call(s32[5]{0:T(128)S(1)} %stack.23.me, bf16[2,160,1152]{2,1,0:T(8,128)(2,1)S(1)} %collective-permute-done.1.refs_0_, ...), custom_call_target="tpu_custom_call" | custom-call | flops 20000000000 | bytes 40000000 | tf_op jit(solution)/shard_map/far_tile/pallas_call | solution.py:217
  90.8 0.1 collective-permute-start.11
  90.9 1.7 %collective-permute-start.16 = (f32[320,128]{1,0:T(8,128)S(1)}, f32[320,128]{1,0:T(8,128)S(1)}, u32[]{:S(2)}, u32[]{:S(2)}) collective-permute-start(f32[320,128]{1,0:T(8,128)S(1)} %get-tuple-element.20), channel_id=1, source_target_pairs={{0,64},{1,65},{2,66},{3,67},{4,68},{5,69},{6,70},{7,71},{8,72},{9,... | collective-permute-start | bytes 491528 | tf_op jit(solution)/shard_map/ppermute | solution.py:34
  92.5 2.3 %collective-permute-start.17 = (f32[320,128]{1,0:T(8,128)S(1)}, f32[320,128]{1,0:T(8,128)S(1)}, u32[]{:S(2)}, u32[]{:S(2)}) collective-permute-start(f32[320,128]{1,0:T(8,128)S(1)} %get-tuple-element.21), channel_id=1, source_target_pairs={{0,32},{1,33},{2,34},{3,35},{4,36},{5,37},{6,38},{7,39},{8,40},{9,... | collective-permute-start | bytes 491528 | tf_op jit(solution)/shard_map/ppermute | solution.py:34
  94.9 0.9 collective-permute-start.18
  95.8 0.1 add.46
  95.9 0.8 collective-permute-start.12
  96.7 0.5 collective-permute-start.13
  97.3 2.3 %collective-permute-done.16 = f32[320,128]{1,0:T(8,128)S(1)} collective-permute-done((f32[320,128]{1,0:T(8,128)S(1)}, f32[320,128]{1,0:T(8,128)S(1)}, u32[]{:S(2)}, u32[]{:S(2)}) %collective-permute-start.16) | collective-permute-done | bytes 163872 | tf_op jit(solution)/shard_map/ppermute | solution.py:34
  99.5 0.5 collective-permute-start.14
  100.0 2.5 %collective-permute-done.17 = f32[320,128]{1,0:T(8,128)S(1)} collective-permute-done((f32[320,128]{1,0:T(8,128)S(1)}, f32[320,128]{1,0:T(8,128)S(1)}, u32[]{:S(2)}, u32[]{:S(2)}) %collective-permute-start.17) | collective-permute-done | bytes 163872 | tf_op jit(solution)/shard_map/ppermute | solution.py:34
  102.5 0.4 collective-permute-done.18
  103.0 1.9 %collective-permute-start.19 = (f32[160,128]{1,0:T(8,128)S(1)}, f32[160,128]{1,0:T(8,128)S(1)}, u32[]{:S(2)}, u32[]{:S(2)}) collective-permute-start(f32[160,128]{1,0:T(8,128)S(1)} %slice.39), channel_id=1, source_target_pairs={{0,16},{1,17},{2,18},{3,19},{4,20},{5,21},{6,22},{7,23},{8,24},{9,... | collective-permute-start | bytes 245768 | tf_op jit(solution)/shard_map/ppermute | solution.py:34
  104.8 1.8 %collective-permute-done.13 = f32[320,128]{1,0:T(8,128)S(1)} collective-permute-done((f32[320,128]{1,0:T(8,128)S(1)}, f32[320,128]{1,0:T(8,128)S(1)}, u32[]{:S(2)}, u32[]{:S(2)}) %collective-permute-start.13) | collective-permute-done | bytes 163872 | tf_op jit(solution)/shard_map/ppermute | solution.py:34
  106.7 0.6 collective-permute-start.15
  107.3 1.7 %collective-permute-done.19 = f32[160,128]{1,0:T(8,128)S(1)} collective-permute-done((f32[160,128]{1,0:T(8,128)S(1)}, f32[160,128]{1,0:T(8,128)S(1)}, u32[]{:S(2)}, u32[]{:S(2)}) %collective-permute-start.19) | collective-permute-done | bytes 81952 | tf_op jit(solution)/shard_map/ppermute | solution.py:34
  109.0 2.3 %collective-permute-done.15 = f32[160,128]{1,0:T(8,128)S(1)} collective-permute-done((f32[160,128]{1,0:T(8,128)S(1)}, f32[160,128]{1,0:T(8,128)S(1)}, u32[]{:S(2)}, u32[]{:S(2)}) %collective-permute-start.15) | collective-permute-done | bytes 81952 | tf_op jit(solution)/shard_map/ppermute | solution.py:34
  111.2 0.7 fusion.3
  (30 shorter events, 0.2 us)
Async XLA Ops:
  1.2 1.0 copy-start.3
  36.6 2.8 %copy-start = (bf16[2,160,1152]{2,1,0:T(8,128)(2,1)}, bf16[2,160,1152]{2,1,0:T(8,128)(2,1)S(1)}, u32[]{:S(2)}) copy-start(bf16[2,160,1152]{2,1,0:T(8,128)(2,1)S(1)} %unpack_cols.1.col_pair.refs_6_.refs_2_) | copy-start | bytes 2211844
  37.3 24.1 %copy-start.4 = (s32[1,16,8,1]{1,3,2,0:T(1,128)S(1)}, s32[1,16,8,1]{1,3,2,0:T(1,128)}, u32[]{:S(2)}) copy-start(s32[1,16,8,1]{1,3,2,0:T(1,128)} %param.7) | copy-start | bytes 1540
  37.3 18.0 %collective-permute-start.2 = (bf16[2,160,1152]{2,1,0:T(8,128)(2,1)S(1)}, bf16[2,160,1152]{2,1,0:T(8,128)(2,1)}, u32[]{:S(2)}, u32[]{:S(2)}) collective-permute-start(bf16[2,160,1152]{2,1,0:T(8,128)(2,1)S(1)} %unpack_rows.1.refs_0_), channel_id=1, source_target_pairs={{0,12},{1,13},{2,14},{3,15},{4,0},{5,1},{6,2},{7,3},{8,4},{9,5},{1... | collective-permute-start | bytes 2211848 | tf_op jit(solution)/shard_map/ppermute | solution.py:34
  37.6 19.0 %collective-permute-start = (bf16[2,160,1152]{2,1,0:T(8,128)(2,1)S(1)}, bf16[2,160,1152]{2,1,0:T(8,128)(2,1)}, u32[]{:S(2)}, u32[]{:S(2)}) collective-permute-start(bf16[2,160,1152]{2,1,0:T(8,128)(2,1)S(1)} %unpack_rows.1.refs_0_), channel_id=1, source_target_pairs={{0,4},{1,5},{2,6},{3,7},{4,8},{5,9},{6,10},{7,11},{8,12},{9,13},{1... | collective-permute-start | bytes 2211848 | tf_op jit(solution)/shard_map/ppermute | solution.py:34
  39.4 18.5 %collective-permute-start.6 = (bf16[2,160,1152]{2,1,0:T(8,128)(2,1)S(1)}, bf16[2,160,1152]{2,1,0:T(8,128)(2,1)S(1)}, u32[]{:S(2)}, u32[]{:S(2)}) collective-permute-start(bf16[2,160,1152]{2,1,0:T(8,128)(2,1)S(1)} %unpack_cols.1.col_pair.refs_6_.refs_2_), channel_id=1, source_target_pairs={{0,32},{1,33},{2,34},{3,35},{4,36},{5,37},{6,38},{7,39},{8,40},{9,... | collective-permute-start | bytes 2211848 | tf_op jit(solution)/shard_map/ppermute | solution.py:34
  39.4 18.6 %collective-permute-start.5 = (bf16[2,160,1152]{2,1,0:T(8,128)(2,1)S(1)}, bf16[2,160,1152]{2,1,0:T(8,128)(2,1)S(1)}, u32[]{:S(2)}, u32[]{:S(2)}) collective-permute-start(bf16[2,160,1152]{2,1,0:T(8,128)(2,1)S(1)} %unpack_cols.1.col_pair.refs_6_.refs_2_), channel_id=1, source_target_pairs={{0,96},{1,97},{2,98},{3,99},{4,100},{5,101},{6,102},{7,103},{8,104... | collective-permute-start | bytes 2211848 | tf_op jit(solution)/shard_map/ppermute | solution.py:34
  42.6 19.6 %collective-permute-start.9 = (bf16[2,160,1152]{2,1,0:T(8,128)(2,1)S(1)}, bf16[2,160,1152]{2,1,0:T(8,128)(2,1)}, u32[]{:S(2)}, u32[]{:S(2)}) collective-permute-start(bf16[2,160,1152]{2,1,0:T(8,128)(2,1)S(1)} %unpack_rows.1.refs_0_), channel_id=1, source_target_pairs={{0,1},{1,0},{2,3},{3,2},{4,5},{5,4},{6,7},{7,6},{8,9},{9,8},{10,11... | collective-permute-start | bytes 2211848 | tf_op jit(solution)/shard_map/ppermute | solution.py:34
  55.3 7.2 %collective-permute-start.3 = (bf16[2,160,1152]{2,1,0:T(8,128)(2,1)}, bf16[2,160,1152]{2,1,0:T(8,128)(2,1)}, u32[]{:S(2)}, u32[]{:S(2)}) collective-permute-start(bf16[2,160,1152]{2,1,0:T(8,128)(2,1)} %collective-permute-done.2.refs_2_), channel_id=1, source_target_pairs={{0,1},{1,0},{2,3},{3,2},{4,5},{5,4},{6,7},{7,6},{8,9},{9,8},{10,11... | collective-permute-start | bytes 2211848 | tf_op jit(solution)/shard_map/ppermute | solution.py:34
  56.6 12.5 %collective-permute-start.10 = (bf16[2,160,1152]{2,1,0:T(8,128)(2,1)}, bf16[2,160,1152]{2,1,0:T(8,128)(2,1)}, u32[]{:S(2)}, u32[]{:S(2)}) collective-permute-start(bf16[2,160,1152]{2,1,0:T(8,128)(2,1)} %collective-permute-done.refs_4_), channel_id=1, source_target_pairs={{0,1},{1,0},{2,3},{3,2},{4,5},{5,4},{6,7},{7,6},{8,9},{9,8},{10,11... | collective-permute-start | bytes 2211848 | tf_op jit(solution)/shard_map/ppermute | solution.py:34
  57.9 4.0 %copy-start.1 = (bf16[2,160,1152]{2,1,0:T(8,128)(2,1)}, bf16[2,160,1152]{2,1,0:T(8,128)(2,1)S(1)}, u32[]{:S(2)}) copy-start(bf16[2,160,1152]{2,1,0:T(8,128)(2,1)S(1)} %collective-permute-done.6.pair.refs_8_.refs_4_) | copy-start | bytes 2211844
  57.9 11.1 %collective-permute-start.7 = (bf16[160,1152]{1,0:T(8,128)(2,1)S(1)}, bf16[160,1152]{1,0:T(8,128)(2,1)}, u32[]{:S(2)}, u32[]{:S(2)}) collective-permute-start(bf16[160,1152]{1,0:T(8,128)(2,1)S(1)} %cut.2), channel_id=1, source_target_pairs={{0,32},{1,33},{2,34},{3,35},{4,36},{5,37},{6,38},{7,39},{8,40},{9,... | collective-permute-start | bytes 1105928 | tf_op jit(solution)/shard_map/ppermute | solution.py:34
  58.0 11.1 %copy-start.2 = (bf16[2,160,1152]{2,1,0:T(8,128)(2,1)}, bf16[2,160,1152]{2,1,0:T(8,128)(2,1)S(1)}, u32[]{:S(2)}) copy-start(bf16[2,160,1152]{2,1,0:T(8,128)(2,1)S(1)} %collective-permute-done.5.pair.refs_7_.refs_3_) | copy-start | bytes 2211844
  58.1 11.0 %collective-permute-start.8 = (bf16[160,1152]{1,0:T(8,128)(2,1)S(1)}, bf16[160,1152]{1,0:T(8,128)(2,1)}, u32[]{:S(2)}, u32[]{:S(2)}) collective-permute-start(bf16[160,1152]{1,0:T(8,128)(2,1)S(1)} %cut.3), channel_id=1, source_target_pairs={{0,96},{1,97},{2,98},{3,99},{4,100},{5,101},{6,102},{7,103},{8,104... | collective-permute-start | bytes 1105928 | tf_op jit(solution)/shard_map/ppermute | solution.py:34
  62.2 21.8 %collective-permute-start.1 = (bf16[2,160,1152]{2,1,0:T(8,128)(2,1)}, bf16[2,160,1152]{2,1,0:T(8,128)(2,1)S(1)}, u32[]{:S(2)}, u32[]{:S(2)}) collective-permute-start(bf16[2,160,1152]{2,1,0:T(8,128)(2,1)} %collective-permute-done.refs_4_), channel_id=1, source_target_pairs={{0,4},{1,5},{2,6},{3,7},{4,8},{5,9},{6,10},{7,11},{8,12},{9,13},{1... | collective-permute-start | bytes 2211848 | tf_op jit(solution)/shard_map/ppermute | solution.py:34
  62.5 21.5 %collective-permute-start.4 = (bf16[2,160,1152]{2,1,0:T(8,128)(2,1)}, bf16[2,160,1152]{2,1,0:T(8,128)(2,1)S(1)}, u32[]{:S(2)}, u32[]{:S(2)}) collective-permute-start(bf16[2,160,1152]{2,1,0:T(8,128)(2,1)} %collective-permute-done.3.refs_3_), channel_id=1, source_target_pairs={{0,12},{1,13},{2,14},{3,15},{4,0},{5,1},{6,2},{7,3},{8,4},{9,5},{1... | collective-permute-start | bytes 2211848 | tf_op jit(solution)/shard_map/ppermute | solution.py:34
  90.8 5.0 %collective-permute-start.11 = (f32[4,320,128]{2,1,0:T(8,128)S(1)}, f32[4,320,128]{2,1,0:T(8,128)S(1)}, u32[]{:S(2)}, u32[]{:S(2)}) collective-permute-start(f32[4,320,128]{2,1,0:T(8,128)S(1)} %get-tuple-element.18), channel_id=1, source_target_pairs={{0,1},{1,0},{2,3},{3,2},{4,5},{5,4},{6,7},{7,6},{8,9},{9,8},{10,11... | collective-permute-start | bytes 1966088 | tf_op jit(solution)/shard_map/ppermute | solution.py:34
  90.9 8.6 %collective-permute-start.16 = (f32[320,128]{1,0:T(8,128)S(1)}, f32[320,128]{1,0:T(8,128)S(1)}, u32[]{:S(2)}, u32[]{:S(2)}) collective-permute-start(f32[320,128]{1,0:T(8,128)S(1)} %get-tuple-element.20), channel_id=1, source_target_pairs={{0,64},{1,65},{2,66},{3,67},{4,68},{5,69},{6,70},{7,71},{8,72},{9,... | collective-permute-start | bytes 491528 | tf_op jit(solution)/shard_map/ppermute | solution.py:34
  92.5 10.0 %collective-permute-start.17 = (f32[320,128]{1,0:T(8,128)S(1)}, f32[320,128]{1,0:T(8,128)S(1)}, u32[]{:S(2)}, u32[]{:S(2)}) collective-permute-start(f32[320,128]{1,0:T(8,128)S(1)} %get-tuple-element.21), channel_id=1, source_target_pairs={{0,32},{1,33},{2,34},{3,35},{4,36},{5,37},{6,38},{7,39},{8,40},{9,... | collective-permute-start | bytes 491528 | tf_op jit(solution)/shard_map/ppermute | solution.py:34
  94.9 8.1 %collective-permute-start.18 = (f32[320,128]{1,0:T(8,128)S(1)}, f32[320,128]{1,0:T(8,128)S(1)}, u32[]{:S(2)}, u32[]{:S(2)}) collective-permute-start(f32[320,128]{1,0:T(8,128)S(1)} %get-tuple-element.22), channel_id=1, source_target_pairs={{0,96},{1,97},{2,98},{3,99},{4,100},{5,101},{6,102},{7,103},{8,104... | collective-permute-start | bytes 491528 | tf_op jit(solution)/shard_map/ppermute | solution.py:34
  95.9 8.9 %collective-permute-start.12 = (f32[320,128]{1,0:T(8,128)S(1)}, f32[320,128]{1,0:T(8,128)S(1)}, u32[]{:S(2)}, u32[]{:S(2)}) collective-permute-start(f32[320,128]{1,0:T(8,128)S(1)} %get-tuple-element.23), channel_id=1, source_target_pairs={{0,8},{1,9},{2,10},{3,11},{4,12},{5,13},{6,14},{7,15},{8,0},{9,1},... | collective-permute-start | bytes 491528 | tf_op jit(solution)/shard_map/ppermute | solution.py:34
  96.7 9.9 %collective-permute-start.13 = (f32[320,128]{1,0:T(8,128)S(1)}, f32[320,128]{1,0:T(8,128)S(1)}, u32[]{:S(2)}, u32[]{:S(2)}) collective-permute-start(f32[320,128]{1,0:T(8,128)S(1)} %get-tuple-element.25), channel_id=1, source_target_pairs={{0,4},{1,5},{2,6},{3,7},{4,8},{5,9},{6,10},{7,11},{8,12},{9,13},{1... | collective-permute-start | bytes 491528 | tf_op jit(solution)/shard_map/ppermute | solution.py:34
  99.5 7.2 %collective-permute-start.14 = (f32[320,128]{1,0:T(8,128)S(1)}, f32[320,128]{1,0:T(8,128)S(1)}, u32[]{:S(2)}, u32[]{:S(2)}) collective-permute-start(f32[320,128]{1,0:T(8,128)S(1)} %get-tuple-element.24), channel_id=1, source_target_pairs={{0,12},{1,13},{2,14},{3,15},{4,0},{5,1},{6,2},{7,3},{8,4},{9,5},{1... | collective-permute-start | bytes 491528 | tf_op jit(solution)/shard_map/ppermute | solution.py:34
  103.0 6.0 %collective-permute-start.19 = (f32[160,128]{1,0:T(8,128)S(1)}, f32[160,128]{1,0:T(8,128)S(1)}, u32[]{:S(2)}, u32[]{:S(2)}) collective-permute-start(f32[160,128]{1,0:T(8,128)S(1)} %slice.39), channel_id=1, source_target_pairs={{0,16},{1,17},{2,18},{3,19},{4,20},{5,21},{6,22},{7,23},{8,24},{9,... | collective-permute-start | bytes 245768 | tf_op jit(solution)/shard_map/ppermute | solution.py:34
  106.7 4.5 %collective-permute-start.15 = (f32[160,128]{1,0:T(8,128)S(1)}, f32[160,128]{1,0:T(8,128)S(1)}, u32[]{:S(2)}, u32[]{:S(2)}) collective-permute-start(f32[160,128]{1,0:T(8,128)S(1)} %slice.37), channel_id=1, source_target_pairs={{0,2},{1,3},{2,0},{3,1},{4,6},{5,7},{6,4},{7,5},{8,10},{9,11},{10,... | collective-permute-start | bytes 245768 | tf_op jit(solution)/shard_map/ppermute | solution.py:34

commit v12 on v11

--- a/solution.py
+++ b/solution.py
@@ -145,7 +145,6 @@
 
     first_copies = [start(col_refs[i].at[b], cols.at[block(step, b)]) for i, step in enumerate((0, 1, 3)) for b in (0, 1)]
     first_copies += [start(col_refs[3 + b], cols.at[block(2, b)]) for b in (0, 1)] + row_copies(0)
-    next_rows, next_kern = [], kern_copies(0)
     if last:
         col_sum[...] = col_in[...]
         for i, at in enumerate((0, 1, 3)):
@@ -155,6 +154,7 @@
         col_sum[...] = jnp.zeros_like(col_sum)
     for copy in first_copies:
         copy.wait()
+    next_rows, next_kern = [], kern_copies(0)
     col_wide = cols[...].reshape(COL_PTS, WIDE)
 
     for t in range(tiles):

time: 112 us -> 112 us (level)
  no operation moved by 1% of the time
where the time goes in v12:
time: 112 us
  blocking collectives  32.9 us (29%)
  waiting for transfers between devices  29.9 us (27%)
  Pallas kernels  23.8 us (21%)
  starting transfers between devices  21.1 us (19%)
  other arithmetic  1.98 us (2%)
  local copies, waits for them, and re-layouts  1.85 us (2%)
    all_to_all x1, blocking collectives, local(): lax.all_to_all(packed, AXES, split_axis=0, concat_axis=0, tiled=True)  32.9 us
    ppermute x20, waiting for transfers between devices, send(): return lax.ppermute(x, AXES, moved(**steps))  29.9 us
    pallas_call x2, Pallas kernels, tile_call(): pl.pallas_call(functools.partial(tile_kernel, z_steps), in_specs=[pl.Bloc...  21.7 us
    ppermute x20, starting transfers between devices, send(): return lax.ppermute(x, AXES, moved(**steps))  21.1 us
  transfers between devices with their start and end apart: 20, of which 10 were waited for; matrix products, arithmetic and copies ran while one was open for 1% of the time, Pallas kernels for 13%

profile of v12, /device:TPU:0, one launch (start us, length us, event | category | flops | bytes accessed | tf_op | source)
XLA Modules:
  0.0 111.9 jit_solution(15480604728438934978)
XLA Ops:
  0.0 1.1 convert_reduce_fusion
  1.1 0.1 reshape.22.tgt
  1.2 0.0 copy-start.3
  1.2 1.0 copy-done.3
  2.2 0.5 pack.1
  2.7 32.9 %all_to_all.5 = bf16[128,8,640]{2,1,0:T(8,128)(2,1)S(1)} all-to-all(bf16[128,8,640]{2,1,0:T(8,128)(2,1)S(1)} %bitcast.29), channel_id=1, replica_groups=mesh['row'=8,'col'=16] {'row','col'}, dimensions={0} | all-to-all | bytes 2621440 | tf_op jit(solution)/shard_map/all_to_all | solution.py:244
  35.6 1.0 unpack_cols.1.col_pair.refs_6_.refs_2_
  36.6 0.6 unpack_rows.1.refs_0_
  37.3 0.0 copy-start.4
  37.3 0.3 collective-permute-start.2
  37.6 1.8 %collective-permute-start = (bf16[2,160,1152]{2,1,0:T(8,128)(2,1)S(1)}, bf16[2,160,1152]{2,1,0:T(8,128)(2,1)}, u32[]{:S(2)}, u32[]{:S(2)}) collective-permute-start(bf16[2,160,1152]{2,1,0:T(8,128)(2,1)S(1)} %unpack_rows.1.refs_0_), channel_id=1, source_target_pairs={{0,4},{1,5},{2,6},{3,7},{4,8},{5,9},{6,10},{7,11},{8,12},{9,13},{1... | collective-permute-start | bytes 2211848 | tf_op jit(solution)/shard_map/ppermute | solution.py:34
  39.4 0.0 collective-permute-start.6
  39.4 3.2 %collective-permute-start.5 = (bf16[2,160,1152]{2,1,0:T(8,128)(2,1)S(1)}, bf16[2,160,1152]{2,1,0:T(8,128)(2,1)S(1)}, u32[]{:S(2)}, u32[]{:S(2)}) collective-permute-start(bf16[2,160,1152]{2,1,0:T(8,128)(2,1)S(1)} %unpack_cols.1.col_pair.refs_6_.refs_2_), channel_id=1, source_target_pairs={{0,96},{1,97},{2,98},{3,99},{4,100},{5,101},{6,102},{7,103},{8,104... | collective-permute-start | bytes 2211848 | tf_op jit(solution)/shard_map/ppermute | solution.py:34
  42.6 12.7 %collective-permute-done.2.refs_2_ = bf16[2,160,1152]{2,1,0:T(8,128)(2,1)} collective-permute-done((bf16[2,160,1152]{2,1,0:T(8,128)(2,1)S(1)}, bf16[2,160,1152]{2,1,0:T(8,128)(2,1)}, u32[]{:S(2)}, u32[]{:S(2)}) %collective-permute-start.2) | collective-permute-done | bytes 737312 | tf_op jit(solution)/shard_map/ppermute | solution.py:34
  55.3 1.3 %collective-permute-done.refs_4_ = bf16[2,160,1152]{2,1,0:T(8,128)(2,1)} collective-permute-done((bf16[2,160,1152]{2,1,0:T(8,128)(2,1)S(1)}, bf16[2,160,1152]{2,1,0:T(8,128)(2,1)}, u32[]{:S(2)}, u32[]{:S(2)}) %collective-permute-start) | collective-permute-done | bytes 737312 | tf_op jit(solution)/shard_map/ppermute | solution.py:34
  56.6 1.3 %collective-permute-done.6.pair.refs_8_.refs_4_ = bf16[2,160,1152]{2,1,0:T(8,128)(2,1)S(1)} collective-permute-done((bf16[2,160,1152]{2,1,0:T(8,128)(2,1)S(1)}, bf16[2,160,1152]{2,1,0:T(8,128)(2,1)S(1)}, u32[]{:S(2)}, u32[]{:S(2)}) %collective-permute-start.6) | collective-permute-done | bytes 737312 | tf_op jit(solution)/shard_map/ppermute | solution.py:34
  57.9 0.1 collective-permute-start.7
  58.1 3.3 %collective-permute-start.8 = (bf16[160,1152]{1,0:T(8,128)(2,1)S(1)}, bf16[160,1152]{1,0:T(8,128)(2,1)}, u32[]{:S(2)}, u32[]{:S(2)}) collective-permute-start(bf16[160,1152]{1,0:T(8,128)(2,1)S(1)} %cut.3), channel_id=1, source_target_pairs={{0,96},{1,97},{2,98},{3,99},{4,100},{5,101},{6,102},{7,103},{8,104... | collective-permute-start | bytes 1105928 | tf_op jit(solution)/shard_map/ppermute | solution.py:34
  61.3 0.1 and_select_fusion
  61.4 0.1 copy.10
  61.5 0.1 broadcast_in_dim.12
  61.6 0.2 reshape_reshape.7.refs_13_.refs_9_
  61.8 0.1 copy.9
  61.8 0.1 broadcast_in_dim.10
  61.9 0.2 reshape_reshape.6.refs_12_.refs_8_
  62.1 0.1 stack.23.me
  62.2 0.3 collective-permute-start.1
  62.5 3.0 %collective-permute-start.4 = (bf16[2,160,1152]{2,1,0:T(8,128)(2,1)}, bf16[2,160,1152]{2,1,0:T(8,128)(2,1)S(1)}, u32[]{:S(2)}, u32[]{:S(2)}) collective-permute-start(bf16[2,160,1152]{2,1,0:T(8,128)(2,1)} %collective-permute-done.3.refs_3_), channel_id=1, source_target_pairs={{0,12},{1,13},{2,14},{3,15},{4,0},{5,1},{6,2},{7,3},{8,4},{9,5},{1... | collective-permute-start | bytes 2211848 | tf_op jit(solution)/shard_map/ppermute | solution.py:34
  65.5 3.6 %collective-permute-done.7.refs_9_.refs_5_ = bf16[160,1152]{1,0:T(8,128)(2,1)} collective-permute-done((bf16[160,1152]{1,0:T(8,128)(2,1)S(1)}, bf16[160,1152]{1,0:T(8,128)(2,1)}, u32[]{:S(2)}, u32[]{:S(2)}) %collective-permute-start.7) | collective-permute-done | bytes 368672 | tf_op jit(solution)/shard_map/ppermute | solution.py:34
  69.1 14.9 %near_tiles.1 = (f32[3,320,128]{2,1,0:T(8,128)S(1)}, f32[3,320,128]{2,1,0:T(8,128)S(1)}, f32[8,160,128]{2,1,0:T(8,128)S(1)}) custom-call(s32[5]{0:T(128)S(1)} %stack.23.me, bf16[2,160,1152]{2,1,0:T(8,128)(2,1)S(1)} %unpack_rows.1.refs_0_, bf16[2,160,1152]{2,1,0:T(8,128)(2,1)} %collective-permute-done.9.refs_1_, ...), custom_call_target="tpu_custom_call" | custom-call | flops 60000002048 | bytes 120000000 | tf_op jit(solution)/shard_map/near_tiles/pallas_call | solution.py:217
  84.1 6.7 %far_tile.1 = (f32[4,320,128]{2,1,0:T(8,128)S(1)}, f32[4,320,128]{2,1,0:T(8,128)S(1)}, f32[320,128]{1,0:T(8,128)S(1)}, f32[320,128]{1,0:T(8,128)S(1)}, f32[320,128]{1,0:T(8,128)S(1)}, /*index=5*/f32[320,128]{1,0:T(8,128)S(1)}) custom-call(s32[5]{0:T(128)S(1)} %stack.23.me, bf16[2,160,1152]{2,1,0:T(8,128)(2,1)S(1)} %collective-permute-done.1.refs_0_, ...), custom_call_target="tpu_custom_call" | custom-call | flops 20000000000 | bytes 40000000 | tf_op jit(solution)/shard_map/far_tile/pallas_call | solution.py:217
  90.8 0.1 collective-permute-start.11
  90.9 1.6 %collective-permute-start.16 = (f32[320,128]{1,0:T(8,128)S(1)}, f32[320,128]{1,0:T(8,128)S(1)}, u32[]{:S(2)}, u32[]{:S(2)}) collective-permute-start(f32[320,128]{1,0:T(8,128)S(1)} %get-tuple-element.20), channel_id=1, source_target_pairs={{0,64},{1,65},{2,66},{3,67},{4,68},{5,69},{6,70},{7,71},{8,72},{9,... | collective-permute-start | bytes 491528 | tf_op jit(solution)/shard_map/ppermute | solution.py:34
  92.5 2.3 %collective-permute-start.17 = (f32[320,128]{1,0:T(8,128)S(1)}, f32[320,128]{1,0:T(8,128)S(1)}, u32[]{:S(2)}, u32[]{:S(2)}) collective-permute-start(f32[320,128]{1,0:T(8,128)S(1)} %get-tuple-element.21), channel_id=1, source_target_pairs={{0,32},{1,33},{2,34},{3,35},{4,36},{5,37},{6,38},{7,39},{8,40},{9,... | collective-permute-start | bytes 491528 | tf_op jit(solution)/shard_map/ppermute | solution.py:34
  94.8 0.9 collective-permute-start.18
  95.7 0.1 add.46
  95.9 0.9 collective-permute-start.12
  96.7 0.5 collective-permute-start.13
  97.2 2.3 %collective-permute-done.16 = f32[320,128]{1,0:T(8,128)S(1)} collective-permute-done((f32[320,128]{1,0:T(8,128)S(1)}, f32[320,128]{1,0:T(8,128)S(1)}, u32[]{:S(2)}, u32[]{:S(2)}) %collective-permute-start.16) | collective-permute-done | bytes 163872 | tf_op jit(solution)/shard_map/ppermute | solution.py:34
  99.5 0.5 collective-permute-start.14
  100.0 2.5 %collective-permute-done.17 = f32[320,128]{1,0:T(8,128)S(1)} collective-permute-done((f32[320,128]{1,0:T(8,128)S(1)}, f32[320,128]{1,0:T(8,128)S(1)}, u32[]{:S(2)}, u32[]{:S(2)}) %collective-permute-start.17) | collective-permute-done | bytes 163872 | tf_op jit(solution)/shard_map/ppermute | solution.py:34
  102.5 0.4 collective-permute-done.18
  103.0 1.9 %collective-permute-start.19 = (f32[160,128]{1,0:T(8,128)S(1)}, f32[160,128]{1,0:T(8,128)S(1)}, u32[]{:S(2)}, u32[]{:S(2)}) collective-permute-start(f32[160,128]{1,0:T(8,128)S(1)} %slice.39), channel_id=1, source_target_pairs={{0,16},{1,17},{2,18},{3,19},{4,20},{5,21},{6,22},{7,23},{8,24},{9,... | collective-permute-start | bytes 245768 | tf_op jit(solution)/shard_map/ppermute | solution.py:34
  104.8 1.8 %collective-permute-done.13 = f32[320,128]{1,0:T(8,128)S(1)} collective-permute-done((f32[320,128]{1,0:T(8,128)S(1)}, f32[320,128]{1,0:T(8,128)S(1)}, u32[]{:S(2)}, u32[]{:S(2)}) %collective-permute-start.13) | collective-permute-done | bytes 163872 | tf_op jit(solution)/shard_map/ppermute | solution.py:34
  106.7 0.5 collective-permute-start.15
  107.2 1.7 %collective-permute-done.19 = f32[160,128]{1,0:T(8,128)S(1)} collective-permute-done((f32[160,128]{1,0:T(8,128)S(1)}, f32[160,128]{1,0:T(8,128)S(1)}, u32[]{:S(2)}, u32[]{:S(2)}) %collective-permute-start.19) | collective-permute-done | bytes 81952 | tf_op jit(solution)/shard_map/ppermute | solution.py:34
  109.0 2.2 %collective-permute-done.15 = f32[160,128]{1,0:T(8,128)S(1)} collective-permute-done((f32[160,128]{1,0:T(8,128)S(1)}, f32[160,128]{1,0:T(8,128)S(1)}, u32[]{:S(2)}, u32[]{:S(2)}) %collective-permute-start.15) | collective-permute-done | bytes 81952 | tf_op jit(solution)/shard_map/ppermute | solution.py:34
  111.2 0.7 fusion.3
  (30 shorter events, 0.2 us)
Async XLA Ops:
  1.2 1.0 copy-start.3
  36.6 2.8 %copy-start = (bf16[2,160,1152]{2,1,0:T(8,128)(2,1)}, bf16[2,160,1152]{2,1,0:T(8,128)(2,1)S(1)}, u32[]{:S(2)}) copy-start(bf16[2,160,1152]{2,1,0:T(8,128)(2,1)S(1)} %unpack_cols.1.col_pair.refs_6_.refs_2_) | copy-start | bytes 2211844
  37.3 24.1 %copy-start.4 = (s32[1,16,8,1]{1,3,2,0:T(1,128)S(1)}, s32[1,16,8,1]{1,3,2,0:T(1,128)}, u32[]{:S(2)}) copy-start(s32[1,16,8,1]{1,3,2,0:T(1,128)} %param.7) | copy-start | bytes 1540
  37.3 18.0 %collective-permute-start.2 = (bf16[2,160,1152]{2,1,0:T(8,128)(2,1)S(1)}, bf16[2,160,1152]{2,1,0:T(8,128)(2,1)}, u32[]{:S(2)}, u32[]{:S(2)}) collective-permute-start(bf16[2,160,1152]{2,1,0:T(8,128)(2,1)S(1)} %unpack_rows.1.refs_0_), channel_id=1, source_target_pairs={{0,12},{1,13},{2,14},{3,15},{4,0},{5,1},{6,2},{7,3},{8,4},{9,5},{1... | collective-permute-start | bytes 2211848 | tf_op jit(solution)/shard_map/ppermute | solution.py:34
  37.6 19.0 %collective-permute-start = (bf16[2,160,1152]{2,1,0:T(8,128)(2,1)S(1)}, bf16[2,160,1152]{2,1,0:T(8,128)(2,1)}, u32[]{:S(2)}, u32[]{:S(2)}) collective-permute-start(bf16[2,160,1152]{2,1,0:T(8,128)(2,1)S(1)} %unpack_rows.1.refs_0_), channel_id=1, source_target_pairs={{0,4},{1,5},{2,6},{3,7},{4,8},{5,9},{6,10},{7,11},{8,12},{9,13},{1... | collective-permute-start | bytes 2211848 | tf_op jit(solution)/shard_map/ppermute | solution.py:34
  39.4 18.5 %collective-permute-start.6 = (bf16[2,160,1152]{2,1,0:T(8,128)(2,1)S(1)}, bf16[2,160,1152]{2,1,0:T(8,128)(2,1)S(1)}, u32[]{:S(2)}, u32[]{:S(2)}) collective-permute-start(bf16[2,160,1152]{2,1,0:T(8,128)(2,1)S(1)} %unpack_cols.1.col_pair.refs_6_.refs_2_), channel_id=1, source_target_pairs={{0,32},{1,33},{2,34},{3,35},{4,36},{5,37},{6,38},{7,39},{8,40},{9,... | collective-permute-start | bytes 2211848 | tf_op jit(solution)/shard_map/ppermute | solution.py:34
  39.4 18.6 %collective-permute-start.5 = (bf16[2,160,1152]{2,1,0:T(8,128)(2,1)S(1)}, bf16[2,160,1152]{2,1,0:T(8,128)(2,1)S(1)}, u32[]{:S(2)}, u32[]{:S(2)}) collective-permute-start(bf16[2,160,1152]{2,1,0:T(8,128)(2,1)S(1)} %unpack_cols.1.col_pair.refs_6_.refs_2_), channel_id=1, source_target_pairs={{0,96},{1,97},{2,98},{3,99},{4,100},{5,101},{6,102},{7,103},{8,104... | collective-permute-start | bytes 2211848 | tf_op jit(solution)/shard_map/ppermute | solution.py:34
  42.6 19.6 %collective-permute-start.9 = (bf16[2,160,1152]{2,1,0:T(8,128)(2,1)S(1)}, bf16[2,160,1152]{2,1,0:T(8,128)(2,1)}, u32[]{:S(2)}, u32[]{:S(2)}) collective-permute-start(bf16[2,160,1152]{2,1,0:T(8,128)(2,1)S(1)} %unpack_rows.1.refs_0_), channel_id=1, source_target_pairs={{0,1},{1,0},{2,3},{3,2},{4,5},{5,4},{6,7},{7,6},{8,9},{9,8},{10,11... | collective-permute-start | bytes 2211848 | tf_op jit(solution)/shard_map/ppermute | solution.py:34
  55.3 7.2 %collective-permute-start.3 = (bf16[2,160,1152]{2,1,0:T(8,128)(2,1)}, bf16[2,160,1152]{2,1,0:T(8,128)(2,1)}, u32[]{:S(2)}, u32[]{:S(2)}) collective-permute-start(bf16[2,160,1152]{2,1,0:T(8,128)(2,1)} %collective-permute-done.2.refs_2_), channel_id=1, source_target_pairs={{0,1},{1,0},{2,3},{3,2},{4,5},{5,4},{6,7},{7,6},{8,9},{9,8},{10,11... | collective-permute-start | bytes 2211848 | tf_op jit(solution)/shard_map/ppermute | solution.py:34
  56.6 12.5 %collective-permute-start.10 = (bf16[2,160,1152]{2,1,0:T(8,128)(2,1)}, bf16[2,160,1152]{2,1,0:T(8,128)(2,1)}, u32[]{:S(2)}, u32[]{:S(2)}) collective-permute-start(bf16[2,160,1152]{2,1,0:T(8,128)(2,1)} %collective-permute-done.refs_4_), channel_id=1, source_target_pairs={{0,1},{1,0},{2,3},{3,2},{4,5},{5,4},{6,7},{7,6},{8,9},{9,8},{10,11... | collective-permute-start | bytes 2211848 | tf_op jit(solution)/shard_map/ppermute | solution.py:34
  57.9 4.0 %copy-start.1 = (bf16[2,160,1152]{2,1,0:T(8,128)(2,1)}, bf16[2,160,1152]{2,1,0:T(8,128)(2,1)S(1)}, u32[]{:S(2)}) copy-start(bf16[2,160,1152]{2,1,0:T(8,128)(2,1)S(1)} %collective-permute-done.6.pair.refs_8_.refs_4_) | copy-start | bytes 2211844
  57.9 11.1 %collective-permute-start.7 = (bf16[160,1152]{1,0:T(8,128)(2,1)S(1)}, bf16[160,1152]{1,0:T(8,128)(2,1)}, u32[]{:S(2)}, u32[]{:S(2)}) collective-permute-start(bf16[160,1152]{1,0:T(8,128)(2,1)S(1)} %cut.2), channel_id=1, source_target_pairs={{0,32},{1,33},{2,34},{3,35},{4,36},{5,37},{6,38},{7,39},{8,40},{9,... | collective-permute-start | bytes 1105928 | tf_op jit(solution)/shard_map/ppermute | solution.py:34
  58.0 11.1 %copy-start.2 = (bf16[2,160,1152]{2,1,0:T(8,128)(2,1)}, bf16[2,160,1152]{2,1,0:T(8,128)(2,1)S(1)}, u32[]{:S(2)}) copy-start(bf16[2,160,1152]{2,1,0:T(8,128)(2,1)S(1)} %collective-permute-done.5.pair.refs_7_.refs_3_) | copy-start | bytes 2211844
  58.1 11.0 %collective-permute-start.8 = (bf16[160,1152]{1,0:T(8,128)(2,1)S(1)}, bf16[160,1152]{1,0:T(8,128)(2,1)}, u32[]{:S(2)}, u32[]{:S(2)}) collective-permute-start(bf16[160,1152]{1,0:T(8,128)(2,1)S(1)} %cut.3), channel_id=1, source_target_pairs={{0,96},{1,97},{2,98},{3,99},{4,100},{5,101},{6,102},{7,103},{8,104... | collective-permute-start | bytes 1105928 | tf_op jit(solution)/shard_map/ppermute | solution.py:34
  62.2 21.8 %collective-permute-start.1 = (bf16[2,160,1152]{2,1,0:T(8,128)(2,1)}, bf16[2,160,1152]{2,1,0:T(8,128)(2,1)S(1)}, u32[]{:S(2)}, u32[]{:S(2)}) collective-permute-start(bf16[2,160,1152]{2,1,0:T(8,128)(2,1)} %collective-permute-done.refs_4_), channel_id=1, source_target_pairs={{0,4},{1,5},{2,6},{3,7},{4,8},{5,9},{6,10},{7,11},{8,12},{9,13},{1... | collective-permute-start | bytes 2211848 | tf_op jit(solution)/shard_map/ppermute | solution.py:34
  62.5 21.5 %collective-permute-start.4 = (bf16[2,160,1152]{2,1,0:T(8,128)(2,1)}, bf16[2,160,1152]{2,1,0:T(8,128)(2,1)S(1)}, u32[]{:S(2)}, u32[]{:S(2)}) collective-permute-start(bf16[2,160,1152]{2,1,0:T(8,128)(2,1)} %collective-permute-done.3.refs_3_), channel_id=1, source_target_pairs={{0,12},{1,13},{2,14},{3,15},{4,0},{5,1},{6,2},{7,3},{8,4},{9,5},{1... | collective-permute-start | bytes 2211848 | tf_op jit(solution)/shard_map/ppermute | solution.py:34
  90.8 5.0 %collective-permute-start.11 = (f32[4,320,128]{2,1,0:T(8,128)S(1)}, f32[4,320,128]{2,1,0:T(8,128)S(1)}, u32[]{:S(2)}, u32[]{:S(2)}) collective-permute-start(f32[4,320,128]{2,1,0:T(8,128)S(1)} %get-tuple-element.18), channel_id=1, source_target_pairs={{0,1},{1,0},{2,3},{3,2},{4,5},{5,4},{6,7},{7,6},{8,9},{9,8},{10,11... | collective-permute-start | bytes 1966088 | tf_op jit(solution)/shard_map/ppermute | solution.py:34
  90.9 8.6 %collective-permute-start.16 = (f32[320,128]{1,0:T(8,128)S(1)}, f32[320,128]{1,0:T(8,128)S(1)}, u32[]{:S(2)}, u32[]{:S(2)}) collective-permute-start(f32[320,128]{1,0:T(8,128)S(1)} %get-tuple-element.20), channel_id=1, source_target_pairs={{0,64},{1,65},{2,66},{3,67},{4,68},{5,69},{6,70},{7,71},{8,72},{9,... | collective-permute-start | bytes 491528 | tf_op jit(solution)/shard_map/ppermute | solution.py:34
  92.5 10.0 %collective-permute-start.17 = (f32[320,128]{1,0:T(8,128)S(1)}, f32[320,128]{1,0:T(8,128)S(1)}, u32[]{:S(2)}, u32[]{:S(2)}) collective-permute-start(f32[320,128]{1,0:T(8,128)S(1)} %get-tuple-element.21), channel_id=1, source_target_pairs={{0,32},{1,33},{2,34},{3,35},{4,36},{5,37},{6,38},{7,39},{8,40},{9,... | collective-permute-start | bytes 491528 | tf_op jit(solution)/shard_map/ppermute | solution.py:34
  94.8 8.1 %collective-permute-start.18 = (f32[320,128]{1,0:T(8,128)S(1)}, f32[320,128]{1,0:T(8,128)S(1)}, u32[]{:S(2)}, u32[]{:S(2)}) collective-permute-start(f32[320,128]{1,0:T(8,128)S(1)} %get-tuple-element.22), channel_id=1, source_target_pairs={{0,96},{1,97},{2,98},{3,99},{4,100},{5,101},{6,102},{7,103},{8,104... | collective-permute-start | bytes 491528 | tf_op jit(solution)/shard_map/ppermute | solution.py:34
  95.9 9.0 %collective-permute-start.12 = (f32[320,128]{1,0:T(8,128)S(1)}, f32[320,128]{1,0:T(8,128)S(1)}, u32[]{:S(2)}, u32[]{:S(2)}) collective-permute-start(f32[320,128]{1,0:T(8,128)S(1)} %get-tuple-element.23), channel_id=1, source_target_pairs={{0,8},{1,9},{2,10},{3,11},{4,12},{5,13},{6,14},{7,15},{8,0},{9,1},... | collective-permute-start | bytes 491528 | tf_op jit(solution)/shard_map/ppermute | solution.py:34
  96.7 9.9 %collective-permute-start.13 = (f32[320,128]{1,0:T(8,128)S(1)}, f32[320,128]{1,0:T(8,128)S(1)}, u32[]{:S(2)}, u32[]{:S(2)}) collective-permute-start(f32[320,128]{1,0:T(8,128)S(1)} %get-tuple-element.25), channel_id=1, source_target_pairs={{0,4},{1,5},{2,6},{3,7},{4,8},{5,9},{6,10},{7,11},{8,12},{9,13},{1... | collective-permute-start | bytes 491528 | tf_op jit(solution)/shard_map/ppermute | solution.py:34
  99.5 7.2 %collective-permute-start.14 = (f32[320,128]{1,0:T(8,128)S(1)}, f32[320,128]{1,0:T(8,128)S(1)}, u32[]{:S(2)}, u32[]{:S(2)}) collective-permute-start(f32[320,128]{1,0:T(8,128)S(1)} %get-tuple-element.24), channel_id=1, source_target_pairs={{0,12},{1,13},{2,14},{3,15},{4,0},{5,1},{6,2},{7,3},{8,4},{9,5},{1... | collective-permute-start | bytes 491528 | tf_op jit(solution)/shard_map/ppermute | solution.py:34
  103.0 6.0 %collective-permute-start.19 = (f32[160,128]{1,0:T(8,128)S(1)}, f32[160,128]{1,0:T(8,128)S(1)}, u32[]{:S(2)}, u32[]{:S(2)}) collective-permute-start(f32[160,128]{1,0:T(8,128)S(1)} %slice.39), channel_id=1, source_target_pairs={{0,16},{1,17},{2,18},{3,19},{4,20},{5,21},{6,22},{7,23},{8,24},{9,... | collective-permute-start | bytes 245768 | tf_op jit(solution)/shard_map/ppermute | solution.py:34
  106.7 4.5 %collective-permute-start.15 = (f32[160,128]{1,0:T(8,128)S(1)}, f32[160,128]{1,0:T(8,128)S(1)}, u32[]{:S(2)}, u32[]{:S(2)}) collective-permute-start(f32[160,128]{1,0:T(8,128)S(1)} %slice.37), channel_id=1, source_target_pairs={{0,2},{1,3},{2,0},{3,1},{4,6},{5,7},{6,4},{7,5},{8,10},{9,11},{10,... | collective-permute-start | bytes 245768 | tf_op jit(solution)/shard_map/ppermute | solution.py:34
